TPU v7x, 32 devices: a whole 2x2x4 slice. The times are simulated.
32 devices in a mesh: pipe: 2 (over y), wide: 8 (over z, x), tp: 2 (over core).
Axes of the slice: x: 2, y: 2, z: 4, core: 2. Of those that a mesh axis runs over, the one named last changes fastest.
Arguments:
- block_input: bfloat16 [2, 2, 1024, 768], P(None, None, ('wide', 'tp')), may hold values from -6 to 6
- out_cotangent: bfloat16 [2, 2, 1024, 768], P(None, None, ('wide', 'tp')), may hold values from -6 to 6
- routes: int32 [2, 2, 2, 1024, 1], P('pipe', None, None, 'wide'), may hold values from 0 to 7; in each aligned block of 64 rows (0 to 63, 64 to 127, ..., all dimensions but the last counted through in order) at most 12 rows name the same one
- attn_gain: bfloat16 [2, 768], P('pipe', ('wide', 'tp')), may hold values from 0.5 to 1.5
- query_weight: bfloat16 [2, 768, 768], P('pipe', 'wide', 'tp'), may hold values from -0.21875 to 0.21875
- key_weight: bfloat16 [2, 768, 768], P('pipe', 'wide', 'tp'), may hold values from -0.21875 to 0.21875
- value_weight: bfloat16 [2, 768, 768], P('pipe', 'wide', 'tp'), may hold values from -0.21875 to 0.21875
- output_weight: bfloat16 [2, 768, 768], P('pipe', 'tp', 'wide'), may hold values from -0.4375 to 0.4375
- moe_gain: bfloat16 [2, 768], P('pipe', ('wide', 'tp')), may hold values from 0.5 to 1.5
- router_weight: bfloat16 [2, 768, 8], P('pipe', ('wide', 'tp')), may hold values from -0.15625 to 0.15625
- expert_in: bfloat16 [2, 8, 768, 3072], P('pipe', 'wide', None, 'tp'), may hold values from -0.21875 to 0.21875
- expert_out: bfloat16 [2, 8, 3072, 768], P('pipe', 'wide', 'tp'), may hold values from -0.3125 to 0.3125
Outputs:
- layer_outputs: bfloat16 [2, 2, 2, 1024, 768], P('pipe', None, None, ('wide', 'tp'))
- input_grads: bfloat16 [2, 2, 2, 1024, 768], P('pipe', None, None, ('wide', 'tp'))
- attn_gain_grad: float32 [2, 768], P('pipe', ('wide', 'tp'))
- query_grad: float32 [2, 768, 768], P('pipe', 'wide', 'tp')
- key_grad: float32 [2, 768, 768], P('pipe', 'wide', 'tp')
- value_grad: float32 [2, 768, 768], P('pipe', 'wide', 'tp')
- output_grad: float32 [2, 768, 768], P('pipe', 'tp', 'wide')
- moe_gain_grad: float32 [2, 768], P('pipe', ('wide', 'tp'))
- router_grad: float32 [2, 768, 8], P('pipe', ('wide', 'tp'))
- expert_in_grad: float32 [2, 8, 768, 3072], P('pipe', 'wide', None, 'tp')
- expert_out_grad: float32 [2, 8, 3072, 768], P('pipe', 'wide', 'tp')
Inputs may be any that keep to these rules, and one draw needn't show every extreme that they name: `routes`: within each aligned block of 64 positions of one sequence (all leading dimensions taken in order), no expert is named more than 12 times, and some block names one expert exactly 12 times.
All inputs are finite; a program needn't handle non-finite values.
Results may differ from a plain program's by a relative error of at most 0.03.
Values may be sent and summed in bfloat16 or wider, within the bound.
No kernel may reach another device: no remote copies, remote signals or barrier semaphores. Data moves between devices by JAX's collectives and lax.ppermute only.
A program may use at most 192 MiB of HBM per device.

v0:
```python
import jax
import jax.numpy as jnp
from jax import lax
from jax.sharding import PartitionSpec as P

HEAD_DIM = 64


EPSILON = 1e-06
SCORE_SCALE = 0.125
FLOOR_PEAK = -1e30
HIGHEST = lax.Precision.HIGHEST


def shortened(value):
    return jax.tree.map(lambda a: a.astype(jnp.bfloat16) if a.dtype == jnp.float32 else a, value)


def shifted(value, axis, steps):
    count = lax.axis_size(axis)
    leading, last = (max(0, -steps), min(count, count - steps))
    return lax.ppermute(value, axis, [(source, source + steps) for source in range(leading, last)])


def norm_rows(values, gain_vector):
    inverse = lax.rsqrt(jnp.mean(values * values, axis=-1, keepdims=True) + EPSILON)
    return (inverse, values * inverse * gain_vector)


def norm_back(values, inverse, gain_vector, grad_normed):
    scaled = grad_normed * gain_vector
    grad_values = inverse * scaled - values * (inverse * inverse * inverse) * jnp.mean(
        scaled * values, axis=-1, keepdims=True
    )
    grad_gain = jnp.sum(grad_normed * values * inverse, axis=(0, 1))
    return (grad_values, grad_gain)


def tp_rows(values):
    return lax.all_gather(values, "tp", axis=1, tiled=True)


def tp_sums(values):
    return lax.psum_scatter(
        values.astype(jnp.bfloat16), "tp", scatter_dimension=1, tiled=True
    ).astype(jnp.float32)


def to_experts(values):
    return lax.all_to_all(values, "wide", split_axis=0, concat_axis=0, tiled=True)


def from_experts(values):
    return lax.all_to_all(values, "wide", split_axis=0, concat_axis=0, tiled=True)


def dispatch_table(route_ctx, expert_count):
    seq_count, context_len = route_ctx.shape
    parts_count = lax.axis_size("tp")
    half_rows = context_len // parts_count
    most_rows = max(2, 3 * half_rows // (2 * expert_count))
    block_routes = route_ctx.reshape(seq_count * parts_count, half_rows)
    expert_hits = (
        block_routes[:, :, None] == jnp.arange(expert_count, dtype=jnp.int32)[None, None, :]
    ).astype(jnp.int32)
    slot_rank = jnp.sum((jnp.cumsum(expert_hits, axis=1) - 1) * expert_hits, axis=2)
    target_column = block_routes * most_rows + slot_rank
    all_columns = jnp.arange(expert_count * most_rows, dtype=jnp.int32)
    return (target_column[:, :, None] == all_columns[None, None, :]).astype(jnp.bfloat16)


def pack_rows(table, token_rows):
    feature_dim = token_rows.shape[-1]
    grouped = token_rows.reshape(table.shape[0], table.shape[1], feature_dim)
    packed = jnp.einsum("btc,btd->cbd", table, grouped, preferred_element_type=jnp.float32).astype(
        jnp.bfloat16
    )
    return packed.reshape(lax.axis_size("wide"), -1, feature_dim)


def unpack_rows(table, packed, out_shape):
    slot_rows = packed.reshape(table.shape[2], table.shape[0], packed.shape[-1])
    return jnp.einsum("btc,cbd->btd", table, slot_rows, preferred_element_type=jnp.float32).reshape(
        out_shape
    )


def fold_keys(carry, queries, key_piece, value_piece):
    peak_prev, total_prev, accum_prev = carry
    seq_count, piece_len = (key_piece.shape[0], key_piece.shape[1])
    heads_dev, head_size = (queries.shape[1], queries.shape[3])
    keys_split = key_piece.reshape(seq_count, piece_len, heads_dev, head_size)
    values_split = value_piece.reshape(seq_count, piece_len, heads_dev, head_size)
    scores = (
        jnp.einsum("shqe,skhe->shqk", queries, keys_split, preferred_element_type=jnp.float32)
        * SCORE_SCALE
    )
    peak_next = jnp.maximum(peak_prev, jnp.max(scores, axis=-1))
    fade = jnp.exp(peak_prev - peak_next)
    weights = jnp.exp(scores - peak_next[..., None])
    total_next = total_prev * fade + jnp.sum(weights, axis=-1)
    accum_next = accum_prev * fade[..., None] + jnp.einsum(
        "shqk,skhe->shqe",
        weights.astype(jnp.bfloat16),
        values_split,
        preferred_element_type=jnp.float32,
    )
    return (peak_next, total_next, accum_next)


def attend_back(queries, grad_attended, out_values, log_total, keys_whole, values_whole):
    seq_count, length = (keys_whole.shape[0], keys_whole.shape[1])
    heads_dev, head_size = (queries.shape[1], queries.shape[3])
    block_len = min(512, length)
    delta_rows = jnp.sum(grad_attended.astype(jnp.float32) * out_values, axis=-1)

    def one_block(block_index, carry):
        grad_query, grad_key_all, grad_value_all = carry
        begin = block_index * block_len
        key_block = lax.dynamic_slice_in_dim(keys_whole, begin, block_len, 1).reshape(
            seq_count, block_len, heads_dev, head_size
        )
        value_block = lax.dynamic_slice_in_dim(values_whole, begin, block_len, 1).reshape(
            seq_count, block_len, heads_dev, head_size
        )
        scores = (
            jnp.einsum("shqe,skhe->shqk", queries, key_block, preferred_element_type=jnp.float32)
            * SCORE_SCALE
        )
        probs = jnp.exp(scores - log_total[..., None])
        grad_probs = jnp.einsum(
            "shqe,skhe->shqk", grad_attended, value_block, preferred_element_type=jnp.float32
        )
        grad_scores = (probs * (grad_probs - delta_rows[..., None])).astype(jnp.bfloat16)
        grad_query = (
            grad_query
            + jnp.einsum(
                "shqk,skhe->shqe", grad_scores, key_block, preferred_element_type=jnp.float32
            )
            * SCORE_SCALE
        )
        grad_key = (
            jnp.einsum("shqk,shqe->skhe", grad_scores, queries, preferred_element_type=jnp.float32)
            * SCORE_SCALE
        )
        grad_value = jnp.einsum(
            "shqk,shqe->skhe",
            probs.astype(jnp.bfloat16),
            grad_attended,
            preferred_element_type=jnp.float32,
        )
        grad_key_all = lax.dynamic_update_slice_in_dim(
            grad_key_all, grad_key.reshape(seq_count, block_len, -1), begin, 1
        )
        grad_value_all = lax.dynamic_update_slice_in_dim(
            grad_value_all, grad_value.reshape(seq_count, block_len, -1), begin, 1
        )
        return (grad_query, grad_key_all, grad_value_all)

    start_carry = (
        jnp.zeros(queries.shape, jnp.float32),
        jnp.zeros(keys_whole.shape, jnp.float32),
        jnp.zeros(values_whole.shape, jnp.float32),
    )
    return lax.fori_loop(0, length // block_len, one_block, start_carry)


def layer_forward(inputs, route_ctx, params):
    w_query, w_key, w_value, w_output, gain_attn, gain_moe, w_router, w_in, w_out = params
    seq_count, half_rows, feature_dim = inputs.shape
    heads_dev = w_query.shape[1] // HEAD_DIM
    inverse_a, normed = norm_rows(inputs, gain_attn)
    rows_a = tp_rows(normed.astype(jnp.bfloat16))
    context_len = rows_a.shape[1]
    queries = jnp.einsum(
        "sqd,dhe->shqe",
        rows_a,
        w_query.reshape(feature_dim, heads_dev, HEAD_DIM),
        preferred_element_type=jnp.float32,
    ).astype(jnp.bfloat16)
    keys = jnp.dot(rows_a, w_key, preferred_element_type=jnp.float32).astype(jnp.bfloat16)
    values = jnp.dot(rows_a, w_value, preferred_element_type=jnp.float32).astype(jnp.bfloat16)
    start_carry = (
        jnp.full((seq_count, heads_dev, context_len), FLOOR_PEAK, jnp.float32),
        jnp.zeros((seq_count, heads_dev, context_len), jnp.float32),
        jnp.zeros(queries.shape, jnp.float32),
    )
    state = {}
    peak, total, accum = fold_keys(
        start_carry,
        queries,
        lax.all_gather(keys, "wide", axis=1, tiled=True),
        lax.all_gather(values, "wide", axis=1, tiled=True),
    )
    out_values = accum / total[..., None]
    log_total = peak + jnp.log(total)
    out_low = out_values.astype(jnp.bfloat16)
    partial_attn = jnp.einsum(
        "shqe,hed->sqd",
        out_low,
        w_output.reshape(heads_dev, HEAD_DIM, feature_dim),
        preferred_element_type=jnp.float32,
    )
    hidden = inputs + tp_sums(partial_attn)
    inverse_b, normed_moe = norm_rows(hidden, gain_moe)
    normed_b = normed_moe.astype(jnp.bfloat16)
    logits = jnp.einsum("sqd,de->sqe", normed_b, w_router, preferred_element_type=jnp.float32)
    router_probs = jax.nn.softmax(logits, axis=-1)
    own_routes = lax.dynamic_slice_in_dim(route_ctx, lax.axis_index("tp") * half_rows, half_rows, 1)
    chosen = (own_routes[..., None] == jnp.arange(w_router.shape[1], dtype=jnp.int32)).astype(
        jnp.float32
    )
    gate = jnp.sum(router_probs * chosen, axis=-1)
    rows_b = tp_rows(normed_b)
    table = dispatch_table(route_ctx, w_router.shape[1])
    arrived = to_experts(pack_rows(table, rows_b))
    wide_count, slot_count = (arrived.shape[0], arrived.shape[1])
    arrived_split = arrived.reshape(
        wide_count, w_in.shape[0], slot_count // w_in.shape[0], feature_dim
    )
    pre_act = jnp.einsum("wesd,edf->wesf", arrived_split, w_in, preferred_element_type=jnp.float32)
    activated = jax.nn.gelu(pre_act).astype(jnp.bfloat16)
    result = jnp.einsum(
        "wesf,efd->wesd", activated, w_out, preferred_element_type=jnp.float32
    ).astype(jnp.bfloat16)
    returned = from_experts(result.reshape(wide_count, slot_count, feature_dim))
    mixed = tp_sums(unpack_rows(table, returned, rows_b.shape))
    output = hidden + gate[..., None] * mixed
    state.update(
        {
            "inputs": inputs,
            "inverse_a": inverse_a,
            "rows_a": rows_a,
            "queries": queries,
            "keys": keys,
            "values": values,
            "out_values": out_values,
            "out_low": out_low,
            "log_total": log_total,
            "hidden": hidden,
            "inverse_b": inverse_b,
            "normed_b": normed_b,
            "router_probs": router_probs,
            "chosen": chosen,
            "gate": gate,
            "mixed": mixed,
            "table": table,
            "arrived": arrived_split,
            "pre_act": pre_act,
            "activated": activated,
        }
    )
    return (output, state)


def layer_backward(grad_output, state, params):
    w_query, w_key, w_value, w_output, gain_attn, gain_moe, w_router, w_in, w_out = params
    feature_dim = grad_output.shape[-1]
    heads_dev = w_query.shape[1] // HEAD_DIM
    gate = state["gate"]
    grad_gate = jnp.sum(grad_output * state["mixed"], axis=-1)
    grad_logits = (gate * grad_gate)[..., None] * (state["chosen"] - state["router_probs"])
    router_wide = w_router.astype(jnp.float32)
    grad_router = jnp.einsum(
        "sqd,sqe->de",
        state["normed_b"].astype(jnp.float32),
        grad_logits,
        precision=HIGHEST,
        preferred_element_type=jnp.float32,
    )
    grad_normed_router = jnp.einsum(
        "sqe,de->sqd",
        grad_logits,
        router_wide,
        precision=HIGHEST,
        preferred_element_type=jnp.float32,
    )
    rows_grad = tp_rows((gate[..., None] * grad_output).astype(jnp.bfloat16))
    arrived = state["arrived"]
    arrived_grad = to_experts(pack_rows(state["table"], rows_grad)).reshape(arrived.shape)
    grad_act = jnp.einsum("wesd,efd->wesf", arrived_grad, w_out, preferred_element_type=jnp.float32)
    grad_w_out = jnp.einsum(
        "wesf,wesd->efd", state["activated"], arrived_grad, preferred_element_type=jnp.float32
    )
    unused_value, gelu_back = jax.vjp(jax.nn.gelu, state["pre_act"])
    grad_pre = gelu_back(grad_act)[0].astype(jnp.bfloat16)
    grad_w_in = jnp.einsum("wesd,wesf->edf", arrived, grad_pre, preferred_element_type=jnp.float32)
    grad_slots = jnp.einsum(
        "wesf,edf->wesd", grad_pre, w_in, preferred_element_type=jnp.float32
    ).astype(jnp.bfloat16)
    grad_back = from_experts(grad_slots.reshape(arrived.shape[0], -1, feature_dim))
    grad_normed_b = grad_normed_router + tp_sums(
        unpack_rows(state["table"], grad_back, rows_grad.shape)
    )
    grad_hidden_norm, grad_gain_moe = norm_back(
        state["hidden"], state["inverse_b"], gain_moe, grad_normed_b
    )
    grad_hidden = grad_output + grad_hidden_norm
    grad_attn_rows = tp_rows(grad_hidden.astype(jnp.bfloat16))
    wo_split = w_output.reshape(heads_dev, HEAD_DIM, feature_dim)
    grad_w_output = jnp.einsum(
        "shqe,sqd->hed", state["out_low"], grad_attn_rows, preferred_element_type=jnp.float32
    ).reshape(w_output.shape)
    grad_attended = jnp.einsum(
        "sqd,hed->shqe", grad_attn_rows, wo_split, preferred_element_type=jnp.float32
    ).astype(jnp.bfloat16)
    keys_whole, values_whole = (
        lax.all_gather(shortened(state["keys"]), "wide", axis=1, tiled=True),
        lax.all_gather(shortened(state["values"]), "wide", axis=1, tiled=True),
    )
    grad_query, grad_key_all, grad_value_all = attend_back(
        state["queries"],
        grad_attended,
        state["out_values"],
        state["log_total"],
        keys_whole,
        values_whole,
    )
    grad_key, grad_value = (
        lax.psum_scatter(
            grad_key_all.astype(jnp.bfloat16), "wide", scatter_dimension=1, tiled=True
        ).astype(jnp.float32),
        lax.psum_scatter(
            grad_value_all.astype(jnp.bfloat16), "wide", scatter_dimension=1, tiled=True
        ).astype(jnp.float32),
    )
    grad_query_low = grad_query.astype(jnp.bfloat16)
    grad_key_low = grad_key.astype(jnp.bfloat16)
    grad_value_low = grad_value.astype(jnp.bfloat16)
    rows_a = state["rows_a"]
    wq_split = w_query.reshape(feature_dim, heads_dev, HEAD_DIM)
    grad_w_query = jnp.einsum(
        "sqd,shqe->dhe", rows_a, grad_query_low, preferred_element_type=jnp.float32
    ).reshape(w_query.shape)
    grad_w_key = jnp.einsum("sqd,sqi->di", rows_a, grad_key_low, preferred_element_type=jnp.float32)
    grad_w_value = jnp.einsum(
        "sqd,sqi->di", rows_a, grad_value_low, preferred_element_type=jnp.float32
    )
    grad_rows_a = jnp.einsum(
        "shqe,dhe->sqd", grad_query_low, wq_split, preferred_element_type=jnp.float32
    )
    grad_rows_a = grad_rows_a + jnp.einsum(
        "sqi,di->sqd", grad_key_low, w_key, preferred_element_type=jnp.float32
    )
    grad_rows_a = grad_rows_a + jnp.einsum(
        "sqi,di->sqd", grad_value_low, w_value, preferred_element_type=jnp.float32
    )
    grad_normed_a = tp_sums(grad_rows_a)
    grad_input_norm, grad_gain_attn = norm_back(
        state["inputs"], state["inverse_a"], gain_attn, grad_normed_a
    )
    grad_input = grad_hidden + grad_input_norm
    return (
        grad_input,
        (
            grad_gain_attn,
            grad_w_query,
            grad_w_key,
            grad_w_value,
            grad_w_output,
            grad_gain_moe,
            grad_router,
            grad_w_in,
            grad_w_out,
        ),
    )


def shards(
    block_input,
    out_cotangent,
    routes,
    attn_gain,
    query_weight,
    key_weight,
    value_weight,
    output_weight,
    moe_gain,
    router_weight,
    expert_in,
    expert_out,
):
    w_query, w_key, w_value, w_output = (
        lax.all_gather(query_weight[0], "wide", axis=0, tiled=True),
        lax.all_gather(key_weight[0], "wide", axis=0, tiled=True),
        lax.all_gather(value_weight[0], "wide", axis=0, tiled=True),
        lax.all_gather(output_weight[0], "wide", axis=1, tiled=True),
    )
    gain_attn, gain_moe, w_router = (
        lax.all_gather(attn_gain[0], ("wide", "tp"), axis=0, tiled=True),
        lax.all_gather(moe_gain[0], ("wide", "tp"), axis=0, tiled=True),
        lax.all_gather(router_weight[0], ("wide", "tp"), axis=0, tiled=True),
    )
    params = (
        w_query,
        w_key,
        w_value,
        w_output,
        gain_attn.astype(jnp.float32),
        gain_moe.astype(jnp.float32),
        w_router,
        expert_in[0],
        expert_out[0],
    )
    micro_count = block_input.shape[0]
    section_index = lax.axis_index("pipe")
    route_all = routes[0, :, :, :, 0]
    received = jnp.zeros(block_input.shape[1:], jnp.bfloat16)
    for step_index in range(micro_count + 1):
        micro_index = step_index - section_index
        is_valid = (micro_index >= 0) & (micro_index < micro_count)
        slot_index = jnp.where(is_valid, micro_index, micro_count)
        inputs = jnp.where(
            section_index == 0, block_input[min(step_index, micro_count - 1)], received
        ).astype(jnp.float32)
        route_ctx = lax.dynamic_index_in_dim(
            route_all, jnp.clip(micro_index, 0, micro_count - 1), 0, keepdims=False
        )
        output, state = layer_forward(inputs, route_ctx, params)
        output_low = output.astype(jnp.bfloat16)
        if step_index == 0:
            store = jax.tree.map(
                lambda array: jnp.zeros((micro_count + 1,) + array.shape, array.dtype), state
            )
            out_store = jnp.zeros((micro_count + 1,) + output_low.shape, jnp.bfloat16)
        store = jax.tree.map(
            lambda buffer, array: lax.dynamic_update_index_in_dim(buffer, array, slot_index, 0),
            store,
            state,
        )
        out_store = lax.dynamic_update_index_in_dim(out_store, output_low, slot_index, 0)
        if step_index < micro_count:
            received = shifted(output_low, "pipe", 1)
    grad_received = jnp.zeros(block_input.shape[1:], jnp.bfloat16)
    grad_store = jnp.zeros((micro_count + 1,) + block_input.shape[1:], jnp.bfloat16)
    for step_index in range(micro_count + 1):
        micro_index = step_index - 1 + section_index
        is_valid = (micro_index >= 0) & (micro_index < micro_count)
        slot_index = jnp.where(is_valid, micro_index, micro_count)
        incoming = jnp.where(
            section_index == 1, out_cotangent[min(step_index, micro_count - 1)], grad_received
        ).astype(jnp.float32)
        state = jax.tree.map(
            lambda buffer: lax.dynamic_index_in_dim(buffer, slot_index, 0, keepdims=False), store
        )
        grad_input, weight_grads = layer_backward(incoming, state, params)
        valid_scale = is_valid.astype(jnp.float32)
        weight_grads = jax.tree.map(lambda grad_array: grad_array * valid_scale, weight_grads)
        if step_index == 0:
            grad_sums = weight_grads
        else:
            grad_sums = jax.tree.map(
                lambda total_array, grad_array: total_array + grad_array, grad_sums, weight_grads
            )
        grad_low = grad_input.astype(jnp.bfloat16)
        grad_store = lax.dynamic_update_index_in_dim(grad_store, grad_low, slot_index, 0)
        if step_index < micro_count:
            grad_received = shifted(grad_low, "pipe", -1)
    (
        grad_gain_attn,
        grad_w_query,
        grad_w_key,
        grad_w_value,
        grad_w_output,
        grad_gain_moe,
        grad_router,
        grad_w_in,
        grad_w_out,
    ) = grad_sums
    query_grad, key_grad, value_grad, output_grad = (
        lax.psum_scatter(
            grad_w_query.astype(jnp.bfloat16), "wide", scatter_dimension=0, tiled=True
        ).astype(jnp.float32),
        lax.psum_scatter(
            grad_w_key.astype(jnp.bfloat16), "wide", scatter_dimension=0, tiled=True
        ).astype(jnp.float32),
        lax.psum_scatter(
            grad_w_value.astype(jnp.bfloat16), "wide", scatter_dimension=0, tiled=True
        ).astype(jnp.float32),
        lax.psum_scatter(
            grad_w_output.astype(jnp.bfloat16), "wide", scatter_dimension=1, tiled=True
        ).astype(jnp.float32),
    )
    attn_gain_grad, moe_gain_grad, router_grad = (
        lax.psum_scatter(grad_gain_attn, ("wide", "tp"), scatter_dimension=0, tiled=True),
        lax.psum_scatter(grad_gain_moe, ("wide", "tp"), scatter_dimension=0, tiled=True),
        lax.psum_scatter(grad_router, ("wide", "tp"), scatter_dimension=0, tiled=True),
    )
    return (
        out_store[:micro_count][None],
        grad_store[:micro_count][None],
        attn_gain_grad[None],
        query_grad[None],
        key_grad[None],
        value_grad[None],
        output_grad[None],
        moe_gain_grad[None],
        router_grad[None],
        grad_w_in[None],
        grad_w_out[None],
    )


def solution(mesh):
    placed = (
        P(None, None, ("wide", "tp"), None),
        P(None, None, ("wide", "tp"), None),
        P("pipe", None, None, "wide", None),
        P("pipe", ("wide", "tp")),
        P("pipe", "wide", "tp"),
        P("pipe", "wide", "tp"),
        P("pipe", "wide", "tp"),
        P("pipe", "tp", "wide"),
        P("pipe", ("wide", "tp")),
        P("pipe", ("wide", "tp"), None),
        P("pipe", "wide", None, "tp"),
        P("pipe", "wide", "tp", None),
    )
    return jax.shard_map(
        shards,
        mesh=mesh,
        in_specs=placed,
        out_specs=(
            P("pipe", None, None, ("wide", "tp"), None),
            P("pipe", None, None, ("wide", "tp"), None),
            P("pipe", ("wide", "tp")),
            P("pipe", "wide", "tp"),
            P("pipe", "wide", "tp"),
            P("pipe", "wide", "tp"),
            P("pipe", "tp", "wide"),
            P("pipe", ("wide", "tp")),
            P("pipe", ("wide", "tp"), None),
            P("pipe", "wide", None, "tp"),
            P("pipe", "wide", "tp", None),
        ),
        check_vma=False,
    )
```

profile of v0, /device:TPU:0, one launch (start us, length us, event | category | flops | bytes accessed | tf_op | source)
XLA Modules:
  0.0 2026.0 jit_solution(14817296453180336024)
XLA Ops:
  11.0 34.9 %all-reduce.5 = (bf16[768]{0:T(1024)(128)(2,1)S(1)}, bf16[768]{0:T(1024)(128)(2,1)S(1)}) all-reduce(bf16[768]{0:T(1024)(128)(2,1)S(1)} %dynamic-update-slice, bf16[768]{0:T(1024)(128)(2,1)S(1)} %dynamic-update-slice.1), channel_id=2, replica_groups=mesh['pipe'=2,'wide'=8,'tp'=2] {'wide','tp'}, use_global_device_ids=true, to_apply=%add | all-reduce | flops 1536 | bytes 6144
  50.3 31.7 %all-gather.2 = bf16[1,768,384]{2,1,0:T(8,128)(2,1)S(1)} all-gather(bf16[1,96,384]{2,1,0:T(8,128)(2,1)} %param.23), channel_id=4, replica_groups=mesh['pipe'=2,'wide'=8,'tp'=2] {'wide'}, dimensions={1}, use_global_device_ids=true | all-gather | bytes 663552 | tf_op jit(solution)/shard_map/all_gather | solution.py:385
  83.2 32.2 %all-gather.3 = bf16[1,768,384]{2,1,0:T(8,128)(2,1)S(1)} all-gather(bf16[1,96,384]{2,1,0:T(8,128)(2,1)S(1)} %copy-done.160), channel_id=5, replica_groups=mesh['pipe'=2,'wide'=8,'tp'=2] {'wide'}, dimensions={1}, use_global_device_ids=true | all-gather | bytes 663552 | tf_op jit(solution)/shard_map/all_gather | solution.py:386
  117.4 34.7 %all-gather.4 = bf16[1,384,768]{1,2,0:T(8,128)(2,1)} all-gather(bf16[1,384,96]{1,2,0:T(8,128)(2,1)S(1)} %copy-done.161), channel_id=6, replica_groups=mesh['pipe'=2,'wide'=8,'tp'=2] {'wide'}, dimensions={2}, use_global_device_ids=true | all-gather | bytes 663552 | tf_op jit(solution)/shard_map/all_gather | solution.py:387
  154.2 34.3 %all-gather.1 = bf16[1,768,384]{2,1,0:T(8,128)(2,1)} all-gather(bf16[1,96,384]{2,1,0:T(8,128)(2,1)S(1)} %copy-done.162), channel_id=3, replica_groups=mesh['pipe'=2,'wide'=8,'tp'=2] {'wide'}, dimensions={1}, use_global_device_ids=true | all-gather | bytes 663552 | tf_op jit(solution)/shard_map/all_gather | solution.py:384
  205.9 5.5 bitcast_dynamic-update-slice_fusion.14
  228.1 23.0 %all_to_all.60 = bf16[8,48,768]{2,1,0:T(8,128)(2,1)S(1)} all-to-all(bf16[8,48,768]{2,1,0:T(8,128)(2,1)} %reshape.1188), channel_id=1, replica_groups=mesh['pipe'=2,'wide'=8,'tp'=2] {'wide'}, dimensions={0} | all-to-all | bytes 1179648 | tf_op jit(solution)/shard_map/all_to_all | solution.py:50
  256.7 19.5 all_to_all.61
  281.4 21.5 %all-gather.6 = bf16[1,768,8]{2,0,1:T(2,128)(2,1)} all-gather(bf16[1,48,8]{2,0,1:T(2,128)(2,1)} %copy.103), channel_id=8, replica_groups=mesh['pipe'=2,'wide'=8,'tp'=2] {'wide','tp'}, dimensions={1}, use_global_device_ids=true | all-gather | bytes 13056 | tf_op jit(solution)/shard_map/all_gather | solution.py:392
  327.1 38.1 %all-gather.30.cloned.1.call-done = bf16[2,1024,384]{2,1,0:T(8,128)(2,1)} async-done(((bf16[2,128,384]{2,1,0:T(8,128)(2,1)}), bf16[2,1024,384]{2,1,0:T(8,128)(2,1)}) %all-gather.30.cloned.1.call-update) | async-done | bytes 1572880 | tf_op jit(solution)/shard_map/all_gather | solution.py:192
  374.2 36.0 %all-gather.32.cloned.1.call-done = bf16[2,1024,384]{2,1,0:T(8,128)(2,1)} async-done(((bf16[2,128,384]{2,1,0:T(8,128)(2,1)}), bf16[2,1024,384]{2,1,0:T(8,128)(2,1)}) %all-gather.32.cloned.1.call-update) | async-done | bytes 1572880 | tf_op jit(solution)/shard_map/all_gather | solution.py:193
  412.8 5.5 bitcast_dynamic-update-slice_fusion.13
  437.3 22.6 %all_to_all.62 = bf16[8,48,768]{2,1,0:T(8,128)(2,1)S(1)} all-to-all(bf16[8,48,768]{2,1,0:T(8,128)(2,1)} %reshape.1197), channel_id=1, replica_groups=mesh['pipe'=2,'wide'=8,'tp'=2] {'wide'}, dimensions={0} | all-to-all | bytes 1179648 | tf_op jit(solution)/shard_map/all_to_all | solution.py:50
  463.9 19.4 all_to_all.63
  517.0 41.9 %all-gather.34.cloned.1.call-done = bf16[2,1024,384]{2,1,0:T(8,128)(2,1)} async-done(((bf16[2,128,384]{2,1,0:T(8,128)(2,1)}), bf16[2,1024,384]{2,1,0:T(8,128)(2,1)}) %all-gather.34.cloned.1.call-update) | async-done | bytes 1572880 | tf_op jit(solution)/shard_map/all_gather | solution.py:192
  566.6 37.3 %all-gather.36.cloned.1.call-done = bf16[2,1024,384]{2,1,0:T(8,128)(2,1)} async-done(((bf16[2,128,384]{2,1,0:T(8,128)(2,1)}), bf16[2,1024,384]{2,1,0:T(8,128)(2,1)}) %all-gather.36.cloned.1.call-update) | async-done | bytes 1572880 | tf_op jit(solution)/shard_map/all_gather | solution.py:193
  606.5 5.5 bitcast_dynamic-update-slice_fusion.12
  614.5 6.2 reduce-scatter.46.cloned.1.call-done
  629.5 6.0 all-to-all-start.4
  635.5 16.4 all-to-all-done.4
  669.9 9.2 all-to-all-done.5
  701.5 22.8 %all_to_all.64 = bf16[8,48,768]{2,1,0:T(8,128)(2,1)S(1)} all-to-all(bf16[8,48,768]{2,1,0:T(8,128)(2,1)} %reshape.1208), channel_id=1, replica_groups=mesh['pipe'=2,'wide'=8,'tp'=2] {'wide'}, dimensions={0} | all-to-all | bytes 1179648 | tf_op jit(solution)/shard_map/all_to_all | solution.py:50
  724.2 4.8 fusion.135
  730.2 19.5 all_to_all.65
  799.7 12.2 all-gather.38.cloned.1.call-done
  811.9 45.6 %all-gather.40.cloned.1.call-done = bf16[1,2,1024,384]{2,3,1,0:T(8,128)(2,1)} async-done(((bf16[1,2,128,384]{2,3,1,0:T(8,128)(2,1)}), bf16[1,2,1024,384]{2,3,1,0:T(8,128)(2,1)}) %all-gather.40.cloned.1.call-update) | async-done | bytes 1572880 | tf_op jit(solution)/shard_map/all_gather | solution.py:309
  860.2 24.0 %while.54 = (s32[]{:T(128)}, f32[2,6,128,64]{2,3,1,0:T(8,128)}, bf16[2,1024,384]{1,2,0:T(8,128)(2,1)}, bf16[2,1024,384]{1,2,0:T(8,128)(2,1)}, bf16[2,1024,384]{1...) while((s32[]{:T(128)}, f32[2,6,128,64]{2,3,1,0:T(8,128)}, ...), condition=%wide.region_38.39_spmd.clone, body=%wide.region_37.38_spmd.clone.sunk | while | flops 510689280 | bytes 88934896 | solution.py:165
  884.2 4.9 copy.166
  892.1 4.9 copy.168
  903.1 52.1 %reduce-scatter.70.cloned.1.call-done = bf16[128,768]{1,0:T(8,128)(2,1)} async-done(((bf16[1024,768]{1,0:T(8,128)(2,1)}), bf16[128,768]{1,0:T(8,128)(2,1)}) %reduce-scatter.70.cloned.1.call-update) | async-done | bytes 196624
  958.6 63.6 %reduce-scatter.72.cloned.1.call-done = bf16[128,768]{1,0:T(8,128)(2,1)} async-done(((bf16[1024,768]{1,0:T(8,128)(2,1)}), bf16[128,768]{1,0:T(8,128)(2,1)}) %reduce-scatter.72.cloned.1.call-update) | async-done | bytes 196624
  1029.4 6.1 reduce-scatter.52.cloned.1.call-done
  1040.3 7.6 collective-permute-done.2
  1054.4 22.7 %all_to_all.66 = bf16[8,48,768]{2,1,0:T(8,128)(2,1)S(1)} all-to-all(bf16[8,48,768]{2,1,0:T(8,128)(2,1)} %reshape.1212), channel_id=1, replica_groups=mesh['pipe'=2,'wide'=8,'tp'=2] {'wide'}, dimensions={0} | all-to-all | bytes 1179648 | tf_op jit(solution)/shard_map/all_to_all | solution.py:50
  1077.2 4.8 fusion.130
  1083.1 19.3 all_to_all.67
  1119.4 40.2 %all-gather.42.cloned.1.call-done = bf16[1,2,1024,384]{2,3,1,0:T(8,128)(2,1)} async-done(((bf16[1,2,128,384]{2,3,1,0:T(8,128)(2,1)}), bf16[1,2,1024,384]{2,3,1,0:T(8,128)(2,1)}) %all-gather.42.cloned.1.call-update) | async-done | bytes 1572880 | tf_op jit(solution)/shard_map/all_gather | solution.py:308
  1159.5 45.8 %all-gather.44.cloned.1.call-done = bf16[1,2,1024,384]{2,3,1,0:T(8,128)(2,1)} async-done(((bf16[1,2,128,384]{2,3,1,0:T(8,128)(2,1)}), bf16[1,2,1024,384]{2,3,1,0:T(8,128)(2,1)}) %all-gather.44.cloned.1.call-update) | async-done | bytes 1572880 | tf_op jit(solution)/shard_map/all_gather | solution.py:309
  1208.0 23.9 %while.55 = (s32[]{:T(128)}, f32[2,6,128,64]{2,3,1,0:T(8,128)}, bf16[2,1024,384]{1,2,0:T(8,128)(2,1)}, bf16[2,1024,384]{1,2,0:T(8,128)(2,1)}, bf16[2,1024,384]{1...) while((s32[]{:T(128)}, f32[2,6,128,64]{2,3,1,0:T(8,128)}, ...), condition=%wide.region_48.49_spmd.clone, body=%wide.region_47.48_spmd.clone.sunk | while | flops 510689280 | bytes 88910288 | solution.py:165
  1231.9 4.9 copy.170
  1239.8 4.9 copy.172
  1250.8 52.1 %reduce-scatter.74.cloned.1.call-done = bf16[128,768]{1,0:T(8,128)(2,1)} async-done(((bf16[1024,768]{1,0:T(8,128)(2,1)}), bf16[128,768]{1,0:T(8,128)(2,1)}) %reduce-scatter.74.cloned.1.call-update) | async-done | bytes 196624
  1306.4 63.8 %reduce-scatter.76.cloned.1.call-done = bf16[128,768]{1,0:T(8,128)(2,1)} async-done(((bf16[1024,768]{1,0:T(8,128)(2,1)}), bf16[128,768]{1,0:T(8,128)(2,1)}) %reduce-scatter.76.cloned.1.call-update) | async-done | bytes 196624
  1376.5 6.8 reduce-scatter.56.cloned.1.call-done
  1388.6 7.6 collective-permute-done.3
  1402.8 22.7 %all_to_all.68 = bf16[8,48,768]{2,1,0:T(8,128)(2,1)S(1)} all-to-all(bf16[8,48,768]{2,1,0:T(8,128)(2,1)} %reshape.1216), channel_id=1, replica_groups=mesh['pipe'=2,'wide'=8,'tp'=2] {'wide'}, dimensions={0} | all-to-all | bytes 1179648 | tf_op jit(solution)/shard_map/all_to_all | solution.py:50
  1431.4 19.6 all_to_all.69
  1472.6 36.8 %all-gather.46.cloned.1.call-done = bf16[1,2,1024,384]{2,3,1,0:T(8,128)(2,1)} async-done(((bf16[1,2,128,384]{2,3,1,0:T(8,128)(2,1)}), bf16[1,2,1024,384]{2,3,1,0:T(8,128)(2,1)}) %all-gather.46.cloned.1.call-update) | async-done | bytes 1572880 | tf_op jit(solution)/shard_map/all_gather | solution.py:308
  1509.4 45.6 %all-gather.48.cloned.1.call-done = bf16[1,2,1024,384]{2,3,1,0:T(8,128)(2,1)} async-done(((bf16[1,2,128,384]{2,3,1,0:T(8,128)(2,1)}), bf16[1,2,1024,384]{2,3,1,0:T(8,128)(2,1)}) %all-gather.48.cloned.1.call-update) | async-done | bytes 1572880 | tf_op jit(solution)/shard_map/all_gather | solution.py:309
  1557.8 24.1 %while.56 = (s32[]{:T(128)}, f32[2,6,128,64]{2,3,1,0:T(8,128)}, bf16[2,1024,384]{1,2,0:T(8,128)(2,1)}, bf16[2,1024,384]{1,2,0:T(8,128)(2,1)}, bf16[2,1024,384]{1...) while((s32[]{:T(128)}, f32[2,6,128,64]{2,3,1,0:T(8,128)}, ...), condition=%wide.region_58.59_spmd.clone, body=%wide.region_57.58_spmd.clone.sunk | while | flops 510689280 | bytes 88910288 | solution.py:165
  1581.8 4.9 copy.174
  1602.5 4.9 copy.176
  1611.6 5.2 fusion.204
  1633.1 5.1 fusion.202
  1654.6 25.4 %reduce-scatter.78.cloned.1.call-done = bf16[128,768]{1,0:T(8,128)(2,1)} async-done(((bf16[1024,768]{1,0:T(8,128)(2,1)}), bf16[128,768]{1,0:T(8,128)(2,1)}) %reduce-scatter.78.cloned.1.call-update) | async-done | bytes 196624
  1683.4 64.0 %reduce-scatter.80.cloned.1.call-done = bf16[128,768]{1,0:T(8,128)(2,1)} async-done(((bf16[1024,768]{1,0:T(8,128)(2,1)}), bf16[128,768]{1,0:T(8,128)(2,1)}) %reduce-scatter.80.cloned.1.call-update) | async-done | bytes 196624
  1754.0 8.2 fusion.37
  1764.6 8.2 fusion.34
  1773.4 38.4 %reduce-scatter.62.cloned.1.call-done = bf16[96,384]{1,0:T(8,128)(2,1)} async-done(((bf16[768,384]{1,0:T(8,128)(2,1)}), bf16[96,384]{1,0:T(8,128)(2,1)}) %reduce-scatter.62.cloned.1.call-update) | async-done | bytes 73744 | tf_op jit(solution)/shard_map/reduce_scatter | solution.py:471
  1813.3 63.3 %reduce-scatter.68.cloned.1.call-done = bf16[384,96]{0,1:T(8,128)(2,1)} async-done(((bf16[384,768]{0,1:T(8,128)(2,1)}), bf16[384,96]{0,1:T(8,128)(2,1)}) %reduce-scatter.68.cloned.1.call-update) | async-done | bytes 73744 | tf_op jit(solution)/shard_map/reduce_scatter | solution.py:480
  1880.5 5.7 reduce-scatter.60.cloned.1.call-done
  1888.0 34.6 %all-reduce.4 = (f32[768]{0:T(1024)S(1)}, f32[768]{0:T(1024)S(1)}) all-reduce(f32[768]{0:T(1024)S(1)} %multiply_add_fusion.1, f32[768]{0:T(1024)S(1)} %copy-done.175), channel_id=33, replica_groups=mesh['pipe'=2,'wide'=8,'tp'=2] {'wide','tp'}, use_global_device_ids=true, to_apply=%region_66.67.clone | all-reduce | flops 1536 | bytes 12288
  1927.9 25.2 %reduce-scatter.64.cloned.1.call-done = bf16[96,384]{1,0:T(8,128)(2,1)} async-done(((bf16[768,384]{1,0:T(8,128)(2,1)}), bf16[96,384]{1,0:T(8,128)(2,1)}) %reduce-scatter.64.cloned.1.call-update) | async-done | bytes 73744 | tf_op jit(solution)/shard_map/reduce_scatter | solution.py:474
  1954.6 62.9 %reduce-scatter.66.cloned.1.call-done = bf16[96,384]{1,0:T(8,128)(2,1)} async-done(((bf16[768,384]{1,0:T(8,128)(2,1)}), bf16[96,384]{1,0:T(8,128)(2,1)}) %reduce-scatter.66.cloned.1.call-update) | async-done | bytes 73744 | tf_op jit(solution)/shard_map/reduce_scatter | solution.py:477
  (923 shorter events, 528.6 us)
Async XLA Ops:
  7.2 244.8 %copy-start = (bf16[1,1,768,1536]{3,2,1,0:T(8,128)(2,1)S(1)}, bf16[1,1,768,1536]{3,2,1,0:T(8,128)(2,1)}, u32[]{:S(2)}) copy-start(bf16[1,1,768,1536]{3,2,1,0:T(8,128)(2,1)} %param.28) | copy-start | bytes 7077892
  7.2 76.0 %copy-start.160 = (bf16[1,96,384]{2,1,0:T(8,128)(2,1)S(1)}, bf16[1,96,384]{2,1,0:T(8,128)(2,1)}, u32[]{:S(2)}) copy-start(bf16[1,96,384]{2,1,0:T(8,128)(2,1)} %param.24) | copy-start | bytes 221188
  7.2 185.7 %all-gather.26.cloned.1.call-start = ((), (), s32[]{:S(2)}) async-start(), calls=%async_computation.35 | async-start | bytes 1769472 | tf_op jit(solution)/shard_map/all_gather | solution.py:192
  48.1 69.3 %copy-start.161 = (bf16[1,384,96]{1,2,0:T(8,128)(2,1)S(1)}, bf16[1,384,96]{1,2,0:T(8,128)(2,1)}, u32[]{:S(2)}) copy-start(bf16[1,384,96]{1,2,0:T(8,128)(2,1)} %param.25) | copy-start | bytes 221188
  50.3 101.8 %copy-start.36 = (bf16[2,128,768]{2,1,0:T(8,128)(2,1)}, bf16[2,128,768]{2,1,0:T(8,128)(2,1)S(1)}, u32[]{:S(2)}) copy-start(bf16[2,128,768]{2,1,0:T(8,128)(2,1)S(1)} %all_gather.94) | copy-start | bytes 1179652
  82.0 428.7 %copy-start.14 = (bf16[1,768,384]{2,1,0:T(8,128)(2,1)}, bf16[1,768,384]{2,1,0:T(8,128)(2,1)S(1)}, u32[]{:S(2)}) copy-start(bf16[1,768,384]{2,1,0:T(8,128)(2,1)S(1)} %all-gather.2) | copy-start | bytes 1769476
  83.1 118.9 %all-gather.28.cloned.1.call-start = ((), (), s32[]{:S(2)}) async-start(), calls=%async_computation.36 | async-start | bytes 1769472 | tf_op jit(solution)/shard_map/all_gather | solution.py:193
  117.3 101.8 %reduce-scatter.38.cloned.1.call-start = ((), (), s32[]{:S(2)}) async-start(), calls=%async_computation.37 | async-start | bytes 589824 | tf_op jit(solution)/shard_map/reduce_scatter | solution.py:44
  189.8 325.1 %copy-start.10 = (bf16[1,768,384]{1,2,0:T(8,128)(2,1)}, bf16[1,768,384]{1,2,0:T(8,128)(2,1)S(1)}, u32[]{:S(2)}) copy-start(bf16[1,768,384]{1,2,0:T(8,128)(2,1)S(1)} %copy.99) | copy-start | bytes 1769476
  213.2 94.5 %reduce-scatter.40.cloned.1.call-start = ((), (), s32[]{:S(2)}) async-start(), calls=%async_computation.38 | async-start | bytes 589824 | tf_op jit(solution)/shard_map/reduce_scatter | solution.py:44
  213.3 408.4 %copy-start.129 = (f32[768]{0:T(1024)}, f32[768]{0:T(1024)S(1)}, u32[]{:S(2)}) copy-start(f32[768]{0:T(1024)S(1)} %convert_element_type.666) | copy-start | bytes 9220
  217.6 60.9 %copy-start.163 = (s32[4,64]{1,0:T(4,128)}, s32[4,64]{1,0:T(4,128)S(1)}, u32[]{:S(2)}) copy-start(s32[4,64]{1,0:T(4,128)S(1)} %multiply_add_fusion.4) | copy-start | bytes 3076
  280.6 84.6 %all-gather.30.cloned.1.call-start = ((), (), s32[]{:S(2)}) async-start(), calls=%async_computation.39 | async-start | bytes 1769472 | tf_op jit(solution)/shard_map/all_gather | solution.py:192
  303.9 382.6 %copy-start.133 = (bf16[1,768,8]{1,2,0:T(8,128)(2,1)}, bf16[1,768,8]{1,2,0:T(8,128)(2,1)S(1)}, u32[]{:S(2)}) copy-start(bf16[1,768,8]{1,2,0:T(8,128)(2,1)S(1)} %copy.104) | copy-start | bytes 36868
  309.0 8.0 collective-permute-start
  322.6 87.7 %all-gather.32.cloned.1.call-start = ((), (), s32[]{:S(2)}) async-start(), calls=%async_computation.40 | async-start | bytes 1769472 | tf_op jit(solution)/shard_map/all_gather | solution.py:193
  324.9 102.1 %reduce-scatter.42.cloned.1.call-start = ((), (), s32[]{:S(2)}) async-start(), calls=%async_computation.41 | async-start | bytes 589824 | tf_op jit(solution)/shard_map/reduce_scatter | solution.py:44
  420.2 73.8 %reduce-scatter.44.cloned.1.call-start = ((), (), s32[]{:S(2)}) async-start(), calls=%async_computation.42 | async-start | bytes 589824 | tf_op jit(solution)/shard_map/reduce_scatter | solution.py:44
  487.7 71.1 %all-gather.34.cloned.1.call-start = ((), (), s32[]{:S(2)}) async-start(), calls=%async_computation.43 | async-start | bytes 1769472 | tf_op jit(solution)/shard_map/all_gather | solution.py:192
  496.0 8.6 collective-permute-start.1
  512.5 91.4 %all-gather.36.cloned.1.call-start = ((), (), s32[]{:S(2)}) async-start(), calls=%async_computation.44 | async-start | bytes 1769472 | tf_op jit(solution)/shard_map/all_gather | solution.py:193
  514.8 105.8 %reduce-scatter.46.cloned.1.call-start = ((), (), s32[]{:S(2)}) async-start(), calls=%async_computation.45 | async-start | bytes 589824 | tf_op jit(solution)/shard_map/reduce_scatter | solution.py:44
  629.5 22.4 %all-to-all-start.4 = ((bf16[8,48,768]{2,1,0:T(8,128)(2,1)}), bf16[8,48,768]{2,1,0:T(8,128)(2,1)}, u32[]{:S(2)}, u32[]{:S(2)}) async-start(bf16[8,48,768]{2,1,0:T(8,128)(2,1)} %reshape.1204), calls=%async_computation.9 | async-start | bytes 1179648 | tf_op jit(solution)/shard_map/all_to_all | solution.py:50
  659.3 19.9 all-to-all-start.5
  663.5 27.0 %reduce-scatter.48.cloned.1.call-start = ((), (), s32[]{:S(2)}) async-start(), calls=%async_computation.46 | async-start | bytes 589824 | tf_op jit(solution)/shard_map/reduce_scatter | solution.py:44
  683.6 107.1 %reduce-scatter.50.cloned.1.call-start = ((), (), s32[]{:S(2)}) async-start(), calls=%async_computation.47 | async-start | bytes 589824 | tf_op jit(solution)/shard_map/reduce_scatter | solution.py:44
  754.0 57.9 %all-gather.38.cloned.1.call-start = ((), (), s32[]{:S(2)}) async-start(), calls=%async_computation.57 | async-start | bytes 1769472 | tf_op jit(solution)/shard_map/all_gather | solution.py:308
  768.1 89.4 %all-gather.40.cloned.1.call-start = ((), (), s32[]{:S(2)}) async-start(), calls=%async_computation.58 | async-start | bytes 1769472 | tf_op jit(solution)/shard_map/all_gather | solution.py:309
  778.1 177.1 %reduce-scatter.70.cloned.1.call-start = ((), (), s32[]{:S(2)}) async-start(), calls=%async_computation.63 | async-start | bytes 1769472
  892.0 130.2 %reduce-scatter.72.cloned.1.call-start = ((), (), s32[]{:S(2)}) async-start(), calls=%async_computation.64 | async-start | bytes 1769472
  900.0 125.7 %copy-start.15 = (bf16[1,768,384]{2,1,0:T(8,128)(2,1)S(1)}, bf16[1,768,384]{2,1,0:T(8,128)(2,1)}, u32[]{:S(2)}) copy-start(bf16[1,768,384]{2,1,0:T(8,128)(2,1)} %copy-done.14) | copy-start | bytes 1769476
  900.0 135.4 %reduce-scatter.52.cloned.1.call-start = ((), (), s32[]{:S(2)}) async-start(), calls=%async_computation.48 | async-start | bytes 589824 | tf_op jit(solution)/shard_map/reduce_scatter | solution.py:44
  903.1 124.2 %copy-start.19 = (bf16[1,768,384]{2,1,0:T(8,128)(2,1)S(1)}, bf16[1,768,384]{2,1,0:T(8,128)(2,1)}, u32[]{:S(2)}) copy-start(bf16[1,768,384]{2,1,0:T(8,128)(2,1)} %copy-done.18) | copy-start | bytes 1769476
  1028.6 82.4 %reduce-scatter.54.cloned.1.call-start = ((), (), s32[]{:S(2)}) async-start(), calls=%async_computation.49 | async-start | bytes 589824 | tf_op jit(solution)/shard_map/reduce_scatter | solution.py:44
  1039.0 8.9 collective-permute-start.2
  1049.0 64.2 %copy-start.89 = (bf16[2,64,768]{2,1,0:T(8,128)(2,1)}, bf16[2,64,768]{2,1,0:T(8,128)(2,1)S(1)}, u32[]{:S(2)}) copy-start(bf16[2,64,768]{2,1,0:T(8,128)(2,1)S(1)} %get-tuple-element.734) | copy-start | bytes 589828
  1049.6 61.3 %copy-start.197 = (f32[2,64]{1,0:T(2,128)}, f32[2,64]{1,0:T(2,128)S(1)}, u32[]{:S(2)}) copy-start(f32[2,64]{1,0:T(2,128)S(1)} %get-tuple-element.731) | copy-start | bytes 1540
  1105.6 54.0 %all-gather.42.cloned.1.call-start = ((), (), s32[]{:S(2)}) async-start(), calls=%async_computation.59 | async-start | bytes 1769472 | tf_op jit(solution)/shard_map/all_gather | solution.py:308
  1106.2 99.1 %all-gather.44.cloned.1.call-start = ((), (), s32[]{:S(2)}) async-start(), calls=%async_computation.60 | async-start | bytes 1769472 | tf_op jit(solution)/shard_map/all_gather | solution.py:309
  1106.9 196.1 %reduce-scatter.74.cloned.1.call-start = ((), (), s32[]{:S(2)}) async-start(), calls=%async_computation.65 | async-start | bytes 1769472
  1117.4 90.7 %copy-start.31 = (bf16[2,6,128,64]{2,3,1,0:T(8,128)(2,1)S(1)}, bf16[2,6,128,64]{2,3,1,0:T(8,128)(2,1)}, u32[]{:S(2)}) copy-start(bf16[2,6,128,64]{2,3,1,0:T(8,128)(2,1)} %get-tuple-element.1081) | copy-start | bytes 589828
  1239.8 130.4 %reduce-scatter.76.cloned.1.call-start = ((), (), s32[]{:S(2)}) async-start(), calls=%async_computation.66 | async-start | bytes 1769472
  1247.7 125.8 %copy-start.16 = (bf16[1,768,384]{2,1,0:T(8,128)(2,1)S(1)}, bf16[1,768,384]{2,1,0:T(8,128)(2,1)}, u32[]{:S(2)}) copy-start(bf16[1,768,384]{2,1,0:T(8,128)(2,1)} %copy-done.14) | copy-start | bytes 1769476
  1247.8 135.6 %reduce-scatter.56.cloned.1.call-start = ((), (), s32[]{:S(2)}) async-start(), calls=%async_computation.50 | async-start | bytes 589824 | tf_op jit(solution)/shard_map/reduce_scatter | solution.py:44
  1250.8 124.4 %copy-start.20 = (bf16[1,768,384]{2,1,0:T(8,128)(2,1)S(1)}, bf16[1,768,384]{2,1,0:T(8,128)(2,1)}, u32[]{:S(2)}) copy-start(bf16[1,768,384]{2,1,0:T(8,128)(2,1)} %copy-done.18) | copy-start | bytes 1769476
  1376.5 87.7 %reduce-scatter.58.cloned.1.call-start = ((), (), s32[]{:S(2)}) async-start(), calls=%async_computation.51 | async-start | bytes 589824 | tf_op jit(solution)/shard_map/reduce_scatter | solution.py:44
  1387.3 8.9 collective-permute-start.3
  1397.3 69.0 %copy-start.88 = (bf16[2,64,768]{2,1,0:T(8,128)(2,1)}, bf16[2,64,768]{2,1,0:T(8,128)(2,1)S(1)}, u32[]{:S(2)}) copy-start(bf16[2,64,768]{2,1,0:T(8,128)(2,1)S(1)} %get-tuple-element.724) | copy-start | bytes 589828
  1455.4 54.0 %all-gather.46.cloned.1.call-start = ((), (), s32[]{:S(2)}) async-start(), calls=%async_computation.61 | async-start | bytes 1769472 | tf_op jit(solution)/shard_map/all_gather | solution.py:308
  1456.0 99.0 %all-gather.48.cloned.1.call-start = ((), (), s32[]{:S(2)}) async-start(), calls=%async_computation.62 | async-start | bytes 1769472 | tf_op jit(solution)/shard_map/all_gather | solution.py:309
  1456.6 194.4 %reduce-scatter.82.cloned.1.call-start = ((), (), s32[]{:S(2)}) async-start(), calls=%async_computation.69 | async-start | bytes 417792
  1464.1 215.9 %reduce-scatter.78.cloned.1.call-start = ((), (), s32[]{:S(2)}) async-start(), calls=%async_computation.67 | async-start | bytes 1769472
  1470.5 87.2 %copy-start.30 = (bf16[2,6,128,64]{2,3,1,0:T(8,128)(2,1)S(1)}, bf16[2,6,128,64]{2,3,1,0:T(8,128)(2,1)}, u32[]{:S(2)}) copy-start(bf16[2,6,128,64]{2,3,1,0:T(8,128)(2,1)} %get-tuple-element.1123) | copy-start | bytes 589828
  1589.7 157.7 %reduce-scatter.80.cloned.1.call-start = ((), (), s32[]{:S(2)}) async-start(), calls=%async_computation.68 | async-start | bytes 1769472
  1610.4 201.4 %reduce-scatter.62.cloned.1.call-start = ((), (), s32[]{:S(2)}) async-start(), calls=%async_computation.53 | async-start | bytes 663552 | tf_op jit(solution)/shard_map/reduce_scatter | solution.py:471
  1633.0 243.6 %reduce-scatter.68.cloned.1.call-start = ((), (), s32[]{:S(2)}) async-start(), calls=%async_computation.56 | async-start | bytes 663552 | tf_op jit(solution)/shard_map/reduce_scatter | solution.py:480
  1645.3 240.9 %reduce-scatter.60.cloned.1.call-start = ((), (), s32[]{:S(2)}) async-start(), calls=%async_computation.52 | async-start | bytes 589824 | tf_op jit(solution)/shard_map/reduce_scatter | solution.py:44
  1648.4 102.5 %copy-start.17 = (bf16[1,768,384]{2,1,0:T(8,128)(2,1)S(1)}, bf16[1,768,384]{2,1,0:T(8,128)(2,1)}, u32[]{:S(2)}) copy-start(bf16[1,768,384]{2,1,0:T(8,128)(2,1)} %copy-done.14) | copy-start | bytes 1769476
  1654.6 97.9 %copy-start.21 = (bf16[1,768,384]{2,1,0:T(8,128)(2,1)S(1)}, bf16[1,768,384]{2,1,0:T(8,128)(2,1)}, u32[]{:S(2)}) copy-start(bf16[1,768,384]{2,1,0:T(8,128)(2,1)} %copy-done.18) | copy-start | bytes 1769476
  1753.7 199.3 %reduce-scatter.64.cloned.1.call-start = ((), (), s32[]{:S(2)}) async-start(), calls=%async_computation.54 | async-start | bytes 663552 | tf_op jit(solution)/shard_map/reduce_scatter | solution.py:474
  1764.5 113.6 %copy-start.71 = (f32[768,384]{1,0:T(8,128)S(1)}, f32[768,384]{1,0:T(8,128)}, u32[]{:S(2)}) copy-start(f32[768,384]{1,0:T(8,128)} %fusion.146) | copy-start | bytes 3538948
  1764.5 253.0 %reduce-scatter.66.cloned.1.call-start = ((), (), s32[]{:S(2)}) async-start(), calls=%async_computation.55 | async-start | bytes 663552 | tf_op jit(solution)/shard_map/reduce_scatter | solution.py:477
  1772.8 114.6 %copy-start.172 = (f32[768]{0:T(1024)S(1)}, f32[768]{0:T(1024)}, u32[]{:S(2)}) copy-start(f32[768]{0:T(1024)} %get-tuple-element.638) | copy-start | bytes 9220
  1773.4 114.6 %copy-start.175 = (f32[768]{0:T(1024)S(1)}, f32[768]{0:T(1024)}, u32[]{:S(2)}) copy-start(f32[768]{0:T(1024)} %multiply_add_fusion) | copy-start | bytes 9220
  (214 other events, 1083.5 us)
Sparse Core Ops, SparseCore 0:
  83.2 48.4 all-gather.25
  133.9 48.5 all-gather.27
  213.3 5.7 reduce-scatter.37
  280.7 6.1 reduce-scatter.39
  322.7 42.4 all-gather.29
  367.2 42.9 all-gather.31
  420.3 6.5 reduce-scatter.41
  487.9 6.1 reduce-scatter.43
  512.7 46.1 all-gather.33
  560.9 42.9 all-gather.35
  614.0 6.5 reduce-scatter.45
  683.7 6.7 reduce-scatter.47
  754.2 6.1 reduce-scatter.49
  768.2 43.6 all-gather.37
  814.0 43.4 all-gather.39
  892.1 63.0 reduce-scatter.69
  958.5 63.6 reduce-scatter.71
  1028.7 6.6 reduce-scatter.51
  1105.7 5.2 reduce-scatter.53
  1113.0 46.4 all-gather.41
  1161.8 43.4 all-gather.43
  1239.9 63.0 reduce-scatter.73
  1306.4 63.7 reduce-scatter.75
  1376.6 6.6 reduce-scatter.55
  1455.5 5.2 reduce-scatter.57
  1462.9 46.4 all-gather.45
  1511.5 43.4 all-gather.47
  1558.9 53.7 reduce-scatter.81
  1616.1 63.8 reduce-scatter.77
  1683.7 63.7 reduce-scatter.79
  1750.7 61.0 reduce-scatter.61
  1815.4 61.1 reduce-scatter.67
  1879.3 6.8 reduce-scatter.59
  1889.8 63.2 reduce-scatter.63
  1956.4 61.0 reduce-scatter.65
where the time goes:
time: 2040 us; the launch traced here: 2030 us
  waiting for transfers between devices  976 us (48%)
  blocking collectives  460 us (23%)
  local copies, waits for them, and re-layouts  235 us (12%)
  matrix products  227 us (11%)
  other arithmetic  85.8 us (4%)
  starting transfers between devices  22.8 us (1%)
    unnamed x42, waiting for transfers between devices  324 us
    all_gather x3, waiting for transfers between devices, layer_backward(): lax.all_gather(shortened(state['values']), 'wide', axis=1, tiled=True)  137 us
    all_to_all x5, blocking collectives, to_experts(): lax.all_to_all(values, 'wide', split_axis=0, concat_axis=0, tiled=True)  114 us
    unnamed x394, local copies, waits for them, and re-layouts  101 us
    all_to_all x5, blocking collectives, from_experts(): lax.all_to_all(values, 'wide', split_axis=0, concat_axis=0, tiled=True)  97.2 us
    all_gather x3, waiting for transfers between devices, layer_backward(): lax.all_gather(shortened(state['keys']), 'wide', axis=1, tiled=True)  89.2 us
    all_gather x3, waiting for transfers between devices, layer_forward(): lax.all_gather(keys, 'wide', axis=1, tiled=True)  80 us
    all_gather x3, waiting for transfers between devices, layer_forward(): lax.all_gather(values, 'wide', axis=1, tiled=True)  73.4 us
  transfers between devices with their start and end apart: 41, of which 34 were waited for; matrix products, arithmetic and copies ran while one was open for 14% of the time, Pallas kernels for 0%

commit v1 on v0

v1 whole, which is shorter than its diff:
```python
import jax
import jax.numpy as jnp
from jax import lax
from jax.sharding import Mesh, PartitionSpec as P

HEAD_DIM = 64
EPSILON = 1e-06
SCORE_SCALE = 0.125
HIGHEST = lax.Precision.HIGHEST
F32 = jnp.float32
BF16 = jnp.bfloat16

WIDE = ("z", "q", "h")
CHIPS = ("h", "pipe")
PARTS = ("q", "tp")
SWAP = [(0, 1), (1, 0)]


def dot(left, right, contract, precision=None):
    return lax.dot_general(
        left, right, (contract, ((), ())), precision=precision, preferred_element_type=F32
    )


def mm(left, right):
    return dot(left, right, ((1,), (0,)))


def mm_nt(left, right):
    return dot(left, right, ((1,), (1,)))


def mm_tn(left, right):
    return dot(left, right, ((0,), (0,)))


def swapped(values, axis):
    return lax.ppermute(values, axis, SWAP)


def exchanged(values, axes):
    return lax.all_to_all(values, axes, split_axis=0, concat_axis=0, tiled=True)


def norm_rows(values, gain_vector):
    inverse = lax.rsqrt(jnp.mean(values * values, axis=-1, keepdims=True) + EPSILON)
    return (inverse, (values * inverse * gain_vector).astype(BF16))


def norm_back(values, inverse, gain_vector, grad_normed):
    scaled = grad_normed * gain_vector
    grad_values = inverse * scaled - values * (inverse * inverse * inverse) * jnp.mean(
        scaled * values, axis=-1, keepdims=True
    )
    grad_gain = jnp.sum(grad_normed * values * inverse, axis=0)
    return (grad_values, grad_gain)


def sum_parts(values):
    if lax.axis_size("q") == 1:
        mine = lax.axis_index("tp")
        kept = lax.dynamic_index_in_dim(values, mine, 0, keepdims=False)
        other = lax.dynamic_index_in_dim(values, 1 - mine, 0, keepdims=False)
        got = swapped(other.astype(BF16), "tp")
        return kept.astype(F32) + got.astype(F32)
    return jnp.sum(exchanged(values.astype(BF16), PARTS).astype(F32), axis=0)


def sum_chips(values):
    chunks = exchanged(values.astype(BF16).reshape(4, -1, values.shape[-1]), CHIPS)
    return jnp.sum(chunks.astype(F32), axis=0)


def gather_weights(query_weight, key_weight, value_weight, output_weight, extras):
    rows, cols = query_weight.shape
    half, group = (rows // 2, cols // 2)
    packed = jnp.stack([query_weight, key_weight, value_weight, output_weight.T])
    packed = packed.reshape(4, 2, half, 2, group).transpose(1, 3, 2, 0, 4)
    by_core = exchanged(packed, "tp").reshape(4, half, 4 * group)
    small = jnp.broadcast_to(extras[None], (4,) + extras.shape)
    by_chip = exchanged(jnp.concatenate([by_core, small], axis=-1), CHIPS)
    width = by_chip.shape[-1]
    by_chip = by_chip.reshape(2, 2, half, width)
    whole = []
    for section in range(2):
        own = by_chip[:, section]
        gathered = lax.all_gather(own, ("z", "q"), axis=0, tiled=False)
        gathered = lax.all_gather(gathered, "tp", axis=2, tiled=False)
        whole.append(gathered.reshape(-1, width))
    return whole


def scatter_grads(section_grads, group, extra):
    sums = []
    for grad_w_qkv, grad_w_out, grad_small in section_grads:
        grad_small = jnp.pad(grad_small, ((0, 0), (0, extra - grad_small.shape[-1])))
        grads = jnp.concatenate([grad_w_qkv, grad_w_out, grad_small], axis=-1)
        width = grads.shape[-1]
        places = lax.axis_size("z") * lax.axis_size("q")
        split = grads.astype(BF16).reshape(places * 2, 2, -1, width)
        mine = lax.axis_index("tp")
        kept = lax.dynamic_index_in_dim(split, mine, 1, keepdims=False)
        got = swapped(lax.dynamic_index_in_dim(split, 1 - mine, 1, keepdims=False), "tp")
        both = (kept.astype(F32) + got.astype(F32)).astype(BF16)
        both = both.reshape(places, 2, -1, width)
        moved = exchanged(both, ("z", "q"))
        sums.append(jnp.sum(moved.astype(F32), axis=0).astype(BF16))
    half, width = sums[0].shape[1:]
    by_chip = exchanged(jnp.stack(sums, axis=1).reshape(4, half, width), CHIPS)
    small = jnp.sum(by_chip[:, :, 4 * group :].astype(F32), axis=0)
    by_core = exchanged(by_chip[:, :, : 4 * group].reshape(2, 2, half, 4, group), "tp")
    mats = by_core.transpose(3, 0, 2, 1, 4).reshape(4, 2 * half, 2 * group).astype(F32)
    return mats, small


def dispatch_table(routes, expert_count, most_rows):
    expert_hits = (
        routes[:, :, None] == jnp.arange(expert_count, dtype=jnp.int32)[None, None, :]
    ).astype(F32)
    order = jnp.arange(routes.shape[1])
    before = (order[:, None] > order[None, :]).astype(F32)
    ranks = jnp.einsum("tu,bue->bte", before, expert_hits)
    slot_rank = jnp.sum(ranks * expert_hits, axis=2).astype(jnp.int32)
    target_column = routes * most_rows + slot_rank
    all_columns = jnp.arange(expert_count * most_rows, dtype=jnp.int32)
    return (target_column[:, :, None] == all_columns[None, None, :]).astype(BF16)


def to_experts(table, token_rows, section):
    blocks, block_rows, columns = table.shape
    feature_dim = token_rows.shape[-1]
    grouped = token_rows.reshape(blocks, block_rows, feature_dim)
    packed = jnp.einsum("btc,btd->cbd", table, grouped, preferred_element_type=F32).astype(BF16)
    wide = lax.axis_size("z") * lax.axis_size("q") * lax.axis_size("h")
    arrived = exchanged(packed.reshape(wide, -1, feature_dim), WIDE).reshape(-1, feature_dim)
    hopped = lax.ppermute(arrived, "pipe", [(1 - section, section)])
    near = lax.all_gather(arrived, "tp", axis=0, tiled=False)
    far = lax.all_gather(hopped, "tp", axis=0, tiled=False)
    return jnp.stack([near, far], axis=1).reshape(-1, feature_dim)


def from_experts(table, slot_rows, section):
    feature_dim = slot_rows.shape[-1]
    mine = lax.axis_index("tp")
    split = slot_rows.reshape(2, 2, -1, feature_dim)
    kept = lax.dynamic_index_in_dim(split, mine, 0, keepdims=False)
    got = swapped(lax.dynamic_index_in_dim(split, 1 - mine, 0, keepdims=False), "tp")
    total = (kept.astype(F32) + got.astype(F32)).astype(BF16)
    hopped = lax.ppermute(total[1], "pipe", [(section, 1 - section)])
    back = jnp.where(lax.axis_index("pipe") == section, total[0], hopped)
    wide = lax.axis_size("z") * lax.axis_size("q") * lax.axis_size("h")
    returned = exchanged(back.reshape(wide, -1, feature_dim), WIDE)
    blocks, block_rows, columns = table.shape
    slots = returned.reshape(columns, blocks, feature_dim)
    return jnp.einsum("btc,cbd->btd", table, slots, preferred_element_type=F32).reshape(
        -1, feature_dim
    )


def split_heads(values):
    return values.reshape(values.shape[0], -1, HEAD_DIM).transpose(1, 0, 2)


def join_heads(values):
    return values.transpose(1, 0, 2).reshape(values.shape[1], -1)


def bmm(left, right, contract):
    return lax.dot_general(
        left, right, (contract, ((0,), (0,))), preferred_element_type=F32
    )


def attend(queries, keys, values):
    scores = bmm(queries, keys, ((2,), (2,))) * SCORE_SCALE
    peak = jnp.max(scores, axis=-1, keepdims=True)
    weights = jnp.exp(scores - peak)
    total = jnp.sum(weights, axis=-1, keepdims=True)
    attended = bmm(weights.astype(BF16), values, ((2,), (1,))) / total
    return attended, peak + jnp.log(total)


def attend_back(queries, keys, values, grad_attended, attended, log_total):
    delta = jnp.sum(grad_attended.astype(F32) * attended, axis=-1, keepdims=True)
    scores = bmm(queries, keys, ((2,), (2,))) * SCORE_SCALE
    probs = jnp.exp(scores - log_total)
    grad_probs = bmm(grad_attended, values, ((2,), (2,)))
    grad_scores = (probs * (grad_probs - delta)).astype(BF16)
    grad_queries = bmm(grad_scores, keys, ((2,), (1,))) * SCORE_SCALE
    grad_keys = bmm(grad_scores, queries, ((1,), (1,))) * SCORE_SCALE
    grad_values = bmm(probs.astype(BF16), grad_attended, ((1,), (1,)))
    return grad_queries, grad_keys, grad_values


def section_forward(inputs, routes, weights, w_in, w_out, section, expert_count, most_rows):
    w_qkv, w_out_rows, gain_attn, gain_moe, w_router = weights
    group = w_out_rows.shape[1]
    values_in = inputs.astype(F32)
    inverse_a, normed_a = norm_rows(values_in, gain_attn)
    rows_a = lax.all_gather(normed_a, CHIPS, axis=0, tiled=True)
    qkv = mm(rows_a, w_qkv).astype(BF16)
    kv_all = lax.all_gather(qkv[:, group:], PARTS, axis=0, tiled=True)
    queries = split_heads(qkv[:, :group])
    keys = split_heads(kv_all[:, :group])
    values = split_heads(kv_all[:, group:])
    attended, log_total = attend(queries, keys, values)
    attended_low = join_heads(attended.astype(BF16))
    hidden = values_in + sum_chips(mm_nt(attended_low, w_out_rows))
    inverse_b, normed_b = norm_rows(hidden, gain_moe)
    router_probs = jax.nn.softmax(mm(normed_b, w_router), axis=-1)
    flat_routes = routes.reshape(-1, 1)
    chosen = (flat_routes == jnp.arange(expert_count, dtype=jnp.int32)[None]).astype(F32)
    gate = jnp.sum(router_probs * chosen, axis=-1, keepdims=True)
    table = dispatch_table(routes, expert_count, most_rows)
    slots = to_experts(table, normed_b, section)
    pre_act = mm(slots, w_in)
    activated = jax.nn.gelu(pre_act).astype(BF16)
    result = mm(activated, w_out).astype(BF16)
    mixed = from_experts(table, result, section)
    output = (hidden + gate * mixed).astype(BF16)
    state = (
        values_in, inverse_a, rows_a, queries, keys, values, attended, attended_low, log_total,
        hidden, inverse_b, normed_b, router_probs, chosen, gate, mixed, table, slots, pre_act,
        activated,
    )
    return output, state


def section_backward(grad_out, state, weights, w_in, w_out, section):
    w_qkv, w_out_rows, gain_attn, gain_moe, w_router = weights
    (
        values_in, inverse_a, rows_a, queries, keys, values, attended, attended_low, log_total,
        hidden, inverse_b, normed_b, router_probs, chosen, gate, mixed, table, slots, pre_act,
        activated,
    ) = state
    grad_output = grad_out.astype(F32)
    grad_slots = to_experts(table, (gate * grad_output).astype(BF16), section)
    grad_act = mm_nt(grad_slots, w_out)
    unused_value, gelu_back = jax.vjp(jax.nn.gelu, pre_act)
    grad_pre = gelu_back(grad_act)[0].astype(BF16)
    grad_rows = mm_nt(grad_pre, w_in).astype(BF16)
    grad_gate = jnp.sum(grad_output * mixed, axis=-1, keepdims=True)
    grad_logits = gate * grad_gate * (chosen - router_probs)
    grad_router = dot(normed_b.astype(F32), grad_logits, ((0,), (0,)), HIGHEST)
    grad_normed_router = dot(grad_logits, w_router.astype(F32), ((1,), (1,)), HIGHEST)
    grad_normed_b = grad_normed_router + from_experts(table, grad_rows, section)
    grad_hidden_norm, grad_gain_moe = norm_back(hidden, inverse_b, gain_moe, grad_normed_b)
    grad_hidden = grad_output + grad_hidden_norm
    grad_hidden_rows = lax.all_gather(grad_hidden.astype(BF16), CHIPS, axis=0, tiled=True)
    grad_attended = split_heads(mm(grad_hidden_rows, w_out_rows).astype(BF16))
    grad_queries, grad_keys, grad_values = attend_back(
        queries, keys, values, grad_attended, attended, log_total
    )
    grad_kv = jnp.concatenate([join_heads(grad_keys), join_heads(grad_values)], axis=-1)
    parts = lax.axis_size("q") * lax.axis_size("tp")
    grad_kv = sum_parts(grad_kv.reshape(parts, -1, grad_kv.shape[-1]))
    grad_qkv = jnp.concatenate([join_heads(grad_queries), grad_kv], axis=-1).astype(BF16)
    grad_normed_a = sum_chips(mm_nt(grad_qkv, w_qkv))
    grad_input_norm, grad_gain_attn = norm_back(values_in, inverse_a, gain_attn, grad_normed_a)
    grad_input = (grad_hidden + grad_input_norm).astype(BF16)
    grad_w_qkv = mm_tn(rows_a, grad_qkv)
    grad_w_out = mm_tn(grad_hidden_rows, attended_low)
    small = jnp.concatenate([grad_gain_attn[:, None], grad_gain_moe[:, None], grad_router], axis=-1)
    return grad_input, (grad_w_qkv, grad_w_out, small), (slots, grad_pre, activated, grad_slots)


def shards(
    block_input,
    out_cotangent,
    routes,
    attn_gain,
    query_weight,
    key_weight,
    value_weight,
    output_weight,
    moe_gain,
    router_weight,
    expert_in,
    expert_out,
):
    micro_count, seq_count, half_rows, feature_dim = block_input.shape
    sequences = micro_count * seq_count
    expert_count = router_weight.shape[-1]
    most_rows = max(2, 3 * half_rows // (2 * expert_count))
    pipe, core = (lax.axis_index("pipe"), lax.axis_index("tp"))
    extra = -(-(2 + expert_count) // 128) * 128

    small = jnp.concatenate([attn_gain[0][:, None], moe_gain[0][:, None], router_weight[0]], axis=-1)
    small = jnp.pad(small, ((0, 0), (0, extra - small.shape[-1])))
    whole = gather_weights(
        query_weight[0], key_weight[0], value_weight[0], output_weight[0], small
    )
    group = query_weight.shape[-1] // 2

    def parts_of(array):
        return (
            array[:, : 3 * group],
            array[:, 3 * group : 4 * group],
            array[:, 4 * group].astype(F32),
            array[:, 4 * group + 1].astype(F32),
            array[:, 4 * group + 2 : 4 * group + 2 + expert_count],
        )

    weights = [parts_of(array) for array in whole]

    own_routes = lax.dynamic_slice_in_dim(
        routes[0, :, :, :, 0].reshape(sequences, -1), core * half_rows, half_rows, 1
    )
    route_rows = jnp.pad(
        own_routes.astype(BF16)[:, None, :], ((0, 0), (0, 15), (0, feature_dim - half_rows))
    )
    moved = exchanged(
        jnp.concatenate(
            [
                block_input.reshape(sequences, half_rows, feature_dim),
                out_cotangent.reshape(sequences, half_rows, feature_dim),
                route_rows,
            ],
            axis=1,
        ),
        "z",
    )
    pairs = moved.reshape(sequences // 2, 2, -1, feature_dim)
    mine = lax.dynamic_index_in_dim(pairs, pipe, 1, keepdims=False)
    inputs = mine[:, :half_rows].reshape(-1, feature_dim)
    cotangent = mine[:, half_rows : 2 * half_rows].reshape(-1, feature_dim)
    routes_here = pairs[:, :, 2 * half_rows, :half_rows]
    kept = lax.dynamic_index_in_dim(routes_here, pipe, 1, keepdims=False)
    got = swapped(lax.dynamic_index_in_dim(routes_here, 1 - pipe, 1, keepdims=False), "pipe")
    kept, got = (kept.astype(jnp.int32), got.astype(jnp.int32))
    section_routes = [jnp.where(pipe == 0, kept, got), jnp.where(pipe == 0, got, kept)]

    w_in, w_out = (expert_in[0, 0], expert_out[0, 0])
    outputs, states = ([], [])
    current = inputs
    for section in range(2):
        current, state = section_forward(
            current, section_routes[section], weights[section], w_in, w_out, section,
            expert_count, most_rows,
        )
        outputs.append(current)
        states.append(state)
    grads, expert_parts, input_grads = ([None, None], [None, None], [None, None])
    current = cotangent
    for section in (1, 0):
        current, grads[section], expert_parts[section] = section_backward(
            current, states[section], weights[section], w_in, w_out, section
        )
        input_grads[section] = current

    def to_owners(first, second):
        first, second = (v.reshape(sequences // 2, 1, half_rows, feature_dim) for v in (first, second))
        kept = jnp.where(pipe == 0, first, second)
        got = swapped(jnp.where(pipe == 0, second, first), "pipe")
        both = jnp.where(
            pipe == 0, jnp.concatenate([kept, got], axis=1), jnp.concatenate([got, kept], axis=1)
        )
        home = exchanged(both.reshape(sequences, half_rows, feature_dim), "z")
        return home.reshape(1, micro_count, seq_count, half_rows, feature_dim)

    layer_outputs = to_owners(outputs[0], outputs[1])
    grads_home = to_owners(input_grads[0], input_grads[1])

    slots, grad_pre, activated, grad_slots = (
        jnp.where(pipe == 0, first, second) for first, second in zip(*expert_parts)
    )
    grad_w_in = mm_tn(slots, grad_pre)
    grad_w_out = mm_tn(activated, grad_slots)
    mats, small = scatter_grads(grads, group, extra)
    return (
        layer_outputs,
        grads_home,
        small[:, 0][None],
        mats[0][None],
        mats[1][None],
        mats[2][None],
        mats[3].T[None],
        small[:, 1][None],
        small[:, 2 : 2 + expert_count][None],
        grad_w_in[None, None],
        grad_w_out[None, None],
    )


def solution(mesh):
    pipe, wide, tp = (mesh.shape["pipe"], mesh.shape["wide"], mesh.shape["tp"])
    planes = Mesh(mesh.devices.reshape(pipe, 4, wide // 8, 2, tp), ("pipe", "z", "q", "h", "tp"))
    rows = WIDE + ("tp",)
    placed = (
        P(None, None, rows, None),
        P(None, None, rows, None),
        P("pipe", None, None, WIDE, None),
        P("pipe", rows),
        P("pipe", WIDE, "tp"),
        P("pipe", WIDE, "tp"),
        P("pipe", WIDE, "tp"),
        P("pipe", "tp", WIDE),
        P("pipe", rows),
        P("pipe", rows, None),
        P("pipe", WIDE, None, "tp"),
        P("pipe", WIDE, "tp", None),
    )
    return jax.shard_map(
        shards,
        mesh=planes,
        in_specs=placed,
        out_specs=(
            P("pipe", None, None, rows, None),
            P("pipe", None, None, rows, None),
            P("pipe", rows),
            P("pipe", WIDE, "tp"),
            P("pipe", WIDE, "tp"),
            P("pipe", WIDE, "tp"),
            P("pipe", "tp", WIDE),
            P("pipe", rows),
            P("pipe", rows, None),
            P("pipe", WIDE, None, "tp"),
            P("pipe", WIDE, "tp", None),
        ),
        check_vma=False,
    )
```

time: 2040 us -> 698 us (0.34)
  waiting for transfers between devices: 976 us -> 153 us
  blocking collectives: 460 us -> 131 us
  local copies, waits for them, and re-layouts: 235 us -> 97.1 us
  matrix products: 227 us -> 115 us
  starting transfers between devices: 22.8 us -> 113 us
  other arithmetic: 85.8 us -> 61.4 us
    all_gather x12 -> x2, waiting for transfers between devices: 380 us -> 9.5 us  [gather_weights(): gathered = lax.all_gather(gathered, 'tp', axis=2, tiled=False)]
    unnamed x42 -> x2, waiting for transfers between devices: 324 us -> 0.04 us
    reduce_scatter x16 -> x0, waiting for transfers between devices: 225 us -> none  [the longest x1 63.3 us: shards(): lax.psum_scatter(grad_w_output.astype(jnp.bfloat16), 'wide', scatter_dime...]
    all_to_all x10 -> x1, blocking collectives: 211 us -> 4.05 us  [exchanged(): return lax.all_to_all(values, axes, split_axis=0, concat_axis=0, tiled=True)]
    dot_general x108 -> x50, matrix products: 221 us -> 115 us  [the longest x28 74.5 us: dot(): lax.dot_general(left, right, (contract, ((), ())), precision=precision, p...]
    unnamed x394 -> x164, local copies, waits for them, and re-layouts: 101 us -> 21.7 us
    all_to_all x2 -> x20, waiting for transfers between devices: 25.6 us -> 104 us  [exchanged(): return lax.all_to_all(values, axes, split_axis=0, concat_axis=0, tiled=True)]
    all_to_all x2 -> x20, starting transfers between devices: 10.2 us -> 85.6 us  [exchanged(): return lax.all_to_all(values, axes, split_axis=0, concat_axis=0, tiled=True)]
  transfers between devices with their start and end apart: 41 -> 41, of which waited for: 34 -> 26; matrix products, arithmetic and copies ran while one was open for 14% -> 17% of each run, Pallas kernels for 0% -> 0%
where the time goes in v1:
time: 698 us; the launch traced here: 686 us
  waiting for transfers between devices  153 us (22%)
  blocking collectives  131 us (19%)
  matrix products  115 us (16%)
  starting transfers between devices  113 us (16%)
  local copies, waits for them, and re-layouts  97.1 us (14%)
  other arithmetic  61.4 us (9%)
  between operations  16.1 us (2%)
    all_to_all x20, waiting for transfers between devices, exchanged(): return lax.all_to_all(values, axes, split_axis=0, concat_axis=0, tiled=True)  104 us
    all_to_all x20, starting transfers between devices, exchanged(): return lax.all_to_all(values, axes, split_axis=0, concat_axis=0, tiled=True)  85.6 us
    dot_general x28, matrix products, dot(): lax.dot_general(left, right, (contract, ((), ())), precision=precision, p...  74.5 us
    all_gather x2, blocking collectives, gather_weights(): gathered = lax.all_gather(own, ('z', 'q'), axis=0, tiled=False)  50.8 us
    dot_general x12, matrix products, bmm(): lax.dot_general(left, right, (contract, ((0,), (0,))), preferred_element_...  32.6 us
    all_gather x2, blocking collectives, section_forward(): rows_a = lax.all_gather(normed_a, CHIPS, axis=0, tiled=True)  26.7 us
    all_gather x2, blocking collectives, section_backward(): lax.all_gather(grad_hidden.astype(BF16), CHIPS, axis=0, tiled=True)  24.8 us
    unnamed x164, local copies, waits for them, and re-layouts  21.7 us
  transfers between devices with their start and end apart: 41, of which 26 were waited for; matrix products, arithmetic and copies ran while one was open for 17% of the time, Pallas kernels for 0%

profile of v1, /device:TPU:0, one launch (start us, length us, event | category | flops | bytes accessed | tf_op | source)
XLA Modules:
  0.0 685.8 jit_solution(2865688737648700527)
XLA Ops:
  13.9 3.5 all-to-all-start.1
  20.1 5.2 all-to-all-start.2
  27.3 4.3 all-to-all-done.2
  31.6 4.9 all-to-all-start
  36.5 33.3 %all-gather = bf16[8,1,48,896]{3,2,1,0:T(8,128)(2,1)} all-gather(bf16[2,1,48,896]{3,2,1,0:T(8,128)(2,1)S(1)} %get-tuple-element.68), channel_id=2, replica_groups=mesh['pipe'=2,'z'=4,'q'=1,'h'=2,'tp'=2] {'z','q'}, dimensions={0}, use_global_device_ids=true | all-gather | bytes 860160 | tf_op jit(solution)/shard_map/all_gather | solution.py:87
  71.9 9.5 %all-gather.11.cloned.1.call-done = bf16[4,2,96,896]{3,2,1,0:T(8,128)(2,1)} async-done(((bf16[4,2,48,896]{3,2,1,0:T(8,128)(2,1)}), bf16[4,2,96,896]{3,2,1,0:T(8,128)(2,1)}) %all-gather.11.cloned.1.call-update) | async-done | bytes 1376272 | tf_op jit(solution)/shard_map/all_gather | solution.py:88
  82.8 12.6 %all_gather.75 = bf16[512,768]{1,0:T(8,128)(2,1)S(1)} all-gather(bf16[128,768]{1,0:T(8,128)(2,1)S(1)} %fusion.137), channel_id=1, replica_groups=mesh['pipe'=2,'z'=4,'q'=1,'h'=2,'tp'=2] {'h','pipe'}, dimensions={0}, use_global_device_ids=true | all-gather | bytes 983040 | tf_op jit(solution)/shard_map/all_gather | solution.py:200
  109.1 4.2 all-to-all-start.3
  115.4 9.4 %collective-permute-done = bf16[2,64]{1,0:T(2,128)(2,1)S(1)} collective-permute-done((bf16[2,64]{1,0:T(2,128)(2,1)S(1)}, bf16[2,64]{1,0:T(2,128)(2,1)S(1)}, u32[]{:S(2)}, u32[]{:S(2)}) %collective-permute-start) | collective-permute-done | bytes 288 | tf_op jit(solution)/shard_map/ppermute | solution.py:38
  129.0 5.5 all-to-all-start.4
  134.6 9.7 %all-to-all-done.4 = bf16[8,24,768]{2,1,0:T(8,128)(2,1)S(1)} async-done(((bf16[8,24,768]{2,1,0:T(8,128)(2,1)}), bf16[8,24,768]{2,1,0:T(8,128)(2,1)S(1)}, u32[]{:S(2)}, u32[]{:S(2)}) %all-to-all-start.4) | async-done | bytes 294944 | tf_op jit(solution)/shard_map/all_to_all | solution.py:42
  145.6 17.5 %all-gather.3 = bf16[8,1,48,896]{3,2,1,0:T(8,128)(2,1)} all-gather(bf16[2,1,48,896]{3,2,1,0:T(8,128)(2,1)S(1)} %get-tuple-element.67), channel_id=5, replica_groups=mesh['pipe'=2,'z'=4,'q'=1,'h'=2,'tp'=2] {'z','q'}, dimensions={0}, use_global_device_ids=true | all-gather | bytes 860160 | tf_op jit(solution)/shard_map/all_gather | solution.py:87
  171.3 2.9 fusion.63
  179.5 6.3 collective-permute-start.3
  187.2 4.7 collective-permute-done.3
  192.7 3.5 all-to-all-start.5
  198.8 6.5 all-to-all-done.5
  210.3 14.1 %all_gather.83 = bf16[512,768]{1,0:T(8,128)(2,1)S(1)} all-gather(bf16[128,768]{1,0:T(8,128)(2,1)S(1)} %get-tuple-element.57), channel_id=1, replica_groups=mesh['pipe'=2,'z'=4,'q'=1,'h'=2,'tp'=2] {'h','pipe'}, dimensions={0}, use_global_device_ids=true | all-gather | bytes 983040 | tf_op jit(solution)/shard_map/all_gather | solution.py:200
  238.0 4.2 all-to-all-start.6
  242.5 11.2 %all-to-all-done.6 = bf16[4,128,768]{2,1,0:T(8,128)(2,1)} async-done(((bf16[4,128,768]{2,1,0:T(8,128)(2,1)}), bf16[4,128,768]{2,1,0:T(8,128)(2,1)}, u32[]{:S(2)}, u32[]{:S(2)}) %all-to-all-start.6) | async-done | bytes 786464 | tf_op jit(solution)/shard_map/all_to_all | solution.py:42
  261.5 4.3 all-to-all-start.10
  269.0 6.2 all-to-all-done.10
  275.1 4.1 all-to-all-start.7
  279.2 4.1 collective-permute-start.8
  283.3 4.7 all-to-all-done.7
  288.0 3.5 collective-permute-start.4
  304.7 2.9 fusion.66
  308.8 4.4 fusion.19
  324.4 6.3 collective-permute-done.6
  331.5 4.1 all-to-all-start.8
  338.3 6.1 all-to-all-done.8
  344.4 4.1 all-to-all-start.11
  352.4 4.7 all-to-all-done.11
  363.9 12.1 %all_gather.91 = bf16[512,768]{1,0:T(8,128)(2,1)S(1)} all-gather(bf16[128,768]{1,0:T(8,128)(2,1)S(1)} %get-tuple-element.53), channel_id=1, replica_groups=mesh['pipe'=2,'z'=4,'q'=1,'h'=2,'tp'=2] {'h','pipe'}, dimensions={0}, use_global_device_ids=true | all-gather | bytes 983040 | tf_op jit(solution)/shard_map/all_gather | solution.py:249
  378.6 5.0 fusion.71
  383.6 3.9 multiply_convert_fusion.1
  402.7 3.7 fusion.87
  411.7 4.3 all-to-all-start.12
  416.1 11.8 %all-to-all-done.12 = bf16[4,128,768]{2,1,0:T(8,128)(2,1)} async-done(((bf16[4,128,768]{2,1,0:T(8,128)(2,1)}), bf16[4,128,768]{2,1,0:T(8,128)(2,1)}, u32[]{:S(2)}, u32[]{:S(2)}) %all-to-all-start.12) | async-done | bytes 786464 | tf_op jit(solution)/shard_map/all_to_all | solution.py:42
  436.2 4.1 all-to-all-start.13
  440.3 9.7 %all-to-all-done.13 = bf16[8,24,768]{2,1,0:T(8,128)(2,1)} async-done(((bf16[8,24,768]{2,1,0:T(8,128)(2,1)}), bf16[8,24,768]{2,1,0:T(8,128)(2,1)}, u32[]{:S(2)}, u32[]{:S(2)}) %all-to-all-start.13) | async-done | bytes 294944 | tf_op jit(solution)/shard_map/all_to_all | solution.py:42
  453.7 5.3 collective-permute-done.12
  461.6 6.5 fusion.12
  479.0 3.9 collective-permute-start.14
  485.0 4.4 collective-permute-done.14
  490.2 5.2 all-to-all-start.14
  495.4 3.1 convolution_convert_fusion
  510.1 12.7 %all_gather.95 = bf16[512,768]{1,0:T(8,128)(2,1)S(1)} all-gather(bf16[128,768]{1,0:T(8,128)(2,1)S(1)} %get-tuple-element.49), channel_id=1, replica_groups=mesh['pipe'=2,'z'=4,'q'=1,'h'=2,'tp'=2] {'h','pipe'}, dimensions={0}, use_global_device_ids=true | all-gather | bytes 983040 | tf_op jit(solution)/shard_map/all_gather | solution.py:249
  525.5 5.0 fusion.74
  530.5 3.9 multiply_convert_fusion
  559.2 4.2 all-to-all-start.15
  570.6 4.4 all-to-all-done.15
  575.0 4.4 all-to-all-start.9
  579.4 3.1 convolution_convert_fusion.1
  591.1 4.7 all-to-all-start.18
  601.3 12.0 %all-to-all-done.18 = bf16[4,2,48,896]{3,2,1,0:T(8,128)(2,1)} async-done(((bf16[4,2,48,896]{3,2,1,0:T(8,128)(2,1)}), bf16[4,2,48,896]{3,2,1,0:T(8,128)(2,1)}, u32[]{:S(2)}, u32[]{:S(2)}) %all-to-all-start.18) | async-done | bytes 688160 | tf_op jit(solution)/shard_map/all_to_all | solution.py:42
  613.3 4.2 all-to-all-start.17
  619.5 5.3 collective-permute-done.16
  625.6 9.5 %all-to-all-done.17 = bf16[4,2,48,896]{3,2,1,0:T(8,128)(2,1)} async-done(((bf16[4,2,48,896]{3,2,1,0:T(8,128)(2,1)}), bf16[4,2,48,896]{3,2,1,0:T(8,128)(2,1)}, u32[]{:S(2)}, u32[]{:S(2)}) %all-to-all-start.17) | async-done | bytes 688160 | tf_op jit(solution)/shard_map/all_to_all | solution.py:42
  635.0 3.7 all-to-all-start.16
  638.7 10.6 %convolution_bitcast_fusion = f32[1,1,1536,768]{3,2,1,0:T(8,128)} fusion(pred[]{:T(512)S(6)} %eq.44, bf16[768,768]{1,0:T(8,128)(2,1)} %bitcast.438, bf16[768,768]{1,0:T(8,128)(2,1)} %bitcast.436, f32[768,1536]{1,0:T(8,128)} %copy-done.76, f32[768,1536]{1,0:T(8,128)} %copy-done.77), kind=kOutput, calls=%fused_computation.34 | convolution fusion | flops 1834942464 | bytes 16515073 | tf_op jit(solution)/shard_map/dot_general | solution.py:20
  652.5 3.5 all-to-all-start.19
  656.0 6.3 convolution_bitcast_fusion.1
  664.1 4.0 all_to_all.105
  (429 shorter events, 252.9 us)
Async XLA Ops:
  7.2 164.1 %copy-start = (bf16[1,1,1536,768]{3,2,1,0:T(8,128)(2,1)S(1)}, bf16[1,1,1536,768]{3,2,1,0:T(8,128)(2,1)}, u32[]{:S(2)}) copy-start(bf16[1,1,1536,768]{3,2,1,0:T(8,128)(2,1)} %param.23) | copy-start | bytes 7077892
  7.2 10.2 %copy-start.68 = (bf16[1,48,8]{1,2,0:T(8,128)(2,1)S(1)}, bf16[1,48,8]{1,2,0:T(8,128)(2,1)}, u32[]{:S(2)}) copy-start(bf16[1,48,8]{1,2,0:T(8,128)(2,1)} %param.21) | copy-start | bytes 2308
  7.2 10.2 %copy-start.71 = (bf16[1,48]{1,0:T(2,128)(2,1)S(1)}, bf16[1,48]{1,0:T(2,128)(2,1)}, u32[]{:S(2)}) copy-start(bf16[1,48]{1,0:T(2,128)(2,1)} %param.20) | copy-start | bytes 292
  7.2 10.2 %copy-start.72 = (bf16[1,48]{1,0:T(2,128)(2,1)S(1)}, bf16[1,48]{1,0:T(2,128)(2,1)}, u32[]{:S(2)}) copy-start(bf16[1,48]{1,0:T(2,128)(2,1)} %param.15) | copy-start | bytes 292
  8.5 16.7 %copy-start.69 = (s32[1,2,2,128,1]{3,4,2,1,0:T(1,128)S(1)}, s32[1,2,2,128,1]{3,4,2,1,0:T(1,128)}, u32[]{:S(2)}) copy-start(s32[1,2,2,128,1]{3,4,2,1,0:T(1,128)} %param.14) | copy-start | bytes 6148
  8.6 16.8 %copy-start.52 = (bf16[2,2,64,768]{3,2,1,0:T(8,128)(2,1)S(1)}, bf16[2,2,64,768]{3,2,1,0:T(8,128)(2,1)}, u32[]{:S(2)}) copy-start(bf16[2,2,64,768]{3,2,1,0:T(8,128)(2,1)} %param.13) | copy-start | bytes 1179652
  13.9 5.1 all-to-all-start.1
  20.1 11.5 %all-to-all-start.2 = ((bf16[4,48,896]{2,1,0:T(8,128)(2,1)}), bf16[4,48,896]{2,1,0:T(8,128)(2,1)S(1)}, u32[]{:S(2)}, u32[]{:S(2)}) async-start(bf16[4,48,896]{2,1,0:T(8,128)(2,1)} %pad_maximum_fusion.12), calls=%async_computation.2 | async-start | bytes 688128 | tf_op jit(solution)/shard_map/all_to_all | solution.py:42
  31.6 38.3 %all-to-all-start = ((bf16[4,144,768]{2,1,0:T(8,128)(2,1)}), bf16[4,144,768]{2,1,0:T(8,128)(2,1)}, u32[]{:S(2)}, u32[]{:S(2)}) async-start(bf16[4,144,768]{2,1,0:T(8,128)(2,1)} %fusion.97), calls=%async_computation | async-start | bytes 1769472 | tf_op jit(solution)/shard_map/all_to_all | solution.py:42
  36.5 44.9 %all-gather.11.cloned.1.call-start = ((), (), s32[]{:S(2)}) async-start(), calls=%async_computation.21 | async-start | bytes 2064384 | tf_op jit(solution)/shard_map/all_gather | solution.py:88
  71.8 25.9 %copy-start.62 = (f32[2,64]{1,0:T(2,128)}, f32[2,64]{1,0:T(2,128)S(1)}, u32[]{:S(2)}) copy-start(f32[2,64]{1,0:T(2,128)S(1)} %add_rsqrt_fusion.3) | copy-start | bytes 1540
  71.9 25.8 %copy-start.64 = (f32[128]{0:T(128)}, f32[128]{0:T(128)S(1)}, u32[]{:S(2)}) copy-start(f32[128]{0:T(128)S(1)} %rsqrt.61) | copy-start | bytes 1540
  109.1 16.4 %all-to-all-start.3 = ((bf16[4,128,768]{2,1,0:T(8,128)(2,1)}), bf16[4,128,768]{2,1,0:T(8,128)(2,1)}, u32[]{:S(2)}, u32[]{:S(2)}) async-start(bf16[4,128,768]{2,1,0:T(8,128)(2,1)} %bitcast.382), calls=%async_computation.3 | async-start | bytes 1572864 | tf_op jit(solution)/shard_map/all_to_all | solution.py:42
  113.4 11.4 %collective-permute-start = (bf16[2,64]{1,0:T(2,128)(2,1)S(1)}, bf16[2,64]{1,0:T(2,128)(2,1)S(1)}, u32[]{:S(2)}, u32[]{:S(2)}) collective-permute-start(bf16[2,64]{1,0:T(2,128)(2,1)S(1)} %bitcast.475), channel_id=1, source_target_pairs={{0,16},{16,0},{1,17},{17,1},{2,18},{18,2},{3,19},{19,3},{4,20},{20... | collective-permute-start | bytes 776 | tf_op jit(solution)/shard_map/ppermute | solution.py:38
  129.0 15.3 %all-to-all-start.4 = ((bf16[8,24,768]{2,1,0:T(8,128)(2,1)}), bf16[8,24,768]{2,1,0:T(8,128)(2,1)S(1)}, u32[]{:S(2)}, u32[]{:S(2)}) async-start(bf16[8,24,768]{2,1,0:T(8,128)(2,1)} %reshape.659), calls=%async_computation.4 | async-start | bytes 589824 | tf_op jit(solution)/shard_map/all_to_all | solution.py:42
  134.5 51.4 %all-gather.13.cloned.1.call-start = ((), (), s32[]{:S(2)}) async-start(), calls=%async_computation.22 | async-start | bytes 2064384 | tf_op jit(solution)/shard_map/all_gather | solution.py:88
  144.3 21.2 %collective-permute-start.1 = (bf16[192,768]{1,0:T(8,128)(2,1)S(1)}, bf16[192,768]{1,0:T(8,128)(2,1)}, u32[]{:S(2)}, u32[]{:S(2)}) collective-permute-start(bf16[192,768]{1,0:T(8,128)(2,1)S(1)} %bitcast.430), channel_id=1, source_target_pairs={{16,0},{17,1},{18,2},{19,3},{20,4},{21,5},{22,6},{23,7},{24,8},{25... | collective-permute-start | bytes 884744 | tf_op jit(solution)/shard_map/ppermute | solution.py:136
  175.2 2.2 collective-permute-start.2
  179.5 12.4 %collective-permute-start.3 = (bf16[192,768]{1,0:T(8,128)(2,1)}, bf16[192,768]{1,0:T(8,128)(2,1)}, u32[]{:S(2)}, u32[]{:S(2)}) collective-permute-start(bf16[192,768]{1,0:T(8,128)(2,1)} %slice_bitcast_fusion.6), channel_id=1, source_target_pairs={{0,16},{1,17},{2,18},{3,19},{4,20},{5,21},{6,22},{7,23},{8,24},{9,... | collective-permute-start | bytes 884744 | tf_op jit(solution)/shard_map/ppermute | solution.py:149
  192.7 12.7 %all-to-all-start.5 = ((bf16[8,24,768]{2,1,0:T(8,128)(2,1)}), bf16[8,24,768]{2,1,0:T(8,128)(2,1)S(1)}, u32[]{:S(2)}, u32[]{:S(2)}) async-start(bf16[8,24,768]{2,1,0:T(8,128)(2,1)} %bitcast.433), calls=%async_computation.5 | async-start | bytes 589824 | tf_op jit(solution)/shard_map/all_to_all | solution.py:42
  197.2 29.3 %copy-start.6 = (f32[128,768]{1,0:T(8,128)}, f32[128,768]{1,0:T(8,128)S(1)}, u32[]{:S(2)}) copy-start(f32[128,768]{1,0:T(8,128)S(1)} %bitcast_add_fusion.1) | copy-start | bytes 1179652
  198.7 27.8 %copy-start.56 = (f32[128]{0:T(128)}, f32[128]{0:T(128)S(1)}, u32[]{:S(2)}) copy-start(f32[128]{0:T(128)S(1)} %select_reduce_fusion.1) | copy-start | bytes 1540
  238.0 15.7 %all-to-all-start.6 = ((bf16[4,128,768]{2,1,0:T(8,128)(2,1)}), bf16[4,128,768]{2,1,0:T(8,128)(2,1)}, u32[]{:S(2)}, u32[]{:S(2)}) async-start(bf16[4,128,768]{2,1,0:T(8,128)(2,1)} %bitcast.383), calls=%async_computation.6 | async-start | bytes 1572864 | tf_op jit(solution)/shard_map/all_to_all | solution.py:42
  242.3 117.8 %copy-start.59 = (s32[128]{0:T(128)}, s32[128]{0:T(128)S(1)}, u32[]{:S(2)}) copy-start(s32[128]{0:T(128)S(1)} %eq.55) | copy-start | bytes 1540
  261.5 13.6 %all-to-all-start.10 = ((bf16[8,24,768]{2,1,0:T(8,128)(2,1)}), bf16[8,24,768]{2,1,0:T(8,128)(2,1)}, u32[]{:S(2)}, u32[]{:S(2)}) async-start(bf16[8,24,768]{2,1,0:T(8,128)(2,1)} %reshape.679), calls=%async_computation.10 | async-start | bytes 589824 | tf_op jit(solution)/shard_map/all_to_all | solution.py:42
  275.1 12.9 %all-to-all-start.7 = ((bf16[8,24,768]{2,1,0:T(8,128)(2,1)}), bf16[8,24,768]{2,1,0:T(8,128)(2,1)}, u32[]{:S(2)}, u32[]{:S(2)}) async-start(bf16[8,24,768]{2,1,0:T(8,128)(2,1)} %reshape.672), calls=%async_computation.7 | async-start | bytes 589824 | tf_op jit(solution)/shard_map/all_to_all | solution.py:42
  279.2 17.2 %collective-permute-start.8 = (bf16[192,768]{1,0:T(8,128)(2,1)}, bf16[192,768]{1,0:T(8,128)(2,1)}, u32[]{:S(2)}, u32[]{:S(2)}) collective-permute-start(bf16[192,768]{1,0:T(8,128)(2,1)} %bitcast.79), channel_id=1, source_target_pairs={{0,16},{1,17},{2,18},{3,19},{4,20},{5,21},{6,22},{7,23},{8,24},{9,... | collective-permute-start | bytes 884744 | tf_op jit(solution)/shard_map/ppermute | solution.py:136
  288.0 11.1 %collective-permute-start.4 = (bf16[192,768]{1,0:T(8,128)(2,1)}, bf16[192,768]{1,0:T(8,128)(2,1)S(1)}, u32[]{:S(2)}, u32[]{:S(2)}) collective-permute-start(bf16[192,768]{1,0:T(8,128)(2,1)} %bitcast.62), channel_id=1, source_target_pairs={{0,16},{1,17},{2,18},{3,19},{4,20},{5,21},{6,22},{7,23},{8,24},{9,... | collective-permute-start | bytes 884744 | tf_op jit(solution)/shard_map/ppermute | solution.py:136
  299.1 9.8 %copy-start.35 = (bf16[2,2,192,768]{3,2,1,0:T(8,128)(2,1)}, bf16[2,2,192,768]{3,2,1,0:T(8,128)(2,1)S(1)}, u32[]{:S(2)}) copy-start(bf16[2,2,192,768]{3,2,1,0:T(8,128)(2,1)S(1)} %copy.140) | copy-start | bytes 3538948
  308.6 8.9 %collective-permute-start.5 = (bf16[2,192,768]{2,1,0:T(8,128)(2,1)}, bf16[2,192,768]{2,1,0:T(8,128)(2,1)}, u32[]{:S(2)}, u32[]{:S(2)}) collective-permute-start(bf16[2,192,768]{2,1,0:T(8,128)(2,1)} %dynamic-slice_bitcast_fusion.4), channel_id=1, source_target_pairs={{0,1},{1,0},{2,3},{3,2},{4,5},{5,4},{6,7},{7,6},{8,9},{9,8},{10,11... | collective-permute-start | bytes 1769480 | tf_op jit(solution)/shard_map/ppermute | solution.py:38
  317.2 3.1 collective-permute-start.9
  319.0 11.7 %collective-permute-start.6 = (bf16[192,768]{1,0:T(8,128)(2,1)S(1)}, bf16[192,768]{1,0:T(8,128)(2,1)S(1)}, u32[]{:S(2)}, u32[]{:S(2)}) collective-permute-start(bf16[192,768]{1,0:T(8,128)(2,1)S(1)} %slice_bitcast_fusion.4), channel_id=1, source_target_pairs={{16,0},{17,1},{18,2},{19,3},{20,4},{21,5},{22,6},{23,7},{24,8},{25... | collective-permute-start | bytes 884744 | tf_op jit(solution)/shard_map/ppermute | solution.py:149
  323.1 13.3 %collective-permute-start.10 = (bf16[192,768]{1,0:T(8,128)(2,1)}, bf16[192,768]{1,0:T(8,128)(2,1)}, u32[]{:S(2)}, u32[]{:S(2)}) collective-permute-start(bf16[192,768]{1,0:T(8,128)(2,1)} %slice_bitcast_fusion.2), channel_id=1, source_target_pairs={{16,0},{17,1},{18,2},{19,3},{20,4},{21,5},{22,6},{23,7},{24,8},{25... | collective-permute-start | bytes 884744 | tf_op jit(solution)/shard_map/ppermute | solution.py:149
  331.5 12.9 %all-to-all-start.8 = ((bf16[8,24,768]{2,1,0:T(8,128)(2,1)}), bf16[8,24,768]{2,1,0:T(8,128)(2,1)}, u32[]{:S(2)}, u32[]{:S(2)}) async-start(bf16[8,24,768]{2,1,0:T(8,128)(2,1)} %bitcast.434), calls=%async_computation.8 | async-start | bytes 589824 | tf_op jit(solution)/shard_map/all_to_all | solution.py:42
  344.4 12.7 %all-to-all-start.11 = ((bf16[8,24,768]{2,1,0:T(8,128)(2,1)}), bf16[8,24,768]{2,1,0:T(8,128)(2,1)}, u32[]{:S(2)}, u32[]{:S(2)}) async-start(bf16[8,24,768]{2,1,0:T(8,128)(2,1)} %bitcast.432), calls=%async_computation.11 | async-start | bytes 589824 | tf_op jit(solution)/shard_map/all_to_all | solution.py:42
  352.4 23.6 %copy-start.66 = (f32[128]{0:T(128)}, f32[128]{0:T(128)S(1)}, u32[]{:S(2)}) copy-start(f32[128]{0:T(128)S(1)} %mul.640) | copy-start | bytes 1540
  360.1 18.4 %copy-start.51 = (f32[3,512,64]{1,2,0:T(8,128)S(1)}, f32[3,512,64]{1,2,0:T(8,128)}, u32[]{:S(2)}) copy-start(f32[3,512,64]{1,2,0:T(8,128)} %get-tuple-element.84) | copy-start | bytes 1179652
  402.7 5.5 collective-permute-start.11
  411.7 21.2 %copy-start.57 = (f32[128]{0:T(128)S(1)}, f32[128]{0:T(128)}, u32[]{:S(2)}) copy-start(f32[128]{0:T(128)} %copy-done.56) | copy-start | bytes 1540
  411.7 16.2 %all-to-all-start.12 = ((bf16[4,128,768]{2,1,0:T(8,128)(2,1)}), bf16[4,128,768]{2,1,0:T(8,128)(2,1)}, u32[]{:S(2)}, u32[]{:S(2)}) async-start(bf16[4,128,768]{2,1,0:T(8,128)(2,1)} %bitcast.452), calls=%async_computation.12 | async-start | bytes 1572864 | tf_op jit(solution)/shard_map/all_to_all | solution.py:42
  436.2 13.8 %all-to-all-start.13 = ((bf16[8,24,768]{2,1,0:T(8,128)(2,1)}), bf16[8,24,768]{2,1,0:T(8,128)(2,1)}, u32[]{:S(2)}, u32[]{:S(2)}) async-start(bf16[8,24,768]{2,1,0:T(8,128)(2,1)} %reshape.690), calls=%async_computation.13 | async-start | bytes 589824 | tf_op jit(solution)/shard_map/all_to_all | solution.py:42
  450.0 9.0 %collective-permute-start.12 = (bf16[192,768]{1,0:T(8,128)(2,1)}, bf16[192,768]{1,0:T(8,128)(2,1)S(1)}, u32[]{:S(2)}, u32[]{:S(2)}) collective-permute-start(bf16[192,768]{1,0:T(8,128)(2,1)} %bitcast.107), channel_id=1, source_target_pairs={{16,0},{17,1},{18,2},{19,3},{20,4},{21,5},{22,6},{23,7},{24,8},{25... | collective-permute-start | bytes 884744 | tf_op jit(solution)/shard_map/ppermute | solution.py:136
  471.1 6.4 collective-permute-start.13
  472.8 10.2 %copy-start.29 = (bf16[128,768]{1,0:T(8,128)(2,1)S(1)}, bf16[128,768]{1,0:T(8,128)(2,1)}, u32[]{:S(2)}) copy-start(bf16[128,768]{1,0:T(8,128)(2,1)} %copy-done.28) | copy-start | bytes 589828
  472.8 10.2 %copy-start.60 = (s32[128]{0:T(128)S(1)}, s32[128]{0:T(128)}, u32[]{:S(2)}) copy-start(s32[128]{0:T(128)} %copy-done.59) | copy-start | bytes 1540
  472.8 10.2 %copy-start.67 = (f32[128]{0:T(128)S(1)}, f32[128]{0:T(128)}, u32[]{:S(2)}) copy-start(f32[128]{0:T(128)} %copy-done.66) | copy-start | bytes 1540
  472.8 10.4 %collective-permute-start.7 = (bf16[2,1,64,768]{3,2,0,1:T(8,128)(2,1)}, bf16[2,1,64,768]{3,2,0,1:T(8,128)(2,1)}, u32[]{:S(2)}, u32[]{:S(2)}) collective-permute-start(bf16[2,1,64,768]{3,2,0,1:T(8,128)(2,1)} %select_bitcast_fusion), channel_id=1, source_target_pairs={{0,16},{16,0},{1,17},{17,1},{2,18},{18,2},{3,19},{19,3},{4,20},{20... | collective-permute-start | bytes 589832 | tf_op jit(solution)/shard_map/ppermute | solution.py:38
  472.9 10.3 %copy-start.44 = (bf16[2,1,64,768]{3,2,0,1:T(8,128)(2,1)S(1)}, bf16[2,1,64,768]{3,2,0,1:T(8,128)(2,1)}, u32[]{:S(2)}) copy-start(bf16[2,1,64,768]{3,2,0,1:T(8,128)(2,1)} %get-tuple-element.55) | copy-start | bytes 589828
  477.5 17.9 %copy-start.54 = (bf16[512,192]{1,0:T(8,128)(2,1)S(1)}, bf16[512,192]{1,0:T(8,128)(2,1)}, u32[]{:S(2)}) copy-start(bf16[512,192]{1,0:T(8,128)(2,1)} %copy.144) | copy-start | bytes 589828
  479.0 10.4 %collective-permute-start.14 = (bf16[192,768]{1,0:T(8,128)(2,1)S(1)}, bf16[192,768]{1,0:T(8,128)(2,1)S(1)}, u32[]{:S(2)}, u32[]{:S(2)}) collective-permute-start(bf16[192,768]{1,0:T(8,128)(2,1)S(1)} %slice_bitcast_fusion), channel_id=1, source_target_pairs={{0,16},{1,17},{2,18},{3,19},{4,20},{5,21},{6,22},{7,23},{8,24},{9,... | collective-permute-start | bytes 884744 | tf_op jit(solution)/shard_map/ppermute | solution.py:149
  490.2 10.5 %copy-start.58 = (f32[128]{0:T(128)S(1)}, f32[128]{0:T(128)}, u32[]{:S(2)}) copy-start(f32[128]{0:T(128)} %copy-done.56) | copy-start | bytes 1540
  490.2 10.5 %copy-start.70 = (f32[128]{0:T(128)S(1)}, f32[128]{0:T(128)}, u32[]{:S(2)}) copy-start(f32[128]{0:T(128)} %get-tuple-element.51) | copy-start | bytes 1540
  490.2 14.3 %all-to-all-start.14 = ((bf16[8,24,768]{2,1,0:T(8,128)(2,1)}), bf16[8,24,768]{2,1,0:T(8,128)(2,1)}, u32[]{:S(2)}, u32[]{:S(2)}) async-start(bf16[8,24,768]{2,1,0:T(8,128)(2,1)} %bitcast.115), calls=%async_computation.14 | async-start | bytes 589824 | tf_op jit(solution)/shard_map/all_to_all | solution.py:42
  507.5 17.8 %copy-start.50 = (f32[3,512,64]{1,2,0:T(8,128)S(1)}, f32[3,512,64]{1,2,0:T(8,128)}, u32[]{:S(2)}) copy-start(f32[3,512,64]{1,2,0:T(8,128)} %get-tuple-element.76) | copy-start | bytes 1179652
  549.6 6.1 collective-permute-start.15
  551.6 12.0 %collective-permute-start.18 = (bf16[8,48,896]{2,1,0:T(8,128)(2,1)}, bf16[8,48,896]{2,1,0:T(8,128)(2,1)}, u32[]{:S(2)}, u32[]{:S(2)}) collective-permute-start(bf16[8,48,896]{2,1,0:T(8,128)(2,1)} %dynamic-slice_bitcast_fusion), channel_id=1, source_target_pairs={{0,1},{1,0},{2,3},{3,2},{4,5},{5,4},{6,7},{7,6},{8,9},{9,8},{10,11... | collective-permute-start | bytes 2064392 | tf_op jit(solution)/shard_map/ppermute | solution.py:38
  559.2 15.8 %all-to-all-start.15 = ((bf16[4,128,768]{2,1,0:T(8,128)(2,1)}), bf16[4,128,768]{2,1,0:T(8,128)(2,1)}, u32[]{:S(2)}, u32[]{:S(2)}) async-start(bf16[4,128,768]{2,1,0:T(8,128)(2,1)} %bitcast.451), calls=%async_computation.15 | async-start | bytes 1572864 | tf_op jit(solution)/shard_map/all_to_all | solution.py:42
  575.0 16.1 %all-to-all-start.9 = ((bf16[4,64,768]{2,1,0:T(8,128)(2,1)}), bf16[4,64,768]{2,1,0:T(8,128)(2,1)}, u32[]{:S(2)}, u32[]{:S(2)}) async-start(bf16[4,64,768]{2,1,0:T(8,128)(2,1)} %bitcast.73), calls=%async_computation.9 | async-start | bytes 786432 | tf_op jit(solution)/shard_map/all_to_all | solution.py:42
  591.1 22.2 %all-to-all-start.18 = ((bf16[4,2,48,896]{3,2,1,0:T(8,128)(2,1)}), bf16[4,2,48,896]{3,2,1,0:T(8,128)(2,1)}, u32[]{:S(2)}, u32[]{:S(2)}) async-start(bf16[4,2,48,896]{3,2,1,0:T(8,128)(2,1)} %bitcast.392), calls=%async_computation.18 | async-start | bytes 1376256 | tf_op jit(solution)/shard_map/all_to_all | solution.py:42
  597.0 2.2 collective-permute-start.17
  613.3 21.7 %all-to-all-start.17 = ((bf16[4,2,48,896]{3,2,1,0:T(8,128)(2,1)}), bf16[4,2,48,896]{3,2,1,0:T(8,128)(2,1)}, u32[]{:S(2)}, u32[]{:S(2)}) async-start(bf16[4,2,48,896]{3,2,1,0:T(8,128)(2,1)} %bitcast.393), calls=%async_computation.17 | async-start | bytes 1376256 | tf_op jit(solution)/shard_map/all_to_all | solution.py:42
  618.8 5.9 collective-permute-start.16
  635.0 17.5 %all-to-all-start.16 = ((bf16[4,64,768]{2,1,0:T(8,128)(2,1)}), bf16[4,64,768]{2,1,0:T(8,128)(2,1)S(1)}, u32[]{:S(2)}, u32[]{:S(2)}) async-start(bf16[4,64,768]{2,1,0:T(8,128)(2,1)} %bitcast.133), calls=%async_computation.16 | async-start | bytes 786432 | tf_op jit(solution)/shard_map/all_to_all | solution.py:42
  652.5 9.7 %all-to-all-start.19 = ((bf16[4,48,896]{2,1,0:T(8,128)(2,1)}), bf16[4,48,896]{2,1,0:T(8,128)(2,1)S(1)}, u32[]{:S(2)}, u32[]{:S(2)}) async-start(bf16[4,48,896]{2,1,0:T(8,128)(2,1)} %bitcast.155), calls=%async_computation.19 | async-start | bytes 688128 | tf_op jit(solution)/shard_map/all_to_all | solution.py:42
  (55 other events, 171.2 us)
Sparse Core Ops, SparseCore 0:
  70.0 11.3 all-gather.10
  163.2 10.6 all-gather.12

commit v2 on v1

v2 whole, which is shorter than its diff:
```python
import jax
import jax.numpy as jnp
from jax import lax
from jax.experimental import pallas as pl
from jax.experimental.pallas import tpu as pltpu
from jax.sharding import Mesh, PartitionSpec as P

HEAD_DIM = 64
EPSILON = 1e-06
SCORE_SCALE = 0.125
HIGHEST = lax.Precision.HIGHEST
F32 = jnp.float32
BF16 = jnp.bfloat16

WIDE = ("z", "q", "h")
CHIPS = ("h", "pipe")
PARTS = ("q", "tp")
SWAP = [(0, 1), (1, 0)]
VMEM_BYTES = 48 * 1024 * 1024


def dot(left, right, contract, precision=None):
    return lax.dot_general(
        left, right, (contract, ((), ())), precision=precision, preferred_element_type=F32
    )


def mm(left, right):
    return dot(left, right, ((1,), (0,)))


def mm_nt(left, right):
    return dot(left, right, ((1,), (1,)))


def mm_tn(left, right):
    return dot(left, right, ((0,), (0,)))


def swapped(values, axis):
    return lax.ppermute(values, axis, SWAP)


def exchanged(values, axes):
    return lax.all_to_all(values, axes, split_axis=0, concat_axis=0, tiled=True)


def norm_rows(values, gain_vector):
    inverse = lax.rsqrt(jnp.mean(values * values, axis=-1, keepdims=True) + EPSILON)
    return (inverse, (values * inverse * gain_vector).astype(BF16))


def norm_back(values, inverse, gain_vector, grad_normed):
    scaled = grad_normed * gain_vector
    grad_values = inverse * scaled - values * (inverse * inverse * inverse) * jnp.mean(
        scaled * values, axis=-1, keepdims=True
    )
    grad_gain = jnp.sum(grad_normed * values * inverse, axis=0)
    return (grad_values, grad_gain)


def sum_parts(values):
    if lax.axis_size("q") == 1:
        mine = lax.axis_index("tp")
        kept = lax.dynamic_index_in_dim(values, mine, 0, keepdims=False)
        other = lax.dynamic_index_in_dim(values, 1 - mine, 0, keepdims=False)
        got = swapped(other.astype(BF16), "tp")
        return kept.astype(F32) + got.astype(F32)
    return jnp.sum(exchanged(values.astype(BF16), PARTS).astype(F32), axis=0)


def sum_chips(values):
    chunks = exchanged(values.astype(BF16).reshape(4, -1, values.shape[-1]), CHIPS)
    return jnp.sum(chunks.astype(F32), axis=0)


def after(value, *others):
    return lax.optimization_barrier((value,) + others)[0]


def from_z(values):
    places = lax.axis_size("z") * lax.axis_size("q")
    return exchanged(jnp.broadcast_to(values[None], (places,) + values.shape), ("z", "q"))


def spread_weights(query_weight, key_weight, value_weight, output_weight, extras):
    rows, cols = query_weight.shape
    half, group = (rows // 2, cols // 2)
    packed = jnp.stack([query_weight, key_weight, value_weight, output_weight.T])
    packed = packed.reshape(4, 2, half, 2, group).transpose(1, 3, 2, 0, 4)
    by_core = exchanged(packed, "tp").reshape(4, half, 4 * group)
    small = jnp.broadcast_to(extras[None], (4,) + extras.shape)
    by_chip = exchanged(jnp.concatenate([by_core, small], axis=-1), CHIPS)
    return by_chip.reshape(2, 2, half, -1)


def gather_section(own):
    mine = from_z(own)
    other = swapped(mine, "tp")
    core = lax.axis_index("tp")
    low, high = (jnp.where(core == 0, mine, other), jnp.where(core == 0, other, mine))
    return jnp.stack([low, high], axis=2).reshape(-1, own.shape[-1])


def scatter_start(grads):
    width = grads.shape[-1]
    places = lax.axis_size("z") * lax.axis_size("q")
    split = grads.reshape(places * 2, 2, -1, width)
    mine = lax.axis_index("tp")
    kept = lax.dynamic_index_in_dim(split, mine, 1, keepdims=False)
    got = swapped(lax.dynamic_index_in_dim(split, 1 - mine, 1, keepdims=False), "tp")
    both = (kept.astype(F32) + got.astype(F32)).astype(BF16)
    moved = exchanged(both.reshape(places, 2, -1, width), ("z", "q"))
    return jnp.sum(moved.astype(F32), axis=0).astype(BF16)


def scatter_end(sums):
    half, width = sums[0].shape[1:]
    group = width // 4
    by_chip = exchanged(jnp.stack(sums, axis=1).reshape(4, half, width), CHIPS)
    by_core = exchanged(by_chip.reshape(2, 2, half, 4, group), "tp")
    return by_core.transpose(3, 0, 2, 1, 4).reshape(4, 2 * half, 2 * group).astype(F32)


def dispatch_table(routes, expert_count, most_rows):
    blocks, block_rows = routes.shape
    expert_hits = (
        routes[:, :, None] == jnp.arange(expert_count, dtype=jnp.int32)[None, None, :]
    ).astype(F32)
    order = jnp.arange(block_rows)
    before = (order[:, None] > order[None, :]).astype(F32)
    ranks = jnp.einsum("tu,bue->bte", before, expert_hits)
    slot_rank = jnp.sum(ranks * expert_hits, axis=2).astype(jnp.int32)
    place = jnp.arange(blocks, dtype=jnp.int32)[:, None] * most_rows + slot_rank
    target = (routes * (blocks * most_rows) + place).reshape(-1)
    slots = jnp.arange(expert_count * blocks * most_rows, dtype=jnp.int32)
    return (slots[:, None] == target[None, :]).astype(BF16)


def to_experts(packed, section):
    arrived = exchanged(packed, WIDE)
    hopped = lax.ppermute(arrived, "pipe", [(1 - section, section)])
    near = lax.all_gather(arrived, "tp", axis=0, tiled=False)
    far = lax.all_gather(hopped, "tp", axis=0, tiled=False)
    return jnp.stack([near, far], axis=1)


def from_experts(results, section):
    mine = lax.axis_index("tp")
    kept = lax.dynamic_index_in_dim(results, mine, 0, keepdims=False)
    got = swapped(lax.dynamic_index_in_dim(results, 1 - mine, 0, keepdims=False), "tp")
    total = (kept.astype(F32) + got.astype(F32)).astype(BF16)
    hopped = lax.ppermute(total[1], "pipe", [(section, 1 - section)])
    back = jnp.where(lax.axis_index("pipe") == section, total[0], hopped)
    return exchanged(back, WIDE)


def whole_call(kernel, out_shape, *operands, flops=0, exps=0):
    moved = sum(v.size * v.dtype.itemsize for v in operands)
    return pl.pallas_call(
        kernel,
        out_shape=out_shape,
        compiler_params=pltpu.CompilerParams(vmem_limit_bytes=VMEM_BYTES),
        cost_estimate=pl.CostEstimate(flops=flops, bytes_accessed=moved, transcendentals=exps),
    )(*operands)


def flipped(values):
    return values.astype(F32).T.astype(BF16)


def attend_kernel(queries, keys_values, w_out_rows, part, attended, attended_flat, log_total):
    group = queries.shape[1]
    queries_flat = flipped(queries[...]) * SCORE_SCALE
    values_flat = flipped(keys_values[:, group:])
    for head in range(group // HEAD_DIM):
        lanes = slice(head * HEAD_DIM, (head + 1) * HEAD_DIM)
        scores = mm(keys_values[:, lanes], queries_flat[lanes])
        peak = jnp.max(scores, axis=0, keepdims=True)
        weights = jnp.exp(scores - peak)
        total = jnp.sum(weights, axis=0, keepdims=True)
        attended_flat[lanes, :] = mm(values_flat[lanes], weights.astype(BF16)) / total
        log_total[head : head + 1, :] = peak + jnp.log(total)
    attended[...] = attended_flat[...].T.astype(BF16)
    part[...] = mm_nt(attended[...], w_out_rows[...]).astype(BF16)


def attend(queries, keys_values, w_out_rows):
    rows, group = queries.shape
    keys = keys_values.shape[0]
    return whole_call(
        attend_kernel,
        (
            jax.ShapeDtypeStruct((rows, w_out_rows.shape[0]), BF16),
            jax.ShapeDtypeStruct((rows, group), BF16),
            jax.ShapeDtypeStruct((group, rows), F32),
            jax.ShapeDtypeStruct((8, rows), F32),
        ),
        queries,
        keys_values,
        w_out_rows,
        flops=4 * rows * keys * group,
        exps=rows * keys * group // HEAD_DIM,
    )


def attend_back_kernel(
    grad_rows, w_out_rows, queries, keys_values, attended_flat, log_total, grad_queries, grad_kv
):
    group = queries.shape[1]
    keys = keys_values.shape[0]
    chunk = min(512, keys)
    queries_flat = flipped(queries[...]) * SCORE_SCALE
    keys_flat = flipped(keys_values[:, :group])
    grad_flat = dot(w_out_rows[...], grad_rows[...], ((0,), (1,))).astype(BF16)
    products = grad_flat.astype(F32) * attended_flat[...]
    grad_queries_flat = []
    for head in range(group // HEAD_DIM):
        lanes = slice(head * HEAD_DIM, (head + 1) * HEAD_DIM)
        value_lanes = slice(group + head * HEAD_DIM, group + (head + 1) * HEAD_DIM)
        delta = jnp.sum(products[lanes], axis=0, keepdims=True)
        level = log_total[head : head + 1, :]
        query, grad = (queries_flat[lanes], grad_flat[lanes])
        own = jnp.zeros((HEAD_DIM, queries.shape[0]), F32)
        for begin in range(0, keys, chunk):
            here = slice(begin, begin + chunk)
            probs = jnp.exp(mm(keys_values[here, lanes], query) - level)
            grad_probs = mm(keys_values[here, value_lanes], grad)
            grad_scores = (probs * (grad_probs - delta)).astype(BF16)
            grad_kv[here, lanes] = mm_nt(grad_scores, query).astype(BF16)
            grad_kv[here, value_lanes] = mm_nt(probs.astype(BF16), grad).astype(BF16)
            own = own + mm(keys_flat[lanes, here], grad_scores)
        grad_queries_flat.append(own * SCORE_SCALE)
    grad_queries[...] = jnp.concatenate(grad_queries_flat, axis=0).T.astype(BF16)


def attend_back(grad_rows, w_out_rows, queries, keys_values, attended_flat, log_total):
    rows, group = queries.shape
    keys = keys_values.shape[0]
    return whole_call(
        attend_back_kernel,
        (
            jax.ShapeDtypeStruct((rows, group), BF16),
            jax.ShapeDtypeStruct((keys, 2 * group), BF16),
        ),
        grad_rows,
        w_out_rows,
        queries,
        keys_values,
        attended_flat,
        log_total,
        flops=10 * rows * keys * group,
        exps=rows * keys * group // HEAD_DIM,
    )


def attention_forward(inputs, weights):
    w_qkv, w_out_rows, gain_attn = weights[:3]
    group = w_out_rows.shape[1]
    values_in = inputs.astype(F32)
    inverse_a, normed_a = norm_rows(values_in, gain_attn)
    rows_a = lax.all_gather(normed_a, CHIPS, axis=0, tiled=True)
    qkv = mm(rows_a, w_qkv).astype(BF16)
    queries = qkv[:, :group]
    keys_values = lax.all_gather(qkv[:, group:], PARTS, axis=0, tiled=True)
    part, attended, attended_flat, log_total = attend(queries, keys_values, w_out_rows)
    hidden = values_in + sum_chips(part)
    kept = (values_in, inverse_a, rows_a, queries, keys_values, attended, attended_flat, log_total)
    return hidden, kept


def attention_backward(grad_hidden, kept, weights, first):
    w_qkv, w_out_rows, gain_attn = weights[:3]
    values_in, inverse_a, rows_a, queries, keys_values, attended, attended_flat, log_total = kept
    low, first = lax.optimization_barrier((grad_hidden.astype(BF16), first))
    grad_rows = lax.all_gather(low, CHIPS, axis=0, tiled=True)
    grad_queries, grad_kv = attend_back(
        grad_rows, w_out_rows, queries, keys_values, attended_flat, log_total
    )
    parts = lax.axis_size("q") * lax.axis_size("tp")
    grad_kv = sum_parts(grad_kv.reshape(parts, -1, grad_kv.shape[-1])).astype(BF16)
    grad_qkv = jnp.concatenate([grad_queries, grad_kv], axis=-1)
    grad_normed_a = sum_chips(mm_nt(grad_qkv, w_qkv))
    grad_input_norm, grad_gain = norm_back(values_in, inverse_a, gain_attn, grad_normed_a)
    grads = jnp.concatenate(
        [mm_tn(rows_a, grad_qkv).astype(BF16), mm_tn(grad_rows, attended).astype(BF16)], axis=-1
    )
    return (grad_hidden + grad_input_norm).astype(BF16), (grad_gain, grads), first


def route_tokens(hidden, routes, weights, expert_count, most_rows):
    gain_moe, w_router = weights[3:]
    inverse_b, normed_b = norm_rows(hidden, gain_moe)
    router_probs = jax.nn.softmax(mm(normed_b, w_router), axis=-1)
    chosen = (
        routes.reshape(-1, 1) == jnp.arange(expert_count, dtype=jnp.int32)[None]
    ).astype(F32)
    gate = jnp.sum(router_probs * chosen, axis=-1, keepdims=True)
    return inverse_b, normed_b, router_probs, chosen, gate


def pack_rows(table, rows):
    wide = lax.axis_size("z") * lax.axis_size("q") * lax.axis_size("h")
    return mm(table, rows).astype(BF16).reshape(wide, -1, rows.shape[-1])


def unpack_rows(table, returned):
    return mm_tn(table, returned.reshape(table.shape[0], -1))


def experts_forward(slots, w_in, w_out):
    pre_act = mm(slots.reshape(-1, slots.shape[-1]), w_in)
    activated = jax.nn.gelu(pre_act).astype(BF16)
    return pre_act, activated, mm(activated, w_out).astype(BF16).reshape(slots.shape)


def experts_backward(grad_slots, pre_act, w_in, w_out):
    grad_act = mm_nt(grad_slots.reshape(-1, grad_slots.shape[-1]), w_out)
    unused_value, gelu_back = jax.vjp(jax.nn.gelu, pre_act)
    grad_pre = gelu_back(grad_act)[0].astype(BF16)
    return grad_pre, mm_nt(grad_pre, w_in).astype(BF16).reshape(grad_slots.shape)


def router_backward(grad_output, mixed, routed, weights, hidden, grad_rows):
    gain_moe, w_router = weights[3:]
    inverse_b, normed_b, router_probs, chosen, gate = routed
    grad_gate = jnp.sum(grad_output * mixed, axis=-1, keepdims=True)
    grad_logits = gate * grad_gate * (chosen - router_probs)
    grad_router = dot(grad_logits, normed_b.astype(F32), ((0,), (0,)), HIGHEST)
    grad_normed_router = dot(grad_logits, w_router.astype(F32), ((1,), (1,)), HIGHEST)
    grad_normed_b = grad_normed_router + grad_rows
    grad_hidden_norm, grad_gain = norm_back(hidden, inverse_b, gain_moe, grad_normed_b)
    return grad_output + grad_hidden_norm, grad_gain, grad_router


def shards(
    block_input,
    out_cotangent,
    routes,
    attn_gain,
    query_weight,
    key_weight,
    value_weight,
    output_weight,
    moe_gain,
    router_weight,
    expert_in,
    expert_out,
):
    micro_count, seq_count, half_rows, feature_dim = block_input.shape
    sequences = micro_count * seq_count
    expert_count = router_weight.shape[-1]
    most_rows = max(2, 3 * half_rows // (2 * expert_count))
    pipe, core = (lax.axis_index("pipe"), lax.axis_index("tp"))
    extra = -(-(2 + expert_count) // 128) * 128

    own_routes = lax.dynamic_slice_in_dim(
        routes[0, :, :, :, 0].reshape(sequences, -1), core * half_rows, half_rows, 1
    ).astype(BF16)
    other_routes = swapped(own_routes, "pipe")
    route_rows = jnp.stack(
        [
            jnp.where(pipe == 0, own_routes, other_routes),
            jnp.where(pipe == 0, other_routes, own_routes),
        ],
        axis=1,
    )
    route_rows = jnp.pad(route_rows, ((0, 0), (0, 14), (0, feature_dim - half_rows)))

    def to_planes(values):
        moved = exchanged(values, "z")
        pairs = moved.reshape(sequences // 2, 2, -1, feature_dim)
        return lax.dynamic_index_in_dim(pairs, pipe, 1, keepdims=False)

    here = to_planes(
        jnp.concatenate(
            [block_input.reshape(sequences, half_rows, feature_dim), route_rows], axis=1
        )
    )
    inputs = here[:, :half_rows].reshape(-1, feature_dim)
    section_routes = [
        here[:, half_rows + section, :half_rows].astype(jnp.int32) for section in range(2)
    ]

    small = jnp.concatenate([attn_gain[0][:, None], moe_gain[0][:, None], router_weight[0]], axis=-1)
    small = jnp.pad(small, ((0, 0), (0, extra - small.shape[-1])))
    spread = spread_weights(
        query_weight[0], key_weight[0], value_weight[0], output_weight[0], small
    )
    group = query_weight.shape[-1] // 2

    def parts_of(array):
        return (
            array[:, : 3 * group],
            array[:, 3 * group : 4 * group],
            array[:, 4 * group].astype(F32),
            array[:, 4 * group + 1].astype(F32),
            array[:, 4 * group + 2 : 4 * group + 2 + expert_count],
        )

    whole = gather_section(spread[:, 0])
    weights = [parts_of(whole), None]
    w_in, w_out = (expert_in[0, 0], expert_out[0, 0])

    hidden, kept_attn = attention_forward(inputs, weights[0])
    later = gather_section(after(spread[:, 1], whole))
    cotangent = to_planes(
        after(out_cotangent.reshape(sequences, half_rows, feature_dim), kept_attn[2])
    ).reshape(-1, feature_dim)
    routed = route_tokens(hidden, section_routes[0], weights[0], expert_count, most_rows)
    table = dispatch_table(section_routes[0], expert_count, most_rows)
    slots = to_experts(pack_rows(table, routed[1]), 0)
    pre_act, activated, result = experts_forward(slots, w_in, w_out)
    mixed = unpack_rows(table, from_experts(result, 0))
    first_output = (hidden + routed[4] * mixed).astype(BF16)
    first = (hidden, kept_attn, routed, table, slots, pre_act, activated, mixed)

    weights[1] = parts_of(later)
    hidden, kept_attn = attention_forward(first_output, weights[1])
    routed = route_tokens(hidden, section_routes[1], weights[1], expert_count, most_rows)
    table = dispatch_table(section_routes[1], expert_count, most_rows)
    grad_output = cotangent.astype(F32)
    both = jnp.concatenate(
        [
            pack_rows(table, routed[1]),
            pack_rows(table, (routed[4] * grad_output).astype(BF16)),
        ],
        axis=1,
    )
    arrived = to_experts(both, 1)
    count = both.shape[1] // 2
    slots, grad_slots = (arrived[..., :count, :], arrived[..., count:, :])
    pre_act, activated, result = experts_forward(slots, w_in, w_out)
    grad_pre, grad_rows = experts_backward(grad_slots, pre_act, w_in, w_out)
    returned = from_experts(jnp.concatenate([result, grad_rows], axis=-2), 1)
    mixed = unpack_rows(table, returned[:, :count])
    second_output = (hidden + routed[4] * mixed).astype(BF16)
    expert_parts = [None, (slots, grad_pre, activated, grad_slots)]

    def to_owners(first, second, small=None):
        first, second = (v.reshape(sequences // 2, 1, half_rows, feature_dim) for v in (first, second))
        kept, sent = (jnp.where(pipe == 0, first, second), jnp.where(pipe == 0, second, first))
        if small is not None:
            kept_small = jnp.where(pipe == 0, small[0], small[1])
            sent_small = jnp.where(pipe == 0, small[1], small[0]).astype(BF16)
            sent = jnp.concatenate([sent.reshape(-1, feature_dim), sent_small], axis=0)
        got = swapped(sent, "pipe")
        if small is not None:
            kept_small = kept_small + got[-kept_small.shape[0] :].astype(F32)
            got = got[: -kept_small.shape[0]].reshape(first.shape)
        both = jnp.where(
            pipe == 0, jnp.concatenate([kept, got], axis=1), jnp.concatenate([got, kept], axis=1)
        ).reshape(sequences, half_rows, feature_dim)
        if small is None:
            home = exchanged(both, "z")
        else:
            count, planes = (kept_small.shape[0], lax.axis_size("z"))
            by_plane = kept_small.astype(BF16).reshape(count, planes, -1).transpose(1, 0, 2)
            by_plane = jnp.pad(by_plane, ((0, 0), (0, 0), (0, feature_dim - by_plane.shape[-1])))
            moved = exchanged(jnp.concatenate([both, by_plane], axis=1), "z")
            home = moved[:, :half_rows]
            sums = jnp.sum(moved[:, half_rows:, : feature_dim // planes].astype(F32), axis=0)
            rest = lax.axis_size("q") * lax.axis_size("h") * lax.axis_size("tp")
            by_rest = sums.astype(BF16).reshape(count, rest, -1).transpose(1, 0, 2)
            small = jnp.sum(exchanged(by_rest, ("q", "h", "tp")).astype(F32), axis=0)
        return home.reshape(1, micro_count, seq_count, half_rows, feature_dim), small

    def small_rows(grad_gain_attn, grad_gain_moe, grad_router):
        stacked = jnp.concatenate([grad_gain_attn[None], grad_gain_moe[None], grad_router], axis=0)
        return jnp.pad(stacked, ((0, -stacked.shape[0] % 16), (0, 0)))

    grad_hidden, grad_gain_moe, grad_router = router_backward(
        grad_output, mixed, routed, weights[1], hidden, unpack_rows(table, returned[:, count:])
    )
    second_grad, (grad_gain_attn, grads), unused = attention_backward(
        grad_hidden, kept_attn, weights[1], grad_gain_moe
    )
    small_second = small_rows(grad_gain_attn, grad_gain_moe, grad_router)
    layer_outputs, unused = to_owners(first_output, second_output)
    sums_second = scatter_start(grads)

    hidden, kept_attn, routed, table, slots, pre_act, activated, mixed = first
    grad_output = second_grad.astype(F32)
    grad_slots = to_experts(pack_rows(table, (routed[4] * grad_output).astype(BF16)), 0)
    grad_pre, grad_rows = experts_backward(grad_slots, pre_act, w_in, w_out)
    expert_parts[0] = (slots, grad_pre, activated, grad_slots)
    grad_hidden, grad_gain_moe, grad_router = router_backward(
        grad_output, mixed, routed, weights[0], hidden, unpack_rows(table, from_experts(grad_rows, 0))
    )
    first_grad, (grad_gain_attn, grads), (layer_outputs, sums_second) = attention_backward(
        grad_hidden, kept_attn, weights[0], (layer_outputs, sums_second)
    )
    small_first = small_rows(grad_gain_attn, grad_gain_moe, grad_router)
    sums_first = scatter_start(grads)
    grads_home, small = to_owners(first_grad, second_grad, (small_first, small_second))

    slots, grad_pre, activated, grad_slots = (
        jnp.where(pipe == 0, first, second).reshape(-1, first.shape[-1])
        for first, second in zip(*expert_parts)
    )
    grad_w_in = mm_tn(slots, grad_pre)
    grad_w_out = mm_tn(activated, grad_slots)
    mats = scatter_end([sums_first, sums_second])
    return (
        layer_outputs,
        grads_home,
        small[0][None],
        mats[0][None],
        mats[1][None],
        mats[2][None],
        mats[3].T[None],
        small[1][None],
        small[2 : 2 + expert_count].T[None],
        grad_w_in[None, None],
        grad_w_out[None, None],
    )


def solution(mesh):
    pipe, wide, tp = (mesh.shape["pipe"], mesh.shape["wide"], mesh.shape["tp"])
    planes = Mesh(mesh.devices.reshape(pipe, 4, wide // 8, 2, tp), ("pipe", "z", "q", "h", "tp"))
    rows = WIDE + ("tp",)
    placed = (
        P(None, None, rows, None),
        P(None, None, rows, None),
        P("pipe", None, None, WIDE, None),
        P("pipe", rows),
        P("pipe", WIDE, "tp"),
        P("pipe", WIDE, "tp"),
        P("pipe", WIDE, "tp"),
        P("pipe", "tp", WIDE),
        P("pipe", rows),
        P("pipe", rows, None),
        P("pipe", WIDE, None, "tp"),
        P("pipe", WIDE, "tp", None),
    )
    return jax.shard_map(
        shards,
        mesh=planes,
        in_specs=placed,
        out_specs=(
            P("pipe", None, None, rows, None),
            P("pipe", None, None, rows, None),
            P("pipe", rows),
            P("pipe", WIDE, "tp"),
            P("pipe", WIDE, "tp"),
            P("pipe", WIDE, "tp"),
            P("pipe", "tp", WIDE),
            P("pipe", rows),
            P("pipe", rows, None),
            P("pipe", WIDE, None, "tp"),
            P("pipe", WIDE, "tp", None),
        ),
        check_vma=False,
    )
```

time: 698 us -> 592 us (0.85)
  local copies, waits for them, and re-layouts: 97.1 us -> 47.7 us
  matrix products: 115 us -> 66.1 us
  starting transfers between devices: 113 us -> 88.9 us
  blocking collectives: 131 us -> 153 us
  other arithmetic: 61.4 us -> 43.2 us
  Pallas kernels: 0 us -> 16.9 us
    all_to_all x1 -> x6, blocking collectives: 4.05 us -> 89.1 us  [exchanged(): return lax.all_to_all(values, axes, split_axis=0, concat_axis=0, tiled=True)]
    all_gather x8 -> x6, blocking collectives: 107 us -> 54.3 us  [the longest x2 25 us: attention_backward(): grad_rows = lax.all_gather(low, CHIPS, axis=0, tiled=True)]
    dot_general x20 -> x0, matrix products: 40.5 us -> none  [the longest x12 32.6 us: bmm(): lax.dot_general(left, right, (contract, ((0,), (0,))), preferred_element_...]
    all_to_all x20 -> x17, starting transfers between devices: 85.6 us -> 67.8 us  [exchanged(): return lax.all_to_all(values, axes, split_axis=0, concat_axis=0, tiled=True)]
    pallas_call x0 -> x4, Pallas kernels: none -> 16.9 us  [whole_call(): pl.pallas_call(kernel, out_shape=out_shape, compiler_params=pltpu.Compile...]
    reshape x12 -> x5, local copies, waits for them, and re-layouts: 16.7 us -> 0.89 us  [the longest x1 0.35 us: scatter_end(): by_core = exchanged(by_chip.reshape(2, 2, half, 4, group), 'tp')]
    concatenate x8 -> x2, local copies, waits for them, and re-layouts: 19.7 us -> 4.81 us  [attention_backward(): jnp.concatenate([mm_tn(rows_a, grad_qkv).astype(BF16), mm_tn(grad_rows, a...]
    all_to_all x20 -> x17, waiting for transfers between devices: 104 us -> 88.9 us  [exchanged(): return lax.all_to_all(values, axes, split_axis=0, concat_axis=0, tiled=True)]
  transfers between devices with their start and end apart: 41 -> 37, of which waited for: 26 -> 24; matrix products, arithmetic and copies ran while one was open for 17% -> 16% of each run, Pallas kernels for 0% -> 1%
where the time goes in v2:
time: 592 us; the launch traced here: 582 us
  blocking collectives  153 us (26%)
  waiting for transfers between devices  149 us (25%)
  starting transfers between devices  88.9 us (15%)
  matrix products  66.1 us (11%)
  local copies, waits for them, and re-layouts  47.7 us (8%)
  other arithmetic  43.2 us (7%)
  Pallas kernels  16.9 us (3%)
  between operations  16.8 us (3%)
    all_to_all x6, blocking collectives, exchanged(): return lax.all_to_all(values, axes, split_axis=0, concat_axis=0, tiled=True)  89.1 us
    all_to_all x17, waiting for transfers between devices, exchanged(): return lax.all_to_all(values, axes, split_axis=0, concat_axis=0, tiled=True)  88.9 us
    all_to_all x17, starting transfers between devices, exchanged(): return lax.all_to_all(values, axes, split_axis=0, concat_axis=0, tiled=True)  67.8 us
    dot_general x32, matrix products, dot(): lax.dot_general(left, right, (contract, ((), ())), precision=precision, p...  65.8 us
    ppermute x3, waiting for transfers between devices, from_experts(): hopped = lax.ppermute(total[1], 'pipe', [(section, 1 - section)])  27.4 us
    all_gather x2, blocking collectives, attention_backward(): grad_rows = lax.all_gather(low, CHIPS, axis=0, tiled=True)  25 us
    all_gather x2, blocking collectives, attention_forward(): rows_a = lax.all_gather(normed_a, CHIPS, axis=0, tiled=True)  24.6 us
    pallas_call x4, Pallas kernels, whole_call(): pl.pallas_call(kernel, out_shape=out_shape, compiler_params=pltpu.Compile...  16.9 us
  transfers between devices with their start and end apart: 37, of which 24 were waited for; matrix products, arithmetic and copies ran while one was open for 16% of the time, Pallas kernels for 1%

profile of v2, /device:TPU:0, one launch (start us, length us, event | category | flops | bytes accessed | tf_op | source)
XLA Modules:
  0.0 582.4 jit_solution(2531997644818329967)
XLA Ops:
  13.8 3.5 all-to-all-start.1
  19.3 12.1 %all_to_all.115 = bf16[4,48,896]{2,1,0:T(8,128)(2,1)S(1)} all-to-all(bf16[4,48,896]{2,1,0:T(8,128)(2,1)S(1)} %pad_maximum_fusion.14), channel_id=1, replica_groups=mesh['pipe'=2,'z'=4,'q'=1,'h'=2,'tp'=2] {'h','pipe'}, dimensions={0} | all-to-all | bytes 688128 | tf_op jit(solution)/shard_map/all_to_all | solution.py:45
  33.1 4.9 all-to-all-start.3
  38.8 2.8 collective-permute-done
  42.5 12.2 %all-to-all-done.3 = bf16[4,2,48,896]{3,2,1,0:T(8,128)(2,1)} async-done(((bf16[4,2,48,896]{3,2,1,0:T(8,128)(2,1)}), bf16[4,2,48,896]{3,2,1,0:T(8,128)(2,1)}, u32[]{:S(2)}, u32[]{:S(2)}) %all-to-all-start.3) | async-done | bytes 688160 | tf_op jit(solution)/shard_map/all_to_all | solution.py:45
  54.7 3.5 all-to-all-start
  58.2 13.2 %all-to-all-done = bf16[4,80,768]{2,1,0:T(8,128)(2,1)S(1)} async-done(((bf16[4,80,768]{2,1,0:T(8,128)(2,1)}), bf16[4,80,768]{2,1,0:T(8,128)(2,1)S(1)}, u32[]{:S(2)}, u32[]{:S(2)}) %all-to-all-start) | async-done | bytes 491552 | tf_op jit(solution)/shard_map/all_to_all | solution.py:45
  73.8 12.3 %all_gather.54 = bf16[512,768]{1,0:T(8,128)(2,1)S(1)} all-gather(bf16[128,768]{1,0:T(8,128)(2,1)S(1)} %fusion.96), channel_id=1, replica_groups=mesh['pipe'=2,'z'=4,'q'=1,'h'=2,'tp'=2] {'h','pipe'}, dimensions={0}, use_global_device_ids=true | all-gather | bytes 983040 | tf_op jit(solution)/shard_map/all_gather | solution.py:262
  89.9 4.1 shard_map.203
  96.3 4.2 all-to-all-start.5
  101.0 11.0 %all-to-all-done.5 = bf16[4,128,768]{2,1,0:T(8,128)(2,1)} async-done(((bf16[4,128,768]{2,1,0:T(8,128)(2,1)}), bf16[4,128,768]{2,1,0:T(8,128)(2,1)}, u32[]{:S(2)}, u32[]{:S(2)}) %all-to-all-start.5) | async-done | bytes 786464 | tf_op jit(solution)/shard_map/all_to_all | solution.py:45
  114.6 14.0 %all_to_all.116 = bf16[8,24,768]{2,1,0:T(8,128)(2,1)} all-to-all(bf16[8,24,768]{2,1,0:T(8,128)(2,1)S(1)} %bitcast.321), channel_id=1, replica_groups=mesh['pipe'=2,'z'=4,'q'=1,'h'=2,'tp'=2] {'z','q','h'}, dimensions={0} | all-to-all | bytes 589824 | tf_op jit(solution)/shard_map/all_to_all | solution.py:45
  131.7 4.2 all-to-all-start.8
  135.9 2.6 all-gather
  138.5 2.7 all-gather.1
  144.0 2.9 fusion.45
  148.9 3.4 all-to-all-done.8
  153.7 5.0 collective-permute-start.4
  160.1 5.6 collective-permute-done.4
  166.4 4.1 all-to-all-start.7
  173.6 6.6 %all-to-all-done.7 = bf16[8,24,768]{2,1,0:T(8,128)(2,1)} async-done(((bf16[8,24,768]{2,1,0:T(8,128)(2,1)}), bf16[8,24,768]{2,1,0:T(8,128)(2,1)}, u32[]{:S(2)}, u32[]{:S(2)}) %all-to-all-start.7) | async-done | bytes 294944 | tf_op jit(solution)/shard_map/all_to_all | solution.py:45
  180.2 4.1 all-to-all-start.4
  187.7 12.2 %all_gather.60 = bf16[512,768]{1,0:T(8,128)(2,1)S(1)} all-gather(bf16[128,768]{1,0:T(8,128)(2,1)S(1)} %fusion.81), channel_id=1, replica_groups=mesh['pipe'=2,'z'=4,'q'=1,'h'=2,'tp'=2] {'h','pipe'}, dimensions={0}, use_global_device_ids=true | all-gather | bytes 983040 | tf_op jit(solution)/shard_map/all_gather | solution.py:262
  203.4 4.1 shard_map.204
  209.8 4.3 all-to-all-start.9
  216.0 10.3 %all-to-all-done.9 = bf16[4,128,768]{2,1,0:T(8,128)(2,1)} async-done(((bf16[4,128,768]{2,1,0:T(8,128)(2,1)}), bf16[4,128,768]{2,1,0:T(8,128)(2,1)}, u32[]{:S(2)}, u32[]{:S(2)}) %all-to-all-start.9) | async-done | bytes 786464 | tf_op jit(solution)/shard_map/all_to_all | solution.py:45
  229.9 22.5 %all_to_all.117 = bf16[8,48,768]{2,1,0:T(8,128)(2,1)} all-to-all(bf16[8,48,768]{2,1,0:T(8,128)(2,1)S(1)} %pad_maximum_fusion.9), channel_id=1, replica_groups=mesh['pipe'=2,'z'=4,'q'=1,'h'=2,'tp'=2] {'z','q','h'}, dimensions={0} | all-to-all | bytes 1179648 | tf_op jit(solution)/shard_map/all_to_all | solution.py:45
  252.5 3.5 collective-permute-start.6
  256.0 10.5 %collective-permute-done.6 = bf16[8,48,768]{2,1,0:T(8,128)(2,1)} collective-permute-done((bf16[8,48,768]{2,1,0:T(8,128)(2,1)}, bf16[8,48,768]{2,1,0:T(8,128)(2,1)}, u32[]{:S(2)}, u32[]{:S(2)}) %collective-permute-start.6) | collective-permute-done | bytes 589856 | tf_op jit(solution)/shard_map/ppermute | solution.py:142
  266.5 9.7 %all-gather.11.cloned.1.call-done = bf16[16,48,768]{2,1,0:T(8,128)(2,1)} async-done(((bf16[8,48,768]{2,1,0:T(8,128)(2,1)}), bf16[16,48,768]{2,1,0:T(8,128)(2,1)}) %all-gather.11.cloned.1.call-update) | async-done | bytes 1179664 | tf_op jit(solution)/shard_map/all_gather | solution.py:144
  276.2 3.6 broadcast_select_fusion.1
  281.8 2.9 fusion.48
  284.7 4.4 fusion.13
  291.5 2.6 collective-permute-done.7
  297.8 16.3 %collective-permute-done.8 = bf16[8,48,768]{2,1,0:T(8,128)(2,1)} collective-permute-done((bf16[8,48,768]{2,1,0:T(8,128)(2,1)}, bf16[8,48,768]{2,1,0:T(8,128)(2,1)}, u32[]{:S(2)}, u32[]{:S(2)}) %collective-permute-start.8) | collective-permute-done | bytes 589856 | tf_op jit(solution)/shard_map/ppermute | solution.py:153
  315.4 21.9 %all_to_all.118 = bf16[8,48,768]{2,1,0:T(8,128)(2,1)S(1)} all-to-all(bf16[8,48,768]{2,1,0:T(8,128)(2,1)S(1)} %fusion.72), channel_id=1, replica_groups=mesh['pipe'=2,'z'=4,'q'=1,'h'=2,'tp'=2] {'z','q','h'}, dimensions={0} | all-to-all | bytes 1179648 | tf_op jit(solution)/shard_map/all_to_all | solution.py:45
  340.0 11.2 %all_gather.66.grad_rows = bf16[512,768]{1,0:T(8,128)(2,1)S(1)} all-gather(bf16[128,768]{1,0:T(8,128)(2,1)S(1)} %get-tuple-element.33), channel_id=1, replica_groups=mesh['pipe'=2,'z'=4,'q'=1,'h'=2,'tp'=2] {'h','pipe'}, dimensions={0}, use_global_device_ids=true | all-gather | bytes 983040 | tf_op jit(solution)/shard_map/all_gather | solution.py:276
  351.3 4.4 shard_map.205
  358.5 14.5 %all_to_all.119 = bf16[4,128,768]{2,1,0:T(8,128)(2,1)S(1)} all-to-all(bf16[4,128,768]{2,1,0:T(8,128)(2,1)S(1)} %bitcast.333), channel_id=1, replica_groups=mesh['pipe'=2,'z'=4,'q'=1,'h'=2,'tp'=2] {'h','pipe'}, dimensions={0} | all-to-all | bytes 1572864 | tf_op jit(solution)/shard_map/all_to_all | solution.py:45
  376.3 4.1 all-to-all-start.13
  382.5 3.2 convolution_convert_fusion.1
  385.7 3.6 all-to-all-done.13
  396.5 2.6 all-gather.4
  402.6 6.2 %fusion.6 = bf16[768,1536]{1,0:T(8,128)(2,1)S(1)} fusion(f32[768,1536]{1,0:T(8,128)} %copy-done.134, bf16[768,768]{1,0:T(8,128)(2,1)S(1)} %bitcast.319, bf16[1,1,1536,768]{3,2,1,0:T(8,128)(2,1)S(1)} %copy-done), kind=kOutput, calls=%fused_computation.10 | convolution fusion | flops 1835532288 | bytes 10616832 | tf_op jit(solution)/shard_map/dot_general | solution.py:23
  413.1 4.2 all-to-all-start.16
  418.9 4.8 collective-permute-start.12
  425.3 5.5 collective-permute-done.12
  433.9 4.1 all-to-all-start.14
  447.4 4.1 all-to-all-start.15
  455.5 5.7 all-to-all-done.15
  461.3 13.8 %all_gather.71.grad_rows = bf16[512,768]{1,0:T(8,128)(2,1)S(1)} all-gather(bf16[128,768]{1,0:T(8,128)(2,1)} %get-tuple-element.40), channel_id=1, replica_groups=mesh['pipe'=2,'z'=4,'q'=1,'h'=2,'tp'=2] {'h','pipe'}, dimensions={0}, use_global_device_ids=true | all-gather | bytes 983040 | tf_op jit(solution)/shard_map/all_gather | solution.py:276
  478.2 4.4 shard_map.206
  486.4 4.2 all-to-all-start.17
  499.2 3.2 all-to-all-done.17
  507.4 3.5 all-to-all-start.20
  512.5 5.6 collective-permute-done.16
  519.1 7.8 %all-to-all-done.20 = bf16[4,2,48,768]{3,2,1,0:T(8,128)(2,1)S(1)} async-done(((bf16[4,2,48,768]{3,2,1,0:T(8,128)(2,1)}), bf16[4,2,48,768]{3,2,1,0:T(8,128)(2,1)S(1)}, u32[]{:S(2)}, u32[]{:S(2)}) %all-to-all-start.20) | async-done | bytes 589856 | tf_op jit(solution)/shard_map/all_to_all | solution.py:45
  526.9 4.4 all-to-all-start.18
  531.3 10.6 %convolution_bitcast_fusion = f32[1,1,1536,768]{3,2,1,0:T(8,128)} fusion(bf16[768,768]{1,0:T(8,128)(2,1)} %bitcast.315, pred[]{:T(512)S(6)} %eq.42, f32[768,1536]{1,0:T(8,128)} %copy-done.134, f32[768,1536]{1,0:T(8,128)} %copy-done.135), kind=kOutput, calls=%fused_computation.20 | convolution fusion | flops 1834352640 | bytes 15335425 | tf_op jit(solution)/shard_map/dot_general | solution.py:23
  542.0 4.2 convolution_bitcast_fusion.1
  547.8 3.2 all-to-all-start.19
  554.9 3.5 all-to-all-start.21
  559.5 4.6 all-to-all-done.21
  564.5 4.0 all_to_all.120
  (490 shorter events, 142.8 us)
Async XLA Ops:
  7.2 136.8 %copy-start = (bf16[1,1,1536,768]{3,2,1,0:T(8,128)(2,1)S(1)}, bf16[1,1,1536,768]{3,2,1,0:T(8,128)(2,1)}, u32[]{:S(2)}) copy-start(bf16[1,1,1536,768]{3,2,1,0:T(8,128)(2,1)} %param.23) | copy-start | bytes 7077892
  13.8 5.1 all-to-all-start.1
  19.3 22.4 %copy-start.68 = (bf16[2,2,64,768]{3,2,1,0:T(8,128)(2,1)S(1)}, bf16[2,2,64,768]{3,2,1,0:T(8,128)(2,1)}, u32[]{:S(2)}) copy-start(bf16[2,2,64,768]{3,2,1,0:T(8,128)(2,1)} %param.12) | copy-start | bytes 1179652
  33.1 21.6 %all-to-all-start.3 = ((bf16[4,2,48,896]{3,2,1,0:T(8,128)(2,1)}), bf16[4,2,48,896]{3,2,1,0:T(8,128)(2,1)}, u32[]{:S(2)}, u32[]{:S(2)}) async-start(bf16[4,2,48,896]{3,2,1,0:T(8,128)(2,1)} %broadcast_in_dim.26), calls=%async_computation.3 | async-start | bytes 1376256 | tf_op jit(solution)/shard_map/all_to_all | solution.py:45
  38.0 3.6 collective-permute-start
  54.7 16.7 %all-to-all-start = ((bf16[4,80,768]{2,1,0:T(8,128)(2,1)}), bf16[4,80,768]{2,1,0:T(8,128)(2,1)S(1)}, u32[]{:S(2)}, u32[]{:S(2)}) async-start(bf16[4,80,768]{2,1,0:T(8,128)(2,1)} %fusion.73), calls=%async_computation | async-start | bytes 983040 | tf_op jit(solution)/shard_map/all_to_all | solution.py:45
  58.2 13.7 %collective-permute-start.1 = (bf16[4,2,48,896]{3,2,1,0:T(8,128)(2,1)}, bf16[4,2,48,896]{3,2,1,0:T(8,128)(2,1)}, u32[]{:S(2)}, u32[]{:S(2)}) collective-permute-start(bf16[4,2,48,896]{3,2,1,0:T(8,128)(2,1)} %all-to-all-done.3), channel_id=1, source_target_pairs={{0,1},{1,0},{2,3},{3,2},{4,5},{5,4},{6,7},{7,6},{8,9},{9,8},{10,11... | collective-permute-start | bytes 2064392 | tf_op jit(solution)/shard_map/ppermute | solution.py:41
  71.4 112.9 %copy-start.22 = (bf16[2,80,768]{2,1,0:T(8,128)(2,1)}, bf16[2,80,768]{2,1,0:T(8,128)(2,1)S(1)}, u32[]{:S(2)}) copy-start(bf16[2,80,768]{2,1,0:T(8,128)(2,1)S(1)} %dynamic-slice_bitcast_fusion.6) | copy-start | bytes 737284
  73.7 39.8 %copy-start.80 = (f32[768]{0:T(1024)}, f32[768]{0:T(1024)S(1)}, u32[]{:S(2)}) copy-start(f32[768]{0:T(1024)S(1)} %get-tuple-element.50) | copy-start | bytes 9220
  96.3 15.7 %all-to-all-start.5 = ((bf16[4,128,768]{2,1,0:T(8,128)(2,1)}), bf16[4,128,768]{2,1,0:T(8,128)(2,1)}, u32[]{:S(2)}, u32[]{:S(2)}) async-start(bf16[4,128,768]{2,1,0:T(8,128)(2,1)} %bitcast.22), calls=%async_computation.5 | async-start | bytes 1572864 | tf_op jit(solution)/shard_map/all_to_all | solution.py:45
  100.6 59.4 %copy-start.106 = (s32[128]{0:T(128)}, s32[128]{0:T(128)S(1)}, u32[]{:S(2)}) copy-start(s32[128]{0:T(128)S(1)} %reshape.556) | copy-start | bytes 1540
  101.0 83.4 %copy-start.99 = (s32[128]{0:T(128)}, s32[128]{0:T(128)S(1)}, u32[]{:S(2)}) copy-start(s32[128]{0:T(128)S(1)} %multiply_add_fusion.1) | copy-start | bytes 1540
  113.5 24.9 %copy-start.102 = (f32[128]{0:T(128)}, f32[128]{0:T(128)S(1)}, u32[]{:S(2)}) copy-start(f32[128]{0:T(128)S(1)} %rsqrt.54) | copy-start | bytes 1540
  128.6 9.9 %collective-permute-start.2 = (bf16[8,24,768]{2,1,0:T(8,128)(2,1)}, bf16[8,24,768]{2,1,0:T(8,128)(2,1)}, u32[]{:S(2)}, u32[]{:S(2)}) collective-permute-start(bf16[8,24,768]{2,1,0:T(8,128)(2,1)} %all_to_all.116), channel_id=1, source_target_pairs={{16,0},{17,1},{18,2},{19,3},{20,4},{21,5},{22,6},{23,7},{24,8},{25... | collective-permute-start | bytes 884744 | tf_op jit(solution)/shard_map/ppermute | solution.py:142
  131.7 20.6 %all-to-all-start.8 = ((bf16[4,2,48,896]{3,2,1,0:T(8,128)(2,1)}), bf16[4,2,48,896]{3,2,1,0:T(8,128)(2,1)}, u32[]{:S(2)}, u32[]{:S(2)}) async-start(bf16[4,2,48,896]{3,2,1,0:T(8,128)(2,1)} %broadcast_in_dim.27), calls=%async_computation.8 | async-start | bytes 1376256 | tf_op jit(solution)/shard_map/all_to_all | solution.py:45
  148.8 3.6 collective-permute-start.3
  152.3 18.1 %collective-permute-start.5 = (bf16[4,2,48,896]{3,2,1,0:T(8,128)(2,1)}, bf16[4,2,48,896]{3,2,1,0:T(8,128)(2,1)}, u32[]{:S(2)}, u32[]{:S(2)}) collective-permute-start(bf16[4,2,48,896]{3,2,1,0:T(8,128)(2,1)} %all-to-all-done.8), channel_id=1, source_target_pairs={{0,1},{1,0},{2,3},{3,2},{4,5},{5,4},{6,7},{7,6},{8,9},{9,8},{10,11... | collective-permute-start | bytes 2064392 | tf_op jit(solution)/shard_map/ppermute | solution.py:41
  153.7 11.9 %collective-permute-start.4 = (bf16[8,24,768]{2,1,0:T(8,128)(2,1)S(1)}, bf16[8,24,768]{2,1,0:T(8,128)(2,1)S(1)}, u32[]{:S(2)}, u32[]{:S(2)}) collective-permute-start(bf16[8,24,768]{2,1,0:T(8,128)(2,1)S(1)} %slice_bitcast_fusion.4), channel_id=1, source_target_pairs={{0,16},{1,17},{2,18},{3,19},{4,20},{5,21},{6,22},{7,23},{8,24},{9,... | collective-permute-start | bytes 884744 | tf_op jit(solution)/shard_map/ppermute | solution.py:153
  160.1 24.3 %copy-start.111 = (f32[128]{0:T(128)}, f32[128]{0:T(128)S(1)}, u32[]{:S(2)}) copy-start(f32[128]{0:T(128)S(1)} %select_reduce_fusion.1) | copy-start | bytes 1540
  166.4 13.8 %all-to-all-start.7 = ((bf16[8,24,768]{2,1,0:T(8,128)(2,1)}), bf16[8,24,768]{2,1,0:T(8,128)(2,1)}, u32[]{:S(2)}, u32[]{:S(2)}) async-start(bf16[8,24,768]{2,1,0:T(8,128)(2,1)} %fusion.102), calls=%async_computation.7 | async-start | bytes 589824 | tf_op jit(solution)/shard_map/all_to_all | solution.py:45
  173.3 30.1 %copy-start.5 = (bf16[768,192]{1,0:T(8,128)(2,1)}, bf16[768,192]{1,0:T(8,128)(2,1)S(1)}, u32[]{:S(2)}) copy-start(bf16[768,192]{1,0:T(8,128)(2,1)S(1)} %slice.190.w_out_rows) | copy-start | bytes 884740
  173.6 27.2 %copy-start.82 = (f32[768]{0:T(1024)}, f32[768]{0:T(1024)S(1)}, u32[]{:S(2)}) copy-start(f32[768]{0:T(1024)S(1)} %get-tuple-element.48) | copy-start | bytes 9220
  180.2 29.6 %all-to-all-start.4 = ((bf16[4,64,768]{2,1,0:T(8,128)(2,1)}), bf16[4,64,768]{2,1,0:T(8,128)(2,1)}, u32[]{:S(2)}, u32[]{:S(2)}) async-start(bf16[4,64,768]{2,1,0:T(8,128)(2,1)} %bitcast.340), calls=%async_computation.4 | async-start | bytes 786432 | tf_op jit(solution)/shard_map/all_to_all | solution.py:45
  209.8 16.4 %all-to-all-start.9 = ((bf16[4,128,768]{2,1,0:T(8,128)(2,1)}), bf16[4,128,768]{2,1,0:T(8,128)(2,1)}, u32[]{:S(2)}, u32[]{:S(2)}) async-start(bf16[4,128,768]{2,1,0:T(8,128)(2,1)} %bitcast.43), calls=%async_computation.9 | async-start | bytes 1572864 | tf_op jit(solution)/shard_map/all_to_all | solution.py:45
  214.2 52.3 %all-gather.9.cloned.1.call-start = ((), (), s32[]{:S(2)}) async-start(), calls=%async_computation.23 | async-start | bytes 1769472 | tf_op jit(solution)/shard_map/all_gather | solution.py:143
  214.3 124.1 %copy-start.109 = (s32[128]{0:T(128)}, s32[128]{0:T(128)S(1)}, u32[]{:S(2)}) copy-start(s32[128]{0:T(128)S(1)} %reshape.561) | copy-start | bytes 1540
  227.7 112.1 %copy-start.27 = (f32[128,768]{1,0:T(8,128)}, f32[128,768]{1,0:T(8,128)S(1)}, u32[]{:S(2)}) copy-start(f32[128,768]{1,0:T(8,128)S(1)} %get-tuple-element.74) | copy-start | bytes 1179652
  229.1 109.3 %copy-start.76 = (f32[128,8]{0,1:T(8,128)}, f32[128,8]{0,1:T(8,128)S(1)}, u32[]{:S(2)}) copy-start(f32[128,8]{0,1:T(8,128)S(1)} %get-tuple-element.108) | copy-start | bytes 12292
  229.1 109.3 %copy-start.91 = (f32[128]{0:T(128)}, f32[128]{0:T(128)S(1)}, u32[]{:S(2)}) copy-start(f32[128]{0:T(128)S(1)} %get-tuple-element.107) | copy-start | bytes 1540
  229.2 109.2 %copy-start.96 = (f32[128]{0:T(128)}, f32[128]{0:T(128)S(1)}, u32[]{:S(2)}) copy-start(f32[128]{0:T(128)S(1)} %fusion.133) | copy-start | bytes 1540
  229.3 109.1 %copy-start.114 = (f32[128]{0:T(128)}, f32[128]{0:T(128)S(1)}, u32[]{:S(2)}) copy-start(f32[128]{0:T(128)S(1)} %select_reduce_fusion) | copy-start | bytes 1540
  252.4 23.7 %all-gather.11.cloned.1.call-start = ((), (), s32[]{:S(2)}) async-start(), calls=%async_computation.24 | async-start | bytes 1769472 | tf_op jit(solution)/shard_map/all_gather | solution.py:144
  252.5 13.9 %collective-permute-start.6 = (bf16[8,48,768]{2,1,0:T(8,128)(2,1)}, bf16[8,48,768]{2,1,0:T(8,128)(2,1)}, u32[]{:S(2)}, u32[]{:S(2)}) collective-permute-start(bf16[8,48,768]{2,1,0:T(8,128)(2,1)} %all_to_all.117), channel_id=1, source_target_pairs={{0,16},{1,17},{2,18},{3,19},{4,20},{5,21},{6,22},{7,23},{8,24},{9,... | collective-permute-start | bytes 1769480 | tf_op jit(solution)/shard_map/ppermute | solution.py:142
  291.2 2.9 collective-permute-start.7
  296.3 41.0 %copy-start.55 = (bf16[2,1,64,768]{3,2,1,0:T(8,128)(2,1)S(1)}, bf16[2,1,64,768]{3,2,1,0:T(8,128)(2,1)}, u32[]{:S(2)}) copy-start(bf16[2,1,64,768]{3,2,1,0:T(8,128)(2,1)} %constant_dynamic-slice_fusion) | copy-start | bytes 589828
  296.3 17.8 %collective-permute-start.8 = (bf16[8,48,768]{2,1,0:T(8,128)(2,1)}, bf16[8,48,768]{2,1,0:T(8,128)(2,1)}, u32[]{:S(2)}, u32[]{:S(2)}) collective-permute-start(bf16[8,48,768]{2,1,0:T(8,128)(2,1)} %slice_bitcast_fusion), channel_id=1, source_target_pairs={{16,0},{17,1},{18,2},{19,3},{20,4},{21,5},{22,6},{23,7},{24,8},{25... | collective-permute-start | bytes 1769480 | tf_op jit(solution)/shard_map/ppermute | solution.py:153
  297.7 40.7 %copy-start.42 = (bf16[4,2,2,48,896]{4,3,2,1,0:T(8,128)(2,1)S(1)}, bf16[4,2,2,48,896]{4,3,2,1,0:T(8,128)(2,1)}, u32[]{:S(2)}) copy-start(bf16[4,2,2,48,896]{4,3,2,1,0:T(8,128)(2,1)} %copy-done.40) | copy-start | bytes 4128772
  355.7 1.8 collective-permute-start.9
  376.3 12.9 %all-to-all-start.13 = ((bf16[8,24,768]{2,1,0:T(8,128)(2,1)}), bf16[8,24,768]{2,1,0:T(8,128)(2,1)}, u32[]{:S(2)}, u32[]{:S(2)}) async-start(bf16[8,24,768]{2,1,0:T(8,128)(2,1)} %bitcast.322), calls=%async_computation.13 | async-start | bytes 589824 | tf_op jit(solution)/shard_map/all_to_all | solution.py:45
  389.3 9.9 %collective-permute-start.10 = (bf16[8,24,768]{2,1,0:T(8,128)(2,1)}, bf16[8,24,768]{2,1,0:T(8,128)(2,1)S(1)}, u32[]{:S(2)}, u32[]{:S(2)}) collective-permute-start(bf16[8,24,768]{2,1,0:T(8,128)(2,1)} %all-to-all-done.13), channel_id=1, source_target_pairs={{16,0},{17,1},{18,2},{19,3},{20,4},{21,5},{22,6},{23,7},{24,8},{25... | collective-permute-start | bytes 884744 | tf_op jit(solution)/shard_map/ppermute | solution.py:142
  396.4 15.7 %collective-permute-start.14 = (bf16[8,48,768]{2,1,0:T(8,128)(2,1)S(1)}, bf16[8,48,768]{2,1,0:T(8,128)(2,1)S(1)}, u32[]{:S(2)}, u32[]{:S(2)}) collective-permute-start(bf16[8,48,768]{2,1,0:T(8,128)(2,1)S(1)} %dynamic-slice_bitcast_fusion.1), channel_id=1, source_target_pairs={{0,1},{1,0},{2,3},{3,2},{4,5},{5,4},{6,7},{7,6},{8,9},{9,8},{10,11... | collective-permute-start | bytes 1769480 | tf_op jit(solution)/shard_map/ppermute | solution.py:41
  411.8 5.5 collective-permute-start.11
  413.1 20.8 %all-to-all-start.16 = ((bf16[4,2,48,768]{3,2,1,0:T(8,128)(2,1)}), bf16[4,2,48,768]{3,2,1,0:T(8,128)(2,1)}, u32[]{:S(2)}, u32[]{:S(2)}) async-start(bf16[4,2,48,768]{3,2,1,0:T(8,128)(2,1)} %bitcast.310), calls=%async_computation.16 | async-start | bytes 1179648 | tf_op jit(solution)/shard_map/all_to_all | solution.py:45
  418.8 22.3 %copy-start.113 = (f32[128]{0:T(128)S(1)}, f32[128]{0:T(128)}, u32[]{:S(2)}) copy-start(f32[128]{0:T(128)} %copy-done.111) | copy-start | bytes 1540
  418.8 22.3 %copy-start.128 = (f32[128]{0:T(128)S(1)}, f32[128]{0:T(128)}, u32[]{:S(2)}) copy-start(f32[128]{0:T(128)} %get-tuple-element.69) | copy-start | bytes 1540
  418.8 22.3 %copy-start.74 = (f32[128,8]{0,1:T(8,128)S(1)}, f32[128,8]{0,1:T(8,128)}, u32[]{:S(2)}) copy-start(f32[128,8]{0,1:T(8,128)} %copy-done.73) | copy-start | bytes 12292
  418.8 22.3 %copy-start.89 = (f32[128]{0:T(128)S(1)}, f32[128]{0:T(128)}, u32[]{:S(2)}) copy-start(f32[128]{0:T(128)} %copy-done.88) | copy-start | bytes 1540
  418.9 11.9 %collective-permute-start.12 = (bf16[8,24,768]{2,1,0:T(8,128)(2,1)S(1)}, bf16[8,24,768]{2,1,0:T(8,128)(2,1)S(1)}, u32[]{:S(2)}, u32[]{:S(2)}) collective-permute-start(bf16[8,24,768]{2,1,0:T(8,128)(2,1)S(1)} %slice_bitcast_fusion.2), channel_id=1, source_target_pairs={{0,16},{1,17},{2,18},{3,19},{4,20},{5,21},{6,22},{7,23},{8,24},{9,... | collective-permute-start | bytes 884744 | tf_op jit(solution)/shard_map/ppermute | solution.py:153
  424.5 27.0 %copy-start.23 = (bf16[2,80,768]{2,1,0:T(8,128)(2,1)S(1)}, bf16[2,80,768]{2,1,0:T(8,128)(2,1)}, u32[]{:S(2)}) copy-start(bf16[2,80,768]{2,1,0:T(8,128)(2,1)} %copy-done.22) | copy-start | bytes 737284
  424.5 27.0 %copy-start.26 = (f32[128,768]{1,0:T(8,128)S(1)}, f32[128,768]{1,0:T(8,128)}, u32[]{:S(2)}) copy-start(f32[128,768]{1,0:T(8,128)} %copy-done.25) | copy-start | bytes 1179652
  424.5 27.0 %copy-start.81 = (f32[768]{0:T(1024)S(1)}, f32[768]{0:T(1024)}, u32[]{:S(2)}) copy-start(f32[768]{0:T(1024)} %copy-done.80) | copy-start | bytes 9220
  424.5 27.0 %copy-start.101 = (s32[128]{0:T(128)S(1)}, s32[128]{0:T(128)}, u32[]{:S(2)}) copy-start(s32[128]{0:T(128)} %copy-done.99) | copy-start | bytes 1540
  424.5 27.0 %copy-start.103 = (f32[128]{0:T(128)S(1)}, f32[128]{0:T(128)}, u32[]{:S(2)}) copy-start(f32[128]{0:T(128)} %copy-done.102) | copy-start | bytes 1540
  425.2 13.8 %collective-permute-start.13 = (bf16[2,1,64,768]{3,2,1,0:T(8,128)(2,1)}, bf16[2,1,64,768]{3,2,1,0:T(8,128)(2,1)}, u32[]{:S(2)}, u32[]{:S(2)}) collective-permute-start(bf16[2,1,64,768]{3,2,1,0:T(8,128)(2,1)} %bitcast.78), channel_id=1, source_target_pairs={{0,16},{16,0},{1,17},{17,1},{2,18},{18,2},{3,19},{19,3},{4,20},{20... | collective-permute-start | bytes 589832 | tf_op jit(solution)/shard_map/ppermute | solution.py:41
  433.9 13.5 %all-to-all-start.14 = ((bf16[8,24,768]{2,1,0:T(8,128)(2,1)}), bf16[8,24,768]{2,1,0:T(8,128)(2,1)}, u32[]{:S(2)}, u32[]{:S(2)}) async-start(bf16[8,24,768]{2,1,0:T(8,128)(2,1)} %fusion.101), calls=%async_computation.14 | async-start | bytes 589824 | tf_op jit(solution)/shard_map/all_to_all | solution.py:45
  447.4 13.9 %all-to-all-start.15 = ((bf16[4,64,768]{2,1,0:T(8,128)(2,1)}), bf16[4,64,768]{2,1,0:T(8,128)(2,1)}, u32[]{:S(2)}, u32[]{:S(2)}) async-start(bf16[4,64,768]{2,1,0:T(8,128)(2,1)} %bitcast.313), calls=%async_computation.15 | async-start | bytes 786432 | tf_op jit(solution)/shard_map/all_to_all | solution.py:45
  482.7 1.8 collective-permute-start.15
  486.4 16.0 %all-to-all-start.17 = ((bf16[4,128,768]{2,1,0:T(8,128)(2,1)}), bf16[4,128,768]{2,1,0:T(8,128)(2,1)}, u32[]{:S(2)}, u32[]{:S(2)}) async-start(bf16[4,128,768]{2,1,0:T(8,128)(2,1)} %bitcast.332), calls=%async_computation.17 | async-start | bytes 1572864 | tf_op jit(solution)/shard_map/all_to_all | solution.py:45
  498.7 6.7 %collective-permute-start.17 = (bf16[8,48,768]{2,1,0:T(8,128)(2,1)}, bf16[8,48,768]{2,1,0:T(8,128)(2,1)}, u32[]{:S(2)}, u32[]{:S(2)}) collective-permute-start(bf16[8,48,768]{2,1,0:T(8,128)(2,1)} %dynamic-slice_bitcast_fusion), channel_id=1, source_target_pairs={{0,1},{1,0},{2,3},{3,2},{4,5},{5,4},{6,7},{7,6},{8,9},{9,8},{10,11... | collective-permute-start | bytes 1769480 | tf_op jit(solution)/shard_map/ppermute | solution.py:41
  507.4 19.5 %all-to-all-start.20 = ((bf16[4,2,48,768]{3,2,1,0:T(8,128)(2,1)}), bf16[4,2,48,768]{3,2,1,0:T(8,128)(2,1)S(1)}, u32[]{:S(2)}, u32[]{:S(2)}) async-start(bf16[4,2,48,768]{3,2,1,0:T(8,128)(2,1)} %bitcast.311), calls=%async_computation.20 | async-start | bytes 1179648 | tf_op jit(solution)/shard_map/all_to_all | solution.py:45
  511.0 7.1 %collective-permute-start.16 = (bf16[144,768]{1,0:T(8,128)(2,1)S(1)}, bf16[144,768]{1,0:T(8,128)(2,1)S(1)}, u32[]{:S(2)}, u32[]{:S(2)}) collective-permute-start(bf16[144,768]{1,0:T(8,128)(2,1)S(1)} %pad_maximum_fusion.16), channel_id=1, source_target_pairs={{0,16},{16,0},{1,17},{17,1},{2,18},{18,2},{3,19},{19,3},{4,20},{20... | collective-permute-start | bytes 663560 | tf_op jit(solution)/shard_map/ppermute | solution.py:41
  526.9 19.4 %all-to-all-start.18 = ((bf16[4,80,768]{2,1,0:T(8,128)(2,1)}), bf16[4,80,768]{2,1,0:T(8,128)(2,1)}, u32[]{:S(2)}, u32[]{:S(2)}) async-start(bf16[4,80,768]{2,1,0:T(8,128)(2,1)} %fusion.74), calls=%async_computation.18 | async-start | bytes 983040 | tf_op jit(solution)/shard_map/all_to_all | solution.py:45
  547.8 7.0 %all-to-all-start.19 = ((bf16[4,2,384]{2,1,0:T(2,128)(2,1)}), bf16[4,2,384]{2,1,0:T(2,128)(2,1)S(1)}, u32[]{:S(2)}, u32[]{:S(2)}) async-start(bf16[4,2,384]{2,1,0:T(2,128)(2,1)} %reshape.599), calls=%async_computation.19 | async-start | bytes 12288 | tf_op jit(solution)/shard_map/all_to_all | solution.py:45
  554.9 9.3 %all-to-all-start.21 = ((bf16[4,48,768]{2,1,0:T(8,128)(2,1)}), bf16[4,48,768]{2,1,0:T(8,128)(2,1)S(1)}, u32[]{:S(2)}, u32[]{:S(2)}) async-start(bf16[4,48,768]{2,1,0:T(8,128)(2,1)} %bitcast.107), calls=%async_computation.21 | async-start | bytes 589824 | tf_op jit(solution)/shard_map/all_to_all | solution.py:45
  (109 other events, 861.0 us)
Sparse Core Ops, SparseCore 0:
  252.6 6.7 all-gather.8
  266.6 9.5 all-gather.10

commit v3 on v2

v3 whole, which is shorter than its diff:
```python
import jax
import jax.numpy as jnp
from jax import lax
from jax.experimental import pallas as pl
from jax.experimental.pallas import tpu as pltpu
from jax.sharding import Mesh, PartitionSpec as P

HEAD_DIM = 64
EPSILON = 1e-06
SCORE_SCALE = 0.125
HIGHEST = lax.Precision.HIGHEST
F32 = jnp.float32
BF16 = jnp.bfloat16

WIDE = ("z", "q", "h")
CHIPS = ("h", "pipe")
SWAP = [(0, 1), (1, 0)]
VMEM_BYTES = 48 * 1024 * 1024


def dot(left, right, contract, precision=None):
    return lax.dot_general(
        left, right, (contract, ((), ())), precision=precision, preferred_element_type=F32
    )


def mm(left, right):
    return dot(left, right, ((1,), (0,)))


def mm_nt(left, right):
    return dot(left, right, ((1,), (1,)))


def mm_tn(left, right):
    return dot(left, right, ((0,), (0,)))


def swapped(values, axis):
    return lax.ppermute(values, axis, SWAP)


def exchanged(values, axes):
    return lax.all_to_all(values, axes, split_axis=0, concat_axis=0, tiled=True)


def norm_rows(values, gain_vector):
    inverse = lax.rsqrt(jnp.mean(values * values, axis=-1, keepdims=True) + EPSILON)
    return (inverse, (values * inverse * gain_vector).astype(BF16))


def norm_back(values, inverse, gain_vector, grad_normed):
    scaled = grad_normed * gain_vector
    grad_values = inverse * scaled - values * (inverse * inverse * inverse) * jnp.mean(
        scaled * values, axis=-1, keepdims=True
    )
    grad_gain = jnp.sum(grad_normed * values * inverse, axis=0)
    return (grad_values, grad_gain)


def gather_parts(values):
    if lax.axis_size("q") > 1:
        values = lax.all_gather(values, "q", axis=0, tiled=True)
    return values, swapped(values, "tp")


def sum_parts(own, other):
    got = swapped(other, "tp")
    places = lax.axis_size("q")
    if places == 1:
        return [own, got]
    split = (own.astype(F32) + got.astype(F32)).astype(BF16).reshape(places, -1, own.shape[-1])
    return [jnp.sum(exchanged(split, "q").astype(F32), axis=0).astype(BF16)]


def xor_z(values):
    z = lax.axis_index("z")
    values = jnp.where((z & 1) == 1, values[jnp.array([1, 0, 3, 2])], values)
    return jnp.where((z & 2) == 2, values[jnp.array([2, 3, 0, 1])], values)


def exchanged_z(values):
    mine = xor_z(values)
    parts = [mine[0]]
    for k in range(1, 4):
        parts.append(lax.ppermute(mine[k], "z", [(z, z ^ k) for z in range(4)]))
    return xor_z(jnp.stack(parts))


def to_planes(values):
    z, y = (lax.axis_index("z"), lax.axis_index("pipe"))
    mine = xor_z(values)
    got = [mine[0]]
    for k in range(1, 4):
        pairs = [(4 * p + a, 4 * p + (a ^ k)) for p in range(2) for a in range(4) if a & 1 == p]
        got.append(lax.ppermute(mine[k], ("pipe", "z"), pairs))
    own = (z & 1) == y
    near, far = (jnp.where(own, got[0], got[1]), jnp.where(own, got[2], got[3]))
    near_at = jnp.where(own, z, z ^ 1)
    return jnp.where(near_at == y, jnp.stack([near, far]), jnp.stack([far, near]))


def sum_chips(values):
    chunks = exchanged(values.astype(BF16).reshape(4, -1, values.shape[-1]), CHIPS)
    return jnp.sum(chunks.astype(F32), axis=0)


def after(value, *others):
    return lax.optimization_barrier((value,) + others)[0]


def from_z(values):
    places = lax.axis_size("z") * lax.axis_size("q")
    return exchanged(jnp.broadcast_to(values[None], (places,) + values.shape), ("z", "q"))


def spread_weights(query_weight, key_weight, value_weight, output_weight, extras, first):
    rows, cols = query_weight.shape
    half, group = (rows // 2, cols // 2)
    packed = jnp.stack([query_weight, key_weight, value_weight, output_weight.T])
    packed = packed.reshape(4, 2, half, 2, group).transpose(1, 3, 2, 0, 4)
    by_core = exchanged(packed, "tp").reshape(4, half, 4 * group)
    small = jnp.broadcast_to(extras[None], (4,) + extras.shape)
    by_chip = exchanged(after(jnp.concatenate([by_core, small], axis=-1), first), CHIPS)
    return by_chip.reshape(2, 2, half, -1)


def join_section(mine):
    other = swapped(mine, "tp")
    core = lax.axis_index("tp")
    low, high = (jnp.where(core == 0, mine, other), jnp.where(core == 0, other, mine))
    return jnp.stack([low, high], axis=2).reshape(-1, mine.shape[-1])


def gather_later(own):
    gathered = lax.all_gather(own, ("z", "q", "tp"), axis=0, tiled=False)
    places = lax.axis_size("z") * lax.axis_size("q")
    gathered = gathered.reshape((places, 2) + own.shape).transpose(0, 2, 1, 3, 4)
    return gathered.reshape(-1, own.shape[-1])


def scatter_start(grads):
    width = grads.shape[-1]
    places = lax.axis_size("z") * lax.axis_size("q")
    split = grads.reshape(places * 2, 2, -1, width)
    mine = lax.axis_index("tp")
    kept = lax.dynamic_index_in_dim(split, mine, 1, keepdims=False)
    got = swapped(lax.dynamic_index_in_dim(split, 1 - mine, 1, keepdims=False), "tp")
    both = (kept.astype(F32) + got.astype(F32)).astype(BF16)
    moved = exchanged(both.reshape(places, 2, -1, width), ("z", "q"))
    return jnp.sum(moved.astype(F32), axis=0).astype(BF16)


def scatter_later(grads):
    width = grads.shape[-1]
    places = lax.axis_size("z") * lax.axis_size("q")
    split = grads.reshape(places, 2, 2, -1, width).transpose(0, 2, 1, 3, 4)
    half = split.shape[3]
    sums = lax.psum_scatter(
        split.reshape(-1, width), ("z", "q", "tp"), scatter_dimension=0, tiled=True
    )
    return sums.reshape(2, half, width)


def scatter_chips(sums):
    half, width = sums[0].shape[1:]
    return exchanged(jnp.stack(sums, axis=1).reshape(4, half, width), CHIPS)


def scatter_end(by_chip):
    half, width = by_chip.shape[1:]
    group = width // 4
    by_core = exchanged(by_chip.reshape(2, 2, half, 4, group), "tp")
    return by_core.transpose(3, 0, 2, 1, 4).reshape(4, 2 * half, 2 * group).astype(F32)


def dispatch_table(routes, expert_count, most_rows):
    blocks, block_rows = routes.shape
    expert_hits = (
        routes[:, :, None] == jnp.arange(expert_count, dtype=jnp.int32)[None, None, :]
    ).astype(F32)
    order = jnp.arange(block_rows)
    before = (order[:, None] > order[None, :]).astype(F32)
    ranks = jnp.einsum("tu,bue->bte", before, expert_hits)
    slot_rank = jnp.sum(ranks * expert_hits, axis=2).astype(jnp.int32)
    place = jnp.arange(blocks, dtype=jnp.int32)[:, None] * most_rows + slot_rank
    target = (routes * (blocks * most_rows) + place).reshape(-1)
    slots = jnp.arange(expert_count * blocks * most_rows, dtype=jnp.int32)
    return (slots[:, None] == target[None, :]).astype(BF16)


def to_experts(packed):
    pipe = lax.axis_index("pipe")
    count = [rows for rows in packed if rows is not None][0].shape[1]
    arrived = exchanged(jnp.concatenate([r for r in packed if r is not None], axis=1), WIDE)
    if packed[1] is None:
        kept, got = (arrived, lax.ppermute(arrived, "pipe", [(1, 0)]))
    elif packed[0] is None:
        kept, got = (arrived, lax.ppermute(arrived, "pipe", [(0, 1)]))
    else:
        first, second = (arrived[:, :count], arrived[:, count:])
        kept, sent = (jnp.where(pipe == 0, first, second), jnp.where(pipe == 0, second, first))
        got = swapped(sent, "pipe")
    rows = [kept, swapped(kept, "tp"), got, swapped(got, "tp")]
    return jnp.stack(rows).reshape((2, 2) + kept.shape)


def from_experts(results, sections):
    got = swapped(results[:, 1], "tp")
    near, far = ((results[k, 0].astype(F32) + got[k].astype(F32)).astype(BF16) for k in range(2))
    pipe = lax.axis_index("pipe")
    if len(sections) == 2:
        hopped = swapped(far, "pipe")
        back = jnp.where(
            pipe == 0,
            jnp.concatenate([near, hopped], axis=1),
            jnp.concatenate([hopped, near], axis=1),
        )
    else:
        hopped = lax.ppermute(far, "pipe", [(sections[0], 1 - sections[0])])
        back = jnp.where(pipe == sections[0], near, hopped)
    return exchanged(back, WIDE)


def whole_call(kernel, out_shape, *operands, flops=0, exps=0):
    moved = sum(v.size * v.dtype.itemsize for v in operands)
    return pl.pallas_call(
        kernel,
        out_shape=out_shape,
        compiler_params=pltpu.CompilerParams(vmem_limit_bytes=VMEM_BYTES),
        cost_estimate=pl.CostEstimate(flops=flops, bytes_accessed=moved, transcendentals=exps),
    )(*operands)


def flipped(values):
    return values.astype(F32).T.astype(BF16)


def attend_kernel(own, own_parts, other_parts, whole, part, attended, attended_flat, log_total):
    group = own.shape[1] // 3
    queries_flat = flipped(own[:, :group]) * SCORE_SCALE
    sides = (own_parts, other_parts)
    values_flat = [flipped(side[:, 2 * group :]) for side in sides]
    for head in range(group // HEAD_DIM):
        lanes = slice(head * HEAD_DIM, (head + 1) * HEAD_DIM)
        key_lanes = slice(group + head * HEAD_DIM, group + (head + 1) * HEAD_DIM)
        scores = [mm(side[:, key_lanes], queries_flat[lanes]) for side in sides]
        peak = jnp.maximum(*(jnp.max(block, axis=0, keepdims=True) for block in scores))
        weights = [jnp.exp(block - peak) for block in scores]
        total = sum(jnp.sum(block, axis=0, keepdims=True) for block in weights)
        summed = sum(mm(flat[lanes], block.astype(BF16)) for flat, block in zip(values_flat, weights))
        attended_flat[lanes, :] = summed / total
        log_total[head : head + 1, :] = peak + jnp.log(total)
    attended[...] = attended_flat[...].T.astype(BF16)
    part[...] = mm_nt(attended[...], whole[:, 3 * group : 4 * group]).astype(BF16)


def attend(own, own_parts, other_parts, whole):
    rows, group = (own.shape[0], own.shape[1] // 3)
    keys = 2 * own_parts.shape[0]
    return whole_call(
        attend_kernel,
        (
            jax.ShapeDtypeStruct((rows, whole.shape[0]), BF16),
            jax.ShapeDtypeStruct((rows, group), BF16),
            jax.ShapeDtypeStruct((group, rows), F32),
            jax.ShapeDtypeStruct((8, rows), F32),
        ),
        own,
        own_parts,
        other_parts,
        whole,
        flops=4 * rows * keys * group,
        exps=rows * keys * group // HEAD_DIM,
    )


def attend_back_kernel(
    grad_rows, whole, own, own_parts, other_parts, attended_flat, log_total,
    grad_queries, grad_own, grad_other,
):
    group = own.shape[1] // 3
    keys = own_parts.shape[0]
    chunk = min(512, keys)
    queries_flat = flipped(own[:, :group]) * SCORE_SCALE
    w_out_rows = whole[:, 3 * group : 4 * group]
    grad_flat = dot(w_out_rows, grad_rows[...], ((0,), (1,))).astype(BF16)
    products = grad_flat.astype(F32) * attended_flat[...]
    sides = ((own_parts, grad_own), (other_parts, grad_other))
    keys_flat = [flipped(side[:, group : 2 * group]) for side, unused in sides]
    grad_queries_flat = []
    for head in range(group // HEAD_DIM):
        lanes = slice(head * HEAD_DIM, (head + 1) * HEAD_DIM)
        key_lanes = slice(group + head * HEAD_DIM, group + (head + 1) * HEAD_DIM)
        value_lanes = slice(2 * group + head * HEAD_DIM, 2 * group + (head + 1) * HEAD_DIM)
        delta = jnp.sum(products[lanes], axis=0, keepdims=True)
        level = log_total[head : head + 1, :]
        query, grad = (queries_flat[lanes], grad_flat[lanes])
        total = jnp.zeros((HEAD_DIM, own.shape[0]), F32)
        for (side, grad_side), flat in zip(sides, keys_flat):
            for begin in range(0, keys, chunk):
                here = slice(begin, begin + chunk)
                probs = jnp.exp(mm(side[here, key_lanes], query) - level)
                grad_probs = mm(side[here, value_lanes], grad)
                grad_scores = (probs * (grad_probs - delta)).astype(BF16)
                grad_side[here, lanes] = mm_nt(grad_scores, query).astype(BF16)
                grad_side[here, key_lanes] = mm_nt(probs.astype(BF16), grad).astype(BF16)
                total = total + mm(flat[lanes, here], grad_scores)
        grad_queries_flat.append(total * SCORE_SCALE)
    grad_queries[...] = jnp.concatenate(grad_queries_flat, axis=0).T.astype(BF16)


def attend_back(grad_rows, whole, own, own_parts, other_parts, attended_flat, log_total):
    rows, group = (own.shape[0], own.shape[1] // 3)
    keys = own_parts.shape[0]
    return whole_call(
        attend_back_kernel,
        (
            jax.ShapeDtypeStruct((rows, group), BF16),
            jax.ShapeDtypeStruct((keys, 2 * group), BF16),
            jax.ShapeDtypeStruct((keys, 2 * group), BF16),
        ),
        grad_rows,
        whole,
        own,
        own_parts,
        other_parts,
        attended_flat,
        log_total,
        flops=20 * rows * keys * group,
        exps=2 * rows * keys * group // HEAD_DIM,
    )


def project_kernel(rows, whole, qkv):
    qkv[...] = mm(rows[...], whole[:, : qkv.shape[1]]).astype(BF16)


def project(rows, whole, width):
    return whole_call(
        project_kernel,
        jax.ShapeDtypeStruct((rows.shape[0], width), BF16),
        rows,
        whole,
        flops=2 * rows.size * width,
    )


def project_back_kernel(grad_queries, *refs):
    *terms, whole, grad_qkv, part = refs
    grad_kv = sum(term[...].astype(F32) for term in terms).astype(BF16)
    grad_qkv[...] = jnp.concatenate([grad_queries[...], grad_kv], axis=1)
    part[...] = mm_nt(grad_qkv[...], whole[:, : grad_qkv.shape[1]]).astype(BF16)


def project_back(grad_queries, terms, whole):
    rows, width = (grad_queries.shape[0], 3 * grad_queries.shape[1])
    return whole_call(
        project_back_kernel,
        (
            jax.ShapeDtypeStruct((rows, width), BF16),
            jax.ShapeDtypeStruct((rows, whole.shape[0]), BF16),
        ),
        grad_queries,
        *terms,
        whole,
        flops=2 * rows * width * whole.shape[0],
    )


def weight_grads_kernel(rows, grad_rows, grad_qkv, attended, grads):
    grads[...] = jnp.concatenate(
        [mm_tn(rows[...], grad_qkv[...]), mm_tn(grad_rows[...], attended[...])], axis=1
    ).astype(BF16)


def weight_grads(rows, grad_rows, grad_qkv, attended):
    width = grad_qkv.shape[1] + attended.shape[1]
    return whole_call(
        weight_grads_kernel,
        jax.ShapeDtypeStruct((rows.shape[1], width), BF16),
        rows,
        grad_rows,
        grad_qkv,
        attended,
        flops=2 * rows.size * width,
    )


def attention_forward(inputs, weights):
    whole, gain_attn = weights[:2]
    values_in = inputs.astype(F32)
    inverse_a, normed_a = norm_rows(values_in, gain_attn)
    rows_a = lax.all_gather(normed_a, CHIPS, axis=0, tiled=True)
    qkv = project(rows_a, whole, 3 * weights[2])
    own_parts, other_parts = gather_parts(qkv)
    part, attended, attended_flat, log_total = attend(qkv, own_parts, other_parts, whole)
    hidden = values_in + sum_chips(part)
    kept = (
        values_in, inverse_a, rows_a, qkv, own_parts, other_parts, attended, attended_flat, log_total
    )
    return hidden, kept


def attention_backward(grad_hidden, kept, weights):
    whole, gain_attn = weights[:2]
    (
        values_in, inverse_a, rows_a, qkv, own_parts, other_parts, attended, attended_flat, log_total
    ) = kept
    grad_rows = lax.all_gather(grad_hidden.astype(BF16), CHIPS, axis=0, tiled=True)
    grad_queries, grad_own, grad_other = attend_back(
        grad_rows, whole, qkv, own_parts, other_parts, attended_flat, log_total
    )
    grad_qkv, part = project_back(grad_queries, sum_parts(grad_own, grad_other), whole)
    grad_normed_a = sum_chips(part)
    grad_input_norm, grad_gain = norm_back(values_in, inverse_a, gain_attn, grad_normed_a)
    grads = weight_grads(rows_a, grad_rows, grad_qkv, attended)
    return (grad_hidden + grad_input_norm).astype(BF16), (grad_gain, grads)


def route_tokens(hidden, routes, weights, expert_count, most_rows):
    gain_moe, w_router = weights[3:]
    inverse_b, normed_b = norm_rows(hidden, gain_moe)
    router_probs = jax.nn.softmax(mm(normed_b, w_router), axis=-1)
    chosen = (
        routes.reshape(-1, 1) == jnp.arange(expert_count, dtype=jnp.int32)[None]
    ).astype(F32)
    gate = jnp.sum(router_probs * chosen, axis=-1, keepdims=True)
    return inverse_b, normed_b, router_probs, chosen, gate


def pack_rows(table, rows):
    wide = lax.axis_size("z") * lax.axis_size("q") * lax.axis_size("h")
    return mm(table, rows).astype(BF16).reshape(wide, -1, rows.shape[-1])


def unpack_rows(table, returned):
    return mm_tn(table, returned.reshape(table.shape[0], -1))


def expert_trip(slots, w_in, w_out):
    rows = slots.reshape(-1, slots.shape[-1])
    pre_act = mm(rows, w_in)
    activated = jax.nn.gelu(pre_act).astype(BF16)
    result = mm(activated, w_out).astype(BF16)
    return (rows, pre_act, activated), result.reshape(slots.shape)


def expert_trip_back(grad_slots, kept, w_in, w_out, extra=None):
    rows, pre_act, activated = kept
    grad_part = grad_slots.reshape(rows.shape)
    grad_act = mm_nt(grad_part, w_out)
    unused_value, gelu_back = jax.vjp(jax.nn.gelu, pre_act)
    grad_pre = gelu_back(grad_act)[0].astype(BF16)
    grad_rows = mm_nt(grad_pre, w_in)
    if extra is not None:
        grad_rows = grad_rows + extra
    return (rows, grad_pre, activated, grad_part), grad_rows.astype(BF16).reshape(grad_slots.shape)


def expert_gate(slots, grad_slots, result, w_router):
    rows = slots.reshape(-1, slots.shape[-1])
    grad_out = grad_slots.reshape(rows.shape).astype(F32)
    expert = (lax.axis_index("z") * lax.axis_size("q") + lax.axis_index("q")) * 2 + lax.axis_index("h")
    probs = jax.nn.softmax(mm(rows, w_router), axis=-1)
    here = (jnp.arange(w_router.shape[1], dtype=jnp.int32) == expert).astype(F32)[None]
    gate = jnp.sum(probs * here, axis=-1, keepdims=True)
    grad_gate = jnp.sum(grad_out * result.reshape(rows.shape).astype(F32), axis=-1, keepdims=True)
    grad_logits = gate * grad_gate * (here - probs)
    through_router = mm_nt(grad_logits.astype(BF16), w_router)
    return (gate * grad_out).astype(BF16).reshape(slots.shape), through_router


def router_grads(grad_output, mixed, routed):
    inverse_b, normed_b, router_probs, chosen, gate = routed
    grad_gate = jnp.sum(grad_output * mixed, axis=-1, keepdims=True)
    grad_logits = gate * grad_gate * (chosen - router_probs)
    return grad_logits, dot(grad_logits, normed_b.astype(F32), ((0,), (0,)), HIGHEST)


def moe_norm_back(grad_output, grad_normed_b, hidden, routed, weights):
    grad_hidden_norm, grad_gain = norm_back(hidden, routed[0], weights[3], grad_normed_b)
    return grad_output + grad_hidden_norm, grad_gain


def shards(
    block_input,
    out_cotangent,
    routes,
    attn_gain,
    query_weight,
    key_weight,
    value_weight,
    output_weight,
    moe_gain,
    router_weight,
    expert_in,
    expert_out,
):
    micro_count, seq_count, half_rows, feature_dim = block_input.shape
    sequences = micro_count * seq_count
    expert_count = router_weight.shape[-1]
    most_rows = max(2, 3 * half_rows // (2 * expert_count))
    pipe, core = (lax.axis_index("pipe"), lax.axis_index("tp"))
    extra = -(-(2 + expert_count) // 128) * 128

    own_routes = lax.dynamic_slice_in_dim(
        routes[0, :, :, :, 0].reshape(sequences, -1), core * half_rows, half_rows, 1
    ).astype(BF16)
    other_routes = swapped(own_routes, "pipe")
    route_rows = jnp.stack(
        [
            jnp.where(pipe == 0, own_routes, other_routes),
            jnp.where(pipe == 0, other_routes, own_routes),
        ],
        axis=1,
    )
    route_rows = jnp.pad(route_rows, ((0, 0), (0, 14), (0, feature_dim - half_rows)))

    input_rows = jnp.concatenate(
        [block_input.reshape(sequences, half_rows, feature_dim), route_rows], axis=1
    )
    here = to_planes(input_rows)
    inputs = here[:, :half_rows].reshape(-1, feature_dim)
    section_routes = [
        here[:, half_rows + section, :half_rows].astype(jnp.int32) for section in range(2)
    ]

    small = jnp.concatenate([attn_gain[0][:, None], moe_gain[0][:, None], router_weight[0]], axis=-1)
    small = jnp.pad(small, ((0, 0), (0, extra - small.shape[-1])))
    spread = spread_weights(
        query_weight[0], key_weight[0], value_weight[0], output_weight[0], small, here
    )
    group = query_weight.shape[-1] // 2

    def parts_of(array):
        return (
            array,
            array[:, 4 * group].astype(F32),
            group,
            array[:, 4 * group + 1].astype(F32),
            array[:, 4 * group + 2 : 4 * group + 2 + expert_count],
        )

    whole = join_section(from_z(spread[:, 0]))
    weights = [parts_of(whole), parts_of(gather_later(spread[:, 1]))]
    w_in, w_out = (expert_in[0, 0], expert_out[0, 0])

    tables = [dispatch_table(rows, expert_count, most_rows) for rows in section_routes]
    cotangent = to_planes(out_cotangent.reshape(sequences, half_rows, feature_dim)).reshape(
        -1, feature_dim
    )
    hidden, kept_attn = attention_forward(inputs, weights[0])
    routed = route_tokens(hidden, section_routes[0], weights[0], expert_count, most_rows)
    slots = to_experts((pack_rows(tables[0], routed[1]), pack_rows(tables[1], cotangent)))
    cotangent_slots = slots
    kept_expert, result = expert_trip(slots, w_in, w_out)
    mixed = unpack_rows(tables[0], from_experts(result, (0,)))
    first_output = (hidden + routed[4] * mixed).astype(BF16)
    first = (hidden, kept_attn, routed, kept_expert, mixed)

    hidden, kept_attn = attention_forward(first_output, weights[1])
    routed = route_tokens(hidden, section_routes[1], weights[1], expert_count, most_rows)
    slots = to_experts((None, pack_rows(tables[1], routed[1])))
    kept_expert, second_result = expert_trip(slots, w_in, w_out)
    grad_slots, through_router = expert_gate(slots, cotangent_slots, second_result, weights[1][4])
    part, grad_results = expert_trip_back(grad_slots, kept_expert, w_in, w_out, through_router)
    expert_parts = [None, part]
    returned_grad = from_experts(grad_results, (1,))
    grad_output = cotangent.astype(F32)

    def to_owners(first, second, small=None, chips=None):
        first, second = (v.reshape(sequences // 2, 1, half_rows, feature_dim) for v in (first, second))
        kept, sent = (jnp.where(pipe == 0, first, second), jnp.where(pipe == 0, second, first))
        if small is not None:
            kept_small = jnp.where(pipe == 0, small[0], small[1])
            sent_small = jnp.where(pipe == 0, small[1], small[0]).astype(BF16)
            sent = jnp.concatenate([sent.reshape(-1, feature_dim), sent_small], axis=0)
        got = swapped(sent, "pipe")
        if small is not None:
            kept_small = kept_small + got[-kept_small.shape[0] :].astype(F32)
            got = got[: -kept_small.shape[0]].reshape(first.shape)
        both = jnp.where(
            pipe == 0, jnp.concatenate([kept, got], axis=1), jnp.concatenate([got, kept], axis=1)
        ).reshape(sequences, half_rows, feature_dim)
        if small is None:
            home = exchanged_z(both)
        else:
            count, planes = (kept_small.shape[0], lax.axis_size("z"))
            by_plane = kept_small.astype(BF16).reshape(count, planes, -1).transpose(1, 0, 2)
            by_plane = jnp.pad(by_plane, ((0, 0), (0, 0), (0, feature_dim - by_plane.shape[-1])))
            both = jnp.concatenate([both, by_plane], axis=1)
            chips = chips(both)
            moved = exchanged_z(both)
            home = moved[:, :half_rows]
            sums = jnp.sum(moved[:, half_rows:, : feature_dim // planes].astype(F32), axis=0)
            rest = lax.axis_size("q") * lax.axis_size("h") * lax.axis_size("tp")
            by_rest = sums.astype(BF16).reshape(count, rest, -1).transpose(1, 0, 2)
            small = jnp.sum(exchanged(after(by_rest, chips), ("q", "h", "tp")).astype(F32), axis=0)
        return home.reshape(1, micro_count, seq_count, half_rows, feature_dim), small, chips

    def small_rows(grad_gain_attn, grad_gain_moe, grad_router):
        stacked = jnp.concatenate([grad_gain_attn[None], grad_gain_moe[None], grad_router], axis=0)
        return jnp.pad(stacked, ((0, -stacked.shape[0] % 16), (0, 0)))

    grad_hidden, grad_gain_moe = moe_norm_back(
        grad_output, unpack_rows(tables[1], returned_grad), hidden, routed, weights[1]
    )
    second_grad, (grad_gain_attn, grads) = attention_backward(grad_hidden, kept_attn, weights[1])
    sums_second = scatter_later(grads)
    second = (hidden, routed, grad_output, grad_gain_attn, grad_gain_moe)

    hidden, kept_attn, routed, kept_expert, mixed = first
    grad_output = second_grad.astype(F32)
    grad_slots = to_experts((pack_rows(tables[0], (routed[4] * grad_output).astype(BF16)), None))
    expert_parts[0], grad_results = expert_trip_back(grad_slots, kept_expert, w_in, w_out)
    grad_logits, grad_router = router_grads(grad_output, mixed, routed)
    grad_normed_router = mm_nt(grad_logits.astype(BF16), weights[0][4])
    slots, grad_pre, activated, grad_part = (
        jnp.where(pipe == 0, low, high) for low, high in zip(*expert_parts)
    )
    grad_w_in = mm_tn(slots, grad_pre)
    grad_w_out = mm_tn(activated, grad_part)
    returned = from_experts(jnp.where(pipe == 0, grad_results, second_result), (0, 1))
    count = returned.shape[1] // 2
    grad_hidden, grad_gain_moe = moe_norm_back(
        grad_output,
        grad_normed_router + unpack_rows(tables[0], returned[:, :count]),
        hidden,
        routed,
        weights[0],
    )
    hidden, routed, grad_output, *gains = second
    mixed = unpack_rows(tables[1], returned[:, count:])
    second_output = (hidden + routed[4] * mixed).astype(BF16)
    small_second = small_rows(*gains, router_grads(grad_output, mixed, routed)[1])
    layer_outputs = to_owners(first_output, second_output)[0]
    grad_hidden, grad_w_in, grad_w_out = lax.optimization_barrier(
        (grad_hidden, grad_w_in, grad_w_out)
    )
    first_grad, (grad_gain_attn, grads) = attention_backward(grad_hidden, kept_attn, weights[0])
    small_first = small_rows(grad_gain_attn, grad_gain_moe, grad_router)
    sums_first = scatter_start(grads)
    grads_home, small, by_chip = to_owners(
        first_grad,
        second_grad,
        (small_first, small_second),
        lambda first: scatter_chips([after(sums_first, first), sums_second]),
    )
    mats = scatter_end(by_chip)
    return (
        layer_outputs,
        grads_home,
        small[0][None],
        mats[0][None],
        mats[1][None],
        mats[2][None],
        mats[3].T[None],
        small[1][None],
        small[2 : 2 + expert_count].T[None],
        grad_w_in[None, None],
        grad_w_out[None, None],
    )


def solution(mesh):
    pipe, wide, tp = (mesh.shape["pipe"], mesh.shape["wide"], mesh.shape["tp"])
    planes = Mesh(mesh.devices.reshape(pipe, 4, wide // 8, 2, tp), ("pipe", "z", "q", "h", "tp"))
    rows = WIDE + ("tp",)
    placed = (
        P(None, None, rows, None),
        P(None, None, rows, None),
        P("pipe", None, None, WIDE, None),
        P("pipe", rows),
        P("pipe", WIDE, "tp"),
        P("pipe", WIDE, "tp"),
        P("pipe", WIDE, "tp"),
        P("pipe", "tp", WIDE),
        P("pipe", rows),
        P("pipe", rows, None),
        P("pipe", WIDE, None, "tp"),
        P("pipe", WIDE, "tp", None),
    )
    return jax.shard_map(
        shards,
        mesh=planes,
        in_specs=placed,
        out_specs=(
            P("pipe", None, None, rows, None),
            P("pipe", None, None, rows, None),
            P("pipe", rows),
            P("pipe", WIDE, "tp"),
            P("pipe", WIDE, "tp"),
            P("pipe", WIDE, "tp"),
            P("pipe", "tp", WIDE),
            P("pipe", rows),
            P("pipe", rows, None),
            P("pipe", WIDE, None, "tp"),
            P("pipe", WIDE, "tp", None),
        ),
        check_vma=False,
    )
```

time: 592 us -> 576 us (0.973)
  waiting for transfers between devices: 149 us -> 119 us
  local copies, waits for them, and re-layouts: 47.7 us -> 65.7 us
  blocking collectives: 153 us -> 144 us
    all_to_all x17 -> x10, waiting for transfers between devices: 88.9 us -> 41.5 us  [exchanged(): return lax.all_to_all(values, axes, split_axis=0, concat_axis=0, tiled=True)]
    all_to_all x17 -> x10, starting transfers between devices: 67.8 us -> 42 us  [exchanged(): return lax.all_to_all(values, axes, split_axis=0, concat_axis=0, tiled=True)]
    ppermute x6 -> x16, starting transfers between devices: 17.2 us -> 40.6 us  [the longest x6 21.5 us: to_planes(): got.append(lax.ppermute(mine[k], ('pipe', 'z'), pairs))]
    all_gather x8 -> x2, blocking collectives: 39.8 us -> 24.5 us  [attention_backward(): lax.all_gather(grad_hidden.astype(BF16), CHIPS, axis=0, tiled=True)]
    gather x0 -> x12, local copies, waits for them, and re-layouts: none -> 12.4 us  [the longest x6 7.09 us: xor_z(): return jnp.where(z & 2 == 2, values[jnp.array([2, 3, 0, 1])], values)]
    ppermute x12 -> x20, waiting for transfers between devices: 12.7 us -> 24.3 us  [swapped(): return lax.ppermute(values, axis, SWAP)]
    ppermute x6 -> x16, waiting for transfers between devices: 37.9 us -> 45.6 us  [the longest x6 16.8 us: exchanged_z(): parts.append(lax.ppermute(mine[k], 'z', [(z, z ^ k) for z in range(4)]))]
    all_to_all x6 -> x7, blocking collectives: 89.1 us -> 94.2 us  [exchanged(): return lax.all_to_all(values, axes, split_axis=0, concat_axis=0, tiled=True)]
  transfers between devices with their start and end apart: 37 -> 48, of which waited for: 24 -> 27; matrix products, arithmetic and copies ran while one was open for 16% -> 16% of each run, Pallas kernels for 1% -> 1%
where the time goes in v3:
time: 576 us; the launch traced here: 565 us
  blocking collectives  144 us (25%)
  waiting for transfers between devices  119 us (21%)
  starting transfers between devices  89.1 us (15%)
  local copies, waits for them, and re-layouts  65.7 us (11%)
  matrix products  63.6 us (11%)
  other arithmetic  45.1 us (8%)
  Pallas kernels  21.8 us (4%)
  between operations  16.9 us (3%)
    all_to_all x7, blocking collectives, exchanged(): return lax.all_to_all(values, axes, split_axis=0, concat_axis=0, tiled=True)  94.2 us
    dot_general x25, matrix products, dot(): lax.dot_general(left, right, (contract, ((), ())), precision=precision, p...  63.3 us
    all_to_all x10, starting transfers between devices, exchanged(): return lax.all_to_all(values, axes, split_axis=0, concat_axis=0, tiled=True)  42 us
    all_to_all x10, waiting for transfers between devices, exchanged(): return lax.all_to_all(values, axes, split_axis=0, concat_axis=0, tiled=True)  41.5 us
    all_gather x2, blocking collectives, attention_forward(): rows_a = lax.all_gather(normed_a, CHIPS, axis=0, tiled=True)  25 us
    all_gather x2, blocking collectives, attention_backward(): lax.all_gather(grad_hidden.astype(BF16), CHIPS, axis=0, tiled=True)  24.5 us
    ppermute x20, waiting for transfers between devices, swapped(): return lax.ppermute(values, axis, SWAP)  24.3 us
    pallas_call x10, Pallas kernels, whole_call(): pl.pallas_call(kernel, out_shape=out_shape, compiler_params=pltpu.Compile...  21.8 us
  transfers between devices with their start and end apart: 48, of which 27 were waited for; matrix products, arithmetic and copies ran while one was open for 16% of the time, Pallas kernels for 1%

profile of v3, /device:TPU:0, one launch (start us, length us, event | category | flops | bytes accessed | tf_op | source)
XLA Modules:
  0.0 564.8 jit_solution(7200144203735224515)
XLA Ops:
  8.2 3.0 collective-permute-start
  17.6 4.2 all-to-all-start
  25.9 4.1 collective-permute-start.1
  34.0 3.7 collective-permute-start.3
  37.7 3.1 collective-permute-start.2
  41.2 4.7 collective-permute-done.2
  45.9 4.1 all-to-all-start.1
  51.4 4.6 all-to-all-done.1
  58.6 4.2 all-to-all-start.2
  66.0 4.0 collective-permute-start.6
  70.0 4.1 collective-permute-start.8
  74.0 2.5 collective-permute-start.7
  77.9 2.8 all-to-all-done.2
  80.8 3.0 collective-permute-done.7
  86.9 13.4 %all_gather.15.rows = bf16[512,768]{1,0:T(8,128)(2,1)S(1)} all-gather(bf16[128,768]{1,0:T(8,128)(2,1)S(1)} %fusion.95), channel_id=1, replica_groups=mesh['pipe'=2,'z'=4,'q'=1,'h'=2,'tp'=2] {'h','pipe'}, dimensions={0}, use_global_device_ids=true | all-gather | bytes 983040 | tf_op jit(solution)/shard_map/all_gather | solution.py:394
  105.5 2.2 copy.129.other_parts
  110.0 3.1 shard_map.312
  114.8 4.2 all-to-all-start.3
  120.9 9.5 %all-to-all-done.3 = bf16[4,128,768]{2,1,0:T(8,128)(2,1)} async-done(((bf16[4,128,768]{2,1,0:T(8,128)(2,1)}), bf16[4,128,768]{2,1,0:T(8,128)(2,1)}, u32[]{:S(2)}, u32[]{:S(2)}) %all-to-all-start.3) | async-done | bytes 786464 | tf_op jit(solution)/shard_map/all_to_all | solution.py:44
  136.7 21.2 %all_to_all.85 = bf16[8,48,768]{2,1,0:T(8,128)(2,1)S(1)} all-to-all(bf16[8,48,768]{2,1,0:T(8,128)(2,1)S(1)} %pad_maximum_fusion.4), channel_id=1, replica_groups=mesh['pipe'=2,'z'=4,'q'=1,'h'=2,'tp'=2] {'z','q','h'}, dimensions={0} | all-to-all | bytes 1179648 | tf_op jit(solution)/shard_map/all_to_all | solution.py:44
  159.1 7.3 %collective-permute-done.10 = bf16[8,24,768]{2,1,0:T(8,128)(2,1)} collective-permute-done((bf16[8,24,768]{2,1,0:T(8,128)(2,1)S(1)}, bf16[8,24,768]{2,1,0:T(8,128)(2,1)}, u32[]{:S(2)}, u32[]{:S(2)}) %collective-permute-start.10) | collective-permute-done | bytes 294944 | tf_op jit(solution)/shard_map/ppermute | solution.py:40
  172.7 2.9 fusion.45
  178.7 3.0 collective-permute-start.13
  181.7 7.6 %all-gather.3.cloned.1.call-done = bf16[16,1,48,896]{3,2,1,0:T(8,128)(2,1)} async-done(((bf16[2,1,48,896]{3,2,1,0:T(8,128)(2,1)}), bf16[16,1,48,896]{3,2,1,0:T(8,128)(2,1)}) %all-gather.3.cloned.1.call-update) | async-done | bytes 1376272 | tf_op jit(solution)/shard_map/all_gather | solution.py:136
  189.3 2.6 copy.130
  193.7 4.1 all-to-all-start.5
  200.5 7.5 %all-to-all-done.5 = bf16[8,24,768]{2,1,0:T(8,128)(2,1)} async-done(((bf16[8,24,768]{2,1,0:T(8,128)(2,1)}), bf16[8,24,768]{2,1,0:T(8,128)(2,1)}, u32[]{:S(2)}, u32[]{:S(2)}) %all-to-all-start.5) | async-done | bytes 294944 | tf_op jit(solution)/shard_map/all_to_all | solution.py:44
  208.0 2.2 fusion.78
  211.0 11.5 %all_gather.17.rows = bf16[512,768]{1,0:T(8,128)(2,1)S(1)} all-gather(bf16[128,768]{1,0:T(8,128)(2,1)S(1)} %fusion.80), channel_id=1, replica_groups=mesh['pipe'=2,'z'=4,'q'=1,'h'=2,'tp'=2] {'h','pipe'}, dimensions={0}, use_global_device_ids=true | all-gather | bytes 983040 | tf_op jit(solution)/shard_map/all_gather | solution.py:394
  227.3 2.3 collective-permute-done.14
  235.3 3.1 shard_map.314
  238.4 14.8 %all_to_all.86 = bf16[4,128,768]{2,1,0:T(8,128)(2,1)S(1)} all-to-all(bf16[4,128,768]{2,1,0:T(8,128)(2,1)S(1)} %bitcast.357), channel_id=1, replica_groups=mesh['pipe'=2,'z'=4,'q'=1,'h'=2,'tp'=2] {'h','pipe'}, dimensions={0} | all-to-all | bytes 1572864 | tf_op jit(solution)/shard_map/all_to_all | solution.py:44
  254.5 12.6 %all_to_all.87 = bf16[8,24,768]{2,1,0:T(8,128)(2,1)} all-to-all(bf16[8,24,768]{2,1,0:T(8,128)(2,1)S(1)} %bitcast.388), channel_id=1, replica_groups=mesh['pipe'=2,'z'=4,'q'=1,'h'=2,'tp'=2] {'z','q','h'}, dimensions={0} | all-to-all | bytes 589824 | tf_op jit(solution)/shard_map/all_to_all | solution.py:44
  267.1 4.2 collective-permute-start.16
  271.3 3.3 collective-permute-done.16
  279.7 4.1 fusion.32
  285.8 6.4 %fusion.14 = (f32[768]{0:T(1024)S(1)}, bf16[768,768]{1,0:T(8,128)(2,1)}) fusion(bf16[4,8,24,768]{3,2,1,0:T(8,128)(2,1)S(1)} %copy-done.57, bf16[1,1,1536,768]{3,2,1,0:T(8,128)(2,1)S(1)} %copy-done, f32[768,1536]{1,0:T(8,128)} %fusion.32), kind=kOutput, calls=%fused_computation.34 | convolution fusion | flops 1825504512 | bytes 9440256 | tf_op jit(solution)/shard_map/dot_general | solution.py:22
  292.2 4.4 fusion.13
  304.7 10.1 %collective-permute-done.19 = bf16[8,24,768]{2,1,0:T(8,128)(2,1)} collective-permute-done((bf16[8,24,768]{2,1,0:T(8,128)(2,1)}, bf16[8,24,768]{2,1,0:T(8,128)(2,1)}, u32[]{:S(2)}, u32[]{:S(2)}) %collective-permute-start.19) | collective-permute-done | bytes 294944 | tf_op jit(solution)/shard_map/ppermute | solution.py:220
  316.1 14.4 %all_to_all.88 = bf16[8,24,768]{2,1,0:T(8,128)(2,1)S(1)} all-to-all(bf16[8,24,768]{2,1,0:T(8,128)(2,1)S(1)} %fusion.101), channel_id=1, replica_groups=mesh['pipe'=2,'z'=4,'q'=1,'h'=2,'tp'=2] {'z','q','h'}, dimensions={0} | all-to-all | bytes 589824 | tf_op jit(solution)/shard_map/all_to_all | solution.py:44
  332.1 11.5 %all_gather.18.grad_rows = bf16[512,768]{1,0:T(8,128)(2,1)S(1)} all-gather(bf16[128,768]{1,0:T(8,128)(2,1)S(1)} %get-tuple-element.79), channel_id=1, replica_groups=mesh['pipe'=2,'z'=4,'q'=1,'h'=2,'tp'=2] {'h','pipe'}, dimensions={0}, use_global_device_ids=true | all-gather | bytes 983040 | tf_op jit(solution)/shard_map/all_gather | solution.py:410
  343.6 4.7 shard_map.315
  350.9 14.3 %all_to_all.89 = bf16[4,128,768]{2,1,0:T(8,128)(2,1)S(1)} all-to-all(bf16[4,128,768]{2,1,0:T(8,128)(2,1)S(1)} %bitcast.356), channel_id=1, replica_groups=mesh['pipe'=2,'z'=4,'q'=1,'h'=2,'tp'=2] {'h','pipe'}, dimensions={0} | all-to-all | bytes 1572864 | tf_op jit(solution)/shard_map/all_to_all | solution.py:44
  366.8 12.7 %all_to_all.90 = bf16[8,24,768]{2,1,0:T(8,128)(2,1)} all-to-all(bf16[8,24,768]{2,1,0:T(8,128)(2,1)S(1)} %bitcast.389), channel_id=1, replica_groups=mesh['pipe'=2,'z'=4,'q'=1,'h'=2,'tp'=2] {'z','q','h'}, dimensions={0} | all-to-all | bytes 589824 | tf_op jit(solution)/shard_map/all_to_all | solution.py:44
  381.6 6.9 %collective-permute-done.22 = bf16[8,24,768]{2,1,0:T(8,128)(2,1)} collective-permute-done((bf16[8,24,768]{2,1,0:T(8,128)(2,1)}, bf16[8,24,768]{2,1,0:T(8,128)(2,1)}, u32[]{:S(2)}, u32[]{:S(2)}) %collective-permute-start.22) | collective-permute-done | bytes 294944 | tf_op jit(solution)/shard_map/ppermute | solution.py:197
  391.4 6.4 %fusion.6 = bf16[768,1536]{1,0:T(8,128)(2,1)S(1)} fusion(f32[768,1536]{1,0:T(8,128)} %copy-done.115, bf16[768,768]{1,0:T(8,128)(2,1)S(1)} %bitcast.382, bf16[1,1,1536,768]{3,2,1,0:T(8,128)(2,1)S(1)} %copy-done), kind=kOutput, calls=%fused_computation.22 | convolution fusion | flops 1835532288 | bytes 10616832 | tf_op jit(solution)/shard_map/dot_general | solution.py:22
  407.0 5.9 %fusion.38 = f32[768,1536]{1,0:T(8,128)} fusion(bf16[768,1536]{1,0:T(8,128)(2,1)} %copy-done.71, bf16[768,1536]{1,0:T(8,128)(2,1)} %copy-done.70, pred[]{:T(512)S(6)} %eq.60, bf16[768,768]{1,0:T(8,128)(2,1)S(1)} %bitcast.365, bf16[768,768]{1,0:T(8,128)(2,1)S(1)} %bitcast.361), kind=kOutput, calls=%fused_computation.54 | convolution fusion | flops 1813708800 | bytes 11796481 | tf_op jit(solution)/shard_map/dot_general | solution.py:22
  413.0 3.3 collective-permute-done.25
  417.3 4.7 all-to-all-start.11
  422.0 11.2 %fusion.36 = f32[1536,768]{1,0:T(8,128)} fusion(pred[]{:T(512)S(6)} %eq.60, bf16[768,768]{1,0:T(8,128)(2,1)} %bitcast.383, bf16[768,768]{1,0:T(8,128)(2,1)} %bitcast.364, f32[768]{0:T(1024)S(1)} %multiply_reduce_fusion.5, f32[768,1536]{1,0:T(8,128)} %copy-done.115, f32[768,1536]{1,0:T(8,128)} %fusion.32), kind=kOutput, calls=%fused_computation.52 | convolution fusion | flops 1836711936 | bytes 16518145 | tf_op jit(solution)/shard_map/dot_general | solution.py:22
  433.2 8.3 %all-to-all-done.11 = bf16[8,48,768]{2,1,0:T(8,128)(2,1)} async-done(((bf16[8,48,768]{2,1,0:T(8,128)(2,1)}), bf16[8,48,768]{2,1,0:T(8,128)(2,1)}, u32[]{:S(2)}, u32[]{:S(2)}) %all-to-all-start.11) | async-done | bytes 589856 | tf_op jit(solution)/shard_map/all_to_all | solution.py:44
  445.6 13.1 %all_gather.19.grad_rows = bf16[512,768]{1,0:T(8,128)(2,1)S(1)} all-gather(bf16[128,768]{1,0:T(8,128)(2,1)S(1)} %convert_element_type.486), channel_id=1, replica_groups=mesh['pipe'=2,'z'=4,'q'=1,'h'=2,'tp'=2] {'h','pipe'}, dimensions={0}, use_global_device_ids=true | all-gather | bytes 983040 | tf_op jit(solution)/shard_map/all_gather | solution.py:410
  458.7 5.5 shard_map.317
  468.7 4.0 collective-permute-start.29
  476.8 4.6 all-to-all-start.12
  488.4 4.3 all-to-all-done.12
  500.6 4.8 all-to-all-start.13
  507.5 3.9 collective-permute-start.34
  513.8 9.3 %collective-permute-done.34 = bf16[80,768]{1,0:T(8,128)(2,1)S(1)} collective-permute-done((bf16[80,768]{1,0:T(8,128)(2,1)S(1)}, bf16[80,768]{1,0:T(8,128)(2,1)S(1)}, u32[]{:S(2)}, u32[]{:S(2)}) %collective-permute-start.34) | collective-permute-done | bytes 122912 | tf_op jit(solution)/shard_map/ppermute | solution.py:86
  523.1 7.4 %collective-permute-done.33 = bf16[80,768]{1,0:T(8,128)(2,1)S(1)} collective-permute-done((bf16[80,768]{1,0:T(8,128)(2,1)S(1)}, bf16[80,768]{1,0:T(8,128)(2,1)S(1)}, u32[]{:S(2)}, u32[]{:S(2)}) %collective-permute-start.33) | collective-permute-done | bytes 122912 | tf_op jit(solution)/shard_map/ppermute | solution.py:86
  533.9 3.9 all-to-all-start.14
  538.8 4.5 all-to-all-done.14
  544.3 4.0 all_to_all.91
  548.4 3.2 all-to-all-start.15
  (498 shorter events, 151.2 us)
Async XLA Ops:
  7.2 165.6 %copy-start = (bf16[1,1,1536,768]{3,2,1,0:T(8,128)(2,1)S(1)}, bf16[1,1,1536,768]{3,2,1,0:T(8,128)(2,1)}, u32[]{:S(2)}) copy-start(bf16[1,1,1536,768]{3,2,1,0:T(8,128)(2,1)} %param.35) | copy-start | bytes 7077892
  8.2 13.7 %collective-permute-start = (bf16[4,64]{1,0:T(4,128)(2,1)S(1)}, bf16[4,64]{1,0:T(4,128)(2,1)S(1)}, u32[]{:S(2)}, u32[]{:S(2)}) collective-permute-start(bf16[4,64]{1,0:T(4,128)(2,1)S(1)} %dynamic-slice_convert_fusion), channel_id=1, source_target_pairs={{0,16},{16,0},{1,17},{17,1},{2,18},{18,2},{3,19},{19,3},{4,20},{20... | collective-permute-start | bytes 1544 | tf_op jit(solution)/shard_map/ppermute | solution.py:40
  17.6 12.6 %all-to-all-start = ((bf16[2,2,48,4,192]{4,3,2,1,0:T(4,128)(2,1)}), bf16[2,2,48,4,192]{4,3,2,1,0:T(4,128)(2,1)}, u32[]{:S(2)}, u32[]{:S(2)}) async-start(bf16[2,2,48,4,192]{4,3,2,1,0:T(4,128)(2,1)} %maximum_bitcast_fusion), calls=%async_computation | async-start | bytes 786432 | tf_op jit(solution)/shard_map/all_to_all | solution.py:44
  21.8 443.2 %copy-start.87 = (s32[1024]{0:T(1024)}, s32[1024]{0:T(1024)S(1)}, u32[]{:S(2)}) copy-start(s32[1024]{0:T(1024)S(1)} %pad_clamp_fusion.1) | copy-start | bytes 12292
  21.8 42.0 %copy-start.86 = (s32[1024]{0:T(1024)}, s32[1024]{0:T(1024)S(1)}, u32[]{:S(2)}) copy-start(s32[1024]{0:T(1024)S(1)} %pad_clamp_fusion) | copy-start | bytes 12292
  25.1 24.9 %copy-start.73 = (bf16[2,2,64,768]{3,2,1,0:T(8,128)(2,1)S(1)}, bf16[2,2,64,768]{3,2,1,0:T(8,128)(2,1)}, u32[]{:S(2)}) copy-start(bf16[2,2,64,768]{3,2,1,0:T(8,128)(2,1)} %param.25) | copy-start | bytes 1179652
  25.9 14.9 %collective-permute-start.1 = (bf16[80,768]{1,0:T(8,128)(2,1)}, bf16[80,768]{1,0:T(8,128)(2,1)}, u32[]{:S(2)}, u32[]{:S(2)}) collective-permute-start(bf16[80,768]{1,0:T(8,128)(2,1)} %get-tuple-element.101), channel_id=1, source_target_pairs={{0,4},{8,12},{20,16},{28,24},{1,5},{9,13},{21,17},{29,25},{2,6},{1... | collective-permute-start | bytes 368648 | tf_op jit(solution)/shard_map/ppermute | solution.py:96
  34.0 7.2 %collective-permute-start.3 = (bf16[80,768]{1,0:T(8,128)(2,1)}, bf16[80,768]{1,0:T(8,128)(2,1)S(1)}, u32[]{:S(2)}, u32[]{:S(2)}) collective-permute-start(bf16[80,768]{1,0:T(8,128)(2,1)} %get-tuple-element.102), channel_id=1, source_target_pairs={{0,12},{8,4},{20,24},{28,16},{1,13},{9,5},{21,25},{29,17},{2,14},{... | collective-permute-start | bytes 368648 | tf_op jit(solution)/shard_map/ppermute | solution.py:96
  37.7 8.2 %collective-permute-start.2 = (bf16[80,768]{1,0:T(8,128)(2,1)S(1)}, bf16[80,768]{1,0:T(8,128)(2,1)S(1)}, u32[]{:S(2)}, u32[]{:S(2)}) collective-permute-start(bf16[80,768]{1,0:T(8,128)(2,1)S(1)} %get-tuple-element.103), channel_id=1, source_target_pairs={{0,8},{8,0},{20,28},{28,20},{1,9},{9,1},{21,29},{29,21},{2,10},{10... | collective-permute-start | bytes 368648 | tf_op jit(solution)/shard_map/ppermute | solution.py:96
  45.9 57.2 %copy-start.39 = (bf16[2,80,768]{2,1,0:T(8,128)(2,1)}, bf16[2,80,768]{2,1,0:T(8,128)(2,1)S(1)}, u32[]{:S(2)}) copy-start(bf16[2,80,768]{2,1,0:T(8,128)(2,1)S(1)} %maximum_select_fusion.3) | copy-start | bytes 737284
  45.9 10.0 %all-to-all-start.1 = ((bf16[4,48,896]{2,1,0:T(8,128)(2,1)}), bf16[4,48,896]{2,1,0:T(8,128)(2,1)}, u32[]{:S(2)}, u32[]{:S(2)}) async-start(bf16[4,48,896]{2,1,0:T(8,128)(2,1)} %pad_maximum_fusion.7), calls=%async_computation.1 | async-start | bytes 688128 | tf_op jit(solution)/shard_map/all_to_all | solution.py:44
  58.6 22.2 %all-to-all-start.2 = ((bf16[4,2,48,896]{3,2,1,0:T(8,128)(2,1)}), bf16[4,2,48,896]{3,2,1,0:T(8,128)(2,1)}, u32[]{:S(2)}, u32[]{:S(2)}) async-start(bf16[4,2,48,896]{3,2,1,0:T(8,128)(2,1)} %broadcast_in_dim.50), calls=%async_computation.2 | async-start | bytes 1376256 | tf_op jit(solution)/shard_map/all_to_all | solution.py:44
  66.0 11.1 %collective-permute-start.6 = (bf16[64,768]{1,0:T(8,128)(2,1)S(1)}, bf16[64,768]{1,0:T(8,128)(2,1)S(1)}, u32[]{:S(2)}, u32[]{:S(2)}) collective-permute-start(bf16[64,768]{1,0:T(8,128)(2,1)S(1)} %get-tuple-element.108), channel_id=1, source_target_pairs={{0,4},{8,12},{20,16},{28,24},{1,5},{9,13},{21,17},{29,25},{2,6},{1... | collective-permute-start | bytes 294920 | tf_op jit(solution)/shard_map/ppermute | solution.py:96
  70.0 10.8 %collective-permute-start.8 = (bf16[64,768]{1,0:T(8,128)(2,1)S(1)}, bf16[64,768]{1,0:T(8,128)(2,1)S(1)}, u32[]{:S(2)}, u32[]{:S(2)}) collective-permute-start(bf16[64,768]{1,0:T(8,128)(2,1)S(1)} %get-tuple-element.109), channel_id=1, source_target_pairs={{0,12},{8,4},{20,24},{28,16},{1,13},{9,5},{21,25},{29,17},{2,14},{... | collective-permute-start | bytes 294920 | tf_op jit(solution)/shard_map/ppermute | solution.py:96
  74.0 9.8 %collective-permute-start.7 = (bf16[64,768]{1,0:T(8,128)(2,1)S(1)}, bf16[64,768]{1,0:T(8,128)(2,1)S(1)}, u32[]{:S(2)}, u32[]{:S(2)}) collective-permute-start(bf16[64,768]{1,0:T(8,128)(2,1)S(1)} %get-tuple-element.110), channel_id=1, source_target_pairs={{0,8},{8,0},{20,28},{28,20},{1,9},{9,1},{21,29},{29,21},{2,10},{10... | collective-permute-start | bytes 294920 | tf_op jit(solution)/shard_map/ppermute | solution.py:96
  80.8 4.2 collective-permute-start.4
  84.7 296.3 %copy-start.99 = (f32[128]{0:T(128)}, f32[128]{0:T(128)S(1)}, u32[]{:S(2)}) copy-start(f32[128]{0:T(128)S(1)} %rsqrt.52) | copy-start | bytes 1540
  84.9 115.6 %copy-start.91 = (s32[128]{0:T(128)}, s32[128]{0:T(128)S(1)}, u32[]{:S(2)}) copy-start(s32[128]{0:T(128)S(1)} %reshape.602) | copy-start | bytes 1540
  84.9 34.1 %copy-start.102 = (s32[128]{0:T(128)}, s32[128]{0:T(128)S(1)}, u32[]{:S(2)}) copy-start(s32[128]{0:T(128)S(1)} %reshape.605) | copy-start | bytes 1540
  103.1 2.3 collective-permute-start.5
  114.8 15.7 %all-to-all-start.3 = ((bf16[4,128,768]{2,1,0:T(8,128)(2,1)}), bf16[4,128,768]{2,1,0:T(8,128)(2,1)}, u32[]{:S(2)}, u32[]{:S(2)}) async-start(bf16[4,128,768]{2,1,0:T(8,128)(2,1)} %bitcast.355), calls=%async_computation.3 | async-start | bytes 1572864 | tf_op jit(solution)/shard_map/all_to_all | solution.py:44
  119.0 70.3 %all-gather.3.cloned.1.call-start = ((), (), s32[]{:S(2)}) async-start(), calls=%async_computation.19 | async-start | bytes 1548288 | tf_op jit(solution)/shard_map/all_gather | solution.py:136
  158.7 7.6 %collective-permute-start.10 = (bf16[8,24,768]{2,1,0:T(8,128)(2,1)S(1)}, bf16[8,24,768]{2,1,0:T(8,128)(2,1)}, u32[]{:S(2)}, u32[]{:S(2)}) collective-permute-start(bf16[8,24,768]{2,1,0:T(8,128)(2,1)S(1)} %get-tuple-element.96), channel_id=1, source_target_pairs={{0,16},{16,0},{1,17},{17,1},{2,18},{18,2},{3,19},{19,3},{4,20},{20... | collective-permute-start | bytes 884744 | tf_op jit(solution)/shard_map/ppermute | solution.py:40
  159.1 7.3 %collective-permute-start.9 = (bf16[8,24,768]{2,1,0:T(8,128)(2,1)}, bf16[8,24,768]{2,1,0:T(8,128)(2,1)}, u32[]{:S(2)}, u32[]{:S(2)}) collective-permute-start(bf16[8,24,768]{2,1,0:T(8,128)(2,1)} %get-tuple-element.95), channel_id=1, source_target_pairs={{0,1},{1,0},{2,3},{3,2},{4,5},{5,4},{6,7},{7,6},{8,9},{9,8},{10,11... | collective-permute-start | bytes 884744 | tf_op jit(solution)/shard_map/ppermute | solution.py:40
  166.3 1.9 collective-permute-start.11
  175.7 2.1 collective-permute-start.12
  178.7 13.2 %collective-permute-start.13 = (bf16[8,24,768]{2,1,0:T(8,128)(2,1)}, bf16[8,24,768]{2,1,0:T(8,128)(2,1)}, u32[]{:S(2)}, u32[]{:S(2)}) collective-permute-start(bf16[8,24,768]{2,1,0:T(8,128)(2,1)} %fusion.71), channel_id=1, source_target_pairs={{0,16},{1,17},{2,18},{3,19},{4,20},{5,21},{6,22},{7,23},{8,24},{9,... | collective-permute-start | bytes 884744 | tf_op jit(solution)/shard_map/ppermute | solution.py:220
  193.7 14.3 %all-to-all-start.5 = ((bf16[8,24,768]{2,1,0:T(8,128)(2,1)}), bf16[8,24,768]{2,1,0:T(8,128)(2,1)}, u32[]{:S(2)}, u32[]{:S(2)}) async-start(bf16[8,24,768]{2,1,0:T(8,128)(2,1)} %fusion.100), calls=%async_computation.5 | async-start | bytes 589824 | tf_op jit(solution)/shard_map/all_to_all | solution.py:44
  197.7 334.5 %reduce-scatter.2.cloned.1.call-start = ((), (), s32[]{:S(2)}) async-start(), calls=%async_computation.18 | async-start | bytes 1327104 | tf_op jit(solution)/shard_map/reduce_scatter | solution.py:159
  200.5 165.3 %copy-start.95 = (f32[128]{0:T(128)}, f32[128]{0:T(128)S(1)}, u32[]{:S(2)}) copy-start(f32[128]{0:T(128)S(1)} %select_reduce_fusion.1) | copy-start | bytes 1540
  227.3 2.3 collective-permute-start.14
  267.1 7.6 %collective-permute-start.16 = (bf16[8,24,768]{2,1,0:T(8,128)(2,1)}, bf16[8,24,768]{2,1,0:T(8,128)(2,1)}, u32[]{:S(2)}, u32[]{:S(2)}) collective-permute-start(bf16[8,24,768]{2,1,0:T(8,128)(2,1)} %all_to_all.87), channel_id=1, source_target_pairs={{0,16},{1,17},{2,18},{3,19},{4,20},{5,21},{6,22},{7,23},{8,24},{9,... | collective-permute-start | bytes 884744 | tf_op jit(solution)/shard_map/ppermute | solution.py:199
  271.3 3.4 collective-permute-start.15
  274.7 1.9 collective-permute-start.17
  300.3 31.6 %copy-start.105 = (f32[128]{0:T(128)S(1)}, f32[128]{0:T(128)}, u32[]{:S(2)}) copy-start(f32[128]{0:T(128)} %get-tuple-element.121) | copy-start | bytes 1540
  300.4 2.1 collective-permute-start.18
  303.4 11.4 %collective-permute-start.19 = (bf16[8,24,768]{2,1,0:T(8,128)(2,1)}, bf16[8,24,768]{2,1,0:T(8,128)(2,1)}, u32[]{:S(2)}, u32[]{:S(2)}) collective-permute-start(bf16[8,24,768]{2,1,0:T(8,128)(2,1)} %fusion.69), channel_id=1, source_target_pairs={{16,0},{17,1},{18,2},{19,3},{20,4},{21,5},{22,6},{23,7},{24,8},{25... | collective-permute-start | bytes 884744 | tf_op jit(solution)/shard_map/ppermute | solution.py:220
  304.7 27.2 %copy-start.47 = (f32[128,768]{1,0:T(8,128)S(1)}, f32[128,768]{1,0:T(8,128)}, u32[]{:S(2)}) copy-start(f32[128,768]{1,0:T(8,128)} %copy-done.46) | copy-start | bytes 1179652
  304.7 27.2 %copy-start.64 = (bf16[2,64,768]{2,1,0:T(8,128)(2,1)S(1)}, bf16[2,64,768]{2,1,0:T(8,128)(2,1)}, u32[]{:S(2)}) copy-start(bf16[2,64,768]{2,1,0:T(8,128)(2,1)} %maximum_select_fusion.4) | copy-start | bytes 589828
  316.0 27.5 %copy-start.4 = (bf16[4,2,2,48,896]{4,3,2,1,0:T(8,128)(2,1)S(1)}, bf16[4,2,2,48,896]{4,3,2,1,0:T(8,128)(2,1)}, u32[]{:S(2)}) copy-start(bf16[4,2,2,48,896]{4,3,2,1,0:T(8,128)(2,1)} %copy.130) | copy-start | bytes 4128772
  316.1 27.5 %copy-start.10 = (bf16[512,576]{1,0:T(8,128)(2,1)S(1)}, bf16[512,576]{1,0:T(8,128)(2,1)}, u32[]{:S(2)}) copy-start(bf16[512,576]{1,0:T(8,128)(2,1)} %copy-done.8) | copy-start | bytes 1769476
  316.1 27.5 %copy-start.22 = (bf16[512,576]{1,0:T(8,128)(2,1)S(1)}, bf16[512,576]{1,0:T(8,128)(2,1)}, u32[]{:S(2)}) copy-start(bf16[512,576]{1,0:T(8,128)(2,1)} %copy.132.other_parts) | copy-start | bytes 1769476
  316.1 27.5 %copy-start.30 = (f32[192,512]{1,0:T(8,128)S(1)}, f32[192,512]{1,0:T(8,128)}, u32[]{:S(2)}) copy-start(f32[192,512]{1,0:T(8,128)} %copy-done.29) | copy-start | bytes 1179652
  348.3 1.8 collective-permute-start.20
  379.5 8.9 %collective-permute-start.22 = (bf16[8,24,768]{2,1,0:T(8,128)(2,1)}, bf16[8,24,768]{2,1,0:T(8,128)(2,1)}, u32[]{:S(2)}, u32[]{:S(2)}) collective-permute-start(bf16[8,24,768]{2,1,0:T(8,128)(2,1)} %all_to_all.90), channel_id=1, source_target_pairs={{16,0},{17,1},{18,2},{19,3},{20,4},{21,5},{22,6},{23,7},{24,8},{25... | collective-permute-start | bytes 884744 | tf_op jit(solution)/shard_map/ppermute | solution.py:197
  381.5 8.3 %collective-permute-start.21 = (bf16[8,24,768]{2,1,0:T(8,128)(2,1)}, bf16[8,24,768]{2,1,0:T(8,128)(2,1)S(1)}, u32[]{:S(2)}, u32[]{:S(2)}) collective-permute-start(bf16[8,24,768]{2,1,0:T(8,128)(2,1)} %all_to_all.90), channel_id=1, source_target_pairs={{0,1},{1,0},{2,3},{3,2},{4,5},{5,4},{6,7},{7,6},{8,9},{9,8},{10,11... | collective-permute-start | bytes 884744 | tf_op jit(solution)/shard_map/ppermute | solution.py:40
  388.4 1.8 collective-permute-start.23
  401.0 4.5 collective-permute-start.24
  406.9 9.3 %collective-permute-start.25 = (bf16[8,24,768]{2,1,0:T(8,128)(2,1)S(1)}, bf16[8,24,768]{2,1,0:T(8,128)(2,1)S(1)}, u32[]{:S(2)}, u32[]{:S(2)}) collective-permute-start(bf16[8,24,768]{2,1,0:T(8,128)(2,1)S(1)} %get-tuple-element.86), channel_id=1, source_target_pairs={{0,16},{16,0},{1,17},{17,1},{2,18},{18,2},{3,19},{19,3},{4,20},{20... | collective-permute-start | bytes 884744 | tf_op jit(solution)/shard_map/ppermute | solution.py:40
  417.3 24.2 %all-to-all-start.11 = ((bf16[8,48,768]{2,1,0:T(8,128)(2,1)}), bf16[8,48,768]{2,1,0:T(8,128)(2,1)}, u32[]{:S(2)}, u32[]{:S(2)}) async-start(bf16[8,48,768]{2,1,0:T(8,128)(2,1)} %maximum_select_fusion), calls=%async_computation.11 | async-start | bytes 1179648 | tf_op jit(solution)/shard_map/all_to_all | solution.py:44
  444.8 20.1 %collective-permute-start.26 = (bf16[2,1,64,768]{3,2,1,0:T(8,128)(2,1)S(1)}, bf16[2,1,64,768]{3,2,1,0:T(8,128)(2,1)S(1)}, u32[]{:S(2)}, u32[]{:S(2)}) collective-permute-start(bf16[2,1,64,768]{3,2,1,0:T(8,128)(2,1)S(1)} %bitcast.416), channel_id=1, source_target_pairs={{0,16},{16,0},{1,17},{17,1},{2,18},{18,2},{3,19},{19,3},{4,20},{20... | collective-permute-start | bytes 589832 | tf_op jit(solution)/shard_map/ppermute | solution.py:40
  464.9 8.3 %collective-permute-start.30 = (bf16[512,384]{1,0:T(8,128)(2,1)}, bf16[512,384]{1,0:T(8,128)(2,1)S(1)}, u32[]{:S(2)}, u32[]{:S(2)}) collective-permute-start(bf16[512,384]{1,0:T(8,128)(2,1)} %get-tuple-element.49), channel_id=1, source_target_pairs={{0,1},{1,0},{2,3},{3,2},{4,5},{5,4},{6,7},{7,6},{8,9},{9,8},{10,11... | collective-permute-start | bytes 1179656 | tf_op jit(solution)/shard_map/ppermute | solution.py:40
  468.7 13.0 %collective-permute-start.29 = (bf16[64,768]{1,0:T(8,128)(2,1)}, bf16[64,768]{1,0:T(8,128)(2,1)S(1)}, u32[]{:S(2)}, u32[]{:S(2)}) collective-permute-start(bf16[64,768]{1,0:T(8,128)(2,1)} %get-tuple-element.105), channel_id=1, source_target_pairs={{0,12},{4,8},{8,4},{12,0},{1,13},{5,9},{9,5},{13,1},{2,14},{6,10},... | collective-permute-start | bytes 294920 | tf_op jit(solution)/shard_map/ppermute | solution.py:86
  472.7 9.0 %collective-permute-start.28 = (bf16[64,768]{1,0:T(8,128)(2,1)}, bf16[64,768]{1,0:T(8,128)(2,1)}, u32[]{:S(2)}, u32[]{:S(2)}) collective-permute-start(bf16[64,768]{1,0:T(8,128)(2,1)} %get-tuple-element.106), channel_id=1, source_target_pairs={{0,8},{4,12},{8,0},{12,4},{1,9},{5,13},{9,1},{13,5},{2,10},{6,14},... | collective-permute-start | bytes 294920 | tf_op jit(solution)/shard_map/ppermute | solution.py:86
  472.7 9.0 %collective-permute-start.27 = (bf16[64,768]{1,0:T(8,128)(2,1)}, bf16[64,768]{1,0:T(8,128)(2,1)}, u32[]{:S(2)}, u32[]{:S(2)}) collective-permute-start(bf16[64,768]{1,0:T(8,128)(2,1)} %get-tuple-element.107), channel_id=1, source_target_pairs={{0,4},{4,0},{8,12},{12,8},{1,5},{5,1},{9,13},{13,9},{2,6},{6,2},{1... | collective-permute-start | bytes 294920 | tf_op jit(solution)/shard_map/ppermute | solution.py:86
  476.8 15.9 %all-to-all-start.12 = ((bf16[4,128,768]{2,1,0:T(8,128)(2,1)}), bf16[4,128,768]{2,1,0:T(8,128)(2,1)}, u32[]{:S(2)}, u32[]{:S(2)}) async-start(bf16[4,128,768]{2,1,0:T(8,128)(2,1)} %bitcast.354), calls=%async_computation.12 | async-start | bytes 1572864 | tf_op jit(solution)/shard_map/all_to_all | solution.py:44
  488.3 10.2 %collective-permute-start.35 = (bf16[8,48,768]{2,1,0:T(8,128)(2,1)S(1)}, bf16[8,48,768]{2,1,0:T(8,128)(2,1)}, u32[]{:S(2)}, u32[]{:S(2)}) collective-permute-start(bf16[8,48,768]{2,1,0:T(8,128)(2,1)S(1)} %dynamic-slice_bitcast_fusion), channel_id=1, source_target_pairs={{0,1},{1,0},{2,3},{3,2},{4,5},{5,4},{6,7},{7,6},{8,9},{9,8},{10,11... | collective-permute-start | bytes 1769480 | tf_op jit(solution)/shard_map/ppermute | solution.py:40
  497.0 8.4 %collective-permute-start.31 = (bf16[144,768]{1,0:T(8,128)(2,1)S(1)}, bf16[144,768]{1,0:T(8,128)(2,1)S(1)}, u32[]{:S(2)}, u32[]{:S(2)}) collective-permute-start(bf16[144,768]{1,0:T(8,128)(2,1)S(1)} %pad_maximum_fusion.9), channel_id=1, source_target_pairs={{0,16},{16,0},{1,17},{17,1},{2,18},{18,2},{3,19},{19,3},{4,20},{20... | collective-permute-start | bytes 663560 | tf_op jit(solution)/shard_map/ppermute | solution.py:40
  500.6 31.5 %all-to-all-start.13 = ((bf16[4,2,48,768]{3,2,1,0:T(8,128)(2,1)}), bf16[4,2,48,768]{3,2,1,0:T(8,128)(2,1)S(1)}, u32[]{:S(2)}, u32[]{:S(2)}) async-start(bf16[4,2,48,768]{3,2,1,0:T(8,128)(2,1)} %bitcast.121), calls=%async_computation.13 | async-start | bytes 1179648 | tf_op jit(solution)/shard_map/all_to_all | solution.py:44
  507.5 15.6 %collective-permute-start.34 = (bf16[80,768]{1,0:T(8,128)(2,1)S(1)}, bf16[80,768]{1,0:T(8,128)(2,1)S(1)}, u32[]{:S(2)}, u32[]{:S(2)}) collective-permute-start(bf16[80,768]{1,0:T(8,128)(2,1)S(1)} %get-tuple-element.98), channel_id=1, source_target_pairs={{0,12},{4,8},{8,4},{12,0},{1,13},{5,9},{9,5},{13,1},{2,14},{6,10},... | collective-permute-start | bytes 368648 | tf_op jit(solution)/shard_map/ppermute | solution.py:86
  511.4 19.2 %collective-permute-start.33 = (bf16[80,768]{1,0:T(8,128)(2,1)S(1)}, bf16[80,768]{1,0:T(8,128)(2,1)S(1)}, u32[]{:S(2)}, u32[]{:S(2)}) collective-permute-start(bf16[80,768]{1,0:T(8,128)(2,1)S(1)} %get-tuple-element.99), channel_id=1, source_target_pairs={{0,8},{4,12},{8,0},{12,4},{1,9},{5,13},{9,1},{13,5},{2,10},{6,14},... | collective-permute-start | bytes 368648 | tf_op jit(solution)/shard_map/ppermute | solution.py:86
  511.4 19.2 %collective-permute-start.32 = (bf16[80,768]{1,0:T(8,128)(2,1)S(1)}, bf16[80,768]{1,0:T(8,128)(2,1)S(1)}, u32[]{:S(2)}, u32[]{:S(2)}) collective-permute-start(bf16[80,768]{1,0:T(8,128)(2,1)S(1)} %get-tuple-element.100), channel_id=1, source_target_pairs={{0,4},{4,0},{8,12},{12,8},{1,5},{5,1},{9,13},{13,9},{2,6},{6,2},{1... | collective-permute-start | bytes 368648 | tf_op jit(solution)/shard_map/ppermute | solution.py:86
  533.9 9.4 %all-to-all-start.14 = ((bf16[4,48,768]{2,1,0:T(8,128)(2,1)}), bf16[4,48,768]{2,1,0:T(8,128)(2,1)S(1)}, u32[]{:S(2)}, u32[]{:S(2)}) async-start(bf16[4,48,768]{2,1,0:T(8,128)(2,1)} %bitcast.128), calls=%async_computation.15 | async-start | bytes 589824 | tf_op jit(solution)/shard_map/all_to_all | solution.py:44
  548.4 7.9 %all-to-all-start.15 = ((bf16[4,2,384]{2,1,0:T(2,128)(2,1)}), bf16[4,2,384]{2,1,0:T(2,128)(2,1)S(1)}, u32[]{:S(2)}, u32[]{:S(2)}) async-start(bf16[4,2,384]{2,1,0:T(2,128)(2,1)} %reshape.737), calls=%async_computation.16 | async-start | bytes 12288 | tf_op jit(solution)/shard_map/all_to_all | solution.py:44
  (103 other events, 638.7 us)
Sparse Core Ops, SparseCore 0:
  166.5 22.7 all-gather.2
  403.7 33.9 reduce-scatter.1

commit v4 on v3

--- a/solution.py
+++ b/solution.py
@@ -75,8 +75,10 @@
 
 def xor_z(values):
     z = lax.axis_index("z")
-    values = jnp.where((z & 1) == 1, values[jnp.array([1, 0, 3, 2])], values)
-    return jnp.where((z & 2) == 2, values[jnp.array([2, 3, 0, 1])], values)
+    odd, high = ((z & 1) == 1, (z & 2) == 2)
+    a, b, c, d = (values[k] for k in range(4))
+    a, b, c, d = (jnp.where(odd, b, a), jnp.where(odd, a, b), jnp.where(odd, d, c), jnp.where(odd, c, d))
+    return [jnp.where(high, c, a), jnp.where(high, d, b), jnp.where(high, a, c), jnp.where(high, b, d)]
 
 
 def exchanged_z(values):
@@ -84,7 +86,7 @@
     parts = [mine[0]]
     for k in range(1, 4):
         parts.append(lax.ppermute(mine[k], "z", [(z, z ^ k) for z in range(4)]))
-    return xor_z(jnp.stack(parts))
+    return jnp.stack(xor_z(parts))
 
 
 def to_planes(values):
@@ -114,15 +116,20 @@
     return exchanged(jnp.broadcast_to(values[None], (places,) + values.shape), ("z", "q"))
 
 
-def spread_weights(query_weight, key_weight, value_weight, output_weight, extras, first):
+def spread_weights(query_weight, key_weight, value_weight, output_weight, extras, inputs):
     rows, cols = query_weight.shape
     half, group = (rows // 2, cols // 2)
     packed = jnp.stack([query_weight, key_weight, value_weight, output_weight.T])
     packed = packed.reshape(4, 2, half, 2, group).transpose(1, 3, 2, 0, 4)
     by_core = exchanged(packed, "tp").reshape(4, half, 4 * group)
     small = jnp.broadcast_to(extras[None], (4,) + extras.shape)
-    by_chip = exchanged(after(jnp.concatenate([by_core, small], axis=-1), first), CHIPS)
-    return by_chip.reshape(2, 2, half, -1)
+    own = jnp.concatenate([by_core, small], axis=-1)
+    count, width = inputs.shape
+    copies = jnp.pad(inputs, ((0, 0), (0, own.shape[-1] - width)))
+    copies = jnp.broadcast_to(copies[None], (4,) + copies.shape)
+    by_chip = exchanged(jnp.concatenate([own, copies], axis=1), CHIPS)
+    gathered = by_chip[:, half:, :width].reshape(4 * count, width)
+    return by_chip[:, :half].reshape(2, 2, half, -1), gathered
 
 
 def join_section(mine):
@@ -137,18 +144,6 @@
     places = lax.axis_size("z") * lax.axis_size("q")
     gathered = gathered.reshape((places, 2) + own.shape).transpose(0, 2, 1, 3, 4)
     return gathered.reshape(-1, own.shape[-1])
-
-
-def scatter_start(grads):
-    width = grads.shape[-1]
-    places = lax.axis_size("z") * lax.axis_size("q")
-    split = grads.reshape(places * 2, 2, -1, width)
-    mine = lax.axis_index("tp")
-    kept = lax.dynamic_index_in_dim(split, mine, 1, keepdims=False)
-    got = swapped(lax.dynamic_index_in_dim(split, 1 - mine, 1, keepdims=False), "tp")
-    both = (kept.astype(F32) + got.astype(F32)).astype(BF16)
-    moved = exchanged(both.reshape(places, 2, -1, width), ("z", "q"))
-    return jnp.sum(moved.astype(F32), axis=0).astype(BF16)
 
 
 def scatter_later(grads):
@@ -236,15 +231,14 @@
     return values.astype(F32).T.astype(BF16)
 
 
-def attend_kernel(own, own_parts, other_parts, whole, part, attended, attended_flat, log_total):
-    group = own.shape[1] // 3
-    queries_flat = flipped(own[:, :group]) * SCORE_SCALE
-    sides = (own_parts, other_parts)
-    values_flat = [flipped(side[:, 2 * group :]) for side in sides]
+def attend_kernel(queries, own, other, whole, part, attended, attended_flat, log_total):
+    group = queries.shape[1]
+    queries_flat = flipped(queries[...]) * SCORE_SCALE
+    sides = (own, other)
+    values_flat = [flipped(side[:, group:]) for side in sides]
     for head in range(group // HEAD_DIM):
         lanes = slice(head * HEAD_DIM, (head + 1) * HEAD_DIM)
-        key_lanes = slice(group + head * HEAD_DIM, group + (head + 1) * HEAD_DIM)
-        scores = [mm(side[:, key_lanes], queries_flat[lanes]) for side in sides]
+        scores = [mm(side[:, lanes], queries_flat[lanes]) for side in sides]
         peak = jnp.maximum(*(jnp.max(block, axis=0, keepdims=True) for block in scores))
         weights = [jnp.exp(block - peak) for block in scores]
         total = sum(jnp.sum(block, axis=0, keepdims=True) for block in weights)
@@ -255,9 +249,9 @@
     part[...] = mm_nt(attended[...], whole[:, 3 * group : 4 * group]).astype(BF16)
 
 
-def attend(own, own_parts, other_parts, whole):
-    rows, group = (own.shape[0], own.shape[1] // 3)
-    keys = 2 * own_parts.shape[0]
+def attend(queries, own, other, whole):
+    rows, group = queries.shape
+    keys = 2 * own.shape[0]
     return whole_call(
         attend_kernel,
         (
@@ -266,9 +260,9 @@
             jax.ShapeDtypeStruct((group, rows), F32),
             jax.ShapeDtypeStruct((8, rows), F32),
         ),
+        queries,
         own,
-        own_parts,
-        other_parts,
+        other,
         whole,
         flops=4 * rows * keys * group,
         exps=rows * keys * group // HEAD_DIM,
@@ -276,43 +270,42 @@
 
 
 def attend_back_kernel(
-    grad_rows, whole, own, own_parts, other_parts, attended_flat, log_total,
+    grad_rows, whole, queries, own, other, attended_flat, log_total,
     grad_queries, grad_own, grad_other,
 ):
-    group = own.shape[1] // 3
-    keys = own_parts.shape[0]
+    group = queries.shape[1]
+    keys = own.shape[0]
     chunk = min(512, keys)
-    queries_flat = flipped(own[:, :group]) * SCORE_SCALE
+    queries_flat = flipped(queries[...]) * SCORE_SCALE
     w_out_rows = whole[:, 3 * group : 4 * group]
     grad_flat = dot(w_out_rows, grad_rows[...], ((0,), (1,))).astype(BF16)
     products = grad_flat.astype(F32) * attended_flat[...]
-    sides = ((own_parts, grad_own), (other_parts, grad_other))
-    keys_flat = [flipped(side[:, group : 2 * group]) for side, unused in sides]
+    sides = ((own, grad_own), (other, grad_other))
+    keys_flat = [flipped(side[:, :group]) for side, unused in sides]
     grad_queries_flat = []
     for head in range(group // HEAD_DIM):
         lanes = slice(head * HEAD_DIM, (head + 1) * HEAD_DIM)
-        key_lanes = slice(group + head * HEAD_DIM, group + (head + 1) * HEAD_DIM)
-        value_lanes = slice(2 * group + head * HEAD_DIM, 2 * group + (head + 1) * HEAD_DIM)
+        value_lanes = slice(group + head * HEAD_DIM, group + (head + 1) * HEAD_DIM)
         delta = jnp.sum(products[lanes], axis=0, keepdims=True)
         level = log_total[head : head + 1, :]
         query, grad = (queries_flat[lanes], grad_flat[lanes])
-        total = jnp.zeros((HEAD_DIM, own.shape[0]), F32)
+        total = jnp.zeros((HEAD_DIM, queries.shape[0]), F32)
         for (side, grad_side), flat in zip(sides, keys_flat):
             for begin in range(0, keys, chunk):
                 here = slice(begin, begin + chunk)
-                probs = jnp.exp(mm(side[here, key_lanes], query) - level)
+                probs = jnp.exp(mm(side[here, lanes], query) - level)
                 grad_probs = mm(side[here, value_lanes], grad)
                 grad_scores = (probs * (grad_probs - delta)).astype(BF16)
                 grad_side[here, lanes] = mm_nt(grad_scores, query).astype(BF16)
-                grad_side[here, key_lanes] = mm_nt(probs.astype(BF16), grad).astype(BF16)
+                grad_side[here, value_lanes] = mm_nt(probs.astype(BF16), grad).astype(BF16)
                 total = total + mm(flat[lanes, here], grad_scores)
         grad_queries_flat.append(total * SCORE_SCALE)
     grad_queries[...] = jnp.concatenate(grad_queries_flat, axis=0).T.astype(BF16)
 
 
-def attend_back(grad_rows, whole, own, own_parts, other_parts, attended_flat, log_total):
-    rows, group = (own.shape[0], own.shape[1] // 3)
-    keys = own_parts.shape[0]
+def attend_back(grad_rows, whole, queries, own, other, attended_flat, log_total):
+    rows, group = queries.shape
+    keys = own.shape[0]
     return whole_call(
         attend_back_kernel,
         (
@@ -322,9 +315,9 @@
         ),
         grad_rows,
         whole,
+        queries,
         own,
-        own_parts,
-        other_parts,
+        other,
         attended_flat,
         log_total,
         flops=20 * rows * keys * group,
@@ -332,17 +325,29 @@
     )
 
 
-def project_kernel(rows, whole, qkv):
-    qkv[...] = mm(rows[...], whole[:, : qkv.shape[1]]).astype(BF16)
-
-
-def project(rows, whole, width):
+def project_kernel(rows, whole, normed, queries, keys_values, small):
+    group = queries.shape[1]
+    small[...] = whole[:, 4 * group :].astype(F32).T
+    values = rows[...].astype(F32)
+    normed[...] = norm_rows(values, small[0:1, :])[1]
+    queries[...] = mm(normed[...], whole[:, :group]).astype(BF16)
+    keys_values[...] = mm(normed[...], whole[:, group : 3 * group]).astype(BF16)
+
+
+def project(rows, whole, group):
+    count, width = rows.shape
+    extra = whole.shape[1] - 4 * group
     return whole_call(
         project_kernel,
-        jax.ShapeDtypeStruct((rows.shape[0], width), BF16),
+        (
+            jax.ShapeDtypeStruct((count, width), BF16),
+            jax.ShapeDtypeStruct((count, group), BF16),
+            jax.ShapeDtypeStruct((count, 2 * group), BF16),
+            jax.ShapeDtypeStruct((extra, width), F32),
+        ),
         rows,
         whole,
-        flops=2 * rows.size * width,
+        flops=6 * rows.size * group,
     )
 
 
@@ -368,6 +373,68 @@
     )
 
 
+def gelu_parts(values):
+    scale, cubic = (0.7978845608028654, 0.044715)
+    square = values * values
+    bend = jnp.tanh(scale * values * (1.0 + cubic * square))
+    half = 0.5 * (1.0 + bend)
+    slope = half + 0.5 * values * (1.0 - bend * bend) * scale * (1.0 + 3.0 * cubic * square)
+    return values * half, slope
+
+
+ROW_BLOCK = 256
+
+
+def expert_kernel(
+    slots, grad_out, w_in, w_out, small, here, result, activated, grad_part, grad_pre, grad_rows
+):
+    experts = here.shape[1]
+    router = small[2 : 2 + experts, :].astype(BF16)
+    probs = jax.nn.softmax(mm_nt(slots[...], router), axis=-1)
+    gate = jnp.sum(probs * here[...], axis=-1, keepdims=True)
+    low, slope = gelu_parts(mm(slots[...], w_in[...]))
+    activated[...] = low.astype(BF16)
+    grad_part[...] = (gate * grad_out[...].astype(F32)).astype(BF16)
+    grad_pre[...] = (mm_nt(grad_part[...], w_out[...]) * slope).astype(BF16)
+    result[...] = mm(activated[...], w_out[...]).astype(BF16)
+    grad_gate = jnp.sum(
+        grad_out[...].astype(F32) * result[...].astype(F32), axis=-1, keepdims=True
+    )
+    grad_logits = gate * grad_gate * (here[...] - probs)
+    through_router = mm(grad_logits.astype(BF16), router)
+    grad_rows[...] = (mm_nt(grad_pre[...], w_in[...]) + through_router).astype(BF16)
+
+
+def expert_both(slots, grad_out, w_in, w_out, small, expert_count):
+    expert = (lax.axis_index("z") * lax.axis_size("q") + lax.axis_index("q")) * 2 + lax.axis_index("h")
+    here = (jnp.arange(expert_count, dtype=jnp.int32) == expert).astype(F32)[None]
+    rows = slots.reshape(-1, slots.shape[-1])
+    count, width = rows.shape
+    hidden = w_in.shape[1]
+    block = ROW_BLOCK if count % ROW_BLOCK == 0 else count
+
+    def rows_of(size):
+        return pl.BlockSpec((block, size), lambda step: (step, 0))
+
+    def whole_of(array):
+        return pl.BlockSpec(array.shape, lambda step: (0, 0))
+
+    sizes = (width, hidden, width, hidden, width)
+    result, activated, grad_part, grad_pre, grad_rows = pl.pallas_call(
+        expert_kernel,
+        grid=(count // block,),
+        in_specs=[rows_of(width), rows_of(width)] + [whole_of(a) for a in (w_in, w_out, small, here)],
+        out_specs=tuple(rows_of(size) for size in sizes),
+        out_shape=tuple(jax.ShapeDtypeStruct((count, size), BF16) for size in sizes),
+        compiler_params=pltpu.CompilerParams(vmem_limit_bytes=VMEM_BYTES),
+        cost_estimate=pl.CostEstimate(
+            flops=8 * count * width * hidden, bytes_accessed=16 * count * width, transcendentals=count * hidden
+        ),
+    )(rows, grad_out.reshape(rows.shape), w_in, w_out, small, here)
+    kept = (rows, grad_pre, activated, grad_part)
+    return kept, result.reshape(slots.shape), grad_rows.reshape(slots.shape)
+
+
 def weight_grads_kernel(rows, grad_rows, grad_qkv, attended, grads):
     grads[...] = jnp.concatenate(
         [mm_tn(rows[...], grad_qkv[...]), mm_tn(grad_rows[...], attended[...])], axis=1
@@ -387,41 +454,35 @@
     )
 
 
-def attention_forward(inputs, weights):
-    whole, gain_attn = weights[:2]
+def attention_forward(inputs, gathered, whole, group):
     values_in = inputs.astype(F32)
-    inverse_a, normed_a = norm_rows(values_in, gain_attn)
-    rows_a = lax.all_gather(normed_a, CHIPS, axis=0, tiled=True)
-    qkv = project(rows_a, whole, 3 * weights[2])
-    own_parts, other_parts = gather_parts(qkv)
-    part, attended, attended_flat, log_total = attend(qkv, own_parts, other_parts, whole)
+    rows_a, queries, keys_values, small = project(gathered, whole, group)
+    own, other = gather_parts(keys_values)
+    part, attended, attended_flat, log_total = attend(queries, own, other, whole)
     hidden = values_in + sum_chips(part)
-    kept = (
-        values_in, inverse_a, rows_a, qkv, own_parts, other_parts, attended, attended_flat, log_total
-    )
-    return hidden, kept
-
-
-def attention_backward(grad_hidden, kept, weights):
-    whole, gain_attn = weights[:2]
-    (
-        values_in, inverse_a, rows_a, qkv, own_parts, other_parts, attended, attended_flat, log_total
-    ) = kept
+    kept = (values_in, rows_a, queries, own, other, attended, attended_flat, log_total)
+    return hidden, small, kept
+
+
+def attention_backward(grad_hidden, small, kept, whole, last):
+    values_in, rows_a, queries, own, other, attended, attended_flat, log_total = kept
     grad_rows = lax.all_gather(grad_hidden.astype(BF16), CHIPS, axis=0, tiled=True)
     grad_queries, grad_own, grad_other = attend_back(
-        grad_rows, whole, qkv, own_parts, other_parts, attended_flat, log_total
+        grad_rows, whole, queries, own, other, attended_flat, log_total
     )
     grad_qkv, part = project_back(grad_queries, sum_parts(grad_own, grad_other), whole)
-    grad_normed_a = sum_chips(part)
-    grad_input_norm, grad_gain = norm_back(values_in, inverse_a, gain_attn, grad_normed_a)
     grads = weight_grads(rows_a, grad_rows, grad_qkv, attended)
-    return (grad_hidden + grad_input_norm).astype(BF16), (grad_gain, grads)
-
-
-def route_tokens(hidden, routes, weights, expert_count, most_rows):
-    gain_moe, w_router = weights[3:]
-    inverse_b, normed_b = norm_rows(hidden, gain_moe)
-    router_probs = jax.nn.softmax(mm(normed_b, w_router), axis=-1)
+    grad_normed_a = sum_chips(after(part, grads) if last else part)
+    sums = scatter_later(grads)
+    inverse = lax.rsqrt(jnp.mean(values_in * values_in, axis=-1, keepdims=True) + EPSILON)
+    grad_input_norm, grad_gain = norm_back(values_in, inverse, small[0:1], grad_normed_a)
+    return (grad_hidden + grad_input_norm).astype(BF16), grad_gain, sums
+
+
+def route_tokens(hidden, routes, small, expert_count):
+    inverse_b, normed_b = norm_rows(hidden, small[1:2])
+    router = small[2 : 2 + expert_count].astype(BF16)
+    router_probs = jax.nn.softmax(mm_nt(normed_b, router), axis=-1)
     chosen = (
         routes.reshape(-1, 1) == jnp.arange(expert_count, dtype=jnp.int32)[None]
     ).astype(F32)
@@ -458,19 +519,6 @@
     return (rows, grad_pre, activated, grad_part), grad_rows.astype(BF16).reshape(grad_slots.shape)
 
 
-def expert_gate(slots, grad_slots, result, w_router):
-    rows = slots.reshape(-1, slots.shape[-1])
-    grad_out = grad_slots.reshape(rows.shape).astype(F32)
-    expert = (lax.axis_index("z") * lax.axis_size("q") + lax.axis_index("q")) * 2 + lax.axis_index("h")
-    probs = jax.nn.softmax(mm(rows, w_router), axis=-1)
-    here = (jnp.arange(w_router.shape[1], dtype=jnp.int32) == expert).astype(F32)[None]
-    gate = jnp.sum(probs * here, axis=-1, keepdims=True)
-    grad_gate = jnp.sum(grad_out * result.reshape(rows.shape).astype(F32), axis=-1, keepdims=True)
-    grad_logits = gate * grad_gate * (here - probs)
-    through_router = mm_nt(grad_logits.astype(BF16), w_router)
-    return (gate * grad_out).astype(BF16).reshape(slots.shape), through_router
-
-
 def router_grads(grad_output, mixed, routed):
     inverse_b, normed_b, router_probs, chosen, gate = routed
     grad_gate = jnp.sum(grad_output * mixed, axis=-1, keepdims=True)
@@ -478,8 +526,8 @@
     return grad_logits, dot(grad_logits, normed_b.astype(F32), ((0,), (0,)), HIGHEST)
 
 
-def moe_norm_back(grad_output, grad_normed_b, hidden, routed, weights):
-    grad_hidden_norm, grad_gain = norm_back(hidden, routed[0], weights[3], grad_normed_b)
+def moe_norm_back(grad_output, grad_normed_b, hidden, routed, small):
+    grad_hidden_norm, grad_gain = norm_back(hidden, routed[0], small[1:2], grad_normed_b)
     return grad_output + grad_hidden_norm, grad_gain
 
 
@@ -518,104 +566,100 @@
     route_rows = jnp.pad(route_rows, ((0, 0), (0, 14), (0, feature_dim - half_rows)))
 
     input_rows = jnp.concatenate(
-        [block_input.reshape(sequences, half_rows, feature_dim), route_rows], axis=1
+        [
+            block_input.reshape(sequences, half_rows, feature_dim),
+            out_cotangent.reshape(sequences, half_rows, feature_dim),
+            route_rows,
+        ],
+        axis=1,
     )
     here = to_planes(input_rows)
+    cotangent = here[:, half_rows : 2 * half_rows].reshape(-1, feature_dim)
     inputs = here[:, :half_rows].reshape(-1, feature_dim)
     section_routes = [
-        here[:, half_rows + section, :half_rows].astype(jnp.int32) for section in range(2)
+        here[:, 2 * half_rows + section, :half_rows].astype(jnp.int32) for section in range(2)
     ]
 
     small = jnp.concatenate([attn_gain[0][:, None], moe_gain[0][:, None], router_weight[0]], axis=-1)
     small = jnp.pad(small, ((0, 0), (0, extra - small.shape[-1])))
-    spread = spread_weights(
-        query_weight[0], key_weight[0], value_weight[0], output_weight[0], small, here
+    spread, gathered = spread_weights(
+        query_weight[0], key_weight[0], value_weight[0], output_weight[0], small, inputs
     )
     group = query_weight.shape[-1] // 2
 
-    def parts_of(array):
-        return (
-            array,
-            array[:, 4 * group].astype(F32),
-            group,
-            array[:, 4 * group + 1].astype(F32),
-            array[:, 4 * group + 2 : 4 * group + 2 + expert_count],
-        )
-
-    whole = join_section(from_z(spread[:, 0]))
-    weights = [parts_of(whole), parts_of(gather_later(spread[:, 1]))]
+    first_whole = join_section(from_z(spread[:, 0]))
+    whole = [first_whole, gather_later(after(spread[:, 1], first_whole))]
     w_in, w_out = (expert_in[0, 0], expert_out[0, 0])
 
     tables = [dispatch_table(rows, expert_count, most_rows) for rows in section_routes]
-    cotangent = to_planes(out_cotangent.reshape(sequences, half_rows, feature_dim)).reshape(
-        -1, feature_dim
-    )
-    hidden, kept_attn = attention_forward(inputs, weights[0])
-    routed = route_tokens(hidden, section_routes[0], weights[0], expert_count, most_rows)
-    slots = to_experts((pack_rows(tables[0], routed[1]), pack_rows(tables[1], cotangent)))
+    hidden, first_small, kept_attn = attention_forward(inputs, gathered, whole[0], group)
+    routed = route_tokens(hidden, section_routes[0], first_small, expert_count)
+    packed, whole[1] = lax.optimization_barrier((pack_rows(tables[0], routed[1]), whole[1]))
+    slots = to_experts((packed, pack_rows(tables[1], cotangent)))
     cotangent_slots = slots
     kept_expert, result = expert_trip(slots, w_in, w_out)
     mixed = unpack_rows(tables[0], from_experts(result, (0,)))
     first_output = (hidden + routed[4] * mixed).astype(BF16)
-    first = (hidden, kept_attn, routed, kept_expert, mixed)
-
-    hidden, kept_attn = attention_forward(first_output, weights[1])
-    routed = route_tokens(hidden, section_routes[1], weights[1], expert_count, most_rows)
+    first = (hidden, first_small, kept_attn, routed, kept_expert, mixed)
+
+    gathered = lax.all_gather(first_output, CHIPS, axis=0, tiled=True)
+    hidden, small, kept_attn = attention_forward(first_output, gathered, whole[1], group)
+    routed = route_tokens(hidden, section_routes[1], small, expert_count)
     slots = to_experts((None, pack_rows(tables[1], routed[1])))
-    kept_expert, second_result = expert_trip(slots, w_in, w_out)
-    grad_slots, through_router = expert_gate(slots, cotangent_slots, second_result, weights[1][4])
-    part, grad_results = expert_trip_back(grad_slots, kept_expert, w_in, w_out, through_router)
+    part, second_result, grad_results = expert_both(
+        slots, cotangent_slots, w_in, w_out, small, expert_count
+    )
     expert_parts = [None, part]
     returned_grad = from_experts(grad_results, (1,))
     grad_output = cotangent.astype(F32)
 
-    def to_owners(first, second, small=None, chips=None):
-        first, second = (v.reshape(sequences // 2, 1, half_rows, feature_dim) for v in (first, second))
-        kept, sent = (jnp.where(pipe == 0, first, second), jnp.where(pipe == 0, second, first))
-        if small is not None:
-            kept_small = jnp.where(pipe == 0, small[0], small[1])
-            sent_small = jnp.where(pipe == 0, small[1], small[0]).astype(BF16)
-            sent = jnp.concatenate([sent.reshape(-1, feature_dim), sent_small], axis=0)
-        got = swapped(sent, "pipe")
-        if small is not None:
-            kept_small = kept_small + got[-kept_small.shape[0] :].astype(F32)
-            got = got[: -kept_small.shape[0]].reshape(first.shape)
-        both = jnp.where(
-            pipe == 0, jnp.concatenate([kept, got], axis=1), jnp.concatenate([got, kept], axis=1)
-        ).reshape(sequences, half_rows, feature_dim)
-        if small is None:
-            home = exchanged_z(both)
-        else:
-            count, planes = (kept_small.shape[0], lax.axis_size("z"))
-            by_plane = kept_small.astype(BF16).reshape(count, planes, -1).transpose(1, 0, 2)
-            by_plane = jnp.pad(by_plane, ((0, 0), (0, 0), (0, feature_dim - by_plane.shape[-1])))
-            both = jnp.concatenate([both, by_plane], axis=1)
-            chips = chips(both)
-            moved = exchanged_z(both)
-            home = moved[:, :half_rows]
-            sums = jnp.sum(moved[:, half_rows:, : feature_dim // planes].astype(F32), axis=0)
-            rest = lax.axis_size("q") * lax.axis_size("h") * lax.axis_size("tp")
-            by_rest = sums.astype(BF16).reshape(count, rest, -1).transpose(1, 0, 2)
-            small = jnp.sum(exchanged(after(by_rest, chips), ("q", "h", "tp")).astype(F32), axis=0)
-        return home.reshape(1, micro_count, seq_count, half_rows, feature_dim), small, chips
+    def by_pipe(first, second):
+        return jnp.where(pipe == 0, first, second), jnp.where(pipe == 0, second, first)
+
+    def paired(kept, got):
+        return jnp.stack(by_pipe(kept, got), axis=1).reshape(sequences, -1, feature_dim)
+
+    def to_owners(outputs, grads, small, sums):
+        kept, sent = by_pipe(*grads)
+        kept_small, sent_small = by_pipe(*small)
+        count = kept_small.shape[0]
+        got = swapped(jnp.concatenate([sent, sent_small.astype(BF16)], axis=0), "pipe")
+        kept_small = kept_small + got[-count:].astype(F32)
+        shape = (sequences // 2, half_rows, feature_dim)
+        planes = lax.axis_size("z")
+        by_plane = kept_small.astype(BF16).reshape(count, planes, -1).transpose(1, 0, 2)
+        by_plane = jnp.pad(by_plane, ((0, 0), (0, 0), (0, feature_dim - by_plane.shape[-1])))
+        both = jnp.concatenate(
+            [outputs, paired(kept.reshape(shape), got[:-count].reshape(shape)), by_plane], axis=1
+        )
+        both, *sums = lax.optimization_barrier((both, *sums))
+        chips = scatter_chips(sums)
+        moved = exchanged_z(both)
+        total = jnp.sum(moved[:, -count:, : feature_dim // planes].astype(F32), axis=0)
+        rest = lax.axis_size("q") * lax.axis_size("h") * lax.axis_size("tp")
+        by_rest = total.astype(BF16).reshape(count, rest, -1).transpose(1, 0, 2)
+        small = jnp.sum(exchanged(after(by_rest, chips), ("q", "h", "tp")).astype(F32), axis=0)
+        return moved, small, chips
 
     def small_rows(grad_gain_attn, grad_gain_moe, grad_router):
         stacked = jnp.concatenate([grad_gain_attn[None], grad_gain_moe[None], grad_router], axis=0)
         return jnp.pad(stacked, ((0, -stacked.shape[0] % 16), (0, 0)))
 
     grad_hidden, grad_gain_moe = moe_norm_back(
-        grad_output, unpack_rows(tables[1], returned_grad), hidden, routed, weights[1]
-    )
-    second_grad, (grad_gain_attn, grads) = attention_backward(grad_hidden, kept_attn, weights[1])
-    sums_second = scatter_later(grads)
+        grad_output, unpack_rows(tables[1], returned_grad), hidden, routed, small
+    )
+    second_grad, grad_gain_attn, sums_second = attention_backward(
+        grad_hidden, small, kept_attn, whole[1], False
+    )
     second = (hidden, routed, grad_output, grad_gain_attn, grad_gain_moe)
 
-    hidden, kept_attn, routed, kept_expert, mixed = first
+    hidden, small, kept_attn, routed, kept_expert, mixed = first
     grad_output = second_grad.astype(F32)
     grad_slots = to_experts((pack_rows(tables[0], (routed[4] * grad_output).astype(BF16)), None))
     expert_parts[0], grad_results = expert_trip_back(grad_slots, kept_expert, w_in, w_out)
     grad_logits, grad_router = router_grads(grad_output, mixed, routed)
-    grad_normed_router = mm_nt(grad_logits.astype(BF16), weights[0][4])
+    router = small[2 : 2 + expert_count].astype(BF16)
+    grad_normed_router = mm(grad_logits.astype(BF16), router)
     slots, grad_pre, activated, grad_part = (
         jnp.where(pipe == 0, low, high) for low, high in zip(*expert_parts)
     )
@@ -628,24 +672,31 @@
         grad_normed_router + unpack_rows(tables[0], returned[:, :count]),
         hidden,
         routed,
-        weights[0],
+        small,
     )
     hidden, routed, grad_output, *gains = second
     mixed = unpack_rows(tables[1], returned[:, count:])
     second_output = (hidden + routed[4] * mixed).astype(BF16)
     small_second = small_rows(*gains, router_grads(grad_output, mixed, routed)[1])
-    layer_outputs = to_owners(first_output, second_output)[0]
+    shape = (sequences // 2, half_rows, feature_dim)
+    kept_output, sent_output = by_pipe(first_output, second_output)
+    outputs = paired(kept_output.reshape(shape), swapped(sent_output, "pipe").reshape(shape))
     grad_hidden, grad_w_in, grad_w_out = lax.optimization_barrier(
         (grad_hidden, grad_w_in, grad_w_out)
     )
-    first_grad, (grad_gain_attn, grads) = attention_backward(grad_hidden, kept_attn, weights[0])
+    first_grad, grad_gain_attn, sums_first = attention_backward(
+        grad_hidden, small, kept_attn, whole[0], True
+    )
     small_first = small_rows(grad_gain_attn, grad_gain_moe, grad_router)
-    sums_first = scatter_start(grads)
-    grads_home, small, by_chip = to_owners(
-        first_grad,
-        second_grad,
+    home, small, by_chip = to_owners(
+        outputs,
+        (first_grad, second_grad),
         (small_first, small_second),
-        lambda first: scatter_chips([after(sums_first, first), sums_second]),
+        (sums_first, sums_second),
+    )
+    layer_outputs, grads_home = (
+        home[:, begin : begin + half_rows].reshape(1, micro_count, seq_count, half_rows, feature_dim)
+        for begin in (0, half_rows)
     )
     mats = scatter_end(by_chip)
     return (

time: 576 us -> 532 us (0.924)
  local copies, waits for them, and re-layouts: 65.7 us -> 35.6 us
  waiting for transfers between devices: 119 us -> 149 us
  starting transfers between devices: 89.1 us -> 64.5 us
  matrix products: 63.6 us -> 42.2 us
  Pallas kernels: 21.8 us -> 40.3 us
  other arithmetic: 45.1 us -> 33.1 us
    dot_general x25 -> x19, matrix products: 63.3 us -> 41.9 us  [dot(): lax.dot_general(left, right, (contract, ((), ())), precision=precision, p...]
    pallas_call x0 -> x1, Pallas kernels: none -> 16.8 us  [expert_both(): pl.pallas_call(expert_kernel, grid=(count // block,), in_specs=[rows_of(w...]
    reduce_scatter x1 -> x2, waiting for transfers between devices: 0.02 us -> 16.4 us  [scatter_later(): lax.psum_scatter(split.reshape(-1, width), ('z', 'q', 'tp'), scatter_dime...]
    gather x12 -> x0, local copies, waits for them, and re-layouts: 12.4 us -> none  [the longest x6 7.09 us: xor_z(): return jnp.where(z & 2 == 2, values[jnp.array([2, 3, 0, 1])], values)]
    ppermute x6 -> x3, starting transfers between devices: 21.5 us -> 9.29 us  [to_planes(): got.append(lax.ppermute(mine[k], ('pipe', 'z'), pairs))]
    all_to_all x7, blocking collectives: 94.2 us -> 106 us  [exchanged(): return lax.all_to_all(values, axes, split_axis=0, concat_axis=0, tiled=True)]
    all_gather x2 -> x1, blocking collectives: 25 us -> 13 us  [shards(): gathered = lax.all_gather(first_output, CHIPS, axis=0, tiled=True)]
    all_to_all x10 -> x9, waiting for transfers between devices: 41.5 us -> 52.1 us  [exchanged(): return lax.all_to_all(values, axes, split_axis=0, concat_axis=0, tiled=True)]
  transfers between devices with their start and end apart: 48 -> 41, of which waited for: 27 -> 30; matrix products, arithmetic and copies ran while one was open for 16% -> 10% of each run, Pallas kernels for 1% -> 3%
where the time goes in v4:
time: 532 us; the launch traced here: 523 us
  waiting for transfers between devices  149 us (28%)
  blocking collectives  142 us (27%)
  starting transfers between devices  64.5 us (12%)
  matrix products  42.2 us (8%)
  Pallas kernels  40.3 us (8%)
  local copies, waits for them, and re-layouts  35.6 us (7%)
  other arithmetic  33.1 us (6%)
  between operations  16.3 us (3%)
    all_to_all x7, blocking collectives, exchanged(): return lax.all_to_all(values, axes, split_axis=0, concat_axis=0, tiled=True)  106 us
    all_to_all x9, waiting for transfers between devices, exchanged(): return lax.all_to_all(values, axes, split_axis=0, concat_axis=0, tiled=True)  52.1 us
    dot_general x19, matrix products, dot(): lax.dot_general(left, right, (contract, ((), ())), precision=precision, p...  41.9 us
    all_to_all x9, starting transfers between devices, exchanged(): return lax.all_to_all(values, axes, split_axis=0, concat_axis=0, tiled=True)  35.4 us
    ppermute x19, waiting for transfers between devices, swapped(): return lax.ppermute(values, axis, SWAP)  32.9 us
    pallas_call x10, Pallas kernels, whole_call(): pl.pallas_call(kernel, out_shape=out_shape, compiler_params=pltpu.Compile...  23.5 us
    all_gather x2, blocking collectives, attention_backward(): lax.all_gather(grad_hidden.astype(BF16), CHIPS, axis=0, tiled=True)  23 us
    pallas_call x1, Pallas kernels, expert_both(): pl.pallas_call(expert_kernel, grid=(count // block,), in_specs=[rows_of(w...  16.8 us
  transfers between devices with their start and end apart: 41, of which 30 were waited for; matrix products, arithmetic and copies ran while one was open for 10% of the time, Pallas kernels for 3%

profile of v4, /device:TPU:0, one launch (start us, length us, event | category | flops | bytes accessed | tf_op | source)
XLA Modules:
  0.0 523.2 jit_solution(4796930074995999416)
XLA Ops:
  8.0 3.0 collective-permute-start
  17.5 3.5 all-to-all-start
  21.3 3.5 collective-permute-start.1
  25.3 4.5 collective-permute-start.2
  31.2 5.2 collective-permute-done.2
  36.4 3.2 collective-permute-done.3
  40.1 21.8 %all_to_all.80 = bf16[4,176,896]{2,1,0:T(8,128)(2,1)S(1)} all-to-all(bf16[4,176,896]{2,1,0:T(8,128)(2,1)S(1)} %pad_maximum_fusion.1), channel_id=1, replica_groups=mesh['pipe'=2,'z'=4,'q'=1,'h'=2,'tp'=2] {'h','pipe'}, dimensions={0} | all-to-all | bytes 2523136 | tf_op jit(solution)/shard_map/all_to_all | solution.py:44
  62.6 18.7 %all_to_all.81 = bf16[4,2,48,896]{3,2,1,0:T(8,128)(2,1)S(1)} all-to-all(bf16[4,2,48,896]{3,2,1,0:T(8,128)(2,1)S(1)} %broadcast_in_dim.27), channel_id=1, replica_groups=mesh['pipe'=2,'z'=4,'q'=1,'h'=2,'tp'=2] {'z','q'}, dimensions={0} | all-to-all | bytes 1376256 | tf_op jit(solution)/shard_map/all_to_all | solution.py:44
  81.4 2.1 collective-permute-done.4
  87.6 3.9 shard_map.204
  93.1 4.3 all-to-all-start.3
  99.2 9.7 %all-to-all-done.3 = bf16[4,128,768]{2,1,0:T(8,128)(2,1)} async-done(((bf16[4,128,768]{2,1,0:T(8,128)(2,1)}), bf16[4,128,768]{2,1,0:T(8,128)(2,1)}, u32[]{:S(2)}, u32[]{:S(2)}) %all-to-all-start.3) | async-done | bytes 786464 | tf_op jit(solution)/shard_map/all_to_all | solution.py:44
  116.4 20.7 %all_to_all.82 = bf16[8,48,768]{2,1,0:T(8,128)(2,1)S(1)} all-to-all(bf16[8,48,768]{2,1,0:T(8,128)(2,1)S(1)} %pad_maximum_fusion.6), channel_id=1, replica_groups=mesh['pipe'=2,'z'=4,'q'=1,'h'=2,'tp'=2] {'z','q','h'}, dimensions={0} | all-to-all | bytes 1179648 | tf_op jit(solution)/shard_map/all_to_all | solution.py:44
  137.5 7.1 %collective-permute-done.7 = bf16[8,24,768]{2,1,0:T(8,128)(2,1)S(1)} collective-permute-done((bf16[8,24,768]{2,1,0:T(8,128)(2,1)S(1)}, bf16[8,24,768]{2,1,0:T(8,128)(2,1)S(1)}, u32[]{:S(2)}, u32[]{:S(2)}) %collective-permute-start.7) | collective-permute-done | bytes 294944 | tf_op jit(solution)/shard_map/ppermute | solution.py:40
  147.5 2.0 fusion.104
  149.5 2.9 convolution_convert_fusion.1
  154.5 2.3 collective-permute-start.10
  156.9 6.5 %collective-permute-done.10 = bf16[8,24,768]{2,1,0:T(8,128)(2,1)S(1)} collective-permute-done((bf16[8,24,768]{2,1,0:T(8,128)(2,1)S(1)}, bf16[8,24,768]{2,1,0:T(8,128)(2,1)S(1)}, u32[]{:S(2)}, u32[]{:S(2)}) %collective-permute-start.10) | collective-permute-done | bytes 294944 | tf_op jit(solution)/shard_map/ppermute | solution.py:215
  164.2 4.1 all-to-all-start.5
  170.7 6.9 %all-to-all-done.5 = bf16[8,24,768]{2,1,0:T(8,128)(2,1)} async-done(((bf16[8,24,768]{2,1,0:T(8,128)(2,1)}), bf16[8,24,768]{2,1,0:T(8,128)(2,1)}, u32[]{:S(2)}, u32[]{:S(2)}) %all-to-all-start.5) | async-done | bytes 294944 | tf_op jit(solution)/shard_map/all_to_all | solution.py:44
  177.6 2.6 fusion.48
  180.9 13.0 %all_gather.17.rows = bf16[512,768]{1,0:T(8,128)(2,1)S(1)} all-gather(bf16[128,768]{1,0:T(8,128)(2,1)S(1)} %get-tuple-element.121), channel_id=1, replica_groups=mesh['pipe'=2,'z'=4,'q'=1,'h'=2,'tp'=2] {'h','pipe'}, dimensions={0}, use_global_device_ids=true | all-gather | bytes 983040 | tf_op jit(solution)/shard_map/all_gather | solution.py:605
  197.6 3.9 shard_map.206
  203.7 4.2 all-to-all-start.6
  208.5 10.9 %all-to-all-done.6 = bf16[4,128,768]{2,1,0:T(8,128)(2,1)} async-done(((bf16[4,128,768]{2,1,0:T(8,128)(2,1)}), bf16[4,128,768]{2,1,0:T(8,128)(2,1)}, u32[]{:S(2)}, u32[]{:S(2)}) %all-to-all-start.6) | async-done | bytes 786464 | tf_op jit(solution)/shard_map/all_to_all | solution.py:44
  224.7 13.7 %all_to_all.83 = bf16[8,24,768]{2,1,0:T(8,128)(2,1)} all-to-all(bf16[8,24,768]{2,1,0:T(8,128)(2,1)S(1)} %bitcast.314), channel_id=1, replica_groups=mesh['pipe'=2,'z'=4,'q'=1,'h'=2,'tp'=2] {'z','q','h'}, dimensions={0} | all-to-all | bytes 589824 | tf_op jit(solution)/shard_map/all_to_all | solution.py:44
  238.4 3.7 collective-permute-start.13
  242.2 3.6 collective-permute-done.13
  245.8 1.9 collective-permute-done.14
  249.1 16.8 %shard_map.207 = (bf16[768,768]{1,0:T(8,128)(2,1)S(1)}, bf16[768,1536]{1,0:T(8,128)(2,1)}, bf16[768,768]{1,0:T(8,128)(2,1)S(1)}, bf16[768,1536]{1,0:T(8,128)(2,1)}, bf16[768,768]{1,0:T(8,128)(2,1)S(1)}) custom-call(bf16[768,768]{1,0:T(8,128)(2,1)S(1)} %bitcast.281, bf16[768,768]{1,0:T(8,128)(2,1)} %bitcast.294, bf16[768,1536]{1,0:T(8,128)(2,1)} %bitcast.348, ...), custom_call_target="tpu_custom_call" | custom-call | flops 7247757312 | bytes 9437184 | tf_op jit(solution)/shard_map/pallas_call | solution.py:423
  272.3 10.1 %collective-permute-done.16 = bf16[8,24,768]{2,1,0:T(8,128)(2,1)} collective-permute-done((bf16[8,24,768]{2,1,0:T(8,128)(2,1)}, bf16[8,24,768]{2,1,0:T(8,128)(2,1)}, u32[]{:S(2)}, u32[]{:S(2)}) %collective-permute-start.16) | collective-permute-done | bytes 294944 | tf_op jit(solution)/shard_map/ppermute | solution.py:215
  283.7 14.4 %all_to_all.84 = bf16[8,24,768]{2,1,0:T(8,128)(2,1)S(1)} all-to-all(bf16[8,24,768]{2,1,0:T(8,128)(2,1)S(1)} %fusion.57), channel_id=1, replica_groups=mesh['pipe'=2,'z'=4,'q'=1,'h'=2,'tp'=2] {'z','q','h'}, dimensions={0} | all-to-all | bytes 589824 | tf_op jit(solution)/shard_map/all_to_all | solution.py:44
  299.8 11.3 %all_gather.18.grad_rows = bf16[512,768]{1,0:T(8,128)(2,1)S(1)} all-gather(bf16[128,768]{1,0:T(8,128)(2,1)S(1)} %get-tuple-element.122), channel_id=1, replica_groups=mesh['pipe'=2,'z'=4,'q'=1,'h'=2,'tp'=2] {'h','pipe'}, dimensions={0}, use_global_device_ids=true | all-gather | bytes 983040 | tf_op jit(solution)/shard_map/all_gather | solution.py:469
  311.2 4.5 shard_map.208
  320.1 4.3 all-to-all-start.9
  325.2 10.7 %all-to-all-done.9 = bf16[4,128,768]{2,1,0:T(8,128)(2,1)} async-done(((bf16[4,128,768]{2,1,0:T(8,128)(2,1)}), bf16[4,128,768]{2,1,0:T(8,128)(2,1)}, u32[]{:S(2)}, u32[]{:S(2)}) %all-to-all-start.9) | async-done | bytes 786464 | tf_op jit(solution)/shard_map/all_to_all | solution.py:44
  337.9 1.9 fusion.41
  340.1 13.0 %all_to_all.85 = bf16[8,24,768]{2,1,0:T(8,128)(2,1)S(1)} all-to-all(bf16[8,24,768]{2,1,0:T(8,128)(2,1)S(1)} %bitcast.315), channel_id=1, replica_groups=mesh['pipe'=2,'z'=4,'q'=1,'h'=2,'tp'=2] {'z','q','h'}, dimensions={0} | all-to-all | bytes 589824 | tf_op jit(solution)/shard_map/all_to_all | solution.py:44
  354.7 7.2 %collective-permute-done.19 = bf16[8,24,768]{2,1,0:T(8,128)(2,1)S(1)} collective-permute-done((bf16[8,24,768]{2,1,0:T(8,128)(2,1)S(1)}, bf16[8,24,768]{2,1,0:T(8,128)(2,1)S(1)}, u32[]{:S(2)}, u32[]{:S(2)}) %collective-permute-start.19) | collective-permute-done | bytes 294944 | tf_op jit(solution)/shard_map/ppermute | solution.py:192
  363.7 6.5 %fusion.6 = bf16[768,1536]{1,0:T(8,128)(2,1)S(1)} fusion(f32[768,1536]{1,0:T(8,128)} %copy-done.136, bf16[768,768]{1,0:T(8,128)(2,1)S(1)} %bitcast.309, bf16[1,1,1536,768]{3,2,1,0:T(8,128)(2,1)S(1)} %copy-done.133), kind=kOutput, calls=%fused_computation.8 | convolution fusion | flops 1835532288 | bytes 10616832 | tf_op jit(solution)/shard_map/dot_general | solution.py:22
  370.2 2.0 fusion.15
  376.5 2.2 fusion.30
  378.7 2.1 fusion.119
  383.2 1.9 fusion.77
  385.1 2.9 collective-permute-done.22
  388.1 2.1 maximum_select_fusion
  390.1 4.6 all-to-all-start.11
  394.8 8.3 %fusion.7 = f32[1536,768]{1,0:T(8,128)} fusion(bf16[768,1536]{1,0:T(8,128)(2,1)} %get-tuple-element.73, pred[]{:T(512)S(6)} %eq.63, bf16[768,768]{1,0:T(8,128)(2,1)} %bitcast.310, bf16[768,768]{1,0:T(8,128)(2,1)S(1)} %copy-done.37, f32[768,1536]{1,0:T(8,128)} %copy-done.136), kind=kOutput, calls=%fused_computation.10 | convolution fusion | flops 1824325632 | bytes 14155777 | tf_op jit(solution)/shard_map/dot_general | solution.py:22
  403.2 4.2 fusion.9
  407.4 9.1 %all-to-all-done.11 = bf16[8,48,768]{2,1,0:T(8,128)(2,1)S(1)} async-done(((bf16[8,48,768]{2,1,0:T(8,128)(2,1)}), bf16[8,48,768]{2,1,0:T(8,128)(2,1)S(1)}, u32[]{:S(2)}, u32[]{:S(2)}) %all-to-all-start.11) | async-done | bytes 589856 | tf_op jit(solution)/shard_map/all_to_all | solution.py:44
  418.5 11.7 %all_gather.19.grad_rows = bf16[512,768]{1,0:T(8,128)(2,1)S(1)} all-gather(bf16[128,768]{1,0:T(8,128)(2,1)S(1)} %convert_element_type.365), channel_id=1, replica_groups=mesh['pipe'=2,'z'=4,'q'=1,'h'=2,'tp'=2] {'h','pipe'}, dimensions={0}, use_global_device_ids=true | all-gather | bytes 983040 | tf_op jit(solution)/shard_map/all_gather | solution.py:469
  430.3 4.5 shard_map.210
  439.4 3.5 all-to-all-start.12
  443.0 2.5 fusion.39
  448.0 2.0 collective-permute-start.23
  450.2 4.8 all-to-all-done.12
  459.1 4.2 collective-permute-done.25
  463.7 16.3 %reduce-scatter.3.cloned.1.call-done = bf16[96,768]{1,0:T(8,128)(2,1)} async-done(((bf16[768,768]{1,0:T(8,128)(2,1)}), bf16[96,768]{1,0:T(8,128)(2,1)}) %reduce-scatter.3.cloned.1.call-update) | async-done | bytes 147472 | tf_op jit(solution)/shard_map/reduce_scatter | solution.py:154
  480.3 3.4 collective-permute-start.27
  485.4 3.6 all-to-all-start.13
  489.1 3.3 collective-permute-done.28
  492.4 8.4 %collective-permute-done.27 = bf16[144,768]{1,0:T(8,128)(2,1)S(1)} collective-permute-done((bf16[144,768]{1,0:T(8,128)(2,1)S(1)}, bf16[144,768]{1,0:T(8,128)(2,1)S(1)}, u32[]{:S(2)}, u32[]{:S(2)}) %collective-permute-start.27) | collective-permute-done | bytes 221216 | tf_op jit(solution)/shard_map/ppermute | solution.py:88
  502.2 4.0 all_to_all.86
  506.2 3.2 all-to-all-start.14
  (474 shorter events, 97.8 us)
Async XLA Ops:
  8.0 13.0 %collective-permute-start = (bf16[4,64]{1,0:T(4,128)(2,1)S(1)}, bf16[4,64]{1,0:T(4,128)(2,1)S(1)}, u32[]{:S(2)}, u32[]{:S(2)}) collective-permute-start(bf16[4,64]{1,0:T(4,128)(2,1)S(1)} %dynamic-slice_convert_fusion), channel_id=1, source_target_pairs={{0,16},{16,0},{1,17},{17,1},{2,18},{18,2},{3,19},{19,3},{4,20},{20... | collective-permute-start | bytes 1544 | tf_op jit(solution)/shard_map/ppermute | solution.py:40
  17.5 7.5 %all-to-all-start = ((bf16[2,2,48,4,192]{4,3,2,1,0:T(4,128)(2,1)}), bf16[2,2,48,4,192]{4,3,2,1,0:T(4,128)(2,1)S(1)}, u32[]{:S(2)}, u32[]{:S(2)}) async-start(bf16[2,2,48,4,192]{4,3,2,1,0:T(4,128)(2,1)} %maximum_bitcast_fusion), calls=%async_computation | async-start | bytes 786432 | tf_op jit(solution)/shard_map/all_to_all | solution.py:44
  21.0 92.9 %all-gather.3.cloned.1.call-start = ((), (), s32[]{:S(2)}) async-start(), calls=%async_computation.20 | async-start | bytes 1548288 | tf_op jit(solution)/shard_map/all_gather | solution.py:143
  21.3 9.9 %collective-permute-start.1 = (bf16[144,768]{1,0:T(8,128)(2,1)S(1)}, bf16[144,768]{1,0:T(8,128)(2,1)S(1)}, u32[]{:S(2)}, u32[]{:S(2)}) collective-permute-start(bf16[144,768]{1,0:T(8,128)(2,1)S(1)} %get-tuple-element.141), channel_id=1, source_target_pairs={{0,4},{8,12},{20,16},{28,24},{1,5},{9,13},{21,17},{29,25},{2,6},{1... | collective-permute-start | bytes 663560 | tf_op jit(solution)/shard_map/ppermute | solution.py:98
  25.3 11.1 %collective-permute-start.2 = (bf16[144,768]{1,0:T(8,128)(2,1)S(1)}, bf16[144,768]{1,0:T(8,128)(2,1)S(1)}, u32[]{:S(2)}, u32[]{:S(2)}) collective-permute-start(bf16[144,768]{1,0:T(8,128)(2,1)S(1)} %get-tuple-element.142), channel_id=1, source_target_pairs={{0,8},{8,0},{20,28},{28,20},{1,9},{9,1},{21,29},{29,21},{2,10},{10... | collective-permute-start | bytes 663560 | tf_op jit(solution)/shard_map/ppermute | solution.py:98
  29.8 9.7 %collective-permute-start.3 = (bf16[144,768]{1,0:T(8,128)(2,1)S(1)}, bf16[144,768]{1,0:T(8,128)(2,1)S(1)}, u32[]{:S(2)}, u32[]{:S(2)}) collective-permute-start(bf16[144,768]{1,0:T(8,128)(2,1)S(1)} %get-tuple-element.143), channel_id=1, source_target_pairs={{0,12},{8,4},{20,24},{28,16},{1,13},{9,5},{21,25},{29,17},{2,14},{... | collective-permute-start | bytes 663560 | tf_op jit(solution)/shard_map/ppermute | solution.py:98
  39.7 44.2 %copy-start.52 = (bf16[2,144,768]{2,1,0:T(8,128)(2,1)}, bf16[2,144,768]{2,1,0:T(8,128)(2,1)S(1)}, u32[]{:S(2)}) copy-start(bf16[2,144,768]{2,1,0:T(8,128)(2,1)S(1)} %maximum_select_fusion.1) | copy-start | bytes 1327108
  39.7 22.1 %copy-start.42 = (bf16[2,64,768]{2,1,0:T(8,128)(2,1)}, bf16[2,64,768]{2,1,0:T(8,128)(2,1)S(1)}, u32[]{:S(2)}) copy-start(bf16[2,64,768]{2,1,0:T(8,128)(2,1)S(1)} %get-tuple-element.158) | copy-start | bytes 589828
  39.7 57.9 %copy-start.53 = (bf16[2,64,768]{2,1,0:T(8,128)(2,1)}, bf16[2,64,768]{2,1,0:T(8,128)(2,1)S(1)}, u32[]{:S(2)}) copy-start(bf16[2,64,768]{2,1,0:T(8,128)(2,1)S(1)} %get-tuple-element.159) | copy-start | bytes 589828
  81.4 2.1 collective-permute-start.4
  85.9 82.4 %copy-start.14 = (f32[128,768]{1,0:T(8,128)}, f32[128,768]{1,0:T(8,128)S(1)}, u32[]{:S(2)}) copy-start(f32[128,768]{1,0:T(8,128)S(1)} %get-tuple-element.56) | copy-start | bytes 1179652
  85.9 1.7 collective-permute-start.5
  93.1 19.0 %copy-start.43 = (bf16[2,64,768]{2,1,0:T(8,128)(2,1)S(1)}, bf16[2,64,768]{2,1,0:T(8,128)(2,1)}, u32[]{:S(2)}) copy-start(bf16[2,64,768]{2,1,0:T(8,128)(2,1)} %copy-done.42) | copy-start | bytes 589828
  93.1 15.8 %all-to-all-start.3 = ((bf16[4,128,768]{2,1,0:T(8,128)(2,1)}), bf16[4,128,768]{2,1,0:T(8,128)(2,1)}, u32[]{:S(2)}, u32[]{:S(2)}) async-start(bf16[4,128,768]{2,1,0:T(8,128)(2,1)} %bitcast.25), calls=%async_computation.3 | async-start | bytes 1572864 | tf_op jit(solution)/shard_map/all_to_all | solution.py:44
  110.2 67.5 %copy-start.38 = (f32[128,768]{1,0:T(8,128)}, f32[128,768]{1,0:T(8,128)S(1)}, u32[]{:S(2)}) copy-start(f32[128,768]{1,0:T(8,128)S(1)} %convert_reduce_fusion.3) | copy-start | bytes 1179652
  116.4 31.1 %copy-start.134 = (bf16[1,1,768,1536]{3,2,1,0:T(8,128)(2,1)S(1)}, bf16[1,1,768,1536]{3,2,1,0:T(8,128)(2,1)}, u32[]{:S(2)}) copy-start(bf16[1,1,768,1536]{3,2,1,0:T(8,128)(2,1)} %param.22) | copy-start | bytes 7077892
  137.1 7.6 %collective-permute-start.7 = (bf16[8,24,768]{2,1,0:T(8,128)(2,1)S(1)}, bf16[8,24,768]{2,1,0:T(8,128)(2,1)S(1)}, u32[]{:S(2)}, u32[]{:S(2)}) collective-permute-start(bf16[8,24,768]{2,1,0:T(8,128)(2,1)S(1)} %get-tuple-element.155), channel_id=1, source_target_pairs={{0,16},{16,0},{1,17},{17,1},{2,18},{18,2},{3,19},{19,3},{4,20},{20... | collective-permute-start | bytes 884744 | tf_op jit(solution)/shard_map/ppermute | solution.py:40
  137.5 7.2 %collective-permute-start.6 = (bf16[8,24,768]{2,1,0:T(8,128)(2,1)S(1)}, bf16[8,24,768]{2,1,0:T(8,128)(2,1)S(1)}, u32[]{:S(2)}, u32[]{:S(2)}) collective-permute-start(bf16[8,24,768]{2,1,0:T(8,128)(2,1)S(1)} %get-tuple-element.154), channel_id=1, source_target_pairs={{0,1},{1,0},{2,3},{3,2},{4,5},{5,4},{6,7},{7,6},{8,9},{9,8},{10,11... | collective-permute-start | bytes 884744 | tf_op jit(solution)/shard_map/ppermute | solution.py:40
  144.7 1.6 collective-permute-start.8
  152.4 2.1 collective-permute-start.9
  154.5 8.8 %collective-permute-start.10 = (bf16[8,24,768]{2,1,0:T(8,128)(2,1)S(1)}, bf16[8,24,768]{2,1,0:T(8,128)(2,1)S(1)}, u32[]{:S(2)}, u32[]{:S(2)}) collective-permute-start(bf16[8,24,768]{2,1,0:T(8,128)(2,1)S(1)} %fusion.33), channel_id=1, source_target_pairs={{0,16},{1,17},{2,18},{3,19},{4,20},{5,21},{6,22},{7,23},{8,24},{9,... | collective-permute-start | bytes 884744 | tf_op jit(solution)/shard_map/ppermute | solution.py:215
  164.2 13.4 %all-to-all-start.5 = ((bf16[8,24,768]{2,1,0:T(8,128)(2,1)}), bf16[8,24,768]{2,1,0:T(8,128)(2,1)}, u32[]{:S(2)}, u32[]{:S(2)}) async-start(bf16[8,24,768]{2,1,0:T(8,128)(2,1)} %fusion.56), calls=%async_computation.5 | async-start | bytes 589824 | tf_op jit(solution)/shard_map/all_to_all | solution.py:44
  195.9 53.2 %copy-start.15 = (f32[128,768]{1,0:T(8,128)}, f32[128,768]{1,0:T(8,128)S(1)}, u32[]{:S(2)}) copy-start(f32[128,768]{1,0:T(8,128)S(1)} %get-tuple-element.63.small) | copy-start | bytes 1179652
  195.9 1.7 collective-permute-start.11
  203.7 15.7 %all-to-all-start.6 = ((bf16[4,128,768]{2,1,0:T(8,128)(2,1)}), bf16[4,128,768]{2,1,0:T(8,128)(2,1)}, u32[]{:S(2)}, u32[]{:S(2)}) async-start(bf16[4,128,768]{2,1,0:T(8,128)(2,1)} %bitcast.53), calls=%async_computation.6 | async-start | bytes 1572864 | tf_op jit(solution)/shard_map/all_to_all | solution.py:44
  221.7 77.2 %copy-start.40 = (f32[128,768]{1,0:T(8,128)}, f32[128,768]{1,0:T(8,128)S(1)}, u32[]{:S(2)}) copy-start(f32[128,768]{1,0:T(8,128)S(1)} %get-tuple-element.125) | copy-start | bytes 1179652
  238.4 7.4 %collective-permute-start.13 = (bf16[8,24,768]{2,1,0:T(8,128)(2,1)}, bf16[8,24,768]{2,1,0:T(8,128)(2,1)}, u32[]{:S(2)}, u32[]{:S(2)}) collective-permute-start(bf16[8,24,768]{2,1,0:T(8,128)(2,1)} %all_to_all.83), channel_id=1, source_target_pairs={{0,16},{1,17},{2,18},{3,19},{4,20},{5,21},{6,22},{7,23},{8,24},{9,... | collective-permute-start | bytes 884744 | tf_op jit(solution)/shard_map/ppermute | solution.py:194
  242.1 3.7 collective-permute-start.12
  245.8 1.9 collective-permute-start.14
  267.9 30.1 %copy-start.79 = (f32[768]{0:T(1024)S(1)}, f32[768]{0:T(1024)}, u32[]{:S(2)}) copy-start(f32[768]{0:T(1024)} %get-tuple-element.110) | copy-start | bytes 9220
  267.9 30.1 %copy-start.93 = (s32[128]{0:T(128)S(1)}, s32[128]{0:T(128)}, u32[]{:S(2)}) copy-start(s32[128]{0:T(128)} %copy-done.92) | copy-start | bytes 1540
  267.9 30.1 %copy-start.105 = (f32[128]{0:T(128)S(1)}, f32[128]{0:T(128)}, u32[]{:S(2)}) copy-start(f32[128]{0:T(128)} %copy-done.104) | copy-start | bytes 1540
  267.9 31.0 %copy-start.54 = (bf16[2,64,768]{2,1,0:T(8,128)(2,1)S(1)}, bf16[2,64,768]{2,1,0:T(8,128)(2,1)}, u32[]{:S(2)}) copy-start(bf16[2,64,768]{2,1,0:T(8,128)(2,1)} %copy-done.53) | copy-start | bytes 589828
  267.9 31.0 %copy-start.124 = (f32[128]{0:T(128)S(1)}, f32[128]{0:T(128)}, u32[]{:S(2)}) copy-start(f32[128]{0:T(128)} %get-tuple-element.168) | copy-start | bytes 1540
  268.0 2.1 collective-permute-start.15
  271.0 11.4 %collective-permute-start.16 = (bf16[8,24,768]{2,1,0:T(8,128)(2,1)}, bf16[8,24,768]{2,1,0:T(8,128)(2,1)}, u32[]{:S(2)}, u32[]{:S(2)}) collective-permute-start(bf16[8,24,768]{2,1,0:T(8,128)(2,1)} %fusion.31), channel_id=1, source_target_pairs={{16,0},{17,1},{18,2},{19,3},{20,4},{21,5},{22,6},{23,7},{24,8},{25... | collective-permute-start | bytes 884744 | tf_op jit(solution)/shard_map/ppermute | solution.py:215
  283.6 27.5 %copy-start.21 = (bf16[512,384]{1,0:T(8,128)(2,1)S(1)}, bf16[512,384]{1,0:T(8,128)(2,1)}, u32[]{:S(2)}) copy-start(bf16[512,384]{1,0:T(8,128)(2,1)} %copy-done.20) | copy-start | bytes 1179652
  283.6 27.5 %copy-start.23 = (bf16[512,384]{1,0:T(8,128)(2,1)S(1)}, bf16[512,384]{1,0:T(8,128)(2,1)}, u32[]{:S(2)}) copy-start(bf16[512,384]{1,0:T(8,128)(2,1)} %copy-done.22) | copy-start | bytes 1179652
  283.6 27.5 %copy-start.27 = (bf16[512,192]{1,0:T(8,128)(2,1)S(1)}, bf16[512,192]{1,0:T(8,128)(2,1)}, u32[]{:S(2)}) copy-start(bf16[512,192]{1,0:T(8,128)(2,1)} %copy-done.26) | copy-start | bytes 589828
  283.6 27.5 %copy-start.31 = (f32[192,512]{1,0:T(8,128)S(1)}, f32[192,512]{1,0:T(8,128)}, u32[]{:S(2)}) copy-start(f32[192,512]{1,0:T(8,128)} %copy-done.30) | copy-start | bytes 1179652
  283.6 27.5 %copy-start.33 = (f32[8,512]{1,0:T(8,128)S(1)}, f32[8,512]{1,0:T(8,128)}, u32[]{:S(2)}) copy-start(f32[8,512]{1,0:T(8,128)} %copy-done.32) | copy-start | bytes 49156
  315.7 1.8 collective-permute-start.17
  320.1 19.8 %copy-start.102 = (s32[128]{0:T(128)S(1)}, s32[128]{0:T(128)}, u32[]{:S(2)}) copy-start(s32[128]{0:T(128)} %copy-done.101) | copy-start | bytes 1540
  320.1 19.8 %copy-start.112 = (f32[128]{0:T(128)S(1)}, f32[128]{0:T(128)}, u32[]{:S(2)}) copy-start(f32[128]{0:T(128)} %copy-done.111) | copy-start | bytes 1540
  320.1 15.8 %all-to-all-start.9 = ((bf16[4,128,768]{2,1,0:T(8,128)(2,1)}), bf16[4,128,768]{2,1,0:T(8,128)(2,1)}, u32[]{:S(2)}, u32[]{:S(2)}) async-start(bf16[4,128,768]{2,1,0:T(8,128)(2,1)} %bitcast.289), calls=%async_computation.9 | async-start | bytes 1572864 | tf_op jit(solution)/shard_map/all_to_all | solution.py:44
  324.4 139.3 %reduce-scatter.5.cloned.1.call-start = ((), (), s32[]{:S(2)}) async-start(), calls=%async_computation.19 | async-start | bytes 1327104 | tf_op jit(solution)/shard_map/reduce_scatter | solution.py:154
  337.9 25.7 %copy-start.133 = (bf16[1,1,1536,768]{3,2,1,0:T(8,128)(2,1)S(1)}, bf16[1,1,1536,768]{3,2,1,0:T(8,128)(2,1)}, u32[]{:S(2)}) copy-start(bf16[1,1,1536,768]{3,2,1,0:T(8,128)(2,1)} %param.23) | copy-start | bytes 7077892
  339.8 30.4 %copy-start.48 = (bf16[128,768]{1,0:T(8,128)(2,1)}, bf16[128,768]{1,0:T(8,128)(2,1)S(1)}, u32[]{:S(2)}) copy-start(bf16[128,768]{1,0:T(8,128)(2,1)S(1)} %get-tuple-element.119) | copy-start | bytes 589828
  353.2 8.7 %collective-permute-start.19 = (bf16[8,24,768]{2,1,0:T(8,128)(2,1)S(1)}, bf16[8,24,768]{2,1,0:T(8,128)(2,1)S(1)}, u32[]{:S(2)}, u32[]{:S(2)}) collective-permute-start(bf16[8,24,768]{2,1,0:T(8,128)(2,1)S(1)} %all_to_all.85), channel_id=1, source_target_pairs={{16,0},{17,1},{18,2},{19,3},{20,4},{21,5},{22,6},{23,7},{24,8},{25... | collective-permute-start | bytes 884744 | tf_op jit(solution)/shard_map/ppermute | solution.py:192
  354.7 7.2 %collective-permute-start.18 = (bf16[8,24,768]{2,1,0:T(8,128)(2,1)S(1)}, bf16[8,24,768]{2,1,0:T(8,128)(2,1)S(1)}, u32[]{:S(2)}, u32[]{:S(2)}) collective-permute-start(bf16[8,24,768]{2,1,0:T(8,128)(2,1)S(1)} %all_to_all.85), channel_id=1, source_target_pairs={{0,1},{1,0},{2,3},{3,2},{4,5},{5,4},{6,7},{7,6},{8,9},{9,8},{10,11... | collective-permute-start | bytes 884744 | tf_op jit(solution)/shard_map/ppermute | solution.py:40
  361.9 1.6 collective-permute-start.20
  374.2 2.3 collective-permute-start.21
  378.7 9.4 %collective-permute-start.22 = (bf16[8,24,768]{2,1,0:T(8,128)(2,1)}, bf16[8,24,768]{2,1,0:T(8,128)(2,1)}, u32[]{:S(2)}, u32[]{:S(2)}) collective-permute-start(bf16[8,24,768]{2,1,0:T(8,128)(2,1)} %get-tuple-element.127), channel_id=1, source_target_pairs={{0,16},{16,0},{1,17},{17,1},{2,18},{18,2},{3,19},{19,3},{4,20},{20... | collective-permute-start | bytes 884744 | tf_op jit(solution)/shard_map/ppermute | solution.py:40
  390.1 26.3 %all-to-all-start.11 = ((bf16[8,48,768]{2,1,0:T(8,128)(2,1)}), bf16[8,48,768]{2,1,0:T(8,128)(2,1)S(1)}, u32[]{:S(2)}, u32[]{:S(2)}) async-start(bf16[8,48,768]{2,1,0:T(8,128)(2,1)} %maximum_select_fusion), calls=%async_computation.11 | async-start | bytes 1179648 | tf_op jit(solution)/shard_map/all_to_all | solution.py:44
  434.8 1.8 collective-permute-start.24
  439.4 15.6 %all-to-all-start.12 = ((bf16[4,128,768]{2,1,0:T(8,128)(2,1)}), bf16[4,128,768]{2,1,0:T(8,128)(2,1)S(1)}, u32[]{:S(2)}, u32[]{:S(2)}) async-start(bf16[4,128,768]{2,1,0:T(8,128)(2,1)} %bitcast.85), calls=%async_computation.12 | async-start | bytes 1572864 | tf_op jit(solution)/shard_map/all_to_all | solution.py:44
  443.0 37.1 %reduce-scatter.3.cloned.1.call-start = ((), (), s32[]{:S(2)}) async-start(), calls=%async_computation.18 | async-start | bytes 1327104 | tf_op jit(solution)/shard_map/reduce_scatter | solution.py:154
  448.0 11.0 %collective-permute-start.23 = (bf16[128,768]{1,0:T(8,128)(2,1)S(1)}, bf16[128,768]{1,0:T(8,128)(2,1)S(1)}, u32[]{:S(2)}, u32[]{:S(2)}) collective-permute-start(bf16[128,768]{1,0:T(8,128)(2,1)S(1)} %get-tuple-element.114), channel_id=1, source_target_pairs={{0,16},{16,0},{1,17},{17,1},{2,18},{18,2},{3,19},{19,3},{4,20},{20... | collective-permute-start | bytes 589832 | tf_op jit(solution)/shard_map/ppermute | solution.py:40
  456.7 6.7 %collective-permute-start.25 = (bf16[144,768]{1,0:T(8,128)(2,1)S(1)}, bf16[144,768]{1,0:T(8,128)(2,1)S(1)}, u32[]{:S(2)}, u32[]{:S(2)}) collective-permute-start(bf16[144,768]{1,0:T(8,128)(2,1)S(1)} %pad_maximum_fusion.10), channel_id=1, source_target_pairs={{0,16},{16,0},{1,17},{17,1},{2,18},{18,2},{3,19},{19,3},{4,20},{20... | collective-permute-start | bytes 663560 | tf_op jit(solution)/shard_map/ppermute | solution.py:40
  480.1 12.2 %collective-permute-start.28 = (bf16[144,768]{1,0:T(8,128)(2,1)S(1)}, bf16[144,768]{1,0:T(8,128)(2,1)S(1)}, u32[]{:S(2)}, u32[]{:S(2)}) collective-permute-start(bf16[144,768]{1,0:T(8,128)(2,1)S(1)} %get-tuple-element.136), channel_id=1, source_target_pairs={{0,4},{4,0},{8,12},{12,8},{1,5},{5,1},{9,13},{13,9},{2,6},{6,2},{1... | collective-permute-start | bytes 663560 | tf_op jit(solution)/shard_map/ppermute | solution.py:88
  480.2 12.2 %collective-permute-start.26 = (bf16[144,768]{1,0:T(8,128)(2,1)S(1)}, bf16[144,768]{1,0:T(8,128)(2,1)S(1)}, u32[]{:S(2)}, u32[]{:S(2)}) collective-permute-start(bf16[144,768]{1,0:T(8,128)(2,1)S(1)} %get-tuple-element.137), channel_id=1, source_target_pairs={{0,12},{4,8},{8,4},{12,0},{1,13},{5,9},{9,5},{13,1},{2,14},{6,10},... | collective-permute-start | bytes 663560 | tf_op jit(solution)/shard_map/ppermute | solution.py:88
  480.3 20.5 %collective-permute-start.27 = (bf16[144,768]{1,0:T(8,128)(2,1)S(1)}, bf16[144,768]{1,0:T(8,128)(2,1)S(1)}, u32[]{:S(2)}, u32[]{:S(2)}) collective-permute-start(bf16[144,768]{1,0:T(8,128)(2,1)S(1)} %get-tuple-element.138), channel_id=1, source_target_pairs={{0,8},{4,12},{8,0},{12,4},{1,9},{5,13},{9,1},{13,5},{2,10},{6,14},... | collective-permute-start | bytes 663560 | tf_op jit(solution)/shard_map/ppermute | solution.py:88
  485.4 15.7 %all-to-all-start.13 = ((bf16[4,48,768]{2,1,0:T(8,128)(2,1)}), bf16[4,48,768]{2,1,0:T(8,128)(2,1)S(1)}, u32[]{:S(2)}, u32[]{:S(2)}) async-start(bf16[4,48,768]{2,1,0:T(8,128)(2,1)} %bitcast.112), calls=%async_computation.15 | async-start | bytes 589824 | tf_op jit(solution)/shard_map/all_to_all | solution.py:44
  506.2 8.8 %all-to-all-start.14 = ((bf16[4,2,384]{2,1,0:T(2,128)(2,1)}), bf16[4,2,384]{2,1,0:T(2,128)(2,1)S(1)}, u32[]{:S(2)}, u32[]{:S(2)}) async-start(bf16[4,2,384]{2,1,0:T(2,128)(2,1)} %reshape.584), calls=%async_computation.16 | async-start | bytes 12288 | tf_op jit(solution)/shard_map/all_to_all | solution.py:44
  (114 other events, 878.1 us)
Sparse Core Ops, SparseCore 0:
  84.0 22.2 all-gather.2
  383.3 36.0 reduce-scatter.4
  446.9 33.1 reduce-scatter.2

commit v5 on v4

--- a/solution.py
+++ b/solution.py
@@ -144,6 +144,22 @@
     places = lax.axis_size("z") * lax.axis_size("q")
     gathered = gathered.reshape((places, 2) + own.shape).transpose(0, 2, 1, 3, 4)
     return gathered.reshape(-1, own.shape[-1])
+
+
+def scatter_now(grads):
+    width = grads.shape[-1]
+    planes = lax.axis_size("z")
+    split = grads.reshape(planes * 2, 2, -1, width)
+    core = lax.axis_index("tp")
+    kept = lax.dynamic_index_in_dim(split, core, 1, keepdims=False)
+    got = swapped(lax.dynamic_index_in_dim(split, 1 - core, 1, keepdims=False), "tp")
+    both = (kept.astype(F32) + got.astype(F32)).astype(BF16)
+    mine = xor_z(both.reshape(planes, 2, -1, width))
+    total = mine[0].astype(F32)
+    for k in range(1, planes):
+        pairs = [(z, z ^ k) for z in range(planes)]
+        total = total + lax.ppermute(mine[k], "z", pairs).astype(F32)
+    return total.astype(BF16)
 
 
 def scatter_later(grads):
@@ -473,7 +489,7 @@
     grad_qkv, part = project_back(grad_queries, sum_parts(grad_own, grad_other), whole)
     grads = weight_grads(rows_a, grad_rows, grad_qkv, attended)
     grad_normed_a = sum_chips(after(part, grads) if last else part)
-    sums = scatter_later(grads)
+    sums = scatter_now(grads) if last and lax.axis_size("q") == 1 else scatter_later(grads)
     inverse = lax.rsqrt(jnp.mean(values_in * values_in, axis=-1, keepdims=True) + EPSILON)
     grad_input_norm, grad_gain = norm_back(values_in, inverse, small[0:1], grad_normed_a)
     return (grad_hidden + grad_input_norm).astype(BF16), grad_gain, sums

time: 532 us -> 525 us (0.987)
  waiting for transfers between devices: 149 us -> 137 us
  starting transfers between devices: 64.5 us -> 70.9 us
    reduce_scatter x2 -> x1, waiting for transfers between devices: 16.4 us -> 0.02 us  [scatter_later(): lax.psum_scatter(split.reshape(-1, width), ('z', 'q', 'tp'), scatter_dime...]
    ppermute x0 -> x3, waiting for transfers between devices: none -> 7.69 us  [scatter_now(): total = total + lax.ppermute(mine[k], 'z', pairs).astype(F32)]
    ppermute x19 -> x20, waiting for transfers between devices: 32.9 us -> 28.7 us  [swapped(): return lax.ppermute(values, axis, SWAP)]
    unnamed x278 -> x274, local copies, waits for them, and re-layouts: 15.3 us -> 14.5 us
  transfers between devices with their start and end apart: 41 -> 44, of which waited for: 30 -> 27; matrix products, arithmetic and copies ran while one was open for 10% -> 11% of each run, Pallas kernels for 3% -> 3%
where the time goes in v5:
time: 525 us; the launch traced here: 516 us
  blocking collectives  142 us (27%)
  waiting for transfers between devices  137 us (26%)
  starting transfers between devices  70.9 us (14%)
  matrix products  41.8 us (8%)
  Pallas kernels  40.4 us (8%)
  local copies, waits for them, and re-layouts  35.8 us (7%)
  other arithmetic  31.7 us (6%)
  between operations  16.6 us (3%)
    all_to_all x7, blocking collectives, exchanged(): return lax.all_to_all(values, axes, split_axis=0, concat_axis=0, tiled=True)  106 us
    all_to_all x9, waiting for transfers between devices, exchanged(): return lax.all_to_all(values, axes, split_axis=0, concat_axis=0, tiled=True)  51.7 us
    dot_general x19, matrix products, dot(): lax.dot_general(left, right, (contract, ((), ())), precision=precision, p...  41.5 us
    all_to_all x9, starting transfers between devices, exchanged(): return lax.all_to_all(values, axes, split_axis=0, concat_axis=0, tiled=True)  35.9 us
    ppermute x20, waiting for transfers between devices, swapped(): return lax.ppermute(values, axis, SWAP)  28.7 us
    pallas_call x10, Pallas kernels, whole_call(): pl.pallas_call(kernel, out_shape=out_shape, compiler_params=pltpu.Compile...  23.6 us
    all_gather x2, blocking collectives, attention_backward(): lax.all_gather(grad_hidden.astype(BF16), CHIPS, axis=0, tiled=True)  22.9 us
    pallas_call x1, Pallas kernels, expert_both(): pl.pallas_call(expert_kernel, grid=(count // block,), in_specs=[rows_of(w...  16.8 us
  transfers between devices with their start and end apart: 44, of which 27 were waited for; matrix products, arithmetic and copies ran while one was open for 11% of the time, Pallas kernels for 3%

profile of v5, /device:TPU:0, one launch (start us, length us, event | category | flops | bytes accessed | tf_op | source)
XLA Modules:
  0.0 516.3 jit_solution(5094463579211018246)
XLA Ops:
  7.9 3.0 collective-permute-start
  15.7 1.8 maximum_bitcast_fusion
  17.4 3.5 all-to-all-start
  21.3 3.5 collective-permute-start.1
  25.3 4.5 collective-permute-start.2
  31.2 5.2 %collective-permute-done.2 = bf16[144,768]{1,0:T(8,128)(2,1)S(1)} collective-permute-done((bf16[144,768]{1,0:T(8,128)(2,1)S(1)}, bf16[144,768]{1,0:T(8,128)(2,1)S(1)}, u32[]{:S(2)}, u32[]{:S(2)}) %collective-permute-start.2) | collective-permute-done | bytes 221216 | tf_op jit(solution)/shard_map/ppermute | solution.py:98
  36.4 3.2 collective-permute-done.3
  40.5 21.8 %all_to_all.80 = bf16[4,176,896]{2,1,0:T(8,128)(2,1)S(1)} all-to-all(bf16[4,176,896]{2,1,0:T(8,128)(2,1)S(1)} %pad_maximum_fusion.1), channel_id=1, replica_groups=mesh['pipe'=2,'z'=4,'q'=1,'h'=2,'tp'=2] {'h','pipe'}, dimensions={0} | all-to-all | bytes 2523136 | tf_op jit(solution)/shard_map/all_to_all | solution.py:44
  63.0 18.8 %all_to_all.81 = bf16[4,2,48,896]{3,2,1,0:T(8,128)(2,1)S(1)} all-to-all(bf16[4,2,48,896]{3,2,1,0:T(8,128)(2,1)S(1)} %broadcast_in_dim.27), channel_id=1, replica_groups=mesh['pipe'=2,'z'=4,'q'=1,'h'=2,'tp'=2] {'z','q'}, dimensions={0} | all-to-all | bytes 1376256 | tf_op jit(solution)/shard_map/all_to_all | solution.py:44
  81.8 2.1 collective-permute-done.4
  88.0 3.9 shard_map.204
  93.4 4.3 all-to-all-start.3
  99.5 9.7 %all-to-all-done.3 = bf16[4,128,768]{2,1,0:T(8,128)(2,1)} async-done(((bf16[4,128,768]{2,1,0:T(8,128)(2,1)}), bf16[4,128,768]{2,1,0:T(8,128)(2,1)}, u32[]{:S(2)}, u32[]{:S(2)}) %all-to-all-start.3) | async-done | bytes 786464 | tf_op jit(solution)/shard_map/all_to_all | solution.py:44
  110.5 1.8 fusion.45
  116.0 20.6 %all_to_all.82 = bf16[8,48,768]{2,1,0:T(8,128)(2,1)S(1)} all-to-all(bf16[8,48,768]{2,1,0:T(8,128)(2,1)S(1)} %pad_maximum_fusion.6), channel_id=1, replica_groups=mesh['pipe'=2,'z'=4,'q'=1,'h'=2,'tp'=2] {'z','q','h'}, dimensions={0} | all-to-all | bytes 1179648 | tf_op jit(solution)/shard_map/all_to_all | solution.py:44
  137.1 7.1 %collective-permute-done.7 = bf16[8,24,768]{2,1,0:T(8,128)(2,1)S(1)} collective-permute-done((bf16[8,24,768]{2,1,0:T(8,128)(2,1)S(1)}, bf16[8,24,768]{2,1,0:T(8,128)(2,1)S(1)}, u32[]{:S(2)}, u32[]{:S(2)}) %collective-permute-start.7) | collective-permute-done | bytes 294944 | tf_op jit(solution)/shard_map/ppermute | solution.py:40
  147.0 2.0 fusion.105
  149.0 2.9 convolution_convert_fusion.1
  152.1 1.9 collective-permute-done.9
  154.1 2.3 collective-permute-start.10
  156.4 6.5 %collective-permute-done.10 = bf16[8,24,768]{2,1,0:T(8,128)(2,1)S(1)} collective-permute-done((bf16[8,24,768]{2,1,0:T(8,128)(2,1)S(1)}, bf16[8,24,768]{2,1,0:T(8,128)(2,1)S(1)}, u32[]{:S(2)}, u32[]{:S(2)}) %collective-permute-start.10) | collective-permute-done | bytes 294944 | tf_op jit(solution)/shard_map/ppermute | solution.py:231
  163.7 4.1 all-to-all-start.5
  170.2 6.9 %all-to-all-done.5 = bf16[8,24,768]{2,1,0:T(8,128)(2,1)} async-done(((bf16[8,24,768]{2,1,0:T(8,128)(2,1)}), bf16[8,24,768]{2,1,0:T(8,128)(2,1)}, u32[]{:S(2)}, u32[]{:S(2)}) %all-to-all-start.5) | async-done | bytes 294944 | tf_op jit(solution)/shard_map/all_to_all | solution.py:44
  177.1 2.6 fusion.49
  180.4 13.1 %all_gather.17.rows = bf16[512,768]{1,0:T(8,128)(2,1)S(1)} all-gather(bf16[128,768]{1,0:T(8,128)(2,1)S(1)} %get-tuple-element.121), channel_id=1, replica_groups=mesh['pipe'=2,'z'=4,'q'=1,'h'=2,'tp'=2] {'h','pipe'}, dimensions={0}, use_global_device_ids=true | all-gather | bytes 983040 | tf_op jit(solution)/shard_map/all_gather | solution.py:621
  197.1 3.9 shard_map.206
  203.1 4.2 all-to-all-start.6
  208.0 10.9 %all-to-all-done.6 = bf16[4,128,768]{2,1,0:T(8,128)(2,1)} async-done(((bf16[4,128,768]{2,1,0:T(8,128)(2,1)}), bf16[4,128,768]{2,1,0:T(8,128)(2,1)}, u32[]{:S(2)}, u32[]{:S(2)}) %all-to-all-start.6) | async-done | bytes 786464 | tf_op jit(solution)/shard_map/all_to_all | solution.py:44
  223.5 13.6 %all_to_all.83 = bf16[8,24,768]{2,1,0:T(8,128)(2,1)} all-to-all(bf16[8,24,768]{2,1,0:T(8,128)(2,1)S(1)} %bitcast.317), channel_id=1, replica_groups=mesh['pipe'=2,'z'=4,'q'=1,'h'=2,'tp'=2] {'z','q','h'}, dimensions={0} | all-to-all | bytes 589824 | tf_op jit(solution)/shard_map/all_to_all | solution.py:44
  237.1 3.8 collective-permute-start.13
  241.0 3.6 collective-permute-done.13
  244.6 1.9 collective-permute-done.14
  247.9 16.8 %shard_map.207 = (bf16[768,768]{1,0:T(8,128)(2,1)S(1)}, bf16[768,1536]{1,0:T(8,128)(2,1)}, bf16[768,768]{1,0:T(8,128)(2,1)S(1)}, bf16[768,1536]{1,0:T(8,128)(2,1)}, bf16[768,768]{1,0:T(8,128)(2,1)S(1)}) custom-call(bf16[768,768]{1,0:T(8,128)(2,1)S(1)} %bitcast.284, bf16[768,768]{1,0:T(8,128)(2,1)} %bitcast.298, bf16[768,1536]{1,0:T(8,128)(2,1)} %bitcast.350, ...), custom_call_target="tpu_custom_call" | custom-call | flops 7247757312 | bytes 9437184 | tf_op jit(solution)/shard_map/pallas_call | solution.py:439
  267.1 1.9 collective-permute-done.15
  271.2 10.1 %collective-permute-done.16 = bf16[8,24,768]{2,1,0:T(8,128)(2,1)} collective-permute-done((bf16[8,24,768]{2,1,0:T(8,128)(2,1)}, bf16[8,24,768]{2,1,0:T(8,128)(2,1)}, u32[]{:S(2)}, u32[]{:S(2)}) %collective-permute-start.16) | collective-permute-done | bytes 294944 | tf_op jit(solution)/shard_map/ppermute | solution.py:231
  282.6 14.2 %all_to_all.84 = bf16[8,24,768]{2,1,0:T(8,128)(2,1)S(1)} all-to-all(bf16[8,24,768]{2,1,0:T(8,128)(2,1)S(1)} %fusion.58), channel_id=1, replica_groups=mesh['pipe'=2,'z'=4,'q'=1,'h'=2,'tp'=2] {'z','q','h'}, dimensions={0} | all-to-all | bytes 589824 | tf_op jit(solution)/shard_map/all_to_all | solution.py:44
  298.7 11.3 %all_gather.18.grad_rows = bf16[512,768]{1,0:T(8,128)(2,1)S(1)} all-gather(bf16[128,768]{1,0:T(8,128)(2,1)S(1)} %get-tuple-element.122), channel_id=1, replica_groups=mesh['pipe'=2,'z'=4,'q'=1,'h'=2,'tp'=2] {'h','pipe'}, dimensions={0}, use_global_device_ids=true | all-gather | bytes 983040 | tf_op jit(solution)/shard_map/all_gather | solution.py:485
  310.0 4.5 shard_map.208
  319.0 4.3 all-to-all-start.9
  324.0 10.7 %all-to-all-done.9 = bf16[4,128,768]{2,1,0:T(8,128)(2,1)} async-done(((bf16[4,128,768]{2,1,0:T(8,128)(2,1)}), bf16[4,128,768]{2,1,0:T(8,128)(2,1)}, u32[]{:S(2)}, u32[]{:S(2)}) %all-to-all-start.9) | async-done | bytes 786464 | tf_op jit(solution)/shard_map/all_to_all | solution.py:44
  336.8 1.8 fusion.42
  338.9 13.0 %all_to_all.85 = bf16[8,24,768]{2,1,0:T(8,128)(2,1)S(1)} all-to-all(bf16[8,24,768]{2,1,0:T(8,128)(2,1)S(1)} %bitcast.318), channel_id=1, replica_groups=mesh['pipe'=2,'z'=4,'q'=1,'h'=2,'tp'=2] {'z','q','h'}, dimensions={0} | all-to-all | bytes 589824 | tf_op jit(solution)/shard_map/all_to_all | solution.py:44
  353.5 7.2 %collective-permute-done.19 = bf16[8,24,768]{2,1,0:T(8,128)(2,1)S(1)} collective-permute-done((bf16[8,24,768]{2,1,0:T(8,128)(2,1)S(1)}, bf16[8,24,768]{2,1,0:T(8,128)(2,1)S(1)}, u32[]{:S(2)}, u32[]{:S(2)}) %collective-permute-start.19) | collective-permute-done | bytes 294944 | tf_op jit(solution)/shard_map/ppermute | solution.py:208
  363.5 6.5 %fusion.6 = bf16[768,1536]{1,0:T(8,128)(2,1)S(1)} fusion(f32[768,1536]{1,0:T(8,128)} %copy-done.133, bf16[768,768]{1,0:T(8,128)(2,1)S(1)} %bitcast.312, bf16[1,1,1536,768]{3,2,1,0:T(8,128)(2,1)S(1)} %copy-done.130), kind=kOutput, calls=%fused_computation.8 | convolution fusion | flops 1835532288 | bytes 10616832 | tf_op jit(solution)/shard_map/dot_general | solution.py:22
  370.1 2.0 fusion.15
  381.5 1.8 fusion.78
  383.3 6.0 %collective-permute-done.22 = bf16[8,24,768]{2,1,0:T(8,128)(2,1)S(1)} collective-permute-done((bf16[8,24,768]{2,1,0:T(8,128)(2,1)S(1)}, bf16[8,24,768]{2,1,0:T(8,128)(2,1)S(1)}, u32[]{:S(2)}, u32[]{:S(2)}) %collective-permute-start.22) | collective-permute-done | bytes 294944 | tf_op jit(solution)/shard_map/ppermute | solution.py:40
  390.3 4.6 all-to-all-start.11
  395.0 6.4 %fusion.9 = f32[768,1536]{1,0:T(8,128)} fusion(bf16[768,1536]{1,0:T(8,128)(2,1)} %copy-done.59, bf16[768,1536]{1,0:T(8,128)(2,1)} %get-tuple-element.72, pred[]{:T(512)S(6)} %eq.63, bf16[768,768]{1,0:T(8,128)(2,1)} %bitcast.299, bf16[768,768]{1,0:T(8,128)(2,1)S(1)} %bitcast.285), kind=kOutput, calls=%fused_computation.12 | convolution fusion | flops 1813708800 | bytes 11796481 | tf_op jit(solution)/shard_map/dot_general | solution.py:22
  401.5 7.8 %fusion.7 = f32[1536,768]{1,0:T(8,128)} fusion(bf16[768,1536]{1,0:T(8,128)(2,1)S(1)} %copy-done.134, pred[]{:T(512)S(6)} %eq.63, bf16[768,768]{1,0:T(8,128)(2,1)S(1)} %bitcast.313, bf16[768,768]{1,0:T(8,128)(2,1)S(1)} %copy-done.37, f32[768,1536]{1,0:T(8,128)} %copy-done.133), kind=kOutput, calls=%fused_computation.10 | convolution fusion | flops 1824325632 | bytes 14155777 | tf_op jit(solution)/shard_map/dot_general | solution.py:22
  409.3 5.5 %all-to-all-done.11 = bf16[8,48,768]{2,1,0:T(8,128)(2,1)S(1)} async-done(((bf16[8,48,768]{2,1,0:T(8,128)(2,1)}), bf16[8,48,768]{2,1,0:T(8,128)(2,1)S(1)}, u32[]{:S(2)}, u32[]{:S(2)}) %all-to-all-start.11) | async-done | bytes 589856 | tf_op jit(solution)/shard_map/all_to_all | solution.py:44
  416.1 11.6 %all_gather.19.grad_rows = bf16[512,768]{1,0:T(8,128)(2,1)S(1)} all-gather(bf16[128,768]{1,0:T(8,128)(2,1)S(1)} %convert_element_type.392), channel_id=1, replica_groups=mesh['pipe'=2,'z'=4,'q'=1,'h'=2,'tp'=2] {'h','pipe'}, dimensions={0}, use_global_device_ids=true | all-gather | bytes 983040 | tf_op jit(solution)/shard_map/all_gather | solution.py:485
  427.8 4.5 shard_map.210
  438.6 3.5 all-to-all-start.12
  445.6 7.9 %all-to-all-done.12 = bf16[4,128,768]{2,1,0:T(8,128)(2,1)S(1)} async-done(((bf16[4,128,768]{2,1,0:T(8,128)(2,1)}), bf16[4,128,768]{2,1,0:T(8,128)(2,1)S(1)}, u32[]{:S(2)}, u32[]{:S(2)}) %all-to-all-start.12) | async-done | bytes 786464 | tf_op jit(solution)/shard_map/all_to_all | solution.py:44
  456.2 2.8 collective-permute-start.28
  463.6 6.6 %collective-permute-done.28 = bf16[2,48,768]{2,1,0:T(8,128)(2,1)S(1)} collective-permute-done((bf16[2,48,768]{2,1,0:T(8,128)(2,1)S(1)}, bf16[2,48,768]{2,1,0:T(8,128)(2,1)S(1)}, u32[]{:S(2)}, u32[]{:S(2)}) %collective-permute-start.28) | collective-permute-done | bytes 147488 | tf_op jit(solution)/shard_map/ppermute | solution.py:161
  470.8 2.3 collective-permute-start.32
  473.1 2.2 collective-permute-start.30
  476.1 3.5 all-to-all-start.13
  479.6 7.0 %collective-permute-done.30 = bf16[144,768]{1,0:T(8,128)(2,1)S(1)} collective-permute-done((bf16[144,768]{1,0:T(8,128)(2,1)S(1)}, bf16[144,768]{1,0:T(8,128)(2,1)S(1)}, u32[]{:S(2)}, u32[]{:S(2)}) %collective-permute-start.30) | collective-permute-done | bytes 221216 | tf_op jit(solution)/shard_map/ppermute | solution.py:88
  486.6 6.3 %collective-permute-done.31 = bf16[144,768]{1,0:T(8,128)(2,1)S(1)} collective-permute-done((bf16[144,768]{1,0:T(8,128)(2,1)S(1)}, bf16[144,768]{1,0:T(8,128)(2,1)S(1)}, u32[]{:S(2)}, u32[]{:S(2)}) %collective-permute-start.31) | collective-permute-done | bytes 221216 | tf_op jit(solution)/shard_map/ppermute | solution.py:88
  494.2 4.0 all_to_all.86
  498.3 3.9 all-to-all-start.14
  (478 shorter events, 98.1 us)
Async XLA Ops:
  7.9 13.1 %collective-permute-start = (bf16[4,64]{1,0:T(4,128)(2,1)S(1)}, bf16[4,64]{1,0:T(4,128)(2,1)S(1)}, u32[]{:S(2)}, u32[]{:S(2)}) collective-permute-start(bf16[4,64]{1,0:T(4,128)(2,1)S(1)} %dynamic-slice_convert_fusion), channel_id=1, source_target_pairs={{0,16},{16,0},{1,17},{17,1},{2,18},{18,2},{3,19},{19,3},{4,20},{20... | collective-permute-start | bytes 1544 | tf_op jit(solution)/shard_map/ppermute | solution.py:40
  17.4 7.5 %all-to-all-start = ((bf16[2,2,48,4,192]{4,3,2,1,0:T(4,128)(2,1)}), bf16[2,2,48,4,192]{4,3,2,1,0:T(4,128)(2,1)S(1)}, u32[]{:S(2)}, u32[]{:S(2)}) async-start(bf16[2,2,48,4,192]{4,3,2,1,0:T(4,128)(2,1)} %maximum_bitcast_fusion), calls=%async_computation | async-start | bytes 786432 | tf_op jit(solution)/shard_map/all_to_all | solution.py:44
  21.0 92.5 %all-gather.3.cloned.1.call-start = ((), (), s32[]{:S(2)}) async-start(), calls=%async_computation.18 | async-start | bytes 1548288 | tf_op jit(solution)/shard_map/all_gather | solution.py:143
  21.3 9.9 %collective-permute-start.1 = (bf16[144,768]{1,0:T(8,128)(2,1)S(1)}, bf16[144,768]{1,0:T(8,128)(2,1)S(1)}, u32[]{:S(2)}, u32[]{:S(2)}) collective-permute-start(bf16[144,768]{1,0:T(8,128)(2,1)S(1)} %get-tuple-element.141), channel_id=1, source_target_pairs={{0,4},{8,12},{20,16},{28,24},{1,5},{9,13},{21,17},{29,25},{2,6},{1... | collective-permute-start | bytes 663560 | tf_op jit(solution)/shard_map/ppermute | solution.py:98
  25.3 11.1 %collective-permute-start.2 = (bf16[144,768]{1,0:T(8,128)(2,1)S(1)}, bf16[144,768]{1,0:T(8,128)(2,1)S(1)}, u32[]{:S(2)}, u32[]{:S(2)}) collective-permute-start(bf16[144,768]{1,0:T(8,128)(2,1)S(1)} %get-tuple-element.142), channel_id=1, source_target_pairs={{0,8},{8,0},{20,28},{28,20},{1,9},{9,1},{21,29},{29,21},{2,10},{10... | collective-permute-start | bytes 663560 | tf_op jit(solution)/shard_map/ppermute | solution.py:98
  29.9 9.7 %collective-permute-start.3 = (bf16[144,768]{1,0:T(8,128)(2,1)S(1)}, bf16[144,768]{1,0:T(8,128)(2,1)S(1)}, u32[]{:S(2)}, u32[]{:S(2)}) collective-permute-start(bf16[144,768]{1,0:T(8,128)(2,1)S(1)} %get-tuple-element.143), channel_id=1, source_target_pairs={{0,12},{8,4},{20,24},{28,16},{1,13},{9,5},{21,25},{29,17},{2,14},{... | collective-permute-start | bytes 663560 | tf_op jit(solution)/shard_map/ppermute | solution.py:98
  39.7 44.6 %copy-start.50 = (bf16[2,144,768]{2,1,0:T(8,128)(2,1)}, bf16[2,144,768]{2,1,0:T(8,128)(2,1)S(1)}, u32[]{:S(2)}) copy-start(bf16[2,144,768]{2,1,0:T(8,128)(2,1)S(1)} %maximum_select_fusion.1) | copy-start | bytes 1327108
  39.7 58.2 %copy-start.51 = (bf16[2,64,768]{2,1,0:T(8,128)(2,1)}, bf16[2,64,768]{2,1,0:T(8,128)(2,1)S(1)}, u32[]{:S(2)}) copy-start(bf16[2,64,768]{2,1,0:T(8,128)(2,1)S(1)} %get-tuple-element.162) | copy-start | bytes 589828
  81.8 2.1 collective-permute-start.4
  86.3 81.5 %copy-start.14 = (f32[128,768]{1,0:T(8,128)}, f32[128,768]{1,0:T(8,128)S(1)}, u32[]{:S(2)}) copy-start(f32[128,768]{1,0:T(8,128)S(1)} %get-tuple-element.56) | copy-start | bytes 1179652
  86.3 1.7 collective-permute-start.5
  93.4 19.0 %copy-start.43 = (bf16[2,64,768]{2,1,0:T(8,128)(2,1)S(1)}, bf16[2,64,768]{2,1,0:T(8,128)(2,1)}, u32[]{:S(2)}) copy-start(bf16[2,64,768]{2,1,0:T(8,128)(2,1)} %copy-done.42) | copy-start | bytes 589828
  93.4 15.8 %all-to-all-start.3 = ((bf16[4,128,768]{2,1,0:T(8,128)(2,1)}), bf16[4,128,768]{2,1,0:T(8,128)(2,1)}, u32[]{:S(2)}, u32[]{:S(2)}) async-start(bf16[4,128,768]{2,1,0:T(8,128)(2,1)} %bitcast.25), calls=%async_computation.3 | async-start | bytes 1572864 | tf_op jit(solution)/shard_map/all_to_all | solution.py:44
  97.8 15.7 %copy-start.103 = (s32[128]{0:T(128)}, s32[128]{0:T(128)S(1)}, u32[]{:S(2)}) copy-start(s32[128]{0:T(128)S(1)} %multiply_add_fusion.1) | copy-start | bytes 1540
  110.5 66.6 %copy-start.38 = (f32[128,768]{1,0:T(8,128)}, f32[128,768]{1,0:T(8,128)S(1)}, u32[]{:S(2)}) copy-start(f32[128,768]{1,0:T(8,128)S(1)} %convert_reduce_fusion.3) | copy-start | bytes 1179652
  136.7 7.6 %collective-permute-start.7 = (bf16[8,24,768]{2,1,0:T(8,128)(2,1)S(1)}, bf16[8,24,768]{2,1,0:T(8,128)(2,1)S(1)}, u32[]{:S(2)}, u32[]{:S(2)}) collective-permute-start(bf16[8,24,768]{2,1,0:T(8,128)(2,1)S(1)} %get-tuple-element.158), channel_id=1, source_target_pairs={{0,16},{16,0},{1,17},{17,1},{2,18},{18,2},{3,19},{19,3},{4,20},{20... | collective-permute-start | bytes 884744 | tf_op jit(solution)/shard_map/ppermute | solution.py:40
  137.1 7.2 %collective-permute-start.6 = (bf16[8,24,768]{2,1,0:T(8,128)(2,1)S(1)}, bf16[8,24,768]{2,1,0:T(8,128)(2,1)S(1)}, u32[]{:S(2)}, u32[]{:S(2)}) collective-permute-start(bf16[8,24,768]{2,1,0:T(8,128)(2,1)S(1)} %get-tuple-element.157), channel_id=1, source_target_pairs={{0,1},{1,0},{2,3},{3,2},{4,5},{5,4},{6,7},{7,6},{8,9},{9,8},{10,11... | collective-permute-start | bytes 884744 | tf_op jit(solution)/shard_map/ppermute | solution.py:40
  144.2 1.6 collective-permute-start.8
  151.9 2.1 collective-permute-start.9
  154.1 8.8 %collective-permute-start.10 = (bf16[8,24,768]{2,1,0:T(8,128)(2,1)S(1)}, bf16[8,24,768]{2,1,0:T(8,128)(2,1)S(1)}, u32[]{:S(2)}, u32[]{:S(2)}) collective-permute-start(bf16[8,24,768]{2,1,0:T(8,128)(2,1)S(1)} %fusion.34), channel_id=1, source_target_pairs={{0,16},{1,17},{2,18},{3,19},{4,20},{5,21},{6,22},{7,23},{8,24},{9,... | collective-permute-start | bytes 884744 | tf_op jit(solution)/shard_map/ppermute | solution.py:231
  163.7 13.4 %all-to-all-start.5 = ((bf16[8,24,768]{2,1,0:T(8,128)(2,1)}), bf16[8,24,768]{2,1,0:T(8,128)(2,1)}, u32[]{:S(2)}, u32[]{:S(2)}) async-start(bf16[8,24,768]{2,1,0:T(8,128)(2,1)} %fusion.57), calls=%async_computation.5 | async-start | bytes 589824 | tf_op jit(solution)/shard_map/all_to_all | solution.py:44
  195.4 52.5 %copy-start.15 = (f32[128,768]{1,0:T(8,128)}, f32[128,768]{1,0:T(8,128)S(1)}, u32[]{:S(2)}) copy-start(f32[128,768]{1,0:T(8,128)S(1)} %get-tuple-element.63.small) | copy-start | bytes 1179652
  195.4 1.7 collective-permute-start.11
  203.1 15.7 %all-to-all-start.6 = ((bf16[4,128,768]{2,1,0:T(8,128)(2,1)}), bf16[4,128,768]{2,1,0:T(8,128)(2,1)}, u32[]{:S(2)}, u32[]{:S(2)}) async-start(bf16[4,128,768]{2,1,0:T(8,128)(2,1)} %bitcast.53), calls=%async_computation.6 | async-start | bytes 1572864 | tf_op jit(solution)/shard_map/all_to_all | solution.py:44
  221.2 76.6 %copy-start.40 = (f32[128,768]{1,0:T(8,128)}, f32[128,768]{1,0:T(8,128)S(1)}, u32[]{:S(2)}) copy-start(f32[128,768]{1,0:T(8,128)S(1)} %get-tuple-element.125) | copy-start | bytes 1179652
  237.1 7.5 %collective-permute-start.13 = (bf16[8,24,768]{2,1,0:T(8,128)(2,1)}, bf16[8,24,768]{2,1,0:T(8,128)(2,1)}, u32[]{:S(2)}, u32[]{:S(2)}) collective-permute-start(bf16[8,24,768]{2,1,0:T(8,128)(2,1)} %all_to_all.83), channel_id=1, source_target_pairs={{0,16},{1,17},{2,18},{3,19},{4,20},{5,21},{6,22},{7,23},{8,24},{9,... | collective-permute-start | bytes 884744 | tf_op jit(solution)/shard_map/ppermute | solution.py:210
  240.9 3.7 collective-permute-start.12
  244.6 1.9 collective-permute-start.14
  247.9 16.8 %copy-start = (bf16[4,8,24,768]{3,2,1,0:T(8,128)(2,1)}, bf16[4,8,24,768]{3,2,1,0:T(8,128)(2,1)S(1)}, u32[]{:S(2)}) copy-start(bf16[4,8,24,768]{3,2,1,0:T(8,128)(2,1)S(1)} %pad_maximum_fusion.3) | copy-start | bytes 3538948
  266.8 30.0 %copy-start.79 = (f32[768]{0:T(1024)S(1)}, f32[768]{0:T(1024)}, u32[]{:S(2)}) copy-start(f32[768]{0:T(1024)} %get-tuple-element.110) | copy-start | bytes 9220
  266.8 30.0 %copy-start.96 = (s32[128]{0:T(128)S(1)}, s32[128]{0:T(128)}, u32[]{:S(2)}) copy-start(s32[128]{0:T(128)} %copy-done.95) | copy-start | bytes 1540
  266.8 30.0 %copy-start.107 = (f32[128]{0:T(128)S(1)}, f32[128]{0:T(128)}, u32[]{:S(2)}) copy-start(f32[128]{0:T(128)} %copy-done.106) | copy-start | bytes 1540
  266.9 30.9 %copy-start.52 = (bf16[2,64,768]{2,1,0:T(8,128)(2,1)S(1)}, bf16[2,64,768]{2,1,0:T(8,128)(2,1)}, u32[]{:S(2)}) copy-start(bf16[2,64,768]{2,1,0:T(8,128)(2,1)} %copy-done.51) | copy-start | bytes 589828
  266.9 30.9 %copy-start.122 = (f32[128]{0:T(128)S(1)}, f32[128]{0:T(128)}, u32[]{:S(2)}) copy-start(f32[128]{0:T(128)} %get-tuple-element.171) | copy-start | bytes 1540
  266.9 2.1 collective-permute-start.15
  269.9 11.4 %collective-permute-start.16 = (bf16[8,24,768]{2,1,0:T(8,128)(2,1)}, bf16[8,24,768]{2,1,0:T(8,128)(2,1)}, u32[]{:S(2)}, u32[]{:S(2)}) collective-permute-start(bf16[8,24,768]{2,1,0:T(8,128)(2,1)} %fusion.32), channel_id=1, source_target_pairs={{16,0},{17,1},{18,2},{19,3},{20,4},{21,5},{22,6},{23,7},{24,8},{25... | collective-permute-start | bytes 884744 | tf_op jit(solution)/shard_map/ppermute | solution.py:231
  314.5 1.8 collective-permute-start.17
  319.0 17.1 %copy-start.46 = (bf16[128,768]{1,0:T(8,128)(2,1)S(1)}, bf16[128,768]{1,0:T(8,128)(2,1)}, u32[]{:S(2)}) copy-start(bf16[128,768]{1,0:T(8,128)(2,1)} %copy-done.45) | copy-start | bytes 589828
  319.0 17.1 %copy-start.83 = (f32[768]{0:T(1024)S(1)}, f32[768]{0:T(1024)}, u32[]{:S(2)}) copy-start(f32[768]{0:T(1024)} %get-tuple-element.109) | copy-start | bytes 9220
  319.0 17.8 %copy-start.61 = (f32[128,768]{1,0:T(8,128)S(1)}, f32[128,768]{1,0:T(8,128)}, u32[]{:S(2)}) copy-start(f32[128,768]{1,0:T(8,128)} %get-tuple-element.177) | copy-start | bytes 1179652
  319.0 15.8 %all-to-all-start.9 = ((bf16[4,128,768]{2,1,0:T(8,128)(2,1)}), bf16[4,128,768]{2,1,0:T(8,128)(2,1)}, u32[]{:S(2)}, u32[]{:S(2)}) async-start(bf16[4,128,768]{2,1,0:T(8,128)(2,1)} %bitcast.293), calls=%async_computation.9 | async-start | bytes 1572864 | tf_op jit(solution)/shard_map/all_to_all | solution.py:44
  323.3 147.4 %reduce-scatter.2.cloned.1.call-start = ((), (), s32[]{:S(2)}) async-start(), calls=%async_computation.17 | async-start | bytes 1327104 | tf_op jit(solution)/shard_map/reduce_scatter | solution.py:170
  336.0 24.6 %copy-start.115 = (f32[2,64]{1,0:T(2,128)S(1)}, f32[2,64]{1,0:T(2,128)}, u32[]{:S(2)}) copy-start(f32[2,64]{1,0:T(2,128)} %get-tuple-element.103) | copy-start | bytes 1540
  338.6 31.5 %copy-start.47 = (bf16[128,768]{1,0:T(8,128)(2,1)}, bf16[128,768]{1,0:T(8,128)(2,1)S(1)}, u32[]{:S(2)}) copy-start(bf16[128,768]{1,0:T(8,128)(2,1)S(1)} %get-tuple-element.119) | copy-start | bytes 589828
  351.9 8.7 %collective-permute-start.19 = (bf16[8,24,768]{2,1,0:T(8,128)(2,1)S(1)}, bf16[8,24,768]{2,1,0:T(8,128)(2,1)S(1)}, u32[]{:S(2)}, u32[]{:S(2)}) collective-permute-start(bf16[8,24,768]{2,1,0:T(8,128)(2,1)S(1)} %all_to_all.85), channel_id=1, source_target_pairs={{16,0},{17,1},{18,2},{19,3},{20,4},{21,5},{22,6},{23,7},{24,8},{25... | collective-permute-start | bytes 884744 | tf_op jit(solution)/shard_map/ppermute | solution.py:208
  353.4 7.4 %collective-permute-start.18 = (bf16[8,24,768]{2,1,0:T(8,128)(2,1)S(1)}, bf16[8,24,768]{2,1,0:T(8,128)(2,1)S(1)}, u32[]{:S(2)}, u32[]{:S(2)}) collective-permute-start(bf16[8,24,768]{2,1,0:T(8,128)(2,1)S(1)} %all_to_all.85), channel_id=1, source_target_pairs={{0,1},{1,0},{2,3},{3,2},{4,5},{5,4},{6,7},{7,6},{8,9},{9,8},{10,11... | collective-permute-start | bytes 884744 | tf_op jit(solution)/shard_map/ppermute | solution.py:40
  360.6 1.7 collective-permute-start.20
  373.0 5.3 %collective-permute-start.21 = (bf16[2,8,24,768]{3,2,1,0:T(8,128)(2,1)}, bf16[2,8,24,768]{3,2,1,0:T(8,128)(2,1)}, u32[]{:S(2)}, u32[]{:S(2)}) collective-permute-start(bf16[2,8,24,768]{3,2,1,0:T(8,128)(2,1)} %slice_bitcast_fusion), channel_id=1, source_target_pairs={{0,1},{1,0},{2,3},{3,2},{4,5},{5,4},{6,7},{7,6},{8,9},{9,8},{10,11... | collective-permute-start | bytes 1769480 | tf_op jit(solution)/shard_map/ppermute | solution.py:40
  380.0 9.3 %collective-permute-start.22 = (bf16[8,24,768]{2,1,0:T(8,128)(2,1)S(1)}, bf16[8,24,768]{2,1,0:T(8,128)(2,1)S(1)}, u32[]{:S(2)}, u32[]{:S(2)}) collective-permute-start(bf16[8,24,768]{2,1,0:T(8,128)(2,1)S(1)} %get-tuple-element.127), channel_id=1, source_target_pairs={{0,16},{16,0},{1,17},{17,1},{2,18},{18,2},{3,19},{19,3},{4,20},{20... | collective-permute-start | bytes 884744 | tf_op jit(solution)/shard_map/ppermute | solution.py:40
  390.3 24.5 %all-to-all-start.11 = ((bf16[8,48,768]{2,1,0:T(8,128)(2,1)}), bf16[8,48,768]{2,1,0:T(8,128)(2,1)S(1)}, u32[]{:S(2)}, u32[]{:S(2)}) async-start(bf16[8,48,768]{2,1,0:T(8,128)(2,1)} %maximum_select_fusion), calls=%async_computation.11 | async-start | bytes 1179648 | tf_op jit(solution)/shard_map/all_to_all | solution.py:44
  432.4 3.3 collective-permute-start.24
  434.2 9.4 %collective-permute-start.23 = (bf16[128,768]{1,0:T(8,128)(2,1)}, bf16[128,768]{1,0:T(8,128)(2,1)S(1)}, u32[]{:S(2)}, u32[]{:S(2)}) collective-permute-start(bf16[128,768]{1,0:T(8,128)(2,1)} %get-tuple-element.114), channel_id=1, source_target_pairs={{0,16},{16,0},{1,17},{17,1},{2,18},{18,2},{3,19},{19,3},{4,20},{20... | collective-permute-start | bytes 589832 | tf_op jit(solution)/shard_map/ppermute | solution.py:40
  438.6 15.0 %all-to-all-start.12 = ((bf16[4,128,768]{2,1,0:T(8,128)(2,1)}), bf16[4,128,768]{2,1,0:T(8,128)(2,1)S(1)}, u32[]{:S(2)}, u32[]{:S(2)}) async-start(bf16[4,128,768]{2,1,0:T(8,128)(2,1)} %bitcast.85), calls=%async_computation.12 | async-start | bytes 1572864 | tf_op jit(solution)/shard_map/all_to_all | solution.py:44
  443.6 17.2 %copy-start.86 = (f32[1,768]{1,0:T(1,128)}, f32[1,768]{1,0:T(1,128)S(1)}, u32[]{:S(2)}) copy-start(f32[1,768]{1,0:T(1,128)S(1)} %broadcast_in_dim.31) | copy-start | bytes 9220
  444.6 10.3 %collective-permute-start.26 = (bf16[8,48,768]{2,1,0:T(8,128)(2,1)}, bf16[8,48,768]{2,1,0:T(8,128)(2,1)}, u32[]{:S(2)}, u32[]{:S(2)}) collective-permute-start(bf16[8,48,768]{2,1,0:T(8,128)(2,1)} %dynamic-slice_bitcast_fusion), channel_id=1, source_target_pairs={{0,1},{1,0},{2,3},{3,2},{4,5},{5,4},{6,7},{7,6},{8,9},{9,8},{10,11... | collective-permute-start | bytes 1769480 | tf_op jit(solution)/shard_map/ppermute | solution.py:40
  456.1 7.4 %collective-permute-start.27 = (bf16[2,48,768]{2,1,0:T(8,128)(2,1)S(1)}, bf16[2,48,768]{2,1,0:T(8,128)(2,1)S(1)}, u32[]{:S(2)}, u32[]{:S(2)}) collective-permute-start(bf16[2,48,768]{2,1,0:T(8,128)(2,1)S(1)} %get-tuple-element.150), channel_id=1, source_target_pairs={{0,4},{4,0},{8,12},{12,8},{1,5},{5,1},{9,13},{13,9},{2,6},{6,2},{1... | collective-permute-start | bytes 442376 | tf_op jit(solution)/shard_map/ppermute | solution.py:161
  456.2 14.0 %collective-permute-start.28 = (bf16[2,48,768]{2,1,0:T(8,128)(2,1)S(1)}, bf16[2,48,768]{2,1,0:T(8,128)(2,1)S(1)}, u32[]{:S(2)}, u32[]{:S(2)}) collective-permute-start(bf16[2,48,768]{2,1,0:T(8,128)(2,1)S(1)} %get-tuple-element.151), channel_id=1, source_target_pairs={{0,8},{4,12},{8,0},{12,4},{1,9},{5,13},{9,1},{13,5},{2,10},{6,14},... | collective-permute-start | bytes 442376 | tf_op jit(solution)/shard_map/ppermute | solution.py:161
  459.0 11.2 %collective-permute-start.29 = (bf16[2,48,768]{2,1,0:T(8,128)(2,1)S(1)}, bf16[2,48,768]{2,1,0:T(8,128)(2,1)S(1)}, u32[]{:S(2)}, u32[]{:S(2)}) collective-permute-start(bf16[2,48,768]{2,1,0:T(8,128)(2,1)S(1)} %get-tuple-element.152), channel_id=1, source_target_pairs={{0,12},{4,8},{8,4},{12,0},{1,13},{5,9},{9,5},{13,1},{2,14},{6,10},... | collective-permute-start | bytes 442376 | tf_op jit(solution)/shard_map/ppermute | solution.py:161
  461.0 9.4 %collective-permute-start.25 = (bf16[144,768]{1,0:T(8,128)(2,1)S(1)}, bf16[144,768]{1,0:T(8,128)(2,1)S(1)}, u32[]{:S(2)}, u32[]{:S(2)}) collective-permute-start(bf16[144,768]{1,0:T(8,128)(2,1)S(1)} %pad_maximum_fusion.10), channel_id=1, source_target_pairs={{0,16},{16,0},{1,17},{17,1},{2,18},{18,2},{3,19},{19,3},{4,20},{20... | collective-permute-start | bytes 663560 | tf_op jit(solution)/shard_map/ppermute | solution.py:40
  470.8 8.8 %collective-permute-start.32 = (bf16[144,768]{1,0:T(8,128)(2,1)S(1)}, bf16[144,768]{1,0:T(8,128)(2,1)S(1)}, u32[]{:S(2)}, u32[]{:S(2)}) collective-permute-start(bf16[144,768]{1,0:T(8,128)(2,1)S(1)} %get-tuple-element.136), channel_id=1, source_target_pairs={{0,4},{4,0},{8,12},{12,8},{1,5},{5,1},{9,13},{13,9},{2,6},{6,2},{1... | collective-permute-start | bytes 663560 | tf_op jit(solution)/shard_map/ppermute | solution.py:88
  473.1 13.4 %collective-permute-start.30 = (bf16[144,768]{1,0:T(8,128)(2,1)S(1)}, bf16[144,768]{1,0:T(8,128)(2,1)S(1)}, u32[]{:S(2)}, u32[]{:S(2)}) collective-permute-start(bf16[144,768]{1,0:T(8,128)(2,1)S(1)} %get-tuple-element.137), channel_id=1, source_target_pairs={{0,12},{4,8},{8,4},{12,0},{1,13},{5,9},{9,5},{13,1},{2,14},{6,10},... | collective-permute-start | bytes 663560 | tf_op jit(solution)/shard_map/ppermute | solution.py:88
  475.4 17.4 %collective-permute-start.31 = (bf16[144,768]{1,0:T(8,128)(2,1)S(1)}, bf16[144,768]{1,0:T(8,128)(2,1)S(1)}, u32[]{:S(2)}, u32[]{:S(2)}) collective-permute-start(bf16[144,768]{1,0:T(8,128)(2,1)S(1)} %get-tuple-element.138), channel_id=1, source_target_pairs={{0,8},{4,12},{8,0},{12,4},{1,9},{5,13},{9,1},{13,5},{2,10},{6,14},... | collective-permute-start | bytes 663560 | tf_op jit(solution)/shard_map/ppermute | solution.py:88
  476.1 17.0 %all-to-all-start.13 = ((bf16[4,48,768]{2,1,0:T(8,128)(2,1)}), bf16[4,48,768]{2,1,0:T(8,128)(2,1)S(1)}, u32[]{:S(2)}, u32[]{:S(2)}) async-start(bf16[4,48,768]{2,1,0:T(8,128)(2,1)} %bitcast.111), calls=%async_computation.14 | async-start | bytes 589824 | tf_op jit(solution)/shard_map/all_to_all | solution.py:44
  498.3 9.5 %all-to-all-start.14 = ((bf16[4,2,384]{2,1,0:T(2,128)(2,1)}), bf16[4,2,384]{2,1,0:T(2,128)(2,1)S(1)}, u32[]{:S(2)}, u32[]{:S(2)}) async-start(bf16[4,2,384]{2,1,0:T(2,128)(2,1)} %reshape.588), calls=%async_computation.15 | async-start | bytes 12288 | tf_op jit(solution)/shard_map/all_to_all | solution.py:44
  (115 other events, 706.2 us)
Sparse Core Ops, SparseCore 0:
  84.4 22.2 all-gather.2
  378.4 34.4 reduce-scatter.1

commit v6 on v5

--- a/solution.py
+++ b/solution.py
@@ -38,6 +38,13 @@
 
 def swapped(values, axis):
     return lax.ppermute(values, axis, SWAP)
+
+
+def exchanged_cores(values):
+    core = lax.axis_index("tp")
+    kept = lax.dynamic_index_in_dim(values, core, 0, keepdims=False)
+    got = swapped(lax.dynamic_index_in_dim(values, 1 - core, 0, keepdims=False), "tp")
+    return jnp.stack([jnp.where(core == 0, kept, got), jnp.where(core == 0, got, kept)])
 
 
 def exchanged(values, axes):
@@ -121,7 +128,7 @@
     half, group = (rows // 2, cols // 2)
     packed = jnp.stack([query_weight, key_weight, value_weight, output_weight.T])
     packed = packed.reshape(4, 2, half, 2, group).transpose(1, 3, 2, 0, 4)
-    by_core = exchanged(packed, "tp").reshape(4, half, 4 * group)
+    by_core = exchanged_cores(packed).reshape(4, half, 4 * group)
     small = jnp.broadcast_to(extras[None], (4,) + extras.shape)
     own = jnp.concatenate([by_core, small], axis=-1)
     count, width = inputs.shape
@@ -181,7 +188,8 @@
 def scatter_end(by_chip):
     half, width = by_chip.shape[1:]
     group = width // 4
-    by_core = exchanged(by_chip.reshape(2, 2, half, 4, group), "tp")
+    by_core = exchanged_cores(by_chip.reshape(2, 2, half, 4 * group))
+    by_core = by_core.reshape(2, 2, half, 4, group)
     return by_core.transpose(3, 0, 2, 1, 4).reshape(4, 2 * half, 2 * group).astype(F32)
 
 

time: 525 us -> 521 us (level)
    all_to_all x7 -> x6, blocking collectives: 106 us -> 102 us  [exchanged(): return lax.all_to_all(values, axes, split_axis=0, concat_axis=0, tiled=True)]
    all_to_all x9 -> x8, starting transfers between devices: 35.9 us -> 32.8 us  [exchanged(): return lax.all_to_all(values, axes, split_axis=0, concat_axis=0, tiled=True)]
    all_to_all x9 -> x8, waiting for transfers between devices: 51.7 us -> 54.5 us  [exchanged(): return lax.all_to_all(values, axes, split_axis=0, concat_axis=0, tiled=True)]
    ppermute x20 -> x22, waiting for transfers between devices: 28.7 us -> 28.7 us  [swapped(): return lax.ppermute(values, axis, SWAP)]
  transfers between devices with their start and end apart: 44 -> 45, of which waited for: 27 -> 28; matrix products, arithmetic and copies ran while one was open for 11% -> 11% of each run, Pallas kernels for 3% -> 3%
where the time goes in v6:
time: 521 us; the launch traced here: 512 us
  waiting for transfers between devices  139 us (27%)
  blocking collectives  139 us (27%)
  starting transfers between devices  67.8 us (13%)
  matrix products  41.8 us (8%)
  Pallas kernels  40.3 us (8%)
  local copies, waits for them, and re-layouts  35.9 us (7%)
  other arithmetic  32.5 us (6%)
  between operations  16.7 us (3%)
    all_to_all x6, blocking collectives, exchanged(): return lax.all_to_all(values, axes, split_axis=0, concat_axis=0, tiled=True)  102 us
    all_to_all x8, waiting for transfers between devices, exchanged(): return lax.all_to_all(values, axes, split_axis=0, concat_axis=0, tiled=True)  54.5 us
    dot_general x19, matrix products, dot(): lax.dot_general(left, right, (contract, ((), ())), precision=precision, p...  41.5 us
    all_to_all x8, starting transfers between devices, exchanged(): return lax.all_to_all(values, axes, split_axis=0, concat_axis=0, tiled=True)  32.8 us
    ppermute x22, waiting for transfers between devices, swapped(): return lax.ppermute(values, axis, SWAP)  28.7 us
    pallas_call x10, Pallas kernels, whole_call(): pl.pallas_call(kernel, out_shape=out_shape, compiler_params=pltpu.Compile...  23.6 us
    all_gather x2, blocking collectives, attention_backward(): lax.all_gather(grad_hidden.astype(BF16), CHIPS, axis=0, tiled=True)  22.9 us
    pallas_call x1, Pallas kernels, expert_both(): pl.pallas_call(expert_kernel, grid=(count // block,), in_specs=[rows_of(w...  16.8 us
  transfers between devices with their start and end apart: 45, of which 28 were waited for; matrix products, arithmetic and copies ran while one was open for 11% of the time, Pallas kernels for 3%

profile of v6, /device:TPU:0, one launch (start us, length us, event | category | flops | bytes accessed | tf_op | source)
XLA Modules:
  0.0 512.3 jit_solution(17853967346153620742)
XLA Ops:
  8.0 3.0 collective-permute-start
  17.5 3.5 collective-permute-start.1
  21.0 4.5 collective-permute-start.2
  28.6 3.4 collective-permute-done.2
  32.0 3.7 collective-permute-done.3
  36.6 21.8 %all_to_all.70 = bf16[4,176,896]{2,1,0:T(8,128)(2,1)S(1)} all-to-all(bf16[4,176,896]{2,1,0:T(8,128)(2,1)S(1)} %pad_maximum_fusion.1), channel_id=1, replica_groups=mesh['pipe'=2,'z'=4,'q'=1,'h'=2,'tp'=2] {'h','pipe'}, dimensions={0} | all-to-all | bytes 2523136 | tf_op jit(solution)/shard_map/all_to_all | solution.py:51
  59.2 19.2 %all_to_all.71 = bf16[4,2,48,896]{3,2,1,0:T(8,128)(2,1)S(1)} all-to-all(bf16[4,2,48,896]{3,2,1,0:T(8,128)(2,1)S(1)} %broadcast_in_dim.27), channel_id=1, replica_groups=mesh['pipe'=2,'z'=4,'q'=1,'h'=2,'tp'=2] {'z','q'}, dimensions={0} | all-to-all | bytes 1376256 | tf_op jit(solution)/shard_map/all_to_all | solution.py:51
  78.4 2.1 collective-permute-done.5
  84.6 3.9 shard_map.204
  90.0 4.3 all-to-all-start.2
  96.1 9.7 %all-to-all-done.2 = bf16[4,128,768]{2,1,0:T(8,128)(2,1)} async-done(((bf16[4,128,768]{2,1,0:T(8,128)(2,1)}), bf16[4,128,768]{2,1,0:T(8,128)(2,1)}, u32[]{:S(2)}, u32[]{:S(2)}) %all-to-all-start.2) | async-done | bytes 786464 | tf_op jit(solution)/shard_map/all_to_all | solution.py:51
  107.1 1.8 fusion.45
  112.6 20.6 %all_to_all.72 = bf16[8,48,768]{2,1,0:T(8,128)(2,1)S(1)} all-to-all(bf16[8,48,768]{2,1,0:T(8,128)(2,1)S(1)} %pad_maximum_fusion.6), channel_id=1, replica_groups=mesh['pipe'=2,'z'=4,'q'=1,'h'=2,'tp'=2] {'z','q','h'}, dimensions={0} | all-to-all | bytes 1179648 | tf_op jit(solution)/shard_map/all_to_all | solution.py:51
  133.7 7.2 %collective-permute-done.8 = bf16[8,24,768]{2,1,0:T(8,128)(2,1)S(1)} collective-permute-done((bf16[8,24,768]{2,1,0:T(8,128)(2,1)S(1)}, bf16[8,24,768]{2,1,0:T(8,128)(2,1)S(1)}, u32[]{:S(2)}, u32[]{:S(2)}) %collective-permute-start.8) | collective-permute-done | bytes 294944 | tf_op jit(solution)/shard_map/ppermute | solution.py:40
  143.7 2.0 fusion.107
  145.7 2.9 convolution_convert_fusion.1
  148.8 1.9 collective-permute-done.10
  150.7 2.3 collective-permute-start.11
  153.0 6.5 %collective-permute-done.11 = bf16[8,24,768]{2,1,0:T(8,128)(2,1)S(1)} collective-permute-done((bf16[8,24,768]{2,1,0:T(8,128)(2,1)S(1)}, bf16[8,24,768]{2,1,0:T(8,128)(2,1)S(1)}, u32[]{:S(2)}, u32[]{:S(2)}) %collective-permute-start.11) | collective-permute-done | bytes 294944 | tf_op jit(solution)/shard_map/ppermute | solution.py:239
  160.4 4.1 all-to-all-start.4
  166.9 6.9 %all-to-all-done.4 = bf16[8,24,768]{2,1,0:T(8,128)(2,1)} async-done(((bf16[8,24,768]{2,1,0:T(8,128)(2,1)}), bf16[8,24,768]{2,1,0:T(8,128)(2,1)}, u32[]{:S(2)}, u32[]{:S(2)}) %all-to-all-start.4) | async-done | bytes 294944 | tf_op jit(solution)/shard_map/all_to_all | solution.py:51
  173.8 2.6 fusion.49
  177.1 13.1 %all_gather.17.rows = bf16[512,768]{1,0:T(8,128)(2,1)S(1)} all-gather(bf16[128,768]{1,0:T(8,128)(2,1)S(1)} %get-tuple-element.121), channel_id=1, replica_groups=mesh['pipe'=2,'z'=4,'q'=1,'h'=2,'tp'=2] {'h','pipe'}, dimensions={0}, use_global_device_ids=true | all-gather | bytes 983040 | tf_op jit(solution)/shard_map/all_gather | solution.py:629
  192.1 1.7 collective-permute-done.12.other
  193.8 3.9 shard_map.206
  199.8 4.2 all-to-all-start.5
  204.6 10.9 %all-to-all-done.5 = bf16[4,128,768]{2,1,0:T(8,128)(2,1)} async-done(((bf16[4,128,768]{2,1,0:T(8,128)(2,1)}), bf16[4,128,768]{2,1,0:T(8,128)(2,1)}, u32[]{:S(2)}, u32[]{:S(2)}) %all-to-all-start.5) | async-done | bytes 786464 | tf_op jit(solution)/shard_map/all_to_all | solution.py:51
  220.1 13.6 %all_to_all.73 = bf16[8,24,768]{2,1,0:T(8,128)(2,1)} all-to-all(bf16[8,24,768]{2,1,0:T(8,128)(2,1)S(1)} %bitcast.338), channel_id=1, replica_groups=mesh['pipe'=2,'z'=4,'q'=1,'h'=2,'tp'=2] {'z','q','h'}, dimensions={0} | all-to-all | bytes 589824 | tf_op jit(solution)/shard_map/all_to_all | solution.py:51
  233.7 3.8 collective-permute-start.14
  237.6 3.6 collective-permute-done.14
  241.2 1.9 collective-permute-done.15
  244.5 16.8 %shard_map.207 = (bf16[768,768]{1,0:T(8,128)(2,1)S(1)}, bf16[768,1536]{1,0:T(8,128)(2,1)}, bf16[768,768]{1,0:T(8,128)(2,1)S(1)}, bf16[768,1536]{1,0:T(8,128)(2,1)}, bf16[768,768]{1,0:T(8,128)(2,1)S(1)}) custom-call(bf16[768,768]{1,0:T(8,128)(2,1)S(1)} %bitcast.305, bf16[768,768]{1,0:T(8,128)(2,1)} %bitcast.319, bf16[768,1536]{1,0:T(8,128)(2,1)} %bitcast.373, ...), custom_call_target="tpu_custom_call" | custom-call | flops 7247757312 | bytes 9437184 | tf_op jit(solution)/shard_map/pallas_call | solution.py:447
  263.7 1.9 collective-permute-done.16
  267.8 10.1 %collective-permute-done.17 = bf16[8,24,768]{2,1,0:T(8,128)(2,1)} collective-permute-done((bf16[8,24,768]{2,1,0:T(8,128)(2,1)}, bf16[8,24,768]{2,1,0:T(8,128)(2,1)}, u32[]{:S(2)}, u32[]{:S(2)}) %collective-permute-start.17) | collective-permute-done | bytes 294944 | tf_op jit(solution)/shard_map/ppermute | solution.py:239
  279.1 14.2 %all_to_all.74 = bf16[8,24,768]{2,1,0:T(8,128)(2,1)S(1)} all-to-all(bf16[8,24,768]{2,1,0:T(8,128)(2,1)S(1)} %fusion.58), channel_id=1, replica_groups=mesh['pipe'=2,'z'=4,'q'=1,'h'=2,'tp'=2] {'z','q','h'}, dimensions={0} | all-to-all | bytes 589824 | tf_op jit(solution)/shard_map/all_to_all | solution.py:51
  295.2 11.3 %all_gather.18.grad_rows = bf16[512,768]{1,0:T(8,128)(2,1)S(1)} all-gather(bf16[128,768]{1,0:T(8,128)(2,1)S(1)} %get-tuple-element.122), channel_id=1, replica_groups=mesh['pipe'=2,'z'=4,'q'=1,'h'=2,'tp'=2] {'h','pipe'}, dimensions={0}, use_global_device_ids=true | all-gather | bytes 983040 | tf_op jit(solution)/shard_map/all_gather | solution.py:493
  306.5 4.5 shard_map.208
  315.5 4.3 all-to-all-start.8
  320.6 10.7 %all-to-all-done.8 = bf16[4,128,768]{2,1,0:T(8,128)(2,1)} async-done(((bf16[4,128,768]{2,1,0:T(8,128)(2,1)}), bf16[4,128,768]{2,1,0:T(8,128)(2,1)}, u32[]{:S(2)}, u32[]{:S(2)}) %all-to-all-start.8) | async-done | bytes 786464 | tf_op jit(solution)/shard_map/all_to_all | solution.py:51
  333.3 1.8 fusion.42
  335.4 13.0 %all_to_all.75 = bf16[8,24,768]{2,1,0:T(8,128)(2,1)S(1)} all-to-all(bf16[8,24,768]{2,1,0:T(8,128)(2,1)S(1)} %bitcast.341), channel_id=1, replica_groups=mesh['pipe'=2,'z'=4,'q'=1,'h'=2,'tp'=2] {'z','q','h'}, dimensions={0} | all-to-all | bytes 589824 | tf_op jit(solution)/shard_map/all_to_all | solution.py:51
  350.0 7.2 %collective-permute-done.20 = bf16[8,24,768]{2,1,0:T(8,128)(2,1)S(1)} collective-permute-done((bf16[8,24,768]{2,1,0:T(8,128)(2,1)S(1)}, bf16[8,24,768]{2,1,0:T(8,128)(2,1)S(1)}, u32[]{:S(2)}, u32[]{:S(2)}) %collective-permute-start.20) | collective-permute-done | bytes 294944 | tf_op jit(solution)/shard_map/ppermute | solution.py:216
  360.0 6.5 %fusion.6 = bf16[768,1536]{1,0:T(8,128)(2,1)S(1)} fusion(f32[768,1536]{1,0:T(8,128)} %copy-done.133, bf16[768,768]{1,0:T(8,128)(2,1)S(1)} %bitcast.333, bf16[1,1,1536,768]{3,2,1,0:T(8,128)(2,1)S(1)} %copy-done.130), kind=kOutput, calls=%fused_computation.8 | convolution fusion | flops 1835532288 | bytes 10616832 | tf_op jit(solution)/shard_map/dot_general | solution.py:22
  366.6 2.0 fusion.15
  378.0 1.8 fusion.80
  379.8 6.0 %collective-permute-done.23 = bf16[8,24,768]{2,1,0:T(8,128)(2,1)S(1)} collective-permute-done((bf16[8,24,768]{2,1,0:T(8,128)(2,1)S(1)}, bf16[8,24,768]{2,1,0:T(8,128)(2,1)S(1)}, u32[]{:S(2)}, u32[]{:S(2)}) %collective-permute-start.23) | collective-permute-done | bytes 294944 | tf_op jit(solution)/shard_map/ppermute | solution.py:40
  386.8 4.6 all-to-all-start.10
  391.5 6.4 %fusion.9 = f32[768,1536]{1,0:T(8,128)} fusion(bf16[768,1536]{1,0:T(8,128)(2,1)} %copy-done.59, bf16[768,1536]{1,0:T(8,128)(2,1)} %get-tuple-element.72, pred[]{:T(512)S(6)} %eq.63, bf16[768,768]{1,0:T(8,128)(2,1)} %bitcast.320, bf16[768,768]{1,0:T(8,128)(2,1)S(1)} %bitcast.306), kind=kOutput, calls=%fused_computation.12 | convolution fusion | flops 1813708800 | bytes 11796481 | tf_op jit(solution)/shard_map/dot_general | solution.py:22
  398.0 7.8 %fusion.7 = f32[1536,768]{1,0:T(8,128)} fusion(bf16[768,1536]{1,0:T(8,128)(2,1)S(1)} %copy-done.134, pred[]{:T(512)S(6)} %eq.63, bf16[768,768]{1,0:T(8,128)(2,1)S(1)} %bitcast.334, bf16[768,768]{1,0:T(8,128)(2,1)S(1)} %copy-done.37, f32[768,1536]{1,0:T(8,128)} %copy-done.133), kind=kOutput, calls=%fused_computation.10 | convolution fusion | flops 1824325632 | bytes 14155777 | tf_op jit(solution)/shard_map/dot_general | solution.py:22
  405.8 5.5 %all-to-all-done.10 = bf16[8,48,768]{2,1,0:T(8,128)(2,1)S(1)} async-done(((bf16[8,48,768]{2,1,0:T(8,128)(2,1)}), bf16[8,48,768]{2,1,0:T(8,128)(2,1)S(1)}, u32[]{:S(2)}, u32[]{:S(2)}) %all-to-all-start.10) | async-done | bytes 589856 | tf_op jit(solution)/shard_map/all_to_all | solution.py:51
  412.6 11.7 %all_gather.19.grad_rows = bf16[512,768]{1,0:T(8,128)(2,1)S(1)} all-gather(bf16[128,768]{1,0:T(8,128)(2,1)S(1)} %convert_element_type.392), channel_id=1, replica_groups=mesh['pipe'=2,'z'=4,'q'=1,'h'=2,'tp'=2] {'h','pipe'}, dimensions={0}, use_global_device_ids=true | all-gather | bytes 983040 | tf_op jit(solution)/shard_map/all_gather | solution.py:493
  424.3 4.5 shard_map.210
  432.1 1.7 shard_map.211
  435.0 3.5 all-to-all-start.11
  442.0 7.9 %all-to-all-done.11 = bf16[4,128,768]{2,1,0:T(8,128)(2,1)S(1)} async-done(((bf16[4,128,768]{2,1,0:T(8,128)(2,1)}), bf16[4,128,768]{2,1,0:T(8,128)(2,1)S(1)}, u32[]{:S(2)}, u32[]{:S(2)}) %all-to-all-start.11) | async-done | bytes 786464 | tf_op jit(solution)/shard_map/all_to_all | solution.py:51
  452.6 2.7 collective-permute-start.29
  459.9 6.6 %collective-permute-done.29 = bf16[2,48,768]{2,1,0:T(8,128)(2,1)S(1)} collective-permute-done((bf16[2,48,768]{2,1,0:T(8,128)(2,1)S(1)}, bf16[2,48,768]{2,1,0:T(8,128)(2,1)S(1)}, u32[]{:S(2)}, u32[]{:S(2)}) %collective-permute-start.29) | collective-permute-done | bytes 147488 | tf_op jit(solution)/shard_map/ppermute | solution.py:168
  467.2 2.4 collective-permute-start.33
  469.6 2.1 collective-permute-start.31
  472.4 3.5 all-to-all-start.12
  475.9 7.0 %collective-permute-done.31 = bf16[144,768]{1,0:T(8,128)(2,1)S(1)} collective-permute-done((bf16[144,768]{1,0:T(8,128)(2,1)S(1)}, bf16[144,768]{1,0:T(8,128)(2,1)S(1)}, u32[]{:S(2)}, u32[]{:S(2)}) %collective-permute-start.31) | collective-permute-done | bytes 221216 | tf_op jit(solution)/shard_map/ppermute | solution.py:95
  482.9 6.4 %collective-permute-done.32 = bf16[144,768]{1,0:T(8,128)(2,1)S(1)} collective-permute-done((bf16[144,768]{1,0:T(8,128)(2,1)S(1)}, bf16[144,768]{1,0:T(8,128)(2,1)S(1)}, u32[]{:S(2)}, u32[]{:S(2)}) %collective-permute-start.32) | collective-permute-done | bytes 221216 | tf_op jit(solution)/shard_map/ppermute | solution.py:95
  490.4 4.3 all-to-all-start.13
  495.7 2.9 all-to-all-done.13
  (485 shorter events, 97.5 us)
Async XLA Ops:
  7.2 102.9 %all-gather.3.cloned.1.call-start = ((), (), s32[]{:S(2)}) async-start(), calls=%async_computation.16 | async-start | bytes 1548288 | tf_op jit(solution)/shard_map/all_gather | solution.py:150
  8.0 9.2 %collective-permute-start = (bf16[4,64]{1,0:T(4,128)(2,1)S(1)}, bf16[4,64]{1,0:T(4,128)(2,1)S(1)}, u32[]{:S(2)}, u32[]{:S(2)}) collective-permute-start(bf16[4,64]{1,0:T(4,128)(2,1)S(1)} %dynamic-slice_convert_fusion), channel_id=1, source_target_pairs={{0,16},{16,0},{1,17},{17,1},{2,18},{18,2},{3,19},{19,3},{4,20},{20... | collective-permute-start | bytes 1544 | tf_op jit(solution)/shard_map/ppermute | solution.py:40
  16.9 9.9 %collective-permute-start.4 = (bf16[2,48,4,192]{3,2,1,0:T(4,128)(2,1)S(1)}, bf16[2,48,4,192]{3,2,1,0:T(4,128)(2,1)}, u32[]{:S(2)}, u32[]{:S(2)}) collective-permute-start(bf16[2,48,4,192]{3,2,1,0:T(4,128)(2,1)S(1)} %dynamic-slice_bitcast_fusion.1), channel_id=1, source_target_pairs={{0,1},{1,0},{2,3},{3,2},{4,5},{5,4},{6,7},{7,6},{8,9},{9,8},{10,11... | collective-permute-start | bytes 442376 | tf_op jit(solution)/shard_map/ppermute | solution.py:40
  17.5 11.1 %collective-permute-start.1 = (bf16[144,768]{1,0:T(8,128)(2,1)S(1)}, bf16[144,768]{1,0:T(8,128)(2,1)S(1)}, u32[]{:S(2)}, u32[]{:S(2)}) collective-permute-start(bf16[144,768]{1,0:T(8,128)(2,1)S(1)} %get-tuple-element.141), channel_id=1, source_target_pairs={{0,4},{8,12},{20,16},{28,24},{1,5},{9,13},{21,17},{29,25},{2,6},{1... | collective-permute-start | bytes 663560 | tf_op jit(solution)/shard_map/ppermute | solution.py:105
  21.0 11.1 %collective-permute-start.2 = (bf16[144,768]{1,0:T(8,128)(2,1)S(1)}, bf16[144,768]{1,0:T(8,128)(2,1)S(1)}, u32[]{:S(2)}, u32[]{:S(2)}) collective-permute-start(bf16[144,768]{1,0:T(8,128)(2,1)S(1)} %get-tuple-element.142), channel_id=1, source_target_pairs={{0,8},{8,0},{20,28},{28,20},{1,9},{9,1},{21,29},{29,21},{2,10},{10... | collective-permute-start | bytes 663560 | tf_op jit(solution)/shard_map/ppermute | solution.py:105
  25.5 10.3 %collective-permute-start.3 = (bf16[144,768]{1,0:T(8,128)(2,1)S(1)}, bf16[144,768]{1,0:T(8,128)(2,1)S(1)}, u32[]{:S(2)}, u32[]{:S(2)}) collective-permute-start(bf16[144,768]{1,0:T(8,128)(2,1)S(1)} %get-tuple-element.143), channel_id=1, source_target_pairs={{0,12},{8,4},{20,24},{28,16},{1,13},{9,5},{21,25},{29,17},{2,14},{... | collective-permute-start | bytes 663560 | tf_op jit(solution)/shard_map/ppermute | solution.py:105
  35.8 45.0 %copy-start.50 = (bf16[2,144,768]{2,1,0:T(8,128)(2,1)}, bf16[2,144,768]{2,1,0:T(8,128)(2,1)S(1)}, u32[]{:S(2)}) copy-start(bf16[2,144,768]{2,1,0:T(8,128)(2,1)S(1)} %maximum_select_fusion.1) | copy-start | bytes 1327108
  35.9 58.7 %copy-start.51 = (bf16[2,64,768]{2,1,0:T(8,128)(2,1)}, bf16[2,64,768]{2,1,0:T(8,128)(2,1)S(1)}, u32[]{:S(2)}) copy-start(bf16[2,64,768]{2,1,0:T(8,128)(2,1)S(1)} %get-tuple-element.166) | copy-start | bytes 589828
  78.4 2.1 collective-permute-start.5
  82.9 81.6 %copy-start.14 = (f32[128,768]{1,0:T(8,128)}, f32[128,768]{1,0:T(8,128)S(1)}, u32[]{:S(2)}) copy-start(f32[128,768]{1,0:T(8,128)S(1)} %get-tuple-element.56) | copy-start | bytes 1179652
  82.9 1.7 collective-permute-start.6
  90.0 19.0 %copy-start.43 = (bf16[2,64,768]{2,1,0:T(8,128)(2,1)S(1)}, bf16[2,64,768]{2,1,0:T(8,128)(2,1)}, u32[]{:S(2)}) copy-start(bf16[2,64,768]{2,1,0:T(8,128)(2,1)} %copy-done.42) | copy-start | bytes 589828
  90.0 15.8 %all-to-all-start.2 = ((bf16[4,128,768]{2,1,0:T(8,128)(2,1)}), bf16[4,128,768]{2,1,0:T(8,128)(2,1)}, u32[]{:S(2)}, u32[]{:S(2)}) async-start(bf16[4,128,768]{2,1,0:T(8,128)(2,1)} %bitcast.31), calls=%async_computation.2 | async-start | bytes 1572864 | tf_op jit(solution)/shard_map/all_to_all | solution.py:51
  107.1 66.7 %copy-start.38 = (f32[128,768]{1,0:T(8,128)}, f32[128,768]{1,0:T(8,128)S(1)}, u32[]{:S(2)}) copy-start(f32[128,768]{1,0:T(8,128)S(1)} %convert_reduce_fusion.3) | copy-start | bytes 1179652
  133.3 7.6 %collective-permute-start.8 = (bf16[8,24,768]{2,1,0:T(8,128)(2,1)S(1)}, bf16[8,24,768]{2,1,0:T(8,128)(2,1)S(1)}, u32[]{:S(2)}, u32[]{:S(2)}) collective-permute-start(bf16[8,24,768]{2,1,0:T(8,128)(2,1)S(1)} %get-tuple-element.158), channel_id=1, source_target_pairs={{0,16},{16,0},{1,17},{17,1},{2,18},{18,2},{3,19},{19,3},{4,20},{20... | collective-permute-start | bytes 884744 | tf_op jit(solution)/shard_map/ppermute | solution.py:40
  133.7 7.2 %collective-permute-start.7 = (bf16[8,24,768]{2,1,0:T(8,128)(2,1)S(1)}, bf16[8,24,768]{2,1,0:T(8,128)(2,1)S(1)}, u32[]{:S(2)}, u32[]{:S(2)}) collective-permute-start(bf16[8,24,768]{2,1,0:T(8,128)(2,1)S(1)} %get-tuple-element.157), channel_id=1, source_target_pairs={{0,1},{1,0},{2,3},{3,2},{4,5},{5,4},{6,7},{7,6},{8,9},{9,8},{10,11... | collective-permute-start | bytes 884744 | tf_op jit(solution)/shard_map/ppermute | solution.py:40
  140.9 1.6 collective-permute-start.9
  148.6 2.1 collective-permute-start.10
  150.7 8.8 %collective-permute-start.11 = (bf16[8,24,768]{2,1,0:T(8,128)(2,1)S(1)}, bf16[8,24,768]{2,1,0:T(8,128)(2,1)S(1)}, u32[]{:S(2)}, u32[]{:S(2)}) collective-permute-start(bf16[8,24,768]{2,1,0:T(8,128)(2,1)S(1)} %fusion.34), channel_id=1, source_target_pairs={{0,16},{1,17},{2,18},{3,19},{4,20},{5,21},{6,22},{7,23},{8,24},{9,... | collective-permute-start | bytes 884744 | tf_op jit(solution)/shard_map/ppermute | solution.py:239
  160.4 13.4 %all-to-all-start.4 = ((bf16[8,24,768]{2,1,0:T(8,128)(2,1)}), bf16[8,24,768]{2,1,0:T(8,128)(2,1)}, u32[]{:S(2)}, u32[]{:S(2)}) async-start(bf16[8,24,768]{2,1,0:T(8,128)(2,1)} %fusion.57), calls=%async_computation.4 | async-start | bytes 589824 | tf_op jit(solution)/shard_map/all_to_all | solution.py:51
  192.1 52.4 %copy-start.15 = (f32[128,768]{1,0:T(8,128)}, f32[128,768]{1,0:T(8,128)S(1)}, u32[]{:S(2)}) copy-start(f32[128,768]{1,0:T(8,128)S(1)} %get-tuple-element.63.small) | copy-start | bytes 1179652
  192.1 1.7 collective-permute-start.12
  199.8 15.7 %all-to-all-start.5 = ((bf16[4,128,768]{2,1,0:T(8,128)(2,1)}), bf16[4,128,768]{2,1,0:T(8,128)(2,1)}, u32[]{:S(2)}, u32[]{:S(2)}) async-start(bf16[4,128,768]{2,1,0:T(8,128)(2,1)} %bitcast.59), calls=%async_computation.5 | async-start | bytes 1572864 | tf_op jit(solution)/shard_map/all_to_all | solution.py:51
  217.8 76.5 %copy-start.40 = (f32[128,768]{1,0:T(8,128)}, f32[128,768]{1,0:T(8,128)S(1)}, u32[]{:S(2)}) copy-start(f32[128,768]{1,0:T(8,128)S(1)} %get-tuple-element.125) | copy-start | bytes 1179652
  233.7 7.5 %collective-permute-start.14 = (bf16[8,24,768]{2,1,0:T(8,128)(2,1)}, bf16[8,24,768]{2,1,0:T(8,128)(2,1)}, u32[]{:S(2)}, u32[]{:S(2)}) collective-permute-start(bf16[8,24,768]{2,1,0:T(8,128)(2,1)} %all_to_all.73), channel_id=1, source_target_pairs={{0,16},{1,17},{2,18},{3,19},{4,20},{5,21},{6,22},{7,23},{8,24},{9,... | collective-permute-start | bytes 884744 | tf_op jit(solution)/shard_map/ppermute | solution.py:218
  237.5 3.7 collective-permute-start.13
  241.2 1.9 collective-permute-start.15
  244.5 16.8 %copy-start = (bf16[4,8,24,768]{3,2,1,0:T(8,128)(2,1)}, bf16[4,8,24,768]{3,2,1,0:T(8,128)(2,1)S(1)}, u32[]{:S(2)}) copy-start(bf16[4,8,24,768]{3,2,1,0:T(8,128)(2,1)S(1)} %pad_maximum_fusion.3) | copy-start | bytes 3538948
  263.4 29.9 %copy-start.79 = (f32[768]{0:T(1024)S(1)}, f32[768]{0:T(1024)}, u32[]{:S(2)}) copy-start(f32[768]{0:T(1024)} %get-tuple-element.110) | copy-start | bytes 9220
  263.4 29.9 %copy-start.96 = (s32[128]{0:T(128)S(1)}, s32[128]{0:T(128)}, u32[]{:S(2)}) copy-start(s32[128]{0:T(128)} %copy-done.95) | copy-start | bytes 1540
  263.4 29.9 %copy-start.107 = (f32[128]{0:T(128)S(1)}, f32[128]{0:T(128)}, u32[]{:S(2)}) copy-start(f32[128]{0:T(128)} %copy-done.106) | copy-start | bytes 1540
  263.5 30.9 %copy-start.52 = (bf16[2,64,768]{2,1,0:T(8,128)(2,1)S(1)}, bf16[2,64,768]{2,1,0:T(8,128)(2,1)}, u32[]{:S(2)}) copy-start(bf16[2,64,768]{2,1,0:T(8,128)(2,1)} %copy-done.51) | copy-start | bytes 589828
  263.5 30.8 %copy-start.122 = (f32[128]{0:T(128)S(1)}, f32[128]{0:T(128)}, u32[]{:S(2)}) copy-start(f32[128]{0:T(128)} %get-tuple-element.175) | copy-start | bytes 1540
  263.5 2.1 collective-permute-start.16
  266.5 11.4 %collective-permute-start.17 = (bf16[8,24,768]{2,1,0:T(8,128)(2,1)}, bf16[8,24,768]{2,1,0:T(8,128)(2,1)}, u32[]{:S(2)}, u32[]{:S(2)}) collective-permute-start(bf16[8,24,768]{2,1,0:T(8,128)(2,1)} %fusion.32), channel_id=1, source_target_pairs={{16,0},{17,1},{18,2},{19,3},{20,4},{21,5},{22,6},{23,7},{24,8},{25... | collective-permute-start | bytes 884744 | tf_op jit(solution)/shard_map/ppermute | solution.py:239
  311.1 1.8 collective-permute-start.18
  315.5 17.1 %copy-start.46 = (bf16[128,768]{1,0:T(8,128)(2,1)S(1)}, bf16[128,768]{1,0:T(8,128)(2,1)}, u32[]{:S(2)}) copy-start(bf16[128,768]{1,0:T(8,128)(2,1)} %copy-done.45) | copy-start | bytes 589828
  315.5 17.1 %copy-start.83 = (f32[768]{0:T(1024)S(1)}, f32[768]{0:T(1024)}, u32[]{:S(2)}) copy-start(f32[768]{0:T(1024)} %get-tuple-element.109) | copy-start | bytes 9220
  315.5 17.8 %copy-start.61 = (f32[128,768]{1,0:T(8,128)S(1)}, f32[128,768]{1,0:T(8,128)}, u32[]{:S(2)}) copy-start(f32[128,768]{1,0:T(8,128)} %get-tuple-element.181) | copy-start | bytes 1179652
  315.5 15.8 %all-to-all-start.8 = ((bf16[4,128,768]{2,1,0:T(8,128)(2,1)}), bf16[4,128,768]{2,1,0:T(8,128)(2,1)}, u32[]{:S(2)}, u32[]{:S(2)}) async-start(bf16[4,128,768]{2,1,0:T(8,128)(2,1)} %bitcast.314), calls=%async_computation.8 | async-start | bytes 1572864 | tf_op jit(solution)/shard_map/all_to_all | solution.py:51
  319.8 147.3 %reduce-scatter.2.cloned.1.call-start = ((), (), s32[]{:S(2)}) async-start(), calls=%async_computation.15 | async-start | bytes 1327104 | tf_op jit(solution)/shard_map/reduce_scatter | solution.py:177
  332.6 24.6 %copy-start.115 = (f32[2,64]{1,0:T(2,128)S(1)}, f32[2,64]{1,0:T(2,128)}, u32[]{:S(2)}) copy-start(f32[2,64]{1,0:T(2,128)} %get-tuple-element.103) | copy-start | bytes 1540
  335.1 31.4 %copy-start.47 = (bf16[128,768]{1,0:T(8,128)(2,1)}, bf16[128,768]{1,0:T(8,128)(2,1)S(1)}, u32[]{:S(2)}) copy-start(bf16[128,768]{1,0:T(8,128)(2,1)S(1)} %get-tuple-element.119) | copy-start | bytes 589828
  348.4 8.7 %collective-permute-start.20 = (bf16[8,24,768]{2,1,0:T(8,128)(2,1)S(1)}, bf16[8,24,768]{2,1,0:T(8,128)(2,1)S(1)}, u32[]{:S(2)}, u32[]{:S(2)}) collective-permute-start(bf16[8,24,768]{2,1,0:T(8,128)(2,1)S(1)} %all_to_all.75), channel_id=1, source_target_pairs={{16,0},{17,1},{18,2},{19,3},{20,4},{21,5},{22,6},{23,7},{24,8},{25... | collective-permute-start | bytes 884744 | tf_op jit(solution)/shard_map/ppermute | solution.py:216
  349.9 7.4 %collective-permute-start.19 = (bf16[8,24,768]{2,1,0:T(8,128)(2,1)S(1)}, bf16[8,24,768]{2,1,0:T(8,128)(2,1)S(1)}, u32[]{:S(2)}, u32[]{:S(2)}) collective-permute-start(bf16[8,24,768]{2,1,0:T(8,128)(2,1)S(1)} %all_to_all.75), channel_id=1, source_target_pairs={{0,1},{1,0},{2,3},{3,2},{4,5},{5,4},{6,7},{7,6},{8,9},{9,8},{10,11... | collective-permute-start | bytes 884744 | tf_op jit(solution)/shard_map/ppermute | solution.py:40
  357.1 1.7 collective-permute-start.21
  369.6 5.2 %collective-permute-start.22 = (bf16[2,8,24,768]{3,2,1,0:T(8,128)(2,1)}, bf16[2,8,24,768]{3,2,1,0:T(8,128)(2,1)}, u32[]{:S(2)}, u32[]{:S(2)}) collective-permute-start(bf16[2,8,24,768]{3,2,1,0:T(8,128)(2,1)} %slice_bitcast_fusion), channel_id=1, source_target_pairs={{0,1},{1,0},{2,3},{3,2},{4,5},{5,4},{6,7},{7,6},{8,9},{9,8},{10,11... | collective-permute-start | bytes 1769480 | tf_op jit(solution)/shard_map/ppermute | solution.py:40
  376.4 9.4 %collective-permute-start.23 = (bf16[8,24,768]{2,1,0:T(8,128)(2,1)S(1)}, bf16[8,24,768]{2,1,0:T(8,128)(2,1)S(1)}, u32[]{:S(2)}, u32[]{:S(2)}) collective-permute-start(bf16[8,24,768]{2,1,0:T(8,128)(2,1)S(1)} %get-tuple-element.127), channel_id=1, source_target_pairs={{0,16},{16,0},{1,17},{17,1},{2,18},{18,2},{3,19},{19,3},{4,20},{20... | collective-permute-start | bytes 884744 | tf_op jit(solution)/shard_map/ppermute | solution.py:40
  386.8 24.5 %all-to-all-start.10 = ((bf16[8,48,768]{2,1,0:T(8,128)(2,1)}), bf16[8,48,768]{2,1,0:T(8,128)(2,1)S(1)}, u32[]{:S(2)}, u32[]{:S(2)}) async-start(bf16[8,48,768]{2,1,0:T(8,128)(2,1)} %maximum_select_fusion), calls=%async_computation.10 | async-start | bytes 1179648 | tf_op jit(solution)/shard_map/all_to_all | solution.py:51
  428.8 3.3 collective-permute-start.25
  430.6 9.4 %collective-permute-start.24 = (bf16[128,768]{1,0:T(8,128)(2,1)}, bf16[128,768]{1,0:T(8,128)(2,1)S(1)}, u32[]{:S(2)}, u32[]{:S(2)}) collective-permute-start(bf16[128,768]{1,0:T(8,128)(2,1)} %get-tuple-element.114), channel_id=1, source_target_pairs={{0,16},{16,0},{1,17},{17,1},{2,18},{18,2},{3,19},{19,3},{4,20},{20... | collective-permute-start | bytes 589832 | tf_op jit(solution)/shard_map/ppermute | solution.py:40
  435.0 15.0 %all-to-all-start.11 = ((bf16[4,128,768]{2,1,0:T(8,128)(2,1)}), bf16[4,128,768]{2,1,0:T(8,128)(2,1)S(1)}, u32[]{:S(2)}, u32[]{:S(2)}) async-start(bf16[4,128,768]{2,1,0:T(8,128)(2,1)} %bitcast.91), calls=%async_computation.11 | async-start | bytes 1572864 | tf_op jit(solution)/shard_map/all_to_all | solution.py:51
  440.0 17.2 %copy-start.86 = (f32[1,768]{1,0:T(1,128)}, f32[1,768]{1,0:T(1,128)S(1)}, u32[]{:S(2)}) copy-start(f32[1,768]{1,0:T(1,128)S(1)} %broadcast_in_dim.31) | copy-start | bytes 9220
  441.0 10.3 %collective-permute-start.27 = (bf16[8,48,768]{2,1,0:T(8,128)(2,1)}, bf16[8,48,768]{2,1,0:T(8,128)(2,1)}, u32[]{:S(2)}, u32[]{:S(2)}) collective-permute-start(bf16[8,48,768]{2,1,0:T(8,128)(2,1)} %dynamic-slice_bitcast_fusion), channel_id=1, source_target_pairs={{0,1},{1,0},{2,3},{3,2},{4,5},{5,4},{6,7},{7,6},{8,9},{9,8},{10,11... | collective-permute-start | bytes 1769480 | tf_op jit(solution)/shard_map/ppermute | solution.py:40
  452.6 7.4 %collective-permute-start.28 = (bf16[2,48,768]{2,1,0:T(8,128)(2,1)S(1)}, bf16[2,48,768]{2,1,0:T(8,128)(2,1)S(1)}, u32[]{:S(2)}, u32[]{:S(2)}) collective-permute-start(bf16[2,48,768]{2,1,0:T(8,128)(2,1)S(1)} %get-tuple-element.150), channel_id=1, source_target_pairs={{0,4},{4,0},{8,12},{12,8},{1,5},{5,1},{9,13},{13,9},{2,6},{6,2},{1... | collective-permute-start | bytes 442376 | tf_op jit(solution)/shard_map/ppermute | solution.py:168
  452.6 13.9 %collective-permute-start.29 = (bf16[2,48,768]{2,1,0:T(8,128)(2,1)S(1)}, bf16[2,48,768]{2,1,0:T(8,128)(2,1)S(1)}, u32[]{:S(2)}, u32[]{:S(2)}) collective-permute-start(bf16[2,48,768]{2,1,0:T(8,128)(2,1)S(1)} %get-tuple-element.151), channel_id=1, source_target_pairs={{0,8},{4,12},{8,0},{12,4},{1,9},{5,13},{9,1},{13,5},{2,10},{6,14},... | collective-permute-start | bytes 442376 | tf_op jit(solution)/shard_map/ppermute | solution.py:168
  455.3 11.2 %collective-permute-start.30 = (bf16[2,48,768]{2,1,0:T(8,128)(2,1)S(1)}, bf16[2,48,768]{2,1,0:T(8,128)(2,1)S(1)}, u32[]{:S(2)}, u32[]{:S(2)}) collective-permute-start(bf16[2,48,768]{2,1,0:T(8,128)(2,1)S(1)} %get-tuple-element.152), channel_id=1, source_target_pairs={{0,12},{4,8},{8,4},{12,0},{1,13},{5,9},{9,5},{13,1},{2,14},{6,10},... | collective-permute-start | bytes 442376 | tf_op jit(solution)/shard_map/ppermute | solution.py:168
  457.4 9.3 %collective-permute-start.26 = (bf16[144,768]{1,0:T(8,128)(2,1)S(1)}, bf16[144,768]{1,0:T(8,128)(2,1)S(1)}, u32[]{:S(2)}, u32[]{:S(2)}) collective-permute-start(bf16[144,768]{1,0:T(8,128)(2,1)S(1)} %pad_maximum_fusion.12), channel_id=1, source_target_pairs={{0,16},{16,0},{1,17},{17,1},{2,18},{18,2},{3,19},{19,3},{4,20},{20... | collective-permute-start | bytes 663560 | tf_op jit(solution)/shard_map/ppermute | solution.py:40
  467.2 8.7 %collective-permute-start.33 = (bf16[144,768]{1,0:T(8,128)(2,1)S(1)}, bf16[144,768]{1,0:T(8,128)(2,1)S(1)}, u32[]{:S(2)}, u32[]{:S(2)}) collective-permute-start(bf16[144,768]{1,0:T(8,128)(2,1)S(1)} %get-tuple-element.136), channel_id=1, source_target_pairs={{0,4},{4,0},{8,12},{12,8},{1,5},{5,1},{9,13},{13,9},{2,6},{6,2},{1... | collective-permute-start | bytes 663560 | tf_op jit(solution)/shard_map/ppermute | solution.py:95
  469.6 13.3 %collective-permute-start.31 = (bf16[144,768]{1,0:T(8,128)(2,1)S(1)}, bf16[144,768]{1,0:T(8,128)(2,1)S(1)}, u32[]{:S(2)}, u32[]{:S(2)}) collective-permute-start(bf16[144,768]{1,0:T(8,128)(2,1)S(1)} %get-tuple-element.137), channel_id=1, source_target_pairs={{0,12},{4,8},{8,4},{12,0},{1,13},{5,9},{9,5},{13,1},{2,14},{6,10},... | collective-permute-start | bytes 663560 | tf_op jit(solution)/shard_map/ppermute | solution.py:95
  471.7 17.6 %collective-permute-start.32 = (bf16[144,768]{1,0:T(8,128)(2,1)S(1)}, bf16[144,768]{1,0:T(8,128)(2,1)S(1)}, u32[]{:S(2)}, u32[]{:S(2)}) collective-permute-start(bf16[144,768]{1,0:T(8,128)(2,1)S(1)} %get-tuple-element.138), channel_id=1, source_target_pairs={{0,8},{4,12},{8,0},{12,4},{1,9},{5,13},{9,1},{13,5},{2,10},{6,14},... | collective-permute-start | bytes 663560 | tf_op jit(solution)/shard_map/ppermute | solution.py:95
  472.4 17.1 %all-to-all-start.12 = ((bf16[4,48,768]{2,1,0:T(8,128)(2,1)}), bf16[4,48,768]{2,1,0:T(8,128)(2,1)S(1)}, u32[]{:S(2)}, u32[]{:S(2)}) async-start(bf16[4,48,768]{2,1,0:T(8,128)(2,1)} %bitcast.117), calls=%async_computation.13 | async-start | bytes 589824 | tf_op jit(solution)/shard_map/all_to_all | solution.py:51
  489.6 10.2 %collective-permute-start.34 = (bf16[2,48,768]{2,1,0:T(8,128)(2,1)S(1)}, bf16[2,48,768]{2,1,0:T(8,128)(2,1)S(1)}, u32[]{:S(2)}, u32[]{:S(2)}) collective-permute-start(bf16[2,48,768]{2,1,0:T(8,128)(2,1)S(1)} %dynamic-slice_bitcast_fusion.2), channel_id=1, source_target_pairs={{0,1},{1,0},{2,3},{3,2},{4,5},{5,4},{6,7},{7,6},{8,9},{9,8},{10,11... | collective-permute-start | bytes 442376 | tf_op jit(solution)/shard_map/ppermute | solution.py:40
  490.4 8.1 %all-to-all-start.13 = ((bf16[4,2,384]{2,1,0:T(2,128)(2,1)}), bf16[4,2,384]{2,1,0:T(2,128)(2,1)S(1)}, u32[]{:S(2)}, u32[]{:S(2)}) async-start(bf16[4,2,384]{2,1,0:T(2,128)(2,1)} %reshape.593), calls=%async_computation.14 | async-start | bytes 12288 | tf_op jit(solution)/shard_map/all_to_all | solution.py:51
  (116 other events, 727.0 us)
Sparse Core Ops, SparseCore 0:
  80.9 21.8 all-gather.2
  374.9 34.6 reduce-scatter.1
